TPU v7x, 128 devices: a whole 4x4x4 slice. The times are simulated.
128 devices in a mesh: shard: 16 (over y_hi, z, core), rep: 8 (over y_lo, x).
Axes of the slice: x: 4, y: 4 (y_hi: 2, y_lo: 2; y = y_hi * 2 + y_lo), z: 4, core: 2. Of those that a mesh axis runs over, the one named last changes fastest.
Arguments:
- tokens: bfloat16 [32, 1024, 1024], P('shard', 'rep'), may hold values from -6 to 6
- cotangent: bfloat16 [32, 1024, 1024], P('shard', 'rep'), may hold values from -6 to 6
- routes: int32 [32, 1024, 8], P('shard', 'rep'), may hold values from 0 to 15, all different within a row; in each aligned block of 128 rows (0 to 127, 128 to 255, ..., all dimensions but the last counted through in order) at most 96 rows name the same one
- picture_starts: int32 [32, 2], P('shard'), may hold values from 0 to 768, as said below
- attn_gain: bfloat16 [1024], P('shard'), may hold values from 0.25 to 1.75
- query_weight: bfloat16 [1024, 1024], P('shard'), may hold values from -0.1875 to 0.1875
- key_weight: bfloat16 [1024, 512], P('shard'), may hold values from -0.1875 to 0.1875
- value_weight: bfloat16 [1024, 512], P('shard'), may hold values from -0.1875 to 0.1875
- query_gain: bfloat16 [1024], P('shard'), may hold values from 0.25 to 1.75
- key_gain: bfloat16 [512], P('shard'), may hold values from 0.25 to 1.75
- output_weight: bfloat16 [1024, 1024], P('shard'), may hold values from -2 to 2
- ffn_gain: bfloat16 [1024], P('shard'), may hold values from 0.25 to 1.75
- router_weight: bfloat16 [1024, 16], P('shard'), may hold values from -0.09375 to 0.09375
- expert_in: bfloat16 [16, 1024, 1024], P('shard'), may hold values from -0.1875 to 0.1875
- expert_down: bfloat16 [16, 512, 1024], P('shard'), may hold values from -1 to 1
Outputs:
- block_out: bfloat16 [32, 1024, 1024], P('shard', 'rep')
- tokens_grad: bfloat16 [32, 1024, 1024], P('shard', 'rep')
- attn_gain_grad: float32 [1024], P('shard')
- query_weight_grad: float32 [1024, 1024], P('shard')
- key_weight_grad: float32 [1024, 512], P('shard')
- value_weight_grad: float32 [1024, 512], P('shard')
- query_gain_grad: float32 [1024], P('shard')
- key_gain_grad: float32 [512], P('shard')
- output_weight_grad: float32 [1024, 1024], P('shard')
- ffn_gain_grad: float32 [1024], P('shard')
- router_weight_grad: float32 [1024, 16], P('shard')
- expert_in_grad: float32 [16, 1024, 1024], P('shard')
- expert_down_grad: float32 [16, 512, 1024], P('shard')
Inputs may be any that keep to these rules, and one draw needn't show every extreme that they name: `routes`: each token names 8 different experts. In each aligned block of 128 positions of a sequence (the rows of one device), no expert is named by more than 96 tokens; in some block one expert is named by exactly 96. `picture_starts`: each row holds 2 different multiples of 256 in rising order.
All inputs are finite; a program needn't handle non-finite values.
Results may differ from a plain program's by a relative error of at most 0.03.
Values may be sent and summed in bfloat16 or wider, within the bound.
A program may use at most 192 MiB of HBM per device.

v0:
```python
import jax
import jax.numpy as jnp
from jax import lax
from jax.sharding import PartitionSpec as P

HEADS = 16
KV_HEADS = 8
HEAD_DIM = 64
PIC = 256


norm_eps = 1e-06
rope_base = 10000.0
masked_score = -1e30


def rms_scale(values, gain):
    return values * lax.rsqrt(jnp.mean(values * values, axis=-1, keepdims=True) + norm_eps) * gain


def rotary_tables(positions, head_size):
    half_size = head_size // 2
    exponent = jnp.arange(half_size, dtype=jnp.float32) * (2.0 / head_size)
    frequency = rope_base ** (-exponent)
    angles = positions.astype(jnp.float32)[:, None] * frequency[None, :]
    cosine_table = jnp.concatenate([jnp.cos(angles), jnp.cos(angles)], axis=-1)
    sine_table = jnp.concatenate([jnp.sin(angles), jnp.sin(angles)], axis=-1)
    return (cosine_table, sine_table)


def rotate(values, cosine_table, sine_table):
    half_size = values.shape[-1] // 2
    turned = jnp.concatenate([-values[..., half_size:], values[..., :half_size]], axis=-1)
    return values * cosine_table[:, None, :] + turned * sine_table[:, None, :]


def piece_index(positions, starts):
    inside = (positions[:, None] >= starts[None, :]) & (positions[:, None] < starts[None, :] + PIC)
    labels = jnp.arange(1, starts.shape[0] + 1, dtype=jnp.int32)
    return jnp.sum(jnp.where(inside, labels[None, :], 0), axis=1) - 1


def allowed_mask(query_pos, key_pos, starts):
    query_piece = piece_index(query_pos, starts)
    key_piece = piece_index(key_pos, starts)
    causal = key_pos[None, :] <= query_pos[:, None]
    shared = (query_piece[:, None] == key_piece[None, :]) & (query_piece[:, None] >= 0)
    return causal | shared


def query_key(query_raw, key_raw, query_gain, key_gain, cosine_table, sine_table):
    row_count = query_raw.shape[0]
    query_rot = rotate(
        rms_scale(query_raw, query_gain).reshape(row_count, HEADS, HEAD_DIM),
        cosine_table,
        sine_table,
    )
    key_rot = rotate(
        rms_scale(key_raw, key_gain).reshape(row_count, KV_HEADS, HEAD_DIM),
        cosine_table,
        sine_table,
    )
    return (query_rot, key_rot)


def rounded(values):
    return lax.optimization_barrier(values.astype(jnp.bfloat16)).astype(jnp.float32)


def swiglu(gate_up, hidden_width):
    return jax.nn.silu(gate_up[..., :hidden_width]) * gate_up[..., hidden_width:]


def swiglu_grad(gate_up, grad_hidden, hidden_width):
    gate_part = gate_up[..., :hidden_width]
    up_part = gate_up[..., hidden_width:]
    sigmoid = jax.nn.sigmoid(gate_part)
    grad_gate = grad_hidden * up_part * sigmoid * (1.0 + gate_part * (1.0 - sigmoid))
    return jnp.concatenate([grad_gate, grad_hidden * gate_part * sigmoid], axis=-1)


def route_slots(route_ids, experts, capacity):
    flat_ids = route_ids.reshape(-1)
    assign_count = flat_ids.shape[0]
    expert_picks = (flat_ids[:, None] == jnp.arange(experts, dtype=jnp.int32)[None, :]).astype(
        jnp.int32
    )
    before = jnp.cumsum(expert_picks, axis=0) - expert_picks
    slot_rank = jnp.sum(before * expert_picks, axis=1)
    slot_index = flat_ids * capacity + slot_rank
    slot_source = (
        jnp.full((experts * capacity,), assign_count, jnp.int32)
        .at[slot_index]
        .set(jnp.arange(assign_count, dtype=jnp.int32))
    )
    return (slot_index, slot_source)


def slot_grads(gate_probs, grad_out, slot_source, experts, capacity):
    row_count, top_count = gate_probs.shape
    model_width = grad_out.shape[1]
    grad_assigned = (
        (gate_probs[:, :, None] * grad_out[:, None, :])
        .astype(jnp.bfloat16)
        .reshape(row_count * top_count, model_width)
    )
    grad_padded = jnp.concatenate(
        [grad_assigned, jnp.zeros((1, model_width), jnp.bfloat16)], axis=0
    )
    return grad_padded[slot_source].reshape(experts, capacity, model_width)


def attention_scores(query_low, keys_all, allowed, score_scale):
    scores = (
        jnp.einsum("qkgd,skd->kgqs", query_low, keys_all, preferred_element_type=jnp.float32)
        * score_scale
    )
    return jnp.where(allowed[None, None], scores, masked_score)


def expert_forward(rows_in, inner, outer, hidden_width):
    gate_up = jnp.einsum("ecd,edf->ecf", rows_in, inner, preferred_element_type=jnp.float32)
    hidden_low = swiglu(gate_up, hidden_width).astype(jnp.bfloat16)
    expert_out = jnp.einsum("ecf,efd->ecd", hidden_low, outer, preferred_element_type=jnp.float32)
    return (gate_up, hidden_low, expert_out)


def expert_backward(gate_up, grad_out_low, inner, outer, hidden_width):
    grad_hidden = jnp.einsum(
        "ecd,efd->ecf", grad_out_low, outer, preferred_element_type=jnp.float32
    )
    grad_gate_up = swiglu_grad(gate_up, grad_hidden, hidden_width).astype(jnp.bfloat16)
    grad_rows = jnp.einsum("ecf,edf->ecd", grad_gate_up, inner, preferred_element_type=jnp.float32)
    return (grad_gate_up, grad_rows)


def full_zeros(local, shard_count):
    return jnp.zeros((local.shape[0] * shard_count,) + local.shape[1:], jnp.float32)


def add_terms(totals, terms):
    return tuple((running + term for running, term in zip(totals, terms)))


def shards(
    tokens,
    cotangent,
    routes,
    picture_starts,
    attn_gain,
    query_weight,
    key_weight,
    value_weight,
    query_gain,
    key_gain,
    output_weight,
    ffn_gain,
    router_weight,
    expert_in,
    expert_down,
):
    micro_count, row_count, model_width = tokens.shape
    top_count = routes.shape[2]
    shard_count = lax.axis_size("shard")
    rep_count = lax.axis_size("rep")
    length = row_count * rep_count
    experts_local = expert_in.shape[0]
    experts = experts_local * shard_count
    hidden_width = expert_down.shape[1]
    capacity = max(2, 3 * row_count * top_count // (2 * experts))
    group_size = HEADS // KV_HEADS
    kv_width = KV_HEADS * HEAD_DIM
    score_scale = HEAD_DIM ** (-0.5)
    query_pos = lax.axis_index("rep") * row_count + jnp.arange(row_count, dtype=jnp.int32)
    key_pos = jnp.arange(length, dtype=jnp.int32)
    cosine_table, sine_table = rotary_tables(query_pos, HEAD_DIM)
    dense_local = (
        attn_gain,
        query_weight,
        key_weight,
        value_weight,
        query_gain,
        key_gain,
        output_weight,
        ffn_gain,
        router_weight,
    )
    inner_total = jnp.zeros(expert_in.shape, jnp.float32)
    outer_total = jnp.zeros(expert_down.shape, jnp.float32)
    kept_state = []
    block_outs = []
    for batch_index in range(micro_count):
        dense_full = (
            lax.all_gather(attn_gain, "shard", axis=0, tiled=True),
            lax.all_gather(query_weight, "shard", axis=0, tiled=True),
            lax.all_gather(key_weight, "shard", axis=0, tiled=True),
            lax.all_gather(value_weight, "shard", axis=0, tiled=True),
            lax.all_gather(query_gain, "shard", axis=0, tiled=True),
            lax.all_gather(key_gain, "shard", axis=0, tiled=True),
            lax.all_gather(output_weight, "shard", axis=0, tiled=True),
            lax.all_gather(ffn_gain, "shard", axis=0, tiled=True),
            lax.all_gather(router_weight, "shard", axis=0, tiled=True),
        )
        gain_a, weight_q, weight_k, weight_v, gain_q, gain_k, weight_o, gain_f, weight_r = (
            dense_full
        )
        inputs = tokens[batch_index].astype(jnp.float32)
        attn_in = rms_scale(inputs, gain_a.astype(jnp.float32)).astype(jnp.bfloat16)
        query_raw = jnp.dot(attn_in, weight_q, preferred_element_type=jnp.float32)
        key_raw = jnp.dot(attn_in, weight_k, preferred_element_type=jnp.float32)
        value_low = jnp.dot(attn_in, weight_v, preferred_element_type=jnp.float32).astype(
            jnp.bfloat16
        )
        query_rot, key_rot = query_key(
            query_raw,
            key_raw,
            gain_q.astype(jnp.float32),
            gain_k.astype(jnp.float32),
            cosine_table,
            sine_table,
        )
        query_low = query_rot.astype(jnp.bfloat16).reshape(
            row_count, KV_HEADS, group_size, HEAD_DIM
        )
        key_low = key_rot.astype(jnp.bfloat16).reshape(row_count, kv_width)
        keys_all, values_all = (
            lax.all_gather(key_low, "rep", axis=0, tiled=True),
            lax.all_gather(value_low, "rep", axis=0, tiled=True),
        )
        keys_all = keys_all.reshape(length, KV_HEADS, HEAD_DIM)
        values_all = values_all.reshape(length, KV_HEADS, HEAD_DIM)
        allowed = allowed_mask(query_pos, key_pos, picture_starts[batch_index])
        scores = attention_scores(query_low, keys_all, allowed, score_scale)
        row_top = jnp.max(scores, axis=-1, keepdims=True)
        exponent = jnp.exp(scores - row_top)
        row_total = jnp.sum(exponent, axis=-1, keepdims=True)
        soft_low = (exponent / row_total).astype(jnp.bfloat16)
        log_total = row_top + jnp.log(row_total)
        mixed_low = (
            jnp.einsum("kgqs,skd->qkgd", soft_low, values_all, preferred_element_type=jnp.float32)
            .reshape(row_count, HEADS * HEAD_DIM)
            .astype(jnp.bfloat16)
        )
        middle = inputs + jnp.dot(mixed_low, weight_o, preferred_element_type=jnp.float32)
        ffn_in = rms_scale(middle, gain_f.astype(jnp.float32)).astype(jnp.bfloat16)
        logits = jnp.dot(ffn_in, weight_r, preferred_element_type=jnp.float32)
        route_ids = routes[batch_index]
        gate_probs = jax.nn.softmax(jnp.take_along_axis(logits, route_ids, axis=1), axis=-1)
        slot_index, slot_source = route_slots(route_ids, experts, capacity)
        padded = jnp.concatenate([ffn_in, jnp.zeros((1, model_width), jnp.bfloat16)], axis=0)
        dispatched = padded[slot_source // top_count].reshape(experts, capacity, model_width)
        received = lax.all_to_all(dispatched, "shard", split_axis=0, concat_axis=1, tiled=True)
        gate_up, hidden_low, expert_out = expert_forward(
            received, expert_in, expert_down, hidden_width
        )
        returned = lax.all_to_all(
            expert_out.astype(jnp.bfloat16), "shard", split_axis=1, concat_axis=0, tiled=True
        )
        expert_keep = (received, gate_up)
        assigned = returned.reshape(experts * capacity, model_width)[slot_index].reshape(
            row_count, top_count, model_width
        )
        result = middle + jnp.einsum(
            "tk,tkd->td", gate_probs, assigned, preferred_element_type=jnp.float32
        )
        block_outs.append(result.astype(jnp.bfloat16))
        kept_state.append(
            (
                inputs,
                attn_in,
                query_raw,
                key_raw,
                query_low,
                keys_all,
                values_all,
                allowed,
                log_total,
                mixed_low,
                middle,
                ffn_in,
                route_ids,
                gate_probs,
                slot_index,
                slot_source,
                assigned,
                expert_keep,
            )
        )
    dense_totals = tuple((full_zeros(local, shard_count) for local in dense_local))
    input_grads = []
    for batch_index in range(micro_count):
        (
            inputs,
            attn_in,
            query_raw,
            key_raw,
            query_low,
            keys_all,
            values_all,
            allowed,
            log_total,
            mixed_low,
            middle,
            ffn_in,
            route_ids,
            gate_probs,
            slot_index,
            slot_source,
            assigned,
            expert_keep,
        ) = kept_state[batch_index]
        dense_full = (
            lax.all_gather(attn_gain, "shard", axis=0, tiled=True),
            lax.all_gather(query_weight, "shard", axis=0, tiled=True),
            lax.all_gather(key_weight, "shard", axis=0, tiled=True),
            lax.all_gather(value_weight, "shard", axis=0, tiled=True),
            lax.all_gather(query_gain, "shard", axis=0, tiled=True),
            lax.all_gather(key_gain, "shard", axis=0, tiled=True),
            lax.all_gather(output_weight, "shard", axis=0, tiled=True),
            lax.all_gather(ffn_gain, "shard", axis=0, tiled=True),
            lax.all_gather(router_weight, "shard", axis=0, tiled=True),
        )
        gain_a, weight_q, weight_k, weight_v, gain_q, gain_k, weight_o, gain_f, weight_r = (
            dense_full
        )
        grad_out = cotangent[batch_index].astype(jnp.float32)
        grad_gates = jnp.einsum(
            "tkd,td->tk", assigned, grad_out, preferred_element_type=jnp.float32
        )
        grad_chosen = gate_probs * (
            grad_gates - jnp.sum(gate_probs * grad_gates, axis=-1, keepdims=True)
        )
        expert_picks = (
            route_ids[:, :, None] == jnp.arange(experts, dtype=jnp.int32)[None, None, :]
        ).astype(jnp.float32)
        grad_logits = jnp.einsum("tk,tke->te", grad_chosen, expert_picks).astype(jnp.bfloat16)
        grad_router = jnp.einsum(
            "td,te->de", ffn_in, grad_logits, preferred_element_type=jnp.float32
        )
        grad_ffn_in = jnp.einsum(
            "te,de->td", grad_logits, weight_r, preferred_element_type=jnp.float32
        )
        grad_slots = slot_grads(gate_probs, grad_out, slot_source, experts, capacity)
        received, gate_up = expert_keep
        grad_received = lax.all_to_all(grad_slots, "shard", split_axis=0, concat_axis=1, tiled=True)
        hidden_low = swiglu(gate_up, hidden_width).astype(jnp.bfloat16)
        grad_gate_up, grad_rows = expert_backward(
            gate_up, grad_received, expert_in, expert_down, hidden_width
        )
        inner_total = inner_total + jnp.einsum(
            "ecd,ecf->edf", received, grad_gate_up, preferred_element_type=jnp.float32
        )
        outer_total = outer_total + jnp.einsum(
            "ecf,ecd->efd", hidden_low, grad_received, preferred_element_type=jnp.float32
        )
        grad_returned = lax.all_to_all(
            grad_rows.astype(jnp.bfloat16), "shard", split_axis=1, concat_axis=0, tiled=True
        )
        grad_tokens = grad_returned.reshape(experts * capacity, model_width)[slot_index].reshape(
            row_count, top_count, model_width
        )
        grad_ffn_in = grad_ffn_in + jnp.sum(grad_tokens, axis=1, dtype=jnp.float32)
        norm_value, norm_pull = jax.vjp(rms_scale, middle, gain_f.astype(jnp.float32))
        grad_middle_part, grad_gain_f = norm_pull(grad_ffn_in)
        grad_middle = grad_out + grad_middle_part
        grad_attn = grad_middle.astype(jnp.bfloat16)
        grad_weight_o = jnp.einsum(
            "tq,td->qd", mixed_low, grad_attn, preferred_element_type=jnp.float32
        )
        grad_mixed = (
            jnp.einsum("td,qd->tq", grad_attn, weight_o, preferred_element_type=jnp.float32)
            .astype(jnp.bfloat16)
            .reshape(row_count, KV_HEADS, group_size, HEAD_DIM)
        )
        scores = attention_scores(query_low, keys_all, allowed, score_scale)
        soft_full = jnp.exp(scores - log_total)
        grad_soft = jnp.einsum(
            "qkgd,skd->kgqs", grad_mixed, values_all, preferred_element_type=jnp.float32
        )
        grad_values = jnp.einsum(
            "kgqs,qkgd->skd",
            soft_full.astype(jnp.bfloat16),
            grad_mixed,
            preferred_element_type=jnp.float32,
        )
        grad_scores = (
            soft_full * (grad_soft - jnp.sum(soft_full * grad_soft, axis=-1, keepdims=True))
        ).astype(jnp.bfloat16)
        grad_query_rot = (
            jnp.einsum("kgqs,skd->qkgd", grad_scores, keys_all, preferred_element_type=jnp.float32)
            * score_scale
        )
        grad_keys = (
            jnp.einsum("kgqs,qkgd->skd", grad_scores, query_low, preferred_element_type=jnp.float32)
            * score_scale
        )
        grad_key_own, grad_value_own = (
            lax.psum_scatter(
                grad_keys.reshape(length, kv_width).astype(jnp.bfloat16),
                "rep",
                scatter_dimension=0,
                tiled=True,
            ).astype(jnp.float32),
            lax.psum_scatter(
                grad_values.reshape(length, kv_width).astype(jnp.bfloat16),
                "rep",
                scatter_dimension=0,
                tiled=True,
            ).astype(jnp.float32),
        )
        grad_query_rot = rounded(grad_query_rot.reshape(row_count, HEADS, HEAD_DIM))
        grad_key_rot = rounded(grad_key_own.reshape(row_count, KV_HEADS, HEAD_DIM))
        grad_value_low = grad_value_own.astype(jnp.bfloat16)

        def turned_pair(query_in, key_in, query_scale, key_scale):
            return query_key(query_in, key_in, query_scale, key_scale, cosine_table, sine_table)

        pair_value, pair_pull = jax.vjp(
            turned_pair, query_raw, key_raw, gain_q.astype(jnp.float32), gain_k.astype(jnp.float32)
        )
        grad_query_raw, grad_key_raw, grad_gain_q, grad_gain_k = pair_pull(
            (grad_query_rot, grad_key_rot)
        )
        grad_query_low = grad_query_raw.astype(jnp.bfloat16)
        grad_key_low = grad_key_raw.astype(jnp.bfloat16)
        grad_weight_q = jnp.einsum(
            "td,tq->dq", attn_in, grad_query_low, preferred_element_type=jnp.float32
        )
        grad_weight_k = jnp.einsum(
            "td,tq->dq", attn_in, grad_key_low, preferred_element_type=jnp.float32
        )
        grad_weight_v = jnp.einsum(
            "td,tq->dq", attn_in, grad_value_low, preferred_element_type=jnp.float32
        )
        grad_attn_in = jnp.einsum(
            "tq,dq->td", grad_query_low, weight_q, preferred_element_type=jnp.float32
        )
        grad_attn_in = grad_attn_in + jnp.einsum(
            "tq,dq->td", grad_key_low, weight_k, preferred_element_type=jnp.float32
        )
        grad_attn_in = grad_attn_in + jnp.einsum(
            "tq,dq->td", grad_value_low, weight_v, preferred_element_type=jnp.float32
        )
        norm_value, norm_pull = jax.vjp(rms_scale, inputs, gain_a.astype(jnp.float32))
        grad_inputs_part, grad_gain_a = norm_pull(grad_attn_in)
        input_grads.append((grad_middle + grad_inputs_part).astype(jnp.bfloat16))
        dense_totals = add_terms(
            dense_totals,
            (
                grad_gain_a,
                grad_weight_q,
                grad_weight_k,
                grad_weight_v,
                grad_gain_q,
                grad_gain_k,
                grad_weight_o,
                grad_gain_f,
                grad_router,
            ),
        )
    (
        total_gain_a,
        total_query,
        total_key,
        total_value,
        total_gain_q,
        total_gain_k,
        total_output,
        total_gain_f,
        total_router,
    ) = dense_totals
    dense_own = (
        lax.psum_scatter(
            total_gain_a.astype(jnp.bfloat16), "shard", scatter_dimension=0, tiled=True
        ).astype(jnp.float32),
        lax.psum_scatter(
            total_query.astype(jnp.bfloat16), "shard", scatter_dimension=0, tiled=True
        ).astype(jnp.float32),
        lax.psum_scatter(
            total_key.astype(jnp.bfloat16), "shard", scatter_dimension=0, tiled=True
        ).astype(jnp.float32),
        lax.psum_scatter(
            total_value.astype(jnp.bfloat16), "shard", scatter_dimension=0, tiled=True
        ).astype(jnp.float32),
        lax.psum_scatter(
            total_gain_q.astype(jnp.bfloat16), "shard", scatter_dimension=0, tiled=True
        ).astype(jnp.float32),
        lax.psum_scatter(
            total_gain_k.astype(jnp.bfloat16), "shard", scatter_dimension=0, tiled=True
        ).astype(jnp.float32),
        lax.psum_scatter(
            total_output.astype(jnp.bfloat16), "shard", scatter_dimension=0, tiled=True
        ).astype(jnp.float32),
        lax.psum_scatter(
            total_gain_f.astype(jnp.bfloat16), "shard", scatter_dimension=0, tiled=True
        ).astype(jnp.float32),
        lax.psum_scatter(
            total_router.astype(jnp.bfloat16), "shard", scatter_dimension=0, tiled=True
        ).astype(jnp.float32),
    )
    (
        own_gain_a,
        own_query,
        own_key,
        own_value,
        own_gain_q,
        own_gain_k,
        own_output,
        own_gain_f,
        own_router,
    ) = dense_own
    summed = (
        lax.psum(own_gain_a.astype(jnp.bfloat16), "rep").astype(jnp.float32),
        lax.psum(own_query.astype(jnp.bfloat16), "rep").astype(jnp.float32),
        lax.psum(own_key.astype(jnp.bfloat16), "rep").astype(jnp.float32),
        lax.psum(own_value.astype(jnp.bfloat16), "rep").astype(jnp.float32),
        lax.psum(own_gain_q.astype(jnp.bfloat16), "rep").astype(jnp.float32),
        lax.psum(own_gain_k.astype(jnp.bfloat16), "rep").astype(jnp.float32),
        lax.psum(own_output.astype(jnp.bfloat16), "rep").astype(jnp.float32),
        lax.psum(own_gain_f.astype(jnp.bfloat16), "rep").astype(jnp.float32),
        lax.psum(own_router.astype(jnp.bfloat16), "rep").astype(jnp.float32),
        lax.psum(inner_total.astype(jnp.bfloat16), "rep").astype(jnp.float32),
        lax.psum(outer_total.astype(jnp.bfloat16), "rep").astype(jnp.float32),
    )
    return (
        jnp.stack(block_outs),
        jnp.stack(input_grads),
        summed[0],
        summed[1],
        summed[2],
        summed[3],
        summed[4],
        summed[5],
        summed[6],
        summed[7],
        summed[8],
        summed[9],
        summed[10],
    )


def solution(mesh):
    in_specs = (
        P("shard", "rep", None),
        P("shard", "rep", None),
        P("shard", "rep", None),
        P("shard", None),
        P("shard"),
        P("shard", None),
        P("shard", None),
        P("shard", None),
        P("shard"),
        P("shard"),
        P("shard", None),
        P("shard"),
        P("shard", None),
        P("shard", None, None),
        P("shard", None, None),
    )
    out_specs = (
        P("shard", "rep", None),
        P("shard", "rep", None),
        P("shard"),
        P("shard", None),
        P("shard", None),
        P("shard", None),
        P("shard"),
        P("shard"),
        P("shard", None),
        P("shard"),
        P("shard", None),
        P("shard", None, None),
        P("shard", None, None),
    )
    return jax.shard_map(shards, mesh=mesh, in_specs=in_specs, out_specs=out_specs, check_vma=False)
```

profile of v0, /device:TPU:0, one launch (start us, length us, event | category | flops | bytes accessed | tf_op | source)
XLA Modules:
  0.0 1767.4 jit_solution(5515855261207505245)
XLA Ops:
  14.7 40.6 %all-reduce.21 = (bf16[1024]{0:T(1024)(128)(2,1)S(1)}, bf16[512]{0:T(512)(128)(2,1)S(1)}, bf16[1024]{0:T(1024)(128)(2,1)}, bf16[1024]{0:T(1024)(128)(2,1)}) all-reduce(bf16[1024]{0:T(1024)(128)(2,1)S(1)} %dynamic-update-slice, bf16[512]{0:T(512)(128)(2,1)S(1)} %dynamic-update-slice.1, ...), channel_id=1, replica_groups=mesh['shard'=16,'rep'=8] {'shard'}, use_global_device_ids=true, to_apply=%add.12 | all-reduce | flops 3584 | bytes 14336
  60.7 43.4 %all-gather.14.cloned.1.call-done = bf16[1024,512]{1,0:T(8,128)(2,1)} async-done(((bf16[64,512]{1,0:T(8,128)(2,1)}), bf16[1024,512]{1,0:T(8,128)(2,1)}) %all-gather.14.cloned.1.call-update) | async-done | bytes 1048592 | tf_op jit(solution)/shard_map/all_gather | solution.py:196
  131.3 12.7 all-gather.12.cloned.1.call-done
  146.3 37.8 %all-gather.16.cloned.1.call-done = bf16[1024,512]{1,0:T(8,128)(2,1)} async-done(((bf16[128,512]{1,0:T(8,128)(2,1)}), bf16[1024,512]{1,0:T(8,128)(2,1)}) %all-gather.16.cloned.1.call-update) | async-done | bytes 1048592 | tf_op jit(solution)/shard_map/all_gather | solution.py:227
  186.4 46.7 %all-gather.18.cloned.1.call-done = bf16[1024,1024]{1,0:T(8,128)(2,1)} async-done(((bf16[64,1024]{1,0:T(8,128)(2,1)}), bf16[1024,1024]{1,0:T(8,128)(2,1)}) %all-gather.18.cloned.1.call-update) | async-done | bytes 2097168 | tf_op jit(solution)/shard_map/all_gather | solution.py:195
  251.8 30.0 %all-gather.20.cloned.1.call-done = bf16[1024,1024]{1,0:T(8,128)(2,1)} async-done(((bf16[64,1024]{1,0:T(8,128)(2,1)}), bf16[1024,1024]{1,0:T(8,128)(2,1)}) %all-gather.20.cloned.1.call-update) | async-done | bytes 2097168 | tf_op jit(solution)/shard_map/all_gather | solution.py:200
  290.7 44.5 %all_to_all.32 = bf16[16,96,1024]{2,1,0:T(8,128)(2,1)S(1)} all-to-all(bf16[16,96,1024]{2,1,0:T(8,128)(2,1)} %bitcast.507), channel_id=1, replica_groups=mesh['shard'=16,'rep'=8] {'shard'}, dimensions={0} | all-to-all | bytes 6291456 | tf_op jit(solution)/shard_map/all_to_all | solution.py:252
  343.4 21.7 %copy.309 = bf16[1,1536,1024]{2,0,1:T(2,128)(2,1)} copy(bf16[1,1536,1024]{2,1,0:T(8,128)(2,1)S(1)} %fusion.20) | data formatting | bytes 6291456 | tf_op jit(solution)/shard_map/convert_element_type | solution.py:257
  365.6 20.0 %reduce = bf16[1536,1024]{1,0:T(8,128)(2,1)} reduce(bf16[1536,1,1024]{2,1,0:T(2,128)(2,1)} %bitcast.494, bf16[]{:T(256)} %broadcast.797), dimensions={1}, to_apply=%bitcast.477.reduce_sub_computation | reduce | bytes 6291458
  397.6 56.4 %all-gather = bf16[16,64,16]{1,2,0:T(8,128)(2,1)S(1)} all-gather(bf16[1,64,16]{1,2,0:T(8,128)(2,1)S(1)} %bitcast.591), channel_id=1, replica_groups=mesh['shard'=16,'rep'=8] {'shard'}, dimensions={0}, use_global_device_ids=true | all-gather | bytes 34816 | tf_op jit(solution)/shard_map/all_gather | solution.py:202
  525.7 29.6 %all-gather.24.cloned.1.call-done = bf16[1024,512]{1,0:T(8,128)(2,1)} async-done(((bf16[128,512]{1,0:T(8,128)(2,1)}), bf16[1024,512]{1,0:T(8,128)(2,1)}) %all-gather.24.cloned.1.call-update) | async-done | bytes 1048592 | tf_op jit(solution)/shard_map/all_gather | solution.py:227
  572.4 21.7 %copy.307 = bf16[1,1536,1024]{2,0,1:T(2,128)(2,1)} copy(bf16[1,1536,1024]{2,1,0:T(8,128)(2,1)S(1)} %fusion.22) | data formatting | bytes 6291456 | tf_op jit(solution)/shard_map/convert_element_type | solution.py:357
  594.0 20.0 %reduce.1 = bf16[1536,1024]{1,0:T(8,128)(2,1)} reduce(bf16[1536,1,1024]{2,1,0:T(2,128)(2,1)} %bitcast.497, bf16[]{:T(256)} %broadcast.797), dimensions={1}, to_apply=%bitcast.475.reduce_sub_computation | reduce | bytes 6291458
  638.8 31.8 %all-to-all-done.5 = bf16[16,2,49152]{2,1,0:T(2,128)(2,1)} async-done(((bf16[16,2,49152]{2,1,0:T(2,128)(2,1)}), bf16[16,2,49152]{2,1,0:T(2,128)(2,1)}, u32[]{:S(2)}, u32[]{:S(2)}) %all-to-all-start.5) | async-done | bytes 3145760 | tf_op jit(solution)/shard_map/all_to_all | solution.py:356
  707.6 50.8 %all_to_all.33 = bf16[16,96,1024]{2,1,0:T(8,128)(2,1)S(1)} all-to-all(bf16[16,96,1024]{2,1,0:T(8,128)(2,1)} %bitcast.508), channel_id=1, replica_groups=mesh['shard'=16,'rep'=8] {'shard'}, dimensions={0} | all-to-all | bytes 6291456 | tf_op jit(solution)/shard_map/all_to_all | solution.py:252
  766.5 21.7 %copy.308 = bf16[1,1536,1024]{2,0,1:T(2,128)(2,1)} copy(bf16[1,1536,1024]{2,1,0:T(8,128)(2,1)S(1)} %fusion.21) | data formatting | bytes 6291456 | tf_op jit(solution)/shard_map/convert_element_type | solution.py:257
  788.1 20.0 %reduce.2 = bf16[1536,1024]{1,0:T(8,128)(2,1)} reduce(bf16[1536,1,1024]{2,1,0:T(2,128)(2,1)} %bitcast.499, bf16[]{:T(256)} %broadcast.797), dimensions={1}, to_apply=%bitcast.476.reduce_sub_computation | reduce | bytes 6291458
  827.8 33.8 %all-to-all-done.3 = bf16[16,2,49152]{2,1,0:T(2,128)(2,1)} async-done(((bf16[16,2,49152]{2,1,0:T(2,128)(2,1)}), bf16[16,2,49152]{2,1,0:T(2,128)(2,1)}, u32[]{:S(2)}, u32[]{:S(2)}) %all-to-all-start.3) | async-done | bytes 3145760 | tf_op jit(solution)/shard_map/all_to_all | solution.py:256
  902.4 50.3 %all_to_all.34 = bf16[16,96,1024]{2,1,0:T(8,128)(2,1)S(1)} all-to-all(bf16[16,96,1024]{2,1,0:T(8,128)(2,1)} %bitcast.509), channel_id=1, replica_groups=mesh['shard'=16,'rep'=8] {'shard'}, dimensions={0} | all-to-all | bytes 6291456 | tf_op jit(solution)/shard_map/all_to_all | solution.py:345
  962.4 21.6 %copy.306 = bf16[1,1536,1024]{2,0,1:T(2,128)(2,1)} copy(bf16[1,1536,1024]{2,1,0:T(8,128)(2,1)S(1)} %fusion.23) | data formatting | bytes 6291456 | tf_op jit(solution)/shard_map/convert_element_type | solution.py:357
  984.0 20.0 %reduce.3 = bf16[1536,1024]{1,0:T(8,128)(2,1)} reduce(bf16[1536,1,1024]{2,1,0:T(2,128)(2,1)} %bitcast.495, bf16[]{:T(256)} %broadcast.797), dimensions={1}, to_apply=%bitcast.474.reduce_sub_computation | reduce | bytes 6291458
  1022.5 34.9 %all-to-all-done.7 = bf16[16,2,49152]{2,1,0:T(2,128)(2,1)} async-done(((bf16[16,2,49152]{2,1,0:T(2,128)(2,1)}), bf16[16,2,49152]{2,1,0:T(2,128)(2,1)}, u32[]{:S(2)}, u32[]{:S(2)}) %all-to-all-start.7) | async-done | bytes 3145760 | tf_op jit(solution)/shard_map/all_to_all | solution.py:356
  1171.5 14.8 reduce-scatter.28.cloned.1.call-done
  1188.8 37.7 %reduce-scatter.30.cloned.1.call-done = bf16[128,512]{1,0:T(8,128)(2,1)} async-done(((bf16[1024,512]{1,0:T(8,128)(2,1)}), bf16[128,512]{1,0:T(8,128)(2,1)}) %reduce-scatter.30.cloned.1.call-update) | async-done | bytes 131088
  1229.3 37.3 %reduce-scatter.34.cloned.1.call-done = bf16[128,512]{1,0:T(8,128)(2,1)} async-done(((bf16[1024,512]{1,0:T(8,128)(2,1)}), bf16[128,512]{1,0:T(8,128)(2,1)}) %reduce-scatter.34.cloned.1.call-update) | async-done | bytes 131088
  1300.1 40.4 %reduce-scatter.26.cloned.1.call-done = bf16[64,1024]{1,0:T(8,128)(2,1)} async-done(((bf16[1024,1024]{1,0:T(8,128)(2,1)}), bf16[64,1024]{1,0:T(8,128)(2,1)}) %reduce-scatter.26.cloned.1.call-update) | async-done | bytes 131088 | tf_op jit(solution)/shard_map/reduce_scatter | solution.py:491
  1340.5 74.9 %reduce-scatter.20.cloned.1.call-done = bf16[64,1024]{1,0:T(8,128)(2,1)} async-done(((bf16[1024,1024]{1,0:T(8,128)(2,1)}), bf16[64,1024]{1,0:T(8,128)(2,1)}) %reduce-scatter.20.cloned.1.call-update) | async-done | bytes 131088 | tf_op jit(solution)/shard_map/reduce_scatter | solution.py:476
  1415.4 69.6 %reduce-scatter.24.cloned.1.call-done = bf16[64,512]{1,0:T(8,128)(2,1)} async-done(((bf16[1024,512]{1,0:T(8,128)(2,1)}), bf16[64,512]{1,0:T(8,128)(2,1)}) %reduce-scatter.24.cloned.1.call-update) | async-done | bytes 65552 | tf_op jit(solution)/shard_map/reduce_scatter | solution.py:482
  1485.0 70.1 %reduce-scatter.22.cloned.1.call-done = bf16[64,512]{1,0:T(8,128)(2,1)} async-done(((bf16[1024,512]{1,0:T(8,128)(2,1)}), bf16[64,512]{1,0:T(8,128)(2,1)}) %reduce-scatter.22.cloned.1.call-update) | async-done | bytes 65552 | tf_op jit(solution)/shard_map/reduce_scatter | solution.py:479
  1556.4 66.9 %reduce-scatter.36.cloned.1.call-done = bf16[64,16]{1,0:T(8,128)(2,1)} async-done(((bf16[1024,16]{1,0:T(8,128)(2,1)}), bf16[64,16]{1,0:T(8,128)(2,1)}) %reduce-scatter.36.cloned.1.call-update) | async-done | bytes 2064
  1635.7 91.1 %all-reduce.20 = (bf16[1024]{0:T(1024)(128)(2,1)S(1)}, bf16[1024]{0:T(1024)(128)(2,1)S(1)}, bf16[512]{0:T(512)(128)(2,1)S(1)}, bf16[1024]{0:T(1024)(128)(2,1)S(1)}) all-reduce(bf16[1024]{0:T(1024)(128)(2,1)S(1)} %get-tuple-element.160, ...), channel_id=6, replica_groups=mesh['shard'=16,'rep'=8] {'shard'}, use_global_device_ids=true, to_apply=%region_48.50.clone | all-reduce | flops 3584 | bytes 14336
  1727.2 16.2 all-reduce.22
  (686 shorter events, 518.4 us)
Async XLA Ops:
  7.2 328.0 %copy-start = (bf16[1,1024,1024]{2,1,0:T(8,128)(2,1)S(1)}, bf16[1,1024,1024]{2,1,0:T(8,128)(2,1)}, u32[]{:S(2)}) copy-start(bf16[1,1024,1024]{2,1,0:T(8,128)(2,1)} %param.30) | copy-start | bytes 6291460
  7.2 51.1 %all-gather.10.cloned.1.call-start = ((), (), s32[]{:S(2)}) async-start(), calls=%async_computation.17 | async-start | bytes 1114112 | tf_op jit(solution)/shard_map/all_gather | solution.py:197
  7.9 96.1 %all-gather.14.cloned.1.call-start = ((), (), s32[]{:S(2)}) async-start(), calls=%async_computation.19 | async-start | bytes 1114112 | tf_op jit(solution)/shard_map/all_gather | solution.py:196
  8.7 135.3 %all-gather.12.cloned.1.call-start = ((), (), s32[]{:S(2)}) async-start(), calls=%async_computation.18 | async-start | bytes 1179648 | tf_op jit(solution)/shard_map/all_gather | solution.py:228
  55.4 180.0 %copy-start.81 = (f32[1024]{0:T(1024)}, f32[1024]{0:T(1024)S(1)}, u32[]{:S(2)}) copy-start(f32[1024]{0:T(1024)S(1)} %convert_element_type.419) | copy-start | bytes 12292
  55.6 187.8 %copy-start.76 = (f32[128,64]{0,1:T(8,128)}, f32[128,64]{0,1:T(8,128)S(1)}, u32[]{:S(2)}) copy-start(f32[128,64]{0,1:T(8,128)S(1)} %pad_maximum_fusion.10) | copy-start | bytes 98308
  56.4 187.0 %copy-start.71 = (f32[128,64]{0,1:T(8,128)}, f32[128,64]{0,1:T(8,128)S(1)}, u32[]{:S(2)}) copy-start(f32[128,64]{0,1:T(8,128)S(1)} %pad_maximum_fusion.11) | copy-start | bytes 98308
  58.2 177.1 %copy-start.111 = (f32[128]{0:T(128)}, f32[128]{0:T(128)S(1)}, u32[]{:S(2)}) copy-start(f32[128]{0:T(128)S(1)} %fusion.155) | copy-start | bytes 1540
  60.6 123.5 %all-gather.16.cloned.1.call-start = ((), (), s32[]{:S(2)}) async-start(), calls=%async_computation.20 | async-start | bytes 1179648 | tf_op jit(solution)/shard_map/all_gather | solution.py:227
  115.8 117.3 %all-gather.18.cloned.1.call-start = ((), (), s32[]{:S(2)}) async-start(), calls=%async_computation.21 | async-start | bytes 2228224 | tf_op jit(solution)/shard_map/all_gather | solution.py:195
  116.4 165.4 %all-gather.20.cloned.1.call-start = ((), (), s32[]{:S(2)}) async-start(), calls=%async_computation.22 | async-start | bytes 2228224 | tf_op jit(solution)/shard_map/all_gather | solution.py:200
  284.9 173.8 %copy-start.33 = (bf16[128,1024]{1,0:T(8,128)(2,1)}, bf16[128,1024]{1,0:T(8,128)(2,1)S(1)}, u32[]{:S(2)}) copy-start(bf16[128,1024]{1,0:T(8,128)(2,1)S(1)} %multiply_convert_fusion.7) | copy-start | bytes 786436
  392.8 73.5 %all-to-all-start.1 = ((bf16[16,2,49152]{2,1,0:T(2,128)(2,1)}), bf16[16,2,49152]{2,1,0:T(2,128)(2,1)}, u32[]{:S(2)}, u32[]{:S(2)}) async-start(bf16[16,2,49152]{2,1,0:T(2,128)(2,1)} %reshape.956), calls=%async_computation.1 | async-start | bytes 6291456 | tf_op jit(solution)/shard_map/all_to_all | solution.py:256
  397.4 126.1 %all-gather.22.cloned.1.call-start = ((), (), s32[]{:S(2)}) async-start(), calls=%async_computation.23 | async-start | bytes 1179648 | tf_op jit(solution)/shard_map/all_gather | solution.py:228
  506.9 54.9 %all-to-all-start.4 = ((bf16[16,96,1024]{2,1,0:T(8,128)(2,1)}), bf16[16,96,1024]{2,1,0:T(8,128)(2,1)}, u32[]{:S(2)}, u32[]{:S(2)}) async-start(bf16[16,96,1024]{2,1,0:T(8,128)(2,1)} %bitcast.506), calls=%async_computation.4 | async-start | bytes 6291456 | tf_op jit(solution)/shard_map/all_to_all | solution.py:345
  511.6 43.8 %all-gather.24.cloned.1.call-start = ((), (), s32[]{:S(2)}) async-start(), calls=%async_computation.24 | async-start | bytes 1179648 | tf_op jit(solution)/shard_map/all_gather | solution.py:227
  621.1 49.5 %all-to-all-start.5 = ((bf16[16,2,49152]{2,1,0:T(2,128)(2,1)}), bf16[16,2,49152]{2,1,0:T(2,128)(2,1)}, u32[]{:S(2)}, u32[]{:S(2)}) async-start(bf16[16,2,49152]{2,1,0:T(2,128)(2,1)} %reshape.960), calls=%async_computation.5 | async-start | bytes 6291456 | tf_op jit(solution)/shard_map/all_to_all | solution.py:356
  815.3 46.4 %all-to-all-start.3 = ((bf16[16,2,49152]{2,1,0:T(2,128)(2,1)}), bf16[16,2,49152]{2,1,0:T(2,128)(2,1)}, u32[]{:S(2)}, u32[]{:S(2)}) async-start(bf16[16,2,49152]{2,1,0:T(2,128)(2,1)} %reshape.954), calls=%async_computation.3 | async-start | bytes 6291456 | tf_op jit(solution)/shard_map/all_to_all | solution.py:256
  1011.2 46.2 %all-to-all-start.7 = ((bf16[16,2,49152]{2,1,0:T(2,128)(2,1)}), bf16[16,2,49152]{2,1,0:T(2,128)(2,1)}, u32[]{:S(2)}, u32[]{:S(2)}) async-start(bf16[16,2,49152]{2,1,0:T(2,128)(2,1)} %reshape.958), calls=%async_computation.7 | async-start | bytes 6291456 | tf_op jit(solution)/shard_map/all_to_all | solution.py:356
  1015.8 154.7 %reduce-scatter.32.cloned.1.call-start = ((), (), s32[]{:S(2)}) async-start(), calls=%async_computation.31 | async-start | bytes 1179648
  1104.6 81.6 %reduce-scatter.28.cloned.1.call-start = ((), (), s32[]{:S(2)}) async-start(), calls=%async_computation.29 | async-start | bytes 1179648
  1132.9 93.6 %reduce-scatter.30.cloned.1.call-start = ((), (), s32[]{:S(2)}) async-start(), calls=%async_computation.30 | async-start | bytes 1179648
  1141.0 125.6 %reduce-scatter.34.cloned.1.call-start = ((), (), s32[]{:S(2)}) async-start(), calls=%async_computation.32 | async-start | bytes 1179648
  1149.1 191.3 %reduce-scatter.26.cloned.1.call-start = ((), (), s32[]{:S(2)}) async-start(), calls=%async_computation.28 | async-start | bytes 2228224 | tf_op jit(solution)/shard_map/reduce_scatter | solution.py:491
  1153.0 262.4 %reduce-scatter.20.cloned.1.call-start = ((), (), s32[]{:S(2)}) async-start(), calls=%async_computation.25 | async-start | bytes 2228224 | tf_op jit(solution)/shard_map/reduce_scatter | solution.py:476
  1170.4 314.6 %reduce-scatter.24.cloned.1.call-start = ((), (), s32[]{:S(2)}) async-start(), calls=%async_computation.27 | async-start | bytes 1114112 | tf_op jit(solution)/shard_map/reduce_scatter | solution.py:482
  1269.8 285.3 %reduce-scatter.22.cloned.1.call-start = ((), (), s32[]{:S(2)}) async-start(), calls=%async_computation.26 | async-start | bytes 1114112 | tf_op jit(solution)/shard_map/reduce_scatter | solution.py:479
  1279.8 343.5 %reduce-scatter.36.cloned.1.call-start = ((), (), s32[]{:S(2)}) async-start(), calls=%async_computation.33 | async-start | bytes 278528
  1281.2 467.4 %all-reduce.26.cloned.1.call-start = ((), (), s32[]{:S(2)}) async-start(), calls=%async_computation.34 | async-start | bytes 7077888 | tf_op jit(solution)/shard_map/psum | solution.py:514
  1300.1 324.7 %copy-start.66 = (bf16[1,128,1024]{2,1,0:T(8,128)(2,1)S(1)}, bf16[1,128,1024]{2,1,0:T(8,128)(2,1)}, u32[]{:S(2)}) copy-start(bf16[1,128,1024]{2,1,0:T(8,128)(2,1)} %get-tuple-element.69) | copy-start | bytes 786436
  1300.1 326.6 %copy-start.119 = (f32[1024]{0:T(1024)S(1)}, f32[1024]{0:T(1024)}, u32[]{:S(2)}) copy-start(f32[1024]{0:T(1024)} %get-tuple-element.16) | copy-start | bytes 12292
  1300.1 328.0 %copy-start.47 = (bf16[128,1024]{1,0:T(8,128)(2,1)S(1)}, bf16[128,1024]{1,0:T(8,128)(2,1)}, u32[]{:S(2)}) copy-start(bf16[128,1024]{1,0:T(8,128)(2,1)} %copy-done.46) | copy-start | bytes 786436
  (171 other events, 2894.3 us)
Sparse Core Ops, SparseCore 0:
  10.5 47.4 all-gather.9
  60.4 43.5 all-gather.13
  106.3 37.6 all-gather.11
  146.1 38.0 all-gather.15
  186.4 46.6 all-gather.17
  235.4 46.3 all-gather.19
  458.8 37.8 all-gather.21
  514.1 41.2 all-gather.23
  1104.8 41.3 reduce-scatter.31
  1148.4 37.8 reduce-scatter.27
  1188.6 37.7 reduce-scatter.29
  1228.7 37.8 reduce-scatter.33
  1270.5 69.9 reduce-scatter.25
  1345.3 70.0 reduce-scatter.19
  1419.0 65.9 reduce-scatter.23
  1489.1 65.9 reduce-scatter.21
  1559.2 64.1 reduce-scatter.35
  1626.8 95.9 all-reduce.25
where the time goes:
time: 1780 us; the launch traced here: 1770 us
  waiting for transfers between devices  720 us (40%)
  blocking collectives  350 us (20%)
  local copies, waits for them, and re-layouts  338 us (19%)
  other arithmetic  157 us (9%)
  matrix products  144 us (8%)
  starting transfers between devices  38.7 us (2%)
  between operations  19.7 us (1%)
    unnamed x23, waiting for transfers between devices  160 us
    unnamed x397, local copies, waits for them, and re-layouts  135 us
    unnamed x2, blocking collectives  132 us
    all_to_all x2, blocking collectives, shards(): lax.all_to_all(dispatched, 'shard', split_axis=0, concat_axis=1, tiled=True)  95.3 us
    unnamed x6, other arithmetic  80.2 us
    reduce_scatter x1, waiting for transfers between devices, shards(): lax.psum_scatter(total_query.astype(jnp.bfloat16), 'shard', scatter_dimen...  74.9 us
    reduce_scatter x1, waiting for transfers between devices, shards(): lax.psum_scatter(total_key.astype(jnp.bfloat16), 'shard', scatter_dimensi...  70.1 us
    reduce_scatter x1, waiting for transfers between devices, shards(): lax.psum_scatter(total_value.astype(jnp.bfloat16), 'shard', scatter_dimen...  69.6 us
  transfers between devices with their start and end apart: 23, of which 18 were waited for; matrix products, arithmetic and copies ran while one was open for 14% of the time, Pallas kernels for 0%

commit v1 on v0

v1 whole, which is shorter than its diff:
```python
import functools

import jax
import jax.numpy as jnp
from jax import lax
from jax.experimental import pallas as pl
from jax.experimental.pallas import tpu as pltpu
from jax.sharding import PartitionSpec as P

HEADS = 16
KV_HEADS = 8
HEAD_DIM = 64
PIC = 256
RING = 4
GROUP = 16
REPS = 8
VMEM_LIMIT = 56 << 20

norm_eps = 1e-06
rope_base = 10000.0
masked_score = -1e30

bf16 = jnp.bfloat16
f32 = jnp.float32


class Place:
    def __init__(self):
        shard = lax.axis_index("shard")
        rep = lax.axis_index("rep")
        self.shard, self.rep = shard, rep
        core = lax.rem(shard, 2)
        ring_z = lax.rem(lax.div(shard, 2), RING)
        y_hi = lax.div(shard, 8)
        ring_x = lax.rem(rep, RING)
        y_lo = lax.div(rep, RING)
        self.core = core

        def shard_of(hi, z, c):
            return (hi * RING + z) * 2 + c

        def rep_of(lo, x):
            return lo * RING + x

        def up(v):
            return lax.rem(v + 1, RING)

        def down(v):
            return lax.rem(v + RING - 1, RING)

        self.twin = (shard_of(y_hi, ring_z, 1 - core), rep)
        self.tokens = Axes(
            y_hi,
            ring_z,
            (shard_of(y_hi, up(ring_z), core), rep),
            (shard_of(y_hi, down(ring_z), core), rep),
            (shard_of(1 - y_hi, ring_z, core), rep_of(1 - y_lo, ring_x)),
        )
        self.copies = Axes(
            y_lo,
            ring_x,
            (shard, rep_of(y_lo, up(ring_x))),
            (shard, rep_of(y_lo, down(ring_x))),
            (shard, rep_of(1 - y_lo, ring_x)),
        )


class Axes:
    def __init__(self, side, spot, ahead, behind, across):
        self.side, self.spot = side, spot
        self.ahead, self.behind, self.across = ahead, behind, across

    def at(self, flip, step):
        return (1 - self.side) if flip else self.side, lax.rem(self.spot + RING + step, RING)

    def neighbours(self):
        return [self.ahead, self.behind, self.across]


def greet(devices):
    barrier = pltpu.get_barrier_semaphore()
    for device in devices:
        pl.semaphore_signal(barrier, inc=1, device_id=device, device_id_type=pl.DeviceIdType.MESH)
    pl.semaphore_wait(barrier, len(devices))


class Line:
    def __init__(self, send_sem, recv_sem):
        self.send_sem, self.recv_sem = send_sem, recv_sem
        self.sent = []

    def send(self, index, source, target, device):
        copy = pltpu.make_async_remote_copy(
            src_ref=source,
            dst_ref=target,
            send_sem=self.send_sem.at[index],
            recv_sem=self.recv_sem.at[index],
            device_id=device,
            device_id_type=pl.DeviceIdType.MESH,
        )
        copy.start()
        self.sent.append(copy)

    def take(self, index, target, device):
        pltpu.make_async_remote_copy(
            src_ref=target,
            dst_ref=target,
            send_sem=self.send_sem.at[index],
            recv_sem=self.recv_sem.at[index],
            device_id=device,
            device_id_type=pl.DeviceIdType.MESH,
        ).wait_recv()

    def finish(self):
        for copy in self.sent:
            copy.wait_send()


def abreast(*parts):
    running = list(parts)
    while running:
        for part in list(running):
            try:
                next(part)
            except StopIteration:
                running.remove(part)


GATHER_SEMS = 20


def gather_parts(axes, line, own, block, rows, local_sem, twin=None):
    half, quarter = rows // 2, rows // 4
    mine, back, front, far = axes.at(0, 0), axes.at(0, -1), axes.at(0, 1), axes.at(0, 2)
    pair, pair_back, pair_front, pair_far = (axes.at(1, n) for n in (0, -1, 1, 2))
    ahead, behind, across = axes.ahead, axes.behind, axes.across

    def full(which):
        return block(which, 0, rows)

    def share(index, which):
        if twin is not None:
            line.send(12 + index, full(which), full(which), twin)

    keep = pltpu.make_async_copy(own, full(mine), local_sem)
    keep.start()
    line.send(0, own, full(mine), ahead)
    line.send(1, own, full(mine), behind)
    line.send(2, own, full(mine), across)
    if twin is not None:
        line.send(12, own, full(mine), twin)
    yield
    line.take(0, full(back), ahead)
    line.send(3, block(back, 0, half), block(back, 0, half), ahead)
    line.send(4, block(back, half, half), block(back, half, half), across)
    share(1, back)
    line.take(1, full(front), behind)
    line.send(5, block(front, half, half), block(front, half, half), behind)
    line.send(6, block(front, half, half), block(front, half, half), across)
    share(2, front)
    line.take(2, full(pair), across)
    line.send(7, block(pair, 0, half), block(pair, 0, half), ahead)
    line.send(8, block(pair, 0, half), block(pair, 0, half), behind)
    share(3, pair)
    yield
    line.take(3, block(far, 0, half), ahead)
    line.take(5, block(far, half, half), behind)
    line.send(9, block(far, half, half), block(far, half, half), across)
    share(4, far)
    line.take(7, block(pair_back, 0, half), ahead)
    line.send(10, block(pair_back, 0, quarter), block(pair_back, 0, quarter), ahead)
    line.take(8, block(pair_front, 0, half), behind)
    line.send(
        11, block(pair_front, quarter, quarter), block(pair_front, quarter, quarter), behind
    )
    line.take(4, block(pair_back, half, half), across)
    share(5, pair_back)
    line.take(6, block(pair_front, half, half), across)
    share(6, pair_front)
    yield
    line.take(10, block(pair_far, 0, quarter), ahead)
    line.take(11, block(pair_far, quarter, quarter), behind)
    line.take(9, block(pair_far, half, half), across)
    share(7, pair_far)
    keep.wait()
    if twin is not None:
        for index, which in enumerate(
            (mine, back, front, pair, far, pair_back, pair_front, pair_far)
        ):
            line.take(12 + index, block(which, 0, rows, True), twin)
    line.finish()


SUM_SEMS = 20


def add_rows(target, source, rows):
    step = 16
    count = rows // step

    def body(index, carry):
        at = pl.ds(pl.multiple_of(index * step, step), step)
        target[at] = (target[at].astype(f32) + source[at].astype(f32)).astype(bf16)
        return carry

    lax.fori_loop(0, count, body, 0)


def stage_rows(rows):
    return 7 * rows


def sum_parts(axes, line, part, stage, rows, result, twin=None):
    half, quarter = rows // 2, rows // 4
    mine, back, front, far = axes.at(0, 0), axes.at(0, -1), axes.at(0, 1), axes.at(0, 2)
    pair, pair_back, pair_front, pair_far = (axes.at(1, n) for n in (0, -1, 1, 2))
    ahead, behind, across = axes.ahead, axes.behind, axes.across
    order = (pair_far, far, pair_back, pair_front, back, front, pair, mine)
    offsets, used = {}, 0
    for name, size in (
        ("Y0", half), ("M0", quarter), ("P0", quarter), ("M1", half), ("Y1", half), ("Y2", half),
        ("P1", half), ("M2", half), ("P2", half), ("M3", rows), ("P3", rows), ("Y3", rows),
    ):
        offsets[name] = (used, size, len(offsets))
        used += size

    def landing(name):
        low, size, _ = offsets[name]
        return stage.at[pl.ds(low, size)]

    def send(name, which, low, device):
        _, size, index = offsets[name]
        line.send(index, part(which, low, size), landing(name), device)

    def add(name, which, low, device):
        _, size, index = offsets[name]
        line.take(index, landing(name), device)
        add_rows(part(which, low, size), landing(name), size)

    def join(*places):
        if twin is not None:
            for place in places:
                line.take(12 + place, twin[2](order[place]), twin[0])
                add_rows(part(order[place], 0, rows), twin[2](order[place]), rows)

    if twin is not None:
        for place, which in enumerate(order):
            line.send(12 + place, twin[1](which), twin[2](which), twin[0])
        yield
    join(0)
    send("Y0", pair_far, half, across)
    send("M0", pair_far, 0, behind)
    send("P0", pair_far, quarter, ahead)
    join(1)
    send("M1", far, 0, behind)
    join(2)
    send("Y1", pair_back, half, across)
    join(3)
    send("Y2", pair_front, half, across)
    yield
    add("M0", pair_back, 0, behind)
    send("M2", pair_back, 0, behind)
    add("P0", pair_front, quarter, ahead)
    send("P2", pair_front, 0, ahead)
    add("Y0", far, half, across)
    send("P1", far, half, ahead)
    join(4, 5, 6, 7)
    yield
    add("M1", back, 0, behind)
    add("Y1", back, half, across)
    send("M3", back, 0, behind)
    add("M2", pair, 0, behind)
    add("P2", pair, 0, ahead)
    send("Y3", pair, 0, across)
    add("P1", front, half, ahead)
    add("Y2", front, half, across)
    send("P3", front, 0, ahead)
    yield
    for name, device in (("M3", behind), ("P3", ahead), ("Y3", across)):
        line.take(offsets[name][2], landing(name), device)
    step = 16

    def body(index, carry):
        low = pl.multiple_of(index * step, step)
        total = part(mine, low, step)[...].astype(f32)
        for name in ("M3", "P3", "Y3"):
            total = total + stage[pl.ds(offsets[name][0] + low, step)].astype(f32)
        result[pl.ds(low, step)] = total.astype(result.dtype)
        return carry

    lax.fori_loop(0, rows // step, body, 0)
    line.finish()


def sems(count):
    return [pltpu.SemaphoreType.DMA((count,)), pltpu.SemaphoreType.DMA((count,))]


ANY = pl.BlockSpec(memory_space=pl.ANY)
IN_VMEM = pl.BlockSpec(memory_space=pltpu.VMEM)


def tokens_gather(place, line, own_ref, all_ref, local_sem):
    rows = own_ref.shape[0]
    axes, core = place.tokens, place.core

    def block(which, low, count, other=False):
        side, spot = which
        index = (side * RING + spot) * 2 + ((1 - core) if other else core)
        return all_ref.at[index, pl.ds(low, count)]

    return gather_parts(axes, line, own_ref, block, rows, local_sem, place.twin)


def copies_gather(place, line, own_ref, all_ref, local_sem):
    rows = own_ref.shape[0]

    def block(which, low, count, other=False):
        side, spot = which
        return all_ref.at[side * RING + spot, pl.ds(low, count)]

    return gather_parts(place.copies, line, own_ref, block, rows, local_sem)


def params(collective_id):
    return pltpu.CompilerParams(
        collective_id=collective_id, has_side_effects=True, vmem_limit_bytes=VMEM_LIMIT
    )


def gather_call(collective_id, over_tokens=None, over_copies=None):
    operands = [v for v in (over_tokens, over_copies) if v is not None]

    def kernel(*refs):
        count = len(operands)
        owns, alls, scratch = refs[:count], refs[count : 2 * count], list(refs[2 * count :])
        place = Place()
        friends, steps, at = [], [], 0
        for kind, value in (("tokens", over_tokens), ("copies", over_copies)):
            if value is None:
                continue
            send_sem, recv_sem, local_sem = scratch[3 * at : 3 * at + 3]
            line = Line(send_sem, recv_sem)
            if kind == "tokens":
                friends += place.tokens.neighbours() + [place.twin]
                steps.append(tokens_gather(place, line, owns[at], alls[at], local_sem))
            else:
                friends += place.copies.neighbours()
                steps.append(copies_gather(place, line, owns[at], alls[at], local_sem))
            at += 1
        greet(friends)
        abreast(*steps)

    sizes = []
    if over_tokens is not None:
        sizes.append(GROUP)
    if over_copies is not None:
        sizes.append(REPS)
    scratch = []
    for _ in operands:
        scratch += sems(GATHER_SEMS) + [pltpu.SemaphoreType.DMA]
    return pl.pallas_call(
        kernel,
        out_shape=[
            jax.ShapeDtypeStruct((size,) + v.shape, v.dtype) for size, v in zip(sizes, operands)
        ],
        in_specs=[ANY] * len(operands),
        out_specs=[ANY] * len(operands),
        scratch_shapes=scratch,
        compiler_params=params(collective_id),
    )(*operands)


def sum_call(collective_id, over_tokens=None, over_copies=None, result=f32):
    operands = [v for v in (over_tokens, over_copies) if v is not None]

    def kernel(*refs):
        count = len(operands)
        terms, outs, scratch = refs[:count], refs[count : 2 * count], list(refs[2 * count :])
        place = Place()
        friends, steps, at = [], [], 0
        if over_tokens is not None:
            friends += place.tokens.neighbours() + [place.twin]
        if over_copies is not None:
            friends += place.copies.neighbours()
        loads = []
        for kind, value in (("tokens", over_tokens), ("copies", over_copies)):
            if value is None:
                continue
            rows = value.shape[1]
            if kind == "tokens":
                held, staged, stage, send_sem, recv_sem, load_sem = scratch[:6]
                del scratch[:6]
                line = Line(send_sem, recv_sem)
                source = terms[at]
                core = place.core

                def index_of(which, c):
                    return (which[0] * RING + which[1]) * 2 + c

                def held_part(which, low, n, held=held):
                    return held.at[which[0] * RING + which[1], pl.ds(low, n)]

                def outgoing(which, source=source, core=core):
                    return source.at[index_of(which, 1 - core)]

                def landed(which, staged=staged):
                    return staged.at[which[0] * RING + which[1]]

                for block in range(8):
                    load = pltpu.make_async_copy(
                        source.at[2 * block + core], held.at[block], load_sem.at[block]
                    )
                    load.start()
                    loads.append(load)
                steps.append(
                    sum_parts(
                        place.tokens, line, held_part, stage, rows, outs[at],
                        (place.twin, outgoing, landed),
                    )
                )
            else:
                held, stage, send_sem, recv_sem, load_sem = scratch[:5]
                del scratch[:5]
                line = Line(send_sem, recv_sem)
                load = pltpu.make_async_copy(terms[at], held, load_sem)
                load.start()
                loads.append(load)

                def copies_part(which, low, n, held=held):
                    return held.at[which[0] * RING + which[1], pl.ds(low, n)]

                steps.append(
                    sum_parts(place.copies, line, copies_part, stage, rows, outs[at])
                )
            at += 1
        greet(friends)
        for load in loads:
            load.wait()
        abreast(*steps)

    scratch = []
    if over_tokens is not None:
        _, rows, columns = over_tokens.shape
        scratch += [
            pltpu.VMEM((8, rows, columns), bf16),
            pltpu.VMEM((8, rows, columns), bf16),
            pltpu.VMEM((stage_rows(rows), columns), bf16),
        ]
        scratch += sems(SUM_SEMS) + [pltpu.SemaphoreType.DMA((8,))]
    if over_copies is not None:
        _, rows, columns = over_copies.shape
        scratch += [
            pltpu.VMEM((8, rows, columns), bf16),
            pltpu.VMEM((stage_rows(rows), columns), bf16),
        ]
        scratch += sems(SUM_SEMS) + [pltpu.SemaphoreType.DMA]
    return pl.pallas_call(
        kernel,
        out_shape=[jax.ShapeDtypeStruct(v.shape[1:], result) for v in operands],
        in_specs=[ANY] * len(operands),
        out_specs=[IN_VMEM] * len(operands),
        scratch_shapes=scratch,
        compiler_params=params(collective_id),
    )(*operands)


def sum_gather_call(collective_id, over_tokens, over_copies):
    _, rows, columns = over_tokens.shape

    def kernel(terms, own, total, every, held, staged, stage, s1, r1, load_sem, s2, r2, local_sem):
        place = Place()
        core = place.core
        loads = []
        for block in range(8):
            load = pltpu.make_async_copy(
                terms.at[2 * block + core], held.at[block], load_sem.at[block]
            )
            load.start()
            loads.append(load)
        greet(place.tokens.neighbours() + [place.twin] + place.copies.neighbours())
        for load in loads:
            load.wait()

        def held_part(which, low, n):
            return held.at[which[0] * RING + which[1], pl.ds(low, n)]

        def outgoing(which):
            return terms.at[(which[0] * RING + which[1]) * 2 + 1 - core]

        def landed(which):
            return staged.at[which[0] * RING + which[1]]

        abreast(
            sum_parts(
                place.tokens, Line(s1, r1), held_part, stage, rows, total,
                (place.twin, outgoing, landed),
            ),
            copies_gather(place, Line(s2, r2), own, every, local_sem),
        )

    return pl.pallas_call(
        kernel,
        out_shape=[
            jax.ShapeDtypeStruct((rows, columns), f32),
            jax.ShapeDtypeStruct((REPS,) + over_copies.shape, over_copies.dtype),
        ],
        in_specs=[ANY, ANY],
        out_specs=[IN_VMEM, ANY],
        scratch_shapes=[
            pltpu.VMEM((8, rows, columns), bf16),
            pltpu.VMEM((8, rows, columns), bf16),
            pltpu.VMEM((stage_rows(rows), columns), bf16),
        ]
        + sems(SUM_SEMS)
        + [pltpu.SemaphoreType.DMA((8,))]
        + sems(GATHER_SEMS)
        + [pltpu.SemaphoreType.DMA],
        compiler_params=params(collective_id),
    )(over_tokens, over_copies)


def copies_total_call(collective_id, terms):
    _, rows, columns = terms.shape

    def kernel(terms_ref, every, held, stage, own, s1, r1, load_sem, s2, r2, local_sem):
        place = Place()
        load = pltpu.make_async_copy(terms_ref, held, load_sem)
        load.start()
        greet(place.copies.neighbours())
        load.wait()

        def held_part(which, low, n):
            return held.at[which[0] * RING + which[1], pl.ds(low, n)]

        abreast(sum_parts(place.copies, Line(s1, r1), held_part, stage, rows, own))
        abreast(copies_gather(place, Line(s2, r2), own, every, local_sem))

    return pl.pallas_call(
        kernel,
        out_shape=jax.ShapeDtypeStruct(terms.shape, bf16),
        in_specs=[ANY],
        out_specs=ANY,
        scratch_shapes=[
            pltpu.VMEM((8, rows, columns), bf16),
            pltpu.VMEM((stage_rows(rows), columns), bf16),
            pltpu.VMEM((rows, columns), bf16),
        ]
        + sems(SUM_SEMS)
        + [pltpu.SemaphoreType.DMA]
        + sems(GATHER_SEMS)
        + [pltpu.SemaphoreType.DMA],
        compiler_params=params(collective_id),
    )(terms)


def copies_total(own):
    rows, columns = own.shape
    wide = -(-columns // (128 * REPS)) * 128 * REPS
    cut = jnp.pad(own.astype(bf16), ((0, 0), (0, wide - columns)))
    cut = cut.reshape(rows, REPS, wide // REPS).transpose(1, 0, 2)
    total = copies_total_call(7, cut)
    return total.transpose(1, 0, 2).reshape(rows, wide)[:, :columns].astype(f32)


def rms_scale(values, gain):
    return values * lax.rsqrt(jnp.mean(values * values, axis=-1, keepdims=True) + norm_eps) * gain


def rotary_tables(positions, head_size):
    half_size = head_size // 2
    exponent = jnp.arange(half_size, dtype=f32) * (2.0 / head_size)
    frequency = rope_base ** (-exponent)
    angles = positions.astype(f32)[:, None] * frequency[None, :]
    cosine_table = jnp.concatenate([jnp.cos(angles), jnp.cos(angles)], axis=-1)
    sine_table = jnp.concatenate([jnp.sin(angles), jnp.sin(angles)], axis=-1)
    return (cosine_table, sine_table)


def rotate(values, cosine_table, sine_table):
    half_size = values.shape[-1] // 2
    turned = jnp.concatenate([-values[..., half_size:], values[..., :half_size]], axis=-1)
    return values * cosine_table[:, None, :] + turned * sine_table[:, None, :]


def piece_index(positions, starts):
    inside = (positions[:, None] >= starts[None, :]) & (positions[:, None] < starts[None, :] + PIC)
    labels = jnp.arange(1, starts.shape[0] + 1, dtype=jnp.int32)
    return jnp.sum(jnp.where(inside, labels[None, :], 0), axis=1) - 1


def allowed_mask(query_pos, key_pos, starts):
    query_piece = piece_index(query_pos, starts)
    key_piece = piece_index(key_pos, starts)
    causal = key_pos[None, :] <= query_pos[:, None]
    shared = (query_piece[:, None] == key_piece[None, :]) & (query_piece[:, None] >= 0)
    return causal | shared


def query_key(query_raw, key_raw, query_gain, key_gain, cosine_table, sine_table):
    row_count = query_raw.shape[0]
    query_rot = rotate(
        rms_scale(query_raw, query_gain).reshape(row_count, HEADS, HEAD_DIM),
        cosine_table,
        sine_table,
    )
    key_rot = rotate(
        rms_scale(key_raw, key_gain).reshape(row_count, KV_HEADS, HEAD_DIM),
        cosine_table,
        sine_table,
    )
    return (query_rot, key_rot)


def dot(a, b):
    return jnp.dot(a, b, preferred_element_type=f32)


def dot_nt(a, b):
    return lax.dot_general(a, b, (((1,), (1,)), ((), ())), preferred_element_type=f32)


def dot_tn(a, b):
    return lax.dot_general(a, b, (((0,), (0,)), ((), ())), preferred_element_type=f32)


SMALL = 128


def pack_rows(wide, router, gain_a, gain_q, gain_f, gain_k):
    rows = router.shape[0]
    short = jnp.concatenate([gain_k, jnp.zeros((rows - gain_k.shape[0],), gain_k.dtype)])
    small = jnp.concatenate(
        [router] + [v[:, None] for v in (gain_a, gain_q, gain_f, short)], axis=1
    )
    small = jnp.pad(small, ((0, 0), (0, SMALL - small.shape[1])))
    return jnp.concatenate(list(wide) + [small], axis=1)


def shards(
    tokens,
    cotangent,
    routes,
    picture_starts,
    attn_gain,
    query_weight,
    key_weight,
    value_weight,
    query_gain,
    key_gain,
    output_weight,
    ffn_gain,
    router_weight,
    expert_in,
    expert_down,
):
    seqs, positions, width = tokens.shape
    top = routes.shape[2]
    count = seqs * positions
    length = positions * REPS
    experts = GROUP
    hidden_width = expert_down.shape[1]
    group = HEADS // KV_HEADS
    query_width = HEADS * HEAD_DIM
    kv_width = KV_HEADS * HEAD_DIM
    score_scale = HEAD_DIM ** (-0.5)
    rows_own = query_weight.shape[0]
    kgain_own = key_gain.shape[0]
    shard = lax.axis_index("shard")
    query_pos = lax.axis_index("rep") * positions + jnp.arange(positions, dtype=jnp.int32)
    key_pos = jnp.arange(length, dtype=jnp.int32)
    cosine_one, sine_one = rotary_tables(query_pos, HEAD_DIM)
    cosine_table = jnp.tile(cosine_one, (seqs, 1))
    sine_table = jnp.tile(sine_one, (seqs, 1))

    packed = pack_rows(
        (query_weight, key_weight, value_weight, output_weight),
        router_weight,
        attn_gain,
        query_gain,
        ffn_gain,
        key_gain,
    )
    (dense,) = gather_call(1, packed)
    columns = packed.shape[1]
    dense = dense.reshape(GROUP * rows_own, columns)
    at_o = query_width + 2 * kv_width
    at_s = at_o + width
    weight_q = dense[:, :query_width]
    weight_k = dense[:, query_width : query_width + kv_width]
    weight_v = dense[:, query_width + kv_width : at_o]
    weight_o = dense[:, at_o:at_s]
    weight_r = dense[:, at_s : at_s + experts]
    gain_a = dense[:, at_s + experts].astype(f32)
    gain_q = dense[:, at_s + experts + 1].astype(f32)
    gain_f = dense[:, at_s + experts + 2].astype(f32)
    gain_k = (
        dense[:, at_s + experts + 3].reshape(GROUP, rows_own)[:, :kgain_own].reshape(-1).astype(f32)
    )

    inputs = tokens.reshape(count, width).astype(f32)
    grad_low = cotangent.reshape(count, width)
    grad_out = grad_low.astype(f32)
    attn_in = rms_scale(inputs, gain_a).astype(bf16)
    query_raw = dot(attn_in, weight_q)
    key_raw = dot(attn_in, weight_k)
    value_low = dot(attn_in, weight_v).astype(bf16)
    query_rot, key_rot = query_key(query_raw, key_raw, gain_q, gain_k, cosine_table, sine_table)
    query_low = query_rot.astype(bf16).reshape(seqs, positions, KV_HEADS, group, HEAD_DIM)
    key_low = key_rot.astype(bf16).reshape(count, kv_width)
    grad_all, pairs_all = gather_call(
        2, grad_low, jnp.concatenate([key_low, value_low], axis=1)
    )
    pairs_all = (
        pairs_all.reshape(REPS, seqs, positions, 2 * kv_width)
        .transpose(1, 0, 2, 3)
        .reshape(seqs, length, 2 * kv_width)
    )
    keys_all = pairs_all[..., :kv_width].reshape(seqs, length, KV_HEADS, HEAD_DIM)
    values_all = pairs_all[..., kv_width:].reshape(seqs, length, KV_HEADS, HEAD_DIM)
    allowed = jax.vmap(lambda starts: allowed_mask(query_pos, key_pos, starts))(picture_starts)

    def scores_of():
        scores = (
            jnp.einsum("bqkgd,bskd->bkgqs", query_low, keys_all, preferred_element_type=f32)
            * score_scale
        )
        return jnp.where(allowed[:, None, None], scores, masked_score)

    scores = scores_of()
    row_top = jnp.max(scores, axis=-1, keepdims=True)
    exponent = jnp.exp(scores - row_top)
    row_total = jnp.sum(exponent, axis=-1, keepdims=True)
    soft_low = (exponent / row_total).astype(bf16)
    log_total = row_top + jnp.log(row_total)
    mixed_low = (
        jnp.einsum("bkgqs,bskd->bqkgd", soft_low, values_all, preferred_element_type=f32)
        .reshape(count, query_width)
        .astype(bf16)
    )
    middle = inputs + dot(mixed_low, weight_o)
    ffn_in = rms_scale(middle, gain_f).astype(bf16)
    logits = dot(ffn_in, weight_r)
    route_ids = routes.reshape(count, top)
    picked = (
        jnp.sum((route_ids[:, :, None] == jnp.arange(experts)[None, None, :]).astype(f32), axis=1)
        > 0.5
    )
    shown = jnp.where(picked, logits, masked_score)
    raised = jnp.exp(shown - jnp.max(shown, axis=-1, keepdims=True))
    gates = raised / jnp.sum(raised, axis=-1, keepdims=True)
    gates_high = gates.astype(bf16)
    gates_rest = (gates - gates_high.astype(f32)).astype(bf16)
    sent = jnp.concatenate(
        [ffn_in, gates_high, gates_rest, jnp.zeros((count, SMALL - 2 * experts), bf16)], axis=1
    )
    (got,) = gather_call(3, sent)
    got = got.reshape(GROUP * count, width + SMALL)
    rows_in = got[:, :width]
    mine = (jnp.arange(SMALL) % experts == shard) & (jnp.arange(SMALL) < 2 * experts)
    gate = jnp.sum(
        jnp.where(mine[None, :], got[:, width:].astype(f32), 0.0), axis=1, keepdims=True
    )

    inner, outer = expert_in[0], expert_down[0]
    grad_rows_out = grad_all.reshape(GROUP * count, width)
    gate_up = dot(rows_in, inner)
    gate_part, up_part = gate_up[:, :hidden_width], gate_up[:, hidden_width:]
    sigmoid = jax.nn.sigmoid(gate_part)
    hidden = (gate_part * sigmoid * up_part).astype(bf16)
    expert_out = dot(hidden, outer).astype(bf16).astype(f32)
    out_terms = (gate * expert_out).astype(bf16)
    grad_expert = (gate * grad_rows_out.astype(f32)).astype(bf16)
    grad_gate_own = jnp.sum(expert_out * grad_rows_out.astype(f32), axis=1, keepdims=True)
    grad_hidden = dot_nt(grad_expert, outer)
    grad_gate_up = jnp.concatenate(
        [
            grad_hidden * up_part * sigmoid * (1.0 + gate_part * (1.0 - sigmoid)),
            grad_hidden * gate_part * sigmoid,
        ],
        axis=1,
    ).astype(bf16)
    grad_rows = dot_nt(grad_gate_up, inner).astype(bf16)
    inner_grad = dot_tn(rows_in, grad_gate_up).astype(bf16)
    outer_grad = dot_tn(hidden, grad_expert).astype(bf16)
    own_high = grad_gate_own.astype(bf16)
    own_rest = (grad_gate_own - own_high.astype(f32)).astype(bf16)
    lanes = jnp.arange(SMALL)[None, :]
    back_columns = jnp.where(lanes == shard, own_high, jnp.zeros((), bf16)) + jnp.where(
        lanes == shard + experts, own_rest, jnp.zeros((), bf16)
    )
    back = jnp.concatenate([grad_rows, back_columns], axis=1)
    expert_terms = jnp.concatenate([inner_grad, outer_grad], axis=0)
    returned, expert_own = sum_call(
        4,
        back.reshape(GROUP, count, width + SMALL),
        expert_terms.reshape(REPS, -1, width),
    )

    grad_gates = returned[:, width : width + experts] + returned[:, width + experts : width + 2 * experts]
    grad_chosen = gates * (grad_gates - jnp.sum(gates * grad_gates, axis=-1, keepdims=True))
    grad_logits = jnp.where(picked, grad_chosen, 0.0).astype(bf16)
    grad_router = dot_tn(ffn_in, grad_logits)
    grad_ffn_in = dot_nt(grad_logits, weight_r) + returned[:, :width]
    _, norm_pull = jax.vjp(rms_scale, middle, gain_f)
    grad_middle_part, grad_gain_f = norm_pull(grad_ffn_in)
    grad_middle = grad_out + grad_middle_part
    grad_attn = grad_middle.astype(bf16)
    grad_weight_o = dot_tn(mixed_low, grad_attn)
    grad_mixed = (
        dot_nt(grad_attn, weight_o).astype(bf16).reshape(seqs, positions, KV_HEADS, group, HEAD_DIM)
    )
    soft_full = jnp.exp(scores_of() - log_total)
    grad_soft = jnp.einsum("bqkgd,bskd->bkgqs", grad_mixed, values_all, preferred_element_type=f32)
    grad_values = jnp.einsum(
        "bkgqs,bqkgd->bskd", soft_full.astype(bf16), grad_mixed, preferred_element_type=f32
    )
    grad_scores = (
        soft_full * (grad_soft - jnp.sum(soft_full * grad_soft, axis=-1, keepdims=True))
    ).astype(bf16)
    grad_query_rot = (
        jnp.einsum("bkgqs,bskd->bqkgd", grad_scores, keys_all, preferred_element_type=f32)
        * score_scale
    )
    grad_keys = (
        jnp.einsum("bkgqs,bqkgd->bskd", grad_scores, query_low, preferred_element_type=f32)
        * score_scale
    )
    grad_pairs = (
        jnp.concatenate(
            [
                grad_keys.reshape(seqs, length, kv_width),
                grad_values.reshape(seqs, length, kv_width),
            ],
            axis=-1,
        )
        .astype(bf16)
        .reshape(seqs, REPS, positions, 2 * kv_width)
        .transpose(1, 0, 2, 3)
        .reshape(REPS, count, 2 * kv_width)
    )
    out_sum, pairs_own = sum_call(5, out_terms.reshape(GROUP, count, width), grad_pairs)
    block_out = (middle + out_sum).astype(bf16)

    grad_query_rot = grad_query_rot.astype(bf16).astype(f32).reshape(count, HEADS, HEAD_DIM)
    grad_key_rot = (
        pairs_own[:, :kv_width].astype(bf16).astype(f32).reshape(count, KV_HEADS, HEAD_DIM)
    )
    grad_value_low = pairs_own[:, kv_width:].astype(bf16)

    def turned_pair(query_in, key_in, query_scale, key_scale):
        return query_key(query_in, key_in, query_scale, key_scale, cosine_table, sine_table)

    _, pair_pull = jax.vjp(turned_pair, query_raw, key_raw, gain_q, gain_k)
    grad_query_raw, grad_key_raw, grad_gain_q, grad_gain_k = pair_pull(
        (grad_query_rot, grad_key_rot)
    )
    grad_query_low = grad_query_raw.astype(bf16)
    grad_key_low = grad_key_raw.astype(bf16)
    grad_weight_q = dot_tn(attn_in, grad_query_low)
    grad_weight_k = dot_tn(attn_in, grad_key_low)
    grad_weight_v = dot_tn(attn_in, grad_value_low)
    grad_attn_in = (
        dot_nt(grad_query_low, weight_q)
        + dot_nt(grad_key_low, weight_k)
        + dot_nt(grad_value_low, weight_v)
    )
    _, norm_pull = jax.vjp(rms_scale, inputs, gain_a)
    grad_inputs_part, grad_gain_a = norm_pull(grad_attn_in)
    tokens_grad = (grad_middle + grad_inputs_part).astype(bf16)

    gain_k_rows = jnp.pad(
        grad_gain_k.reshape(GROUP, kgain_own), ((0, 0), (0, rows_own - kgain_own))
    ).reshape(-1)
    dense_terms = pack_rows(
        tuple(v.astype(bf16) for v in (grad_weight_q, grad_weight_k, grad_weight_v, grad_weight_o)),
        grad_router.astype(bf16),
        grad_gain_a.astype(bf16),
        grad_gain_q.astype(bf16),
        grad_gain_f.astype(bf16),
        gain_k_rows.astype(bf16),
    ).reshape(GROUP, rows_own, columns)
    dense_own, expert_all = sum_gather_call(6, dense_terms, expert_own.astype(bf16))
    expert_all = expert_all.reshape(-1, width)
    inner_rows = expert_in.shape[1]
    expert_in_grad = expert_all[:inner_rows].astype(f32)[None]
    expert_down_grad = expert_all[inner_rows:].astype(f32)[None]
    dense_sum = copies_total(dense_own)
    return (
        block_out.reshape(tokens.shape),
        tokens_grad.reshape(tokens.shape),
        dense_sum[:, at_s + experts],
        dense_sum[:, :query_width],
        dense_sum[:, query_width : query_width + kv_width],
        dense_sum[:, query_width + kv_width : at_o],
        dense_sum[:, at_s + experts + 1],
        dense_sum[:kgain_own, at_s + experts + 3],
        dense_sum[:, at_o:at_s],
        dense_sum[:, at_s + experts + 2],
        dense_sum[:, at_s : at_s + experts],
        expert_in_grad,
        expert_down_grad,
    )


def solution(mesh):
    by_tokens = P("shard", "rep", None)
    rows, line, block = P("shard", None), P("shard"), P("shard", None, None)
    in_specs = (
        by_tokens, by_tokens, by_tokens, rows, line, rows, rows, rows, line, line, rows, line, rows, block, block,
    )
    out_specs = (
        by_tokens, by_tokens, line, rows, rows, rows, line, line, rows, line, rows, block, block,
    )
    return jax.shard_map(shards, mesh=mesh, in_specs=in_specs, out_specs=out_specs, check_vma=False)
```

time: 1780 us -> 598 us (0.34)
  waiting for transfers between devices: 720 us -> 0 us
  blocking collectives: 350 us -> 0 us
  Pallas kernels: 0 us -> 256 us
  local copies, waits for them, and re-layouts: 338 us -> 92.6 us
  other arithmetic: 157 us -> 87.4 us
  starting transfers between devices: 38.7 us -> 0 us
    pallas_call x0 -> x7, Pallas kernels: none -> 256 us  [the longest x3 113 us: gather_call(): pl.pallas_call(kernel, out_shape=[jax.ShapeDtypeStruct((size,) + v.shape,...]
    reduce_scatter x4 -> x0, waiting for transfers between devices: 255 us -> none  [the longest x1 74.9 us: shards(): lax.psum_scatter(total_query.astype(jnp.bfloat16), 'shard', scatter_dimen...]
    all_gather x8 -> x0, waiting for transfers between devices: 200 us -> none  [the longest x2 67.5 us: shards(): lax.all_gather(key_low, 'rep', axis=0, tiled=True)]
    unnamed x23 -> x0, waiting for transfers between devices: 160 us -> none
    all_to_all x3 -> x0, blocking collectives: 146 us -> none  [the longest x2 95.3 us: shards(): lax.all_to_all(dispatched, 'shard', split_axis=0, concat_axis=1, tiled=True)]
    unnamed x2 -> x0, blocking collectives: 132 us -> none
    unnamed x397 -> x132, local copies, waits for them, and re-layouts: 135 us -> 16.8 us
    all_to_all x5 -> x0, waiting for transfers between devices: 105 us -> none  [the longest x2 66.7 us: shards(): lax.all_to_all(grad_rows.astype(jnp.bfloat16), 'shard', split_axis=1, con...]
  transfers between devices with their start and end apart: 23 -> 0, of which waited for: 18 -> 0; matrix products, arithmetic and copies ran while one was open for 14% -> 0% of each run, Pallas kernels for 0% -> 0%
where the time goes in v1:
time: 598 us; the launch traced here: 589 us
  Pallas kernels  256 us (43%)
  matrix products  151 us (25%)
  local copies, waits for them, and re-layouts  92.6 us (15%)
  other arithmetic  87.4 us (15%)
    pallas_call x3, Pallas kernels, gather_call(): pl.pallas_call(kernel, out_shape=[jax.ShapeDtypeStruct((size,) + v.shape,...  113 us
    pallas_call x2, Pallas kernels, sum_call(): pl.pallas_call(kernel, out_shape=[jax.ShapeDtypeStruct(v.shape[1:], resul...  83.4 us
    dot_general x7, matrix products, dot(): return jnp.dot(a, b, preferred_element_type=f32)  38.7 us
    dot_general x7, matrix products, dot_nt(): lax.dot_general(a, b, (((1,), (1,)), ((), ())), preferred_element_type=f32)  37.9 us
    pallas_call x1, Pallas kernels, sum_gather_call(): pl.pallas_call(kernel, out_shape=[jax.ShapeDtypeStruct((rows, columns), f...  35.3 us
    dot_general x7, matrix products, dot_tn(): lax.dot_general(a, b, (((0,), (0,)), ((), ())), preferred_element_type=f32)  31.6 us
    pallas_call x1, Pallas kernels, copies_total_call(): pl.pallas_call(kernel, out_shape=jax.ShapeDtypeStruct(terms.shape, bf16),...  24.6 us
    unnamed x132, local copies, waits for them, and re-layouts  16.8 us

profile of v1, /device:TPU:0, one launch (start us, length us, event | category | flops | bytes accessed | tf_op | source)
XLA Modules:
  0.0 589.2 jit_solution(6104798754142285751)
XLA Ops:
  18.2 33.6 %shard_map.246 = bf16[16,64,3200]{2,1,0:T(8,128)(2,1)} custom-call(bf16[64,3200]{1,0:T(8,128)(2,1)} %constant_dynamic-update-slice_fusion.refs_0_), custom_call_target="tpu_custom_call" | custom-call | tf_op jit(solution)/shard_map/pallas_call | solution.py:362
  51.8 2.7 slice_convert_fusion.2
  86.2 38.0 %shard_map.247 = (bf16[16,256,1024]{2,1,0:T(8,128)(2,1)}, bf16[8,256,1024]{2,1,0:T(8,128)(2,1)}) custom-call(bf16[256,1024]{1,0:T(8,128)(2,1)} %bitcast.253, bf16[256,1024]{1,0:T(8,128)(2,1)} %pad_maximum_fusion.8.refs_1_), custom_call_target="tpu_custom_call" | custom-call | tf_op jit(solution)/shard_map/pallas_call | solution.py:362
  124.3 2.6 copy.179
  129.3 4.0 copy.181
  133.3 4.1 copy.180
  137.4 10.2 %fusion.97 = (f32[2,8,2,128]{3,2,1,0:T(2,128)S(1)}, f32[2,8,2,128,1024]{3,4,2,1,0:T(8,128)}) fusion(bf16[2,1024,8,64,1]{1,3,4,2,0:T(8,128)(2,1)} %bitcast.209, bf16[2,128,8,2,64]{1,0,4,3,2:T(2,128)(2,1)S(1)} %fusion.53, pred[2,128,1024]{1,2,0:T(8,128)(4,1)S(1)} %copy-done.28), kind=kOutput, calls=%fused_computation.219 | convolution fusion | flops 549449728 | bytes 19677184 | tf_op jit(solution)/shard_map/bqkgd,bskd->bkgqs/dot_general | solution.py:725
  147.6 8.4 %fusion.7 = f32[2,8,2,128]{3,2,1,0:T(2,128)S(1)} fusion(f32[2,8,2,128,1024]{3,4,2,1,0:T(8,128)} %get-tuple-element.140, f32[2,8,2,128]{3,2,1,0:T(2,128)S(1)} %get-tuple-element.139), kind=kLoop, calls=%fused_computation.17 | loop fusion | flops 8384512 | bytes 16809984 | tf_op jit(solution)/shard_map/reduce_sum | solution.py:733
  156.6 7.4 %fusion.46 = bf16[2,128,8,2,64]{1,4,3,2,0:T(8,128)(2,1)S(1)} fusion(bf16[2,1024,8,64,1]{1,3,4,2,0:T(8,128)(2,1)S(1)} %bitcast.230, f32[2,8,2,128,1024]{3,4,2,1,0:T(8,128)} %get-tuple-element.140, f32[2,8,2,128]{3,2,1,0:T(2,128)S(1)} %fusion.7, f32[2,8,2,128]{3,2,1,0:T(2,128)S(1)} %get-tuple-element.139), kind=kOutput, calls=%fused_computation.73 | convolution fusion | flops 549715968 | bytes 19431424 | tf_op jit(solution)/shard_map/bkgqs,bskd->bqkgd/dot_general | solution.py:737
  172.9 41.2 %shard_map.248 = bf16[16,256,1152]{2,1,0:T(8,128)(2,1)} custom-call(bf16[256,1152]{1,0:T(8,128)(2,1)} %concatenate.67.refs_0_), custom_call_target="tpu_custom_call" | custom-call | tf_op jit(solution)/shard_map/pallas_call | solution.py:362
  215.7 8.0 %fusion.5 = bf16[16,256,1024]{2,1,0:T(8,128)(2,1)} fusion(bf16[16,256,1024]{2,1,0:T(8,128)(2,1)} %get-tuple-element.22, f32[16,256]{1,0:T(8,128)S(1)} %mul.453), kind=kLoop, calls=%fused_computation.11 | loop fusion | flops 12582912 | bytes 16793600 | tf_op jit(solution)/shard_map/convert_element_type | solution.py:773
  223.8 14.9 %fusion.15 = f32[4096,1024]{0,1:T(8,128)} fusion(bf16[4096,1152]{1,0:T(8,128)(2,1)} %bitcast.226, bf16[1,1024,1024]{2,1,0:T(8,128)(2,1)S(1)} %copy-done), kind=kOutput, calls=%fused_computation.32 | convolution fusion | flops 8589934592 | bytes 27262976 | tf_op jit(solution)/shard_map/dot_general | solution.py:616
  238.7 16.3 %multiply_convert_fusion.1 = (bf16[4096,512]{0,1:T(8,128)(2,1)}, bf16[4096,512]{0,1:T(8,128)(2,1)}, bf16[4096,512]{0,1:T(8,128)(2,1)}) fusion(f32[4096,1024]{0,1:T(8,128)} %fusion.15, bf16[4096,1024]{1,0:T(8,128)(2,1)} %bitcast.229, bf16[1,512,1024]{2,1,0:T(8,128)(2,1)S(1)} %copy-done.59), kind=kOutput, calls=%fused_computation.23 | convolution fusion | flops 4328521728 | bytes 38797312 | tf_op jit(solution)/shard_map/dot_general | solution.py:620
  255.1 14.5 %fusion.23 = bf16[1024,1024]{1,0:T(8,128)(2,1)S(1)} fusion(bf16[4096,512]{0,1:T(8,128)(2,1)} %get-tuple-element.108, bf16[4096,512]{0,1:T(8,128)(2,1)} %get-tuple-element.107, bf16[4096,1152]{1,0:T(8,128)(2,1)} %bitcast.227), kind=kOutput, calls=%fused_computation.46 | convolution fusion | flops 8607760384 | bytes 18874368 | tf_op jit(solution)/shard_map/dot_general | solution.py:624
  269.5 11.3 %convolution_convert_fusion = bf16[4096,1024]{0,1:T(8,128)(2,1)S(1)} fusion(bf16[4096,512]{0,1:T(8,128)(2,1)} %get-tuple-element.108, bf16[4096,512]{0,1:T(8,128)(2,1)} %get-tuple-element.107, bf16[1,1024,1024]{2,1,0:T(8,128)(2,1)S(1)} %copy-done), kind=kOutput, calls=%fused_computation.28 | convolution fusion | flops 8610906112 | bytes 18874368 | tf_op jit(solution)/shard_map/dot_general | solution.py:620
  280.8 13.1 %fusion.6 = (bf16[4096,1024]{1,0:T(8,128)(2,1)}, f32[4096]{0:T(1024)S(1)}, bf16[4096,1024]{1,0:T(8,128)(2,1)}) fusion(bf16[16,256,1024]{2,1,0:T(8,128)(2,1)} %get-tuple-element.22, f32[4096]{0:T(1024)S(1)} %select_reduce_fusion, bf16[4096,512]{0,1:T(8,128)(2,1)} %get-tuple-element.109, bf16[1,512,1024]{2,1,0:T(8,128)(2,1)} %param.29), kind=kOutput, calls=%fused_computation.12 | convolution fusion | flops 4332711936 | bytes 30441472 | tf_op jit(solution)/shard_map/dot_general | solution.py:616
  294.0 9.2 %convolution_convert_fusion.2 = bf16[512,1024]{1,0:T(8,128)(2,1)S(1)} fusion(bf16[4096,512]{0,1:T(8,128)(2,1)} %get-tuple-element.109, bf16[4096,1024]{1,0:T(8,128)(2,1)} %get-tuple-element.110), kind=kOutput, calls=%fused_computation.58 | convolution fusion | flops 4295491584 | bytes 13631488 | tf_op jit(solution)/shard_map/dot_general | solution.py:624
  305.3 7.2 %pad_maximum_fusion = bf16[4096,1152]{0,1:T(8,128)(2,1)} fusion(bf16[4096,128]{0,1:T(8,128)(2,1)S(1)} %select_add_fusion, bf16[4096,1024]{0,1:T(8,128)(2,1)S(1)} %convolution_convert_fusion), kind=kLoop, calls=%fused_computation.19 | loop fusion | flops 18874368 | bytes 18874368 | tf_op jit(solution)/shard_map/concatenate | solution.py:792
  312.5 12.8 %copy.191 = bf16[4096,1152]{1,0:T(8,128)(2,1)} copy(bf16[4096,1152]{0,1:T(8,128)(2,1)} %pad_maximum_fusion) | data formatting | bytes 18874368 | tf_op jit(solution)/shard_map/concatenate | solution.py:792
  325.3 43.5 %shard_map.249 = (f32[256,1152]{1,0:T(8,128)}, f32[192,1024]{1,0:T(8,128)}) custom-call(bf16[16,256,1152]{2,1,0:T(8,128)(2,1)} %bitcast.207, bf16[8,192,1024]{2,1,0:T(8,128)(2,1)} %bitcast.224), custom_call_target="tpu_custom_call" | custom-call | tf_op jit(solution)/shard_map/pallas_call | solution.py:458
  383.4 8.6 %bitcast_convert_fusion = bf16[2,8,64,1024]{3,2,1,0:T(8,128)(2,1)S(1)} fusion(bf16[2,128,8,2,64]{1,4,3,2,0:T(8,128)(2,1)S(1)} %copy.193, f32[2,8,2,128,1024]{3,4,2,1,0:T(8,128)} %get-tuple-element.140, f32[2,8,2,128]{3,2,1,0:T(2,128)S(1)} %bitcast.263), kind=kOutput, calls=%fused_computation.35 | convolution fusion | flops 546308096 | bytes 19415040 | tf_op jit(solution)/shard_map/bkgqs,bqkgd->bskd/dot_general | solution.py:815
  394.0 4.4 copy.199
  398.4 11.3 %fusion.2 = (f32[2,8,2,128]{3,2,1,0:T(2,128)S(1)}, f32[2,8,1024,128,2]{3,2,4,1,0:T(8,128)}) fusion(f32[2,8,2,128,1024]{3,4,2,1,0:T(8,128)} %get-tuple-element.140, f32[2,8,2,128]{3,2,1,0:T(2,128)S(1)} %bitcast.264, bf16[2,1024,8,64,1]{1,3,4,2,0:T(8,128)(2,1)S(1)} %bitcast.231, bf16[2,128,8,2,64]{1,4,3,2,0:T(8,128)(2,1)} %copy-done.14), kind=kOutput, calls=%fused_computation.6 | convolution fusion | flops 549449728 | bytes 36208640 | tf_op jit(solution)/shard_map/bqkgd,bskd->bkgqs/dot_general | solution.py:814
  409.6 11.9 %fusion.4 = bf16[2,8,2,128,1024]{3,4,2,1,0:T(8,128)(2,1)S(1)} fusion(f32[2,8,1024,128,2]{3,2,4,1,0:T(8,128)} %get-tuple-element.147, f32[2,8,2,128,1024]{3,4,2,1,0:T(8,128)} %get-tuple-element.140, f32[2,8,2,128]{3,2,1,0:T(2,128)S(1)} %get-tuple-element.146, f32[2,8,2,128]{3,2,1,0:T(2,128)S(1)} %bitcast.265), kind=kLoop, calls=%fused_computation.8 | loop fusion | flops 16777216 | bytes 41975808 | tf_op jit(solution)/shard_map/convert_element_type | solution.py:820
  424.1 2.6 fusion.17
  429.9 4.8 pad_maximum_fusion.4
  434.8 39.9 %shard_map.250 = (f32[256,1024]{1,0:T(8,128)}, f32[256,1024]{1,0:T(8,128)}) custom-call(bf16[16,256,1024]{2,1,0:T(8,128)(2,1)} %bitcast.232, bf16[8,256,1024]{2,1,0:T(8,128)(2,1)} %bitcast.211), custom_call_target="tpu_custom_call" | custom-call | tf_op jit(solution)/shard_map/pallas_call | solution.py:458
  505.3 9.6 %copy.207 = bf16[1024,3200]{1,0:T(8,128)(2,1)} copy(bf16[1024,3200]{0,1:T(8,128)(2,1)} %pad_dynamic-update-slice_fusion) | data formatting | bytes 13107200 | tf_op jit(solution)/shard_map/concatenate | solution.py:637
  514.9 35.3 %shard_map.251 = (f32[64,3200]{1,0:T(8,128)}, bf16[8,192,1024]{2,1,0:T(8,128)(2,1)}) custom-call(bf16[16,64,3200]{2,1,0:T(8,128)(2,1)} %bitcast.208, bf16[192,1024]{1,0:T(8,128)(2,1)} %convert_element_type.360.own), custom_call_target="tpu_custom_call" | custom-call | tf_op jit(solution)/shard_map/pallas_call | solution.py:502
  552.3 24.6 %shard_map.252 = bf16[8,64,512]{2,1,0:T(8,128)(2,1)} custom-call(bf16[8,64,512]{2,1,0:T(8,128)(2,1)} %bitcast.250), custom_call_target="tpu_custom_call" | custom-call | tf_op jit(solution)/shard_map/pallas_call | solution.py:539
  581.9 2.8 fusion.51
  584.7 4.1 fusion.20
  (258 shorter events, 124.0 us)
Async XLA Ops:
  0.6 223.1 %copy-start = (bf16[1,1024,1024]{2,1,0:T(8,128)(2,1)S(1)}, bf16[1,1024,1024]{2,1,0:T(8,128)(2,1)}, u32[]{:S(2)}) copy-start(bf16[1,1024,1024]{2,1,0:T(8,128)(2,1)} %param.28) | copy-start | bytes 6291460
  5.8 51.5 %copy-start.48 = (f32[256]{0:T(256)}, f32[256]{0:T(256)S(1)}, u32[]{:S(2)}) copy-start(f32[256]{0:T(256)S(1)} %bitcast_rsqrt_fusion) | copy-start | bytes 3076
  9.0 56.9 %copy-start.31 = (f32[8,8,2,128]{3,1,2,0:T(8,128)}, f32[8,8,2,128]{3,1,2,0:T(8,128)S(1)}, u32[]{:S(2)}) copy-start(f32[8,8,2,128]{3,1,2,0:T(8,128)S(1)} %copy.257) | copy-start | bytes 196612
  9.1 46.6 %copy-start.29 = (f32[8,8,2,128]{3,1,2,0:T(8,128)}, f32[8,8,2,128]{3,1,2,0:T(8,128)S(1)}, u32[]{:S(2)}) copy-start(f32[8,8,2,128]{3,1,2,0:T(8,128)S(1)} %copy.258) | copy-start | bytes 196612
  14.9 42.4 %copy-start.15 = (bf16[2,128,1024]{2,1,0:T(8,128)(2,1)S(1)}, bf16[2,128,1024]{2,1,0:T(8,128)(2,1)}, u32[]{:S(2)}) copy-start(bf16[2,128,1024]{2,1,0:T(8,128)(2,1)} %param.15) | copy-start | bytes 1572868
  57.0 17.4 %copy-start.37 = (f32[1024,1]{0,1:T(1,128)}, f32[1024,1]{0,1:T(1,128)S(1)}, u32[]{:S(2)}) copy-start(f32[1024,1]{0,1:T(1,128)S(1)} %copy.235) | copy-start | bytes 12292
  57.1 13.0 %copy-start.39 = (f32[512]{0:T(512)}, f32[512]{0:T(512)S(1)}, u32[]{:S(2)}) copy-start(f32[512]{0:T(512)S(1)} %reshape.442) | copy-start | bytes 6148
  57.3 14.7 %copy-start.41 = (f32[1024,1]{0,1:T(1,128)}, f32[1024,1]{0,1:T(1,128)S(1)}, u32[]{:S(2)}) copy-start(f32[1024,1]{0,1:T(1,128)S(1)} %copy.234) | copy-start | bytes 12292
  57.5 16.8 %copy-start.20 = (bf16[256,1024]{1,0:T(8,128)(2,1)}, bf16[256,1024]{1,0:T(8,128)(2,1)S(1)}, u32[]{:S(2)}) copy-start(bf16[256,1024]{1,0:T(8,128)(2,1)S(1)} %fusion.60) | copy-start | bytes 1572868
  61.8 12.6 %copy-start.9 = (f32[256,512]{1,0:T(8,128)}, f32[256,512]{1,0:T(8,128)S(1)}, u32[]{:S(2)}) copy-start(f32[256,512]{1,0:T(8,128)S(1)} %get-tuple-element.136) | copy-start | bytes 1572868
  61.8 14.7 %copy-start.53 = (f32[256]{0:T(256)}, f32[256]{0:T(256)S(1)}, u32[]{:S(2)}) copy-start(f32[256]{0:T(256)S(1)} %get-tuple-element.135) | copy-start | bytes 3076
  61.9 14.7 %copy-start.43 = (f32[256]{0:T(256)}, f32[256]{0:T(256)S(1)}, u32[]{:S(2)}) copy-start(f32[256]{0:T(256)S(1)} %fusion.85) | copy-start | bytes 3076
  74.4 11.8 %copy-start.52 = (f32[256]{0:T(256)}, f32[256]{0:T(256)S(1)}, u32[]{:S(2)}) copy-start(f32[256]{0:T(256)S(1)} %get-tuple-element.137) | copy-start | bytes 3076
  75.4 10.8 %copy-start.45 = (f32[256]{0:T(256)}, f32[256]{0:T(256)S(1)}, u32[]{:S(2)}) copy-start(f32[256]{0:T(256)S(1)} %fusion.86) | copy-start | bytes 3076
  86.2 51.1 %copy-start.18 = (bf16[2,128,8,2,64]{1,0,4,3,2:T(2,128)(2,1)}, bf16[2,128,8,2,64]{1,0,4,3,2:T(2,128)(2,1)S(1)}, u32[]{:S(2)}) copy-start(bf16[2,128,8,2,64]{1,0,4,3,2:T(2,128)(2,1)S(1)} %fusion.53) | copy-start | bytes 1572868
  126.9 10.5 %copy-start.28 = (pred[2,128,1024]{1,2,0:T(8,128)(4,1)S(1)}, pred[2,128,1024]{1,2,0:T(8,128)(4,1)}, u32[]{:S(2)}) copy-start(pred[2,128,1024]{1,2,0:T(8,128)(4,1)} %and_or_fusion) | copy-start | bytes 786436
  147.6 9.0 %copy-start.7 = (bf16[2,1024,512]{1,2,0:T(8,128)(2,1)S(1)}, bf16[2,1024,512]{1,2,0:T(8,128)(2,1)}, u32[]{:S(2)}) copy-start(bf16[2,1024,512]{1,2,0:T(8,128)(2,1)} %copy.180) | copy-start | bytes 6291460
  156.6 8.0 %copy-start.16 = (bf16[2,128,1024]{2,1,0:T(8,128)(2,1)S(1)}, bf16[2,128,1024]{2,1,0:T(8,128)(2,1)}, u32[]{:S(2)}) copy-start(bf16[2,128,1024]{2,1,0:T(8,128)(2,1)} %param.15) | copy-start | bytes 1572868
  223.8 15.0 %copy-start.59 = (bf16[1,512,1024]{2,1,0:T(8,128)(2,1)S(1)}, bf16[1,512,1024]{2,1,0:T(8,128)(2,1)}, u32[]{:S(2)}) copy-start(bf16[1,512,1024]{2,1,0:T(8,128)(2,1)} %param.29) | copy-start | bytes 3145732
  294.0 11.2 %copy-start.57 = (pred[128]{0:T(512)(128)(4,1)S(1)}, pred[128]{0:T(512)(128)(4,1)}, u32[]{:S(2)}) copy-start(pred[128]{0:T(512)(128)(4,1)} %iota_compare_fusion.2) | copy-start | bytes 388
  294.0 11.2 %copy-start.58 = (pred[128]{0:T(512)(128)(4,1)S(1)}, pred[128]{0:T(512)(128)(4,1)}, u32[]{:S(2)}) copy-start(pred[128]{0:T(512)(128)(4,1)} %get-tuple-element.152) | copy-start | bytes 388
  325.3 47.9 %copy-start.12 = (bf16[256,1024]{1,0:T(8,128)(2,1)S(1)}, bf16[256,1024]{1,0:T(8,128)(2,1)}, u32[]{:S(2)}) copy-start(bf16[256,1024]{1,0:T(8,128)(2,1)} %copy-done.11) | copy-start | bytes 1572868
  325.3 50.6 %copy-start.56 = (f32[256]{0:T(256)S(1)}, f32[256]{0:T(256)}, u32[]{:S(2)}) copy-start(f32[256]{0:T(256)} %copy-done.55) | copy-start | bytes 3076
  325.3 50.6 %copy-start.24 = (bf16[2,128,1024]{2,1,0:T(8,128)(2,1)S(1)}, bf16[2,128,1024]{2,1,0:T(8,128)(2,1)}, u32[]{:S(2)}) copy-start(bf16[2,128,1024]{2,1,0:T(8,128)(2,1)} %param.16) | copy-start | bytes 1572868
  374.1 9.3 %copy-start.35 = (f32[2,2,8,128]{3,2,1,0:T(8,128)S(1)}, f32[2,2,8,128]{3,2,1,0:T(8,128)}, u32[]{:S(2)}) copy-start(f32[2,2,8,128]{3,2,1,0:T(8,128)} %log_add_fusion) | copy-start | bytes 49156
  376.2 15.8 %copy-start.3 = (f32[256,1024]{1,0:T(8,128)}, f32[256,1024]{1,0:T(8,128)S(1)}, u32[]{:S(2)}) copy-start(f32[256,1024]{1,0:T(8,128)S(1)} %fusion.47) | copy-start | bytes 3145732
  383.3 8.7 %copy-start.14 = (bf16[2,128,8,2,64]{1,4,3,2,0:T(8,128)(2,1)}, bf16[2,128,8,2,64]{1,4,3,2,0:T(8,128)(2,1)S(1)}, u32[]{:S(2)}) copy-start(bf16[2,128,8,2,64]{1,4,3,2,0:T(8,128)(2,1)S(1)} %copy.193) | copy-start | bytes 1572868
  409.6 11.9 %copy-start.2 = (bf16[2,1024,512]{1,2,0:T(8,128)(2,1)S(1)}, bf16[2,1024,512]{1,2,0:T(8,128)(2,1)}, u32[]{:S(2)}) copy-start(bf16[2,1024,512]{1,2,0:T(8,128)(2,1)} %copy.181) | copy-start | bytes 6291460
  434.8 42.1 %copy-start.13 = (f32[2,128,8,2,64]{1,4,3,2,0:T(8,128)S(1)}, f32[2,128,8,2,64]{1,4,3,2,0:T(8,128)}, u32[]{:S(2)}) copy-start(f32[2,128,8,2,64]{1,4,3,2,0:T(8,128)} %fusion.44) | copy-start | bytes 3145732
  490.0 7.4 %copy-start.47 = (bf16[1024,1]{0,1:T(2,128)(2,1)S(1)}, bf16[1024,1]{0,1:T(2,128)(2,1)}, u32[]{:S(2)}) copy-start(bf16[1024,1]{0,1:T(2,128)(2,1)} %convert_element_type.358) | copy-start | bytes 6148
  490.0 7.4 %copy-start.21 = (bf16[256,1024]{1,0:T(8,128)(2,1)S(1)}, bf16[256,1024]{1,0:T(8,128)(2,1)}, u32[]{:S(2)}) copy-start(bf16[256,1024]{1,0:T(8,128)(2,1)} %copy-done.20) | copy-start | bytes 1572868
  576.9 11.8 %copy-start.1 = (bf16[1,1024,1024]{2,1,0:T(8,128)(2,1)S(1)}, bf16[1,1024,1024]{2,1,0:T(8,128)(2,1)}, u32[]{:S(2)}) copy-start(bf16[1,1024,1024]{2,1,0:T(8,128)(2,1)} %param.28) | copy-start | bytes 6291460
  (28 other events, 140.8 us)

commit v2 on v1

--- a/solution.py
+++ b/solution.py
@@ -69,9 +69,12 @@
     def __init__(self, side, spot, ahead, behind, across):
         self.side, self.spot = side, spot
         self.ahead, self.behind, self.across = ahead, behind, across
+        sides = (side, 1 - side)
+        spots = [lax.rem(spot + step, RING) for step in range(RING)]
+        self.places = [[(sides[flip], spots[step]) for step in range(RING)] for flip in range(2)]
 
     def at(self, flip, step):
-        return (1 - self.side) if flip else self.side, lax.rem(self.spot + RING + step, RING)
+        return self.places[flip][step % RING]
 
     def neighbours(self):
         return [self.ahead, self.behind, self.across]
@@ -89,31 +92,26 @@
         self.send_sem, self.recv_sem = send_sem, recv_sem
         self.sent = []
 
-    def send(self, index, source, target, device):
-        copy = pltpu.make_async_remote_copy(
-            src_ref=source,
-            dst_ref=target,
+    def copy(self, index, source, target, device):
+        return pltpu.make_async_remote_copy(
+            src_ref=source(),
+            dst_ref=target(),
             send_sem=self.send_sem.at[index],
             recv_sem=self.recv_sem.at[index],
             device_id=device,
             device_id_type=pl.DeviceIdType.MESH,
         )
-        copy.start()
-        self.sent.append(copy)
+
+    def send(self, index, source, target, device):
+        self.copy(index, source, target, device).start()
+        self.sent.append((index, source, target, device))
 
     def take(self, index, target, device):
-        pltpu.make_async_remote_copy(
-            src_ref=target,
-            dst_ref=target,
-            send_sem=self.send_sem.at[index],
-            recv_sem=self.recv_sem.at[index],
-            device_id=device,
-            device_id_type=pl.DeviceIdType.MESH,
-        ).wait_recv()
+        self.copy(index, target, target, device).wait_recv()
 
     def finish(self):
-        for copy in self.sent:
-            copy.wait_send()
+        for sent in self.sent:
+            self.copy(*sent).wait_send()
 
 
 def abreast(*parts):
@@ -129,65 +127,70 @@
 GATHER_SEMS = 20
 
 
-def gather_parts(axes, line, own, block, rows, local_sem, twin=None):
+def gather_parts(axes, line, own, block, rows, local_sem, twin=None, twin_later=False):
     half, quarter = rows // 2, rows // 4
     mine, back, front, far = axes.at(0, 0), axes.at(0, -1), axes.at(0, 1), axes.at(0, 2)
     pair, pair_back, pair_front, pair_far = (axes.at(1, n) for n in (0, -1, 1, 2))
     ahead, behind, across = axes.ahead, axes.behind, axes.across
 
-    def full(which):
-        return block(which, 0, rows)
+    def rows_of(which, low=0, count=rows, other=False):
+        return lambda: block(which, low, count, other)
+
+    def first(index, device):
+        line.send(index, lambda: own, rows_of(mine), device)
+
+    def relay(index, device, which, low=0, count=rows):
+        line.send(index, rows_of(which, low, count), rows_of(which, low, count), device)
 
     def share(index, which):
         if twin is not None:
-            line.send(12 + index, full(which), full(which), twin)
-
-    keep = pltpu.make_async_copy(own, full(mine), local_sem)
-    keep.start()
-    line.send(0, own, full(mine), ahead)
-    line.send(1, own, full(mine), behind)
-    line.send(2, own, full(mine), across)
+            relay(12 + index, twin, which)
+
+    def keep():
+        return pltpu.make_async_copy(own, block(mine, 0, rows), local_sem)
+
+    keep().start()
     if twin is not None:
-        line.send(12, own, full(mine), twin)
+        first(12, twin)
+    first(0, ahead)
+    first(1, behind)
+    first(2, across)
+    keep().wait()
     yield
-    line.take(0, full(back), ahead)
-    line.send(3, block(back, 0, half), block(back, 0, half), ahead)
-    line.send(4, block(back, half, half), block(back, half, half), across)
+    line.take(0, rows_of(back), ahead)
+    relay(3, ahead, back, 0, half)
+    relay(4, across, back, half, half)
     share(1, back)
-    line.take(1, full(front), behind)
-    line.send(5, block(front, half, half), block(front, half, half), behind)
-    line.send(6, block(front, half, half), block(front, half, half), across)
+    line.take(1, rows_of(front), behind)
+    relay(5, behind, front, half, half)
+    relay(6, across, front, half, half)
     share(2, front)
-    line.take(2, full(pair), across)
-    line.send(7, block(pair, 0, half), block(pair, 0, half), ahead)
-    line.send(8, block(pair, 0, half), block(pair, 0, half), behind)
+    line.take(2, rows_of(pair), across)
+    relay(7, ahead, pair, 0, half)
+    relay(8, behind, pair, 0, half)
     share(3, pair)
     yield
-    line.take(3, block(far, 0, half), ahead)
-    line.take(5, block(far, half, half), behind)
-    line.send(9, block(far, half, half), block(far, half, half), across)
+    line.take(3, rows_of(far, 0, half), ahead)
+    line.take(5, rows_of(far, half, half), behind)
+    relay(9, across, far, half, half)
     share(4, far)
-    line.take(7, block(pair_back, 0, half), ahead)
-    line.send(10, block(pair_back, 0, quarter), block(pair_back, 0, quarter), ahead)
-    line.take(8, block(pair_front, 0, half), behind)
-    line.send(
-        11, block(pair_front, quarter, quarter), block(pair_front, quarter, quarter), behind
-    )
-    line.take(4, block(pair_back, half, half), across)
+    line.take(7, rows_of(pair_back, 0, half), ahead)
+    relay(10, ahead, pair_back, 0, quarter)
+    line.take(8, rows_of(pair_front, 0, half), behind)
+    relay(11, behind, pair_front, quarter, quarter)
+    line.take(4, rows_of(pair_back, half, half), across)
     share(5, pair_back)
-    line.take(6, block(pair_front, half, half), across)
+    line.take(6, rows_of(pair_front, half, half), across)
     share(6, pair_front)
     yield
-    line.take(10, block(pair_far, 0, quarter), ahead)
-    line.take(11, block(pair_far, quarter, quarter), behind)
-    line.take(9, block(pair_far, half, half), across)
+    line.take(10, rows_of(pair_far, 0, quarter), ahead)
+    line.take(11, rows_of(pair_far, quarter, quarter), behind)
+    line.take(9, rows_of(pair_far, half, half), across)
     share(7, pair_far)
-    keep.wait()
-    if twin is not None:
-        for index, which in enumerate(
-            (mine, back, front, pair, far, pair_back, pair_front, pair_far)
-        ):
-            line.take(12 + index, block(which, 0, rows, True), twin)
+    yield
+    if twin is not None and not twin_later:
+        for index, which in enumerate(gather_order(axes)):
+            line.take(12 + index, rows_of(which, other=True), twin)
     line.finish()
 
 
@@ -200,7 +203,7 @@
 
     def body(index, carry):
         at = pl.ds(pl.multiple_of(index * step, step), step)
-        target[at] = (target[at].astype(f32) + source[at].astype(f32)).astype(bf16)
+        target[at] = target[at] + source[at]
         return carry
 
     lax.fori_loop(0, count, body, 0)
@@ -208,6 +211,14 @@
 
 def stage_rows(rows):
     return 7 * rows
+
+
+def gather_order(axes):
+    return [axes.at(*v) for v in ((0, 0), (0, -1), (0, 1), (1, 0), (0, 2), (1, -1), (1, 1), (1, 2))]
+
+
+def sum_order(axes):
+    return [axes.at(*v) for v in ((1, 2), (0, 2), (1, -1), (1, 1), (0, -1), (0, 1), (1, 0), (0, 0))]
 
 
 def sum_parts(axes, line, part, stage, rows, result, twin=None):
@@ -215,7 +226,7 @@
     mine, back, front, far = axes.at(0, 0), axes.at(0, -1), axes.at(0, 1), axes.at(0, 2)
     pair, pair_back, pair_front, pair_far = (axes.at(1, n) for n in (0, -1, 1, 2))
     ahead, behind, across = axes.ahead, axes.behind, axes.across
-    order = (pair_far, far, pair_back, pair_front, back, front, pair, mine)
+    order = sum_order(axes)
     offsets, used = {}, 0
     for name, size in (
         ("Y0", half), ("M0", quarter), ("P0", quarter), ("M1", half), ("Y1", half), ("Y2", half),
@@ -226,27 +237,33 @@
 
     def landing(name):
         low, size, _ = offsets[name]
-        return stage.at[pl.ds(low, size)]
+        return lambda: stage.at[pl.ds(low, size)]
 
     def send(name, which, low, device):
         _, size, index = offsets[name]
-        line.send(index, part(which, low, size), landing(name), device)
+        line.send(index, lambda: part(which, low, size), landing(name), device)
 
     def add(name, which, low, device):
         _, size, index = offsets[name]
         line.take(index, landing(name), device)
-        add_rows(part(which, low, size), landing(name), size)
+        add_rows(part(which, low, size), landing(name)(), size)
 
     def join(*places):
         if twin is not None:
             for place in places:
-                line.take(12 + place, twin[2](order[place]), twin[0])
+                line.take(12 + place, lambda: twin[2](order[place]), twin[0])
                 add_rows(part(order[place], 0, rows), twin[2](order[place]), rows)
 
-    if twin is not None:
-        for place, which in enumerate(order):
-            line.send(12 + place, twin[1](which), twin[2](which), twin[0])
-        yield
+    def hand(*places):
+        if twin is not None:
+            for place in places:
+                which = order[place]
+                line.send(
+                    12 + place, lambda w=which: twin[1](w), lambda w=which: twin[2](w), twin[0]
+                )
+
+    hand(0, 1, 2, 3)
+    yield
     join(0)
     send("Y0", pair_far, half, across)
     send("M0", pair_far, 0, behind)
@@ -258,14 +275,15 @@
     join(3)
     send("Y2", pair_front, half, across)
     yield
+    hand(4, 5, 6, 7)
     add("M0", pair_back, 0, behind)
     send("M2", pair_back, 0, behind)
     add("P0", pair_front, quarter, ahead)
     send("P2", pair_front, 0, ahead)
     add("Y0", far, half, across)
     send("P1", far, half, ahead)
+    yield
     join(4, 5, 6, 7)
-    yield
     add("M1", back, 0, behind)
     add("Y1", back, half, across)
     send("M3", back, 0, behind)
@@ -563,6 +581,266 @@
     return total.transpose(1, 0, 2).reshape(rows, wide)[:, :columns].astype(f32)
 
 
+def dot(a, b):
+    return jnp.dot(a, b, preferred_element_type=f32)
+
+
+def dot_nt(a, b):
+    return lax.dot_general(a, b, (((1,), (1,)), ((), ())), preferred_element_type=f32)
+
+
+def dot_tn(a, b):
+    return lax.dot_general(a, b, (((0,), (0,)), ((), ())), preferred_element_type=f32)
+
+
+def pick(index, values):
+    chosen = values[-1]
+    for at in range(len(values) - 2, -1, -1):
+        chosen = jnp.where(index == at, values[at], chosen)
+    return chosen
+
+
+def moe_call(collective_id, sent, grad_all, inner, outer):
+    count, columns = sent.shape
+    width = inner.shape[0]
+    hidden_width = outer.shape[0]
+    small = columns - width
+    half = count // 2
+    both = 2 * half
+    chips = GROUP // 2
+
+    def kernel(
+        sent_ref, grad_ref, inner_ref, outer_ref,
+        out_terms, returned, terms,
+        rows_in, grads, hidden, back_gu, total, back, staged, stage, outbox,
+        gs0, gr0, gs1, gr1, ss0, sr0, ss1, sr1, own_sem, grad_sem, out_sem,
+    ):
+        place = Place()
+        axes, core, shard = place.tokens, place.core, place.shard
+        gather_lines = (Line(gs0, gr0), Line(gs1, gr1))
+        sum_lines = (Line(ss0, sr0), Line(ss1, sr1))
+
+        def blocks(which, other=False):
+            return (which[0] * RING + which[1]) * 2 + ((1 - core) if other else core)
+
+        def gather_of(chunk):
+            def block(which, low, n, other=False):
+                return rows_in.at[chunk, blocks(which, other), pl.ds(low, n)]
+
+            return gather_parts(
+                axes, gather_lines[chunk], sent_ref.at[pl.ds(chunk * half, half)], block, half,
+                own_sem.at[chunk], place.twin, twin_later=chunk == 0,
+            )
+
+        def sum_of(chunk):
+            def part(which, low, n):
+                return back.at[chunk, blocks(which), pl.ds(low, n)]
+
+            def outgoing(which):
+                return back.at[chunk, blocks(which, True)]
+
+            def landed(which):
+                return staged.at[chunk, which[0] * RING + which[1]]
+
+            return sum_parts(
+                axes, sum_lines[chunk], part, stage.at[chunk], half,
+                returned.at[pl.ds(chunk * half, half)], (place.twin, outgoing, landed),
+            )
+
+        def grad_load(chunk):
+            return pltpu.make_async_copy(
+                grad_ref.at[:, pl.ds(chunk * half, half)], grads, grad_sem
+            )
+
+        def out_copy(chunk, chip, slot):
+            return pltpu.make_async_copy(
+                outbox.at[slot],
+                out_terms.at[pl.ds(chip * 2, 2), pl.ds(chunk * half, half)],
+                out_sem.at[slot],
+            )
+
+        lanes = lax.broadcasted_iota(jnp.int32, (both, small), 1)
+        is_high, is_rest = lanes == shard, lanes == shard + GROUP
+
+        def tile(chunk, chip, slot, wait_first):
+            at = pl.ds(chip * 2, 2)
+            row_block = rows_in[chunk, at].reshape(both, columns)
+            rows = row_block[:, :width]
+            gate = jnp.sum(
+                jnp.where(is_high | is_rest, row_block[:, width:].astype(f32), 0.0),
+                axis=1, keepdims=True,
+            )
+            gate_up = dot(rows, inner_ref[...])
+            gate_part, up_part = gate_up[:, :hidden_width], gate_up[:, hidden_width:]
+            sigmoid = 1.0 / (1.0 + jnp.exp(-gate_part))
+            active = gate_part * sigmoid
+            product = active * up_part
+            hidden_low = product.astype(bf16)
+            hidden[at] = hidden_low.reshape(2, half, hidden_width)
+            out = (gate * dot(hidden_low, outer_ref[...])).astype(bf16)
+
+            @pl.when(wait_first)
+            def _():
+                out_copy(chunk, chip, slot).wait()
+
+            outbox[slot] = out.reshape(2, half, width)
+            out_copy(chunk, chip, slot).start()
+            grad = grads[at].reshape(both, width)
+            grad_hidden = dot_nt(grad, outer_ref[...])
+            grad_gate = jnp.sum(grad_hidden * product, axis=1, keepdims=True)
+            grad_hidden = grad_hidden * gate
+            grad_gate_up = jnp.concatenate(
+                [
+                    grad_hidden * up_part * sigmoid * (1.0 + gate_part * (1.0 - sigmoid)),
+                    grad_hidden * active,
+                ],
+                axis=1,
+            ).astype(bf16)
+            back_gu[at] = grad_gate_up.reshape(2, half, 2 * hidden_width)
+            grads[at] = (gate * grad.astype(f32)).astype(bf16).reshape(2, half, width)
+            grad_rows = dot_nt(grad_gate_up, inner_ref[...]).astype(bf16)
+            back[chunk, at, :, pl.ds(0, width)] = grad_rows.reshape(2, half, width)
+            high = grad_gate.astype(bf16).astype(f32)
+            tail = jnp.where(is_high, high, jnp.where(is_rest, grad_gate - high, 0.0))
+            back[chunk, at, :, pl.ds(width, small)] = tail.astype(bf16).reshape(2, half, small)
+
+        def weight_step(chunk, index):
+            low = pl.multiple_of(index * 256, 256)
+            terms_at = pl.ds(low, 256)
+            rows = rows_in[chunk, :, :, pl.ds(low, 256)].reshape(GROUP * half, 256)
+            return terms_at, dot_tn(rows, back_gu[...].reshape(GROUP * half, 2 * hidden_width))
+
+        def down_step(index):
+            low = pl.multiple_of(index * 256, 256)
+            terms_at = pl.ds(width + low, 256)
+            rows = hidden[:, :, pl.ds(low, 256)].reshape(GROUP * half, 256)
+            return terms_at, dot_tn(rows, grads[...].reshape(GROUP * half, width))
+
+        greet(axes.neighbours() + [place.twin])
+        gather0, gather1, sum0, sum1 = gather_of(0), gather_of(1), sum_of(0), sum_of(1)
+        next(gather0)
+        grad_load(0).start()
+        chips0 = [w[0] * RING + w[1] for w in gather_order(axes)]
+        chips1 = [w[0] * RING + w[1] for w in sum_order(axes)]
+        grad_load(0).wait()
+
+        def first_tiles(t, carry):
+            @pl.when(t == 1)
+            def _():
+                next(gather0)
+                next(gather1)
+
+            @pl.when(t == 4)
+            def _():
+                next(gather0)
+                next(gather1)
+
+            @pl.when(t == 7)
+            def _():
+                next(gather0)
+                next(gather1)
+
+            chip = pick(t, chips0)
+            gather_lines[0].take(
+                12 + t, lambda: rows_in.at[0, chip * 2 + 1 - core], place.twin
+            )
+            tile(0, chip, lax.rem(t, 2), t >= 2)
+            return carry
+
+        lax.fori_loop(0, chips, first_tiles, 0)
+        for _ in gather0:
+            pass
+        next(sum0)
+
+        def first_weights(index, carry):
+            at, value = weight_step(0, index)
+            total[at] = value
+            return carry
+
+        def first_downs(index, carry):
+            at, value = down_step(index)
+            total[at] = value
+            return carry
+
+        lax.fori_loop(0, width // 256, first_weights, 0)
+        next(sum0)
+        lax.fori_loop(0, hidden_width // 256, first_downs, 0)
+        grad_load(1).start()
+        for _ in gather1:
+            pass
+        grad_load(1).wait()
+
+        def second_tiles(t, carry):
+            @pl.when(t == 1)
+            def _():
+                next(sum0)
+
+            @pl.when(t == 3)
+            def _():
+                next(sum0)
+
+            @pl.when(t == 4)
+            def _():
+                next(sum1)
+
+            @pl.when(t == 6)
+            def _():
+                for _ in sum0:
+                    pass
+                next(sum1)
+
+            tile(1, pick(t, chips1), lax.rem(t, 2), t >= 0)
+            return carry
+
+        lax.fori_loop(0, chips, second_tiles, 0)
+        next(sum1)
+
+        def second_weights(index, carry):
+            at, value = weight_step(1, index)
+            terms[at] = (total[at] + value).astype(bf16)
+            return carry
+
+        def second_downs(index, carry):
+            at, value = down_step(index)
+            terms[at] = (total[at] + value).astype(bf16)
+            return carry
+
+        lax.fori_loop(0, width // 256, second_weights, 0)
+        next(sum1)
+        lax.fori_loop(0, hidden_width // 256, second_downs, 0)
+        for _ in sum1:
+            pass
+        for slot in range(2):
+            out_copy(1, 0, slot).wait()
+
+    term_rows = width + hidden_width
+    return pl.pallas_call(
+        kernel,
+        out_shape=[
+            jax.ShapeDtypeStruct((GROUP, count, width), bf16),
+            jax.ShapeDtypeStruct((count, columns), f32),
+            jax.ShapeDtypeStruct((term_rows, width), bf16),
+        ],
+        in_specs=[ANY, ANY, IN_VMEM, IN_VMEM],
+        out_specs=[ANY, IN_VMEM, IN_VMEM],
+        scratch_shapes=[
+            pltpu.VMEM((2, GROUP, half, columns), bf16),
+            pltpu.VMEM((GROUP, half, width), bf16),
+            pltpu.VMEM((GROUP, half, hidden_width), bf16),
+            pltpu.VMEM((GROUP, half, 2 * hidden_width), bf16),
+            pltpu.VMEM((term_rows, width), f32),
+            pltpu.VMEM((2, GROUP, half, columns), bf16),
+            pltpu.VMEM((2, chips, half, columns), bf16),
+            pltpu.VMEM((2, stage_rows(half), columns), bf16),
+            pltpu.VMEM((2, 2, half, width), bf16),
+        ]
+        + sems(GATHER_SEMS) * 2
+        + sems(SUM_SEMS) * 2
+        + [pltpu.SemaphoreType.DMA((2,)), pltpu.SemaphoreType.DMA, pltpu.SemaphoreType.DMA((2,))],
+        compiler_params=params(collective_id),
+    )(sent, grad_all, inner, outer)
+
+
 def rms_scale(values, gain):
     return values * lax.rsqrt(jnp.mean(values * values, axis=-1, keepdims=True) + norm_eps) * gain
 
@@ -610,18 +888,6 @@
         sine_table,
     )
     return (query_rot, key_rot)
-
-
-def dot(a, b):
-    return jnp.dot(a, b, preferred_element_type=f32)
-
-
-def dot_nt(a, b):
-    return lax.dot_general(a, b, (((1,), (1,)), ((), ())), preferred_element_type=f32)
-
-
-def dot_tn(a, b):
-    return lax.dot_general(a, b, (((0,), (0,)), ((), ())), preferred_element_type=f32)
 
 
 SMALL = 128
@@ -659,7 +925,6 @@
     count = seqs * positions
     length = positions * REPS
     experts = GROUP
-    hidden_width = expert_down.shape[1]
     group = HEADS // KV_HEADS
     query_width = HEADS * HEAD_DIM
     kv_width = KV_HEADS * HEAD_DIM
@@ -754,48 +1019,10 @@
     sent = jnp.concatenate(
         [ffn_in, gates_high, gates_rest, jnp.zeros((count, SMALL - 2 * experts), bf16)], axis=1
     )
-    (got,) = gather_call(3, sent)
-    got = got.reshape(GROUP * count, width + SMALL)
-    rows_in = got[:, :width]
-    mine = (jnp.arange(SMALL) % experts == shard) & (jnp.arange(SMALL) < 2 * experts)
-    gate = jnp.sum(
-        jnp.where(mine[None, :], got[:, width:].astype(f32), 0.0), axis=1, keepdims=True
-    )
-
-    inner, outer = expert_in[0], expert_down[0]
-    grad_rows_out = grad_all.reshape(GROUP * count, width)
-    gate_up = dot(rows_in, inner)
-    gate_part, up_part = gate_up[:, :hidden_width], gate_up[:, hidden_width:]
-    sigmoid = jax.nn.sigmoid(gate_part)
-    hidden = (gate_part * sigmoid * up_part).astype(bf16)
-    expert_out = dot(hidden, outer).astype(bf16).astype(f32)
-    out_terms = (gate * expert_out).astype(bf16)
-    grad_expert = (gate * grad_rows_out.astype(f32)).astype(bf16)
-    grad_gate_own = jnp.sum(expert_out * grad_rows_out.astype(f32), axis=1, keepdims=True)
-    grad_hidden = dot_nt(grad_expert, outer)
-    grad_gate_up = jnp.concatenate(
-        [
-            grad_hidden * up_part * sigmoid * (1.0 + gate_part * (1.0 - sigmoid)),
-            grad_hidden * gate_part * sigmoid,
-        ],
-        axis=1,
-    ).astype(bf16)
-    grad_rows = dot_nt(grad_gate_up, inner).astype(bf16)
-    inner_grad = dot_tn(rows_in, grad_gate_up).astype(bf16)
-    outer_grad = dot_tn(hidden, grad_expert).astype(bf16)
-    own_high = grad_gate_own.astype(bf16)
-    own_rest = (grad_gate_own - own_high.astype(f32)).astype(bf16)
-    lanes = jnp.arange(SMALL)[None, :]
-    back_columns = jnp.where(lanes == shard, own_high, jnp.zeros((), bf16)) + jnp.where(
-        lanes == shard + experts, own_rest, jnp.zeros((), bf16)
-    )
-    back = jnp.concatenate([grad_rows, back_columns], axis=1)
-    expert_terms = jnp.concatenate([inner_grad, outer_grad], axis=0)
-    returned, expert_own = sum_call(
-        4,
-        back.reshape(GROUP, count, width + SMALL),
-        expert_terms.reshape(REPS, -1, width),
-    )
+    out_terms, returned, expert_terms = moe_call(
+        3, sent, grad_all, expert_in[0], expert_down[0]
+    )
+    (expert_own,) = sum_call(4, None, expert_terms.reshape(REPS, -1, width))
 
     grad_gates = returned[:, width : width + experts] + returned[:, width + experts : width + 2 * experts]
     grad_chosen = gates * (grad_gates - jnp.sum(gates * grad_gates, axis=-1, keepdims=True))
@@ -839,7 +1066,7 @@
         .transpose(1, 0, 2, 3)
         .reshape(REPS, count, 2 * kv_width)
     )
-    out_sum, pairs_own = sum_call(5, out_terms.reshape(GROUP, count, width), grad_pairs)
+    out_sum, pairs_own = sum_call(5, out_terms, grad_pairs)
     block_out = (middle + out_sum).astype(bf16)
 
     grad_query_rot = grad_query_rot.astype(bf16).astype(f32).reshape(count, HEADS, HEAD_DIM)

time: 598 us -> 529 us (0.88)
  matrix products: 151 us -> 70 us
  Pallas kernels: 256 us -> 320 us
  other arithmetic: 87.4 us -> 58.8 us
  local copies, waits for them, and re-layouts: 92.6 us -> 68.3 us
    pallas_call x0 -> x1, Pallas kernels: none -> 92.5 us  [moe_call(): pl.pallas_call(kernel, out_shape=[jax.ShapeDtypeStruct((GROUP, count, wid...]
    dot_general x7 -> x5, matrix products: 38.7 us -> 10.6 us  [dot(): return jnp.dot(a, b, preferred_element_type=f32)]
    dot_general x7 -> x5, matrix products: 37.9 us -> 10.7 us  [dot_nt(): lax.dot_general(a, b, (((1,), (1,)), ((), ())), preferred_element_type=f32)]
    dot_general x7 -> x5, matrix products: 31.6 us -> 8.09 us  [dot_tn(): lax.dot_general(a, b, (((0,), (0,)), ((), ())), preferred_element_type=f32)]
    pallas_call x2, Pallas kernels: 83.4 us -> 63.8 us  [sum_call(): pl.pallas_call(kernel, out_shape=[jax.ShapeDtypeStruct(v.shape[1:], resul...]
    pallas_call x3 -> x2, Pallas kernels: 113 us -> 95.2 us  [gather_call(): pl.pallas_call(kernel, out_shape=[jax.ShapeDtypeStruct((size,) + v.shape,...]
    concatenate x1 -> x0, local copies, waits for them, and re-layouts: 12.8 us -> none  [shards(): back = jnp.concatenate([grad_rows, back_columns], axis=1)]
    pallas_call x1, Pallas kernels: 35.3 us -> 44.7 us  [sum_gather_call(): pl.pallas_call(kernel, out_shape=[jax.ShapeDtypeStruct((rows, columns), f...]
where the time goes in v2:
time: 529 us; the launch traced here: 520 us
  Pallas kernels  320 us (60%)
  matrix products  70 us (13%)
  local copies, waits for them, and re-layouts  68.3 us (13%)
  other arithmetic  58.8 us (11%)
    pallas_call x2, Pallas kernels, gather_call(): pl.pallas_call(kernel, out_shape=[jax.ShapeDtypeStruct((size,) + v.shape,...  95.2 us
    pallas_call x1, Pallas kernels, moe_call(): pl.pallas_call(kernel, out_shape=[jax.ShapeDtypeStruct((GROUP, count, wid...  92.5 us
    pallas_call x2, Pallas kernels, sum_call(): pl.pallas_call(kernel, out_shape=[jax.ShapeDtypeStruct(v.shape[1:], resul...  63.8 us
    pallas_call x1, Pallas kernels, sum_gather_call(): pl.pallas_call(kernel, out_shape=[jax.ShapeDtypeStruct((rows, columns), f...  44.7 us
    pallas_call x1, Pallas kernels, copies_total_call(): pl.pallas_call(kernel, out_shape=jax.ShapeDtypeStruct(terms.shape, bf16),...  24.3 us
    unnamed x126, local copies, waits for them, and re-layouts  13.2 us
    dot_general x1, matrix products, shards(): jnp.einsum('bqkgd,bskd->bkgqs', grad_mixed, values_all, preferred_element...  11.8 us
    convert_element_type x1, other arithmetic, shards(): grad_scores = (soft_full * (grad_soft - jnp.sum(soft_full * grad_soft, ax...  11.7 us

profile of v2, /device:TPU:0, one launch (start us, length us, event | category | flops | bytes accessed | tf_op | source)
XLA Modules:
  0.0 519.7 jit_solution(1455655510295203702)
XLA Ops:
  13.5 36.6 %shard_map.246 = bf16[16,64,3200]{2,1,0:T(8,128)(2,1)} custom-call(bf16[64,3200]{1,0:T(8,128)(2,1)} %copy-done.25), custom_call_target="tpu_custom_call" | custom-call | tf_op jit(solution)/shard_map/pallas_call | solution.py:380
  53.2 2.6 convolution_convert_fusion.2
  60.1 2.4 multiply_reduce_fusion.5
  66.0 58.6 %shard_map.247 = (bf16[16,256,1024]{2,1,0:T(8,128)(2,1)}, bf16[8,256,1024]{2,1,0:T(8,128)(2,1)}) custom-call(bf16[256,1024]{1,0:T(8,128)(2,1)} %bitcast.222, bf16[256,1024]{1,0:T(8,128)(2,1)} %pad_maximum_fusion.1.refs_1_), custom_call_target="tpu_custom_call" | custom-call | tf_op jit(solution)/shard_map/pallas_call | solution.py:380
  124.6 2.6 copy.175
  127.3 2.4 fusion.74
  129.7 3.0 copy.177
  132.7 3.9 copy.176
  136.6 7.6 %fusion.79 = (f32[2,8,2,128]{3,2,1,0:T(2,128)S(1)}, f32[2,8,2,128,1024]{3,4,2,1,0:T(8,128)}) fusion(bf16[2,1024,8,64,1]{1,3,4,2,0:T(8,128)(2,1)S(1)} %bitcast.183, bf16[2,128,8,2,64]{1,0,4,3,2:T(2,128)(2,1)S(1)} %fusion.40, pred[2,128,1024]{1,2,0:T(8,128)(4,1)S(1)} %copy-done.24), kind=kOutput, calls=%fused_computation.182 | convolution fusion | flops 549449728 | bytes 19677184 | tf_op jit(solution)/shard_map/bqkgd,bskd->bkgqs/dot_general | solution.py:990
  144.3 8.4 %fusion.3 = f32[2,8,2,128]{3,2,1,0:T(2,128)S(1)} fusion(f32[2,8,2,128,1024]{3,4,2,1,0:T(8,128)} %get-tuple-element.134, f32[2,8,2,128]{3,2,1,0:T(2,128)S(1)} %get-tuple-element.133), kind=kLoop, calls=%fused_computation.9 | loop fusion | flops 8384512 | bytes 16809984 | tf_op jit(solution)/shard_map/reduce_sum | solution.py:998
  152.7 7.4 %fusion.33 = bf16[2,128,8,2,64]{1,4,3,2,0:T(8,128)(2,1)S(1)} fusion(bf16[2,1024,8,64,1]{1,3,4,2,0:T(8,128)(2,1)S(1)} %bitcast.200, f32[2,8,2,128,1024]{3,4,2,1,0:T(8,128)} %get-tuple-element.134, f32[2,8,2,128]{3,2,1,0:T(2,128)S(1)} %fusion.3, f32[2,8,2,128]{3,2,1,0:T(2,128)S(1)} %get-tuple-element.133), kind=kOutput, calls=%fused_computation.47 | convolution fusion | flops 549715968 | bytes 19431424 | tf_op jit(solution)/shard_map/bkgqs,bskd->bqkgd/dot_general | solution.py:1002
  160.7 2.6 multiply_reduce_fusion.4
  170.2 92.5 %shard_map.248 = (bf16[16,256,1024]{2,1,0:T(8,128)(2,1)}, f32[256,1152]{1,0:T(8,128)}, bf16[1536,1024]{1,0:T(8,128)(2,1)}) custom-call(bf16[256,1152]{1,0:T(8,128)(2,1)} %concatenate.57.sent_ref, bf16[16,256,1024]{2,1,0:T(8,128)(2,1)} %get-tuple-element.23.grad_ref, bf16[1024,1024]{1,0:T(8,128)(2,1)} %bitcast.223, bf16[512,1024]{1,0:T(8,128)(2,1)} %bitcast.225), custom_call_target="tpu_custom_call" | custom-call | tf_op jit(solution)/shard_map/pallas_call | solution.py:817
  262.8 25.4 %shard_map.250 = f32[192,1024]{1,0:T(8,128)} custom-call(bf16[8,192,1024]{2,1,0:T(8,128)(2,1)} %bitcast.212), custom_call_target="tpu_custom_call" | custom-call | tf_op jit(solution)/shard_map/pallas_call | solution.py:476
  296.1 3.2 fusion.26
  299.3 3.4 reshape.398
  302.7 3.6 copy.188
  306.3 8.6 %bitcast_convert_fusion = bf16[2,8,64,1024]{3,2,1,0:T(8,128)(2,1)S(1)} fusion(bf16[2,128,8,2,64]{1,4,3,2,0:T(8,128)(2,1)} %copy.188, f32[2,8,2,128,1024]{3,4,2,1,0:T(8,128)} %get-tuple-element.134, f32[2,8,2,128]{3,2,1,0:T(2,128)S(1)} %bitcast.234), kind=kOutput, calls=%fused_computation.15 | convolution fusion | flops 546308096 | bytes 19415040 | tf_op jit(solution)/shard_map/bkgqs,bqkgd->bskd/dot_general | solution.py:1042
  316.9 4.3 copy.194
  321.2 11.8 %fusion = (f32[2,8,2,128]{3,2,1,0:T(2,128)S(1)}, f32[2,8,1024,128,2]{3,2,4,1,0:T(8,128)}) fusion(f32[2,8,2,128,1024]{3,4,2,1,0:T(8,128)} %get-tuple-element.134, f32[2,8,2,128]{3,2,1,0:T(2,128)S(1)} %bitcast.235, bf16[2,1024,8,64,1]{1,3,4,2,0:T(8,128)(2,1)} %bitcast.199, bf16[2,128,8,2,64]{1,4,3,2,0:T(8,128)(2,1)} %copy.188), kind=kOutput, calls=%fused_computation.2 | convolution fusion | flops 549449728 | bytes 36208640 | tf_op jit(solution)/shard_map/bqkgd,bskd->bkgqs/dot_general | solution.py:1041
  333.0 11.7 %fusion.2 = bf16[2,8,2,128,1024]{3,4,2,1,0:T(8,128)(2,1)S(1)} fusion(f32[2,8,1024,128,2]{3,2,4,1,0:T(8,128)} %get-tuple-element.141, f32[2,8,2,128,1024]{3,4,2,1,0:T(8,128)} %get-tuple-element.134, f32[2,8,2,128]{3,2,1,0:T(2,128)S(1)} %get-tuple-element.140, f32[2,8,2,128]{3,2,1,0:T(2,128)S(1)} %bitcast.236), kind=kLoop, calls=%fused_computation.4 | loop fusion | flops 16777216 | bytes 41975808 | tf_op jit(solution)/shard_map/convert_element_type | solution.py:1047
  344.7 2.5 fusion.31
  347.2 2.6 fusion.9
  350.5 2.6 copy.193
  353.1 4.8 pad_maximum_fusion
  357.9 38.4 %shard_map.249 = (f32[256,1024]{1,0:T(8,128)}, f32[256,1024]{1,0:T(8,128)}) custom-call(bf16[16,256,1024]{2,1,0:T(8,128)(2,1)} %get-tuple-element.24.refs_0_, bf16[8,256,1024]{2,1,0:T(8,128)(2,1)} %bitcast.185), custom_call_target="tpu_custom_call" | custom-call | tf_op jit(solution)/shard_map/pallas_call | solution.py:476
  411.6 2.4 fusion.17
  427.0 9.6 %copy.202 = bf16[1024,3200]{1,0:T(8,128)(2,1)} copy(bf16[1024,3200]{0,1:T(8,128)(2,1)} %pad_dynamic-update-slice_fusion) | data formatting | bytes 13107200 | tf_op jit(solution)/shard_map/concatenate | solution.py:903
  436.6 44.7 %shard_map.251 = (f32[64,3200]{1,0:T(8,128)}, bf16[8,192,1024]{2,1,0:T(8,128)(2,1)}) custom-call(bf16[16,64,3200]{2,1,0:T(8,128)(2,1)} %bitcast.182, bf16[192,1024]{1,0:T(8,128)(2,1)} %convert_element_type.273.own), custom_call_target="tpu_custom_call" | custom-call | tf_op jit(solution)/shard_map/pallas_call | solution.py:520
  483.3 24.3 %shard_map.252 = bf16[8,64,512]{2,1,0:T(8,128)(2,1)} custom-call(bf16[8,64,512]{2,1,0:T(8,128)(2,1)} %bitcast.219), custom_call_target="tpu_custom_call" | custom-call | tf_op jit(solution)/shard_map/pallas_call | solution.py:557
  512.4 2.8 fusion.38
  515.2 4.1 fusion.12
  (236 shorter events, 76.1 us)
Async XLA Ops:
  4.6 48.4 %copy-start.48 = (f32[256]{0:T(256)}, f32[256]{0:T(256)S(1)}, u32[]{:S(2)}) copy-start(f32[256]{0:T(256)S(1)} %bitcast_rsqrt_fusion) | copy-start | bytes 3076
  11.8 41.2 %copy-start.10 = (bf16[2,128,1024]{2,1,0:T(8,128)(2,1)S(1)}, bf16[2,128,1024]{2,1,0:T(8,128)(2,1)}, u32[]{:S(2)}) copy-start(bf16[2,128,1024]{2,1,0:T(8,128)(2,1)} %param.15) | copy-start | bytes 1572868
  52.4 110.9 %copy-start.31 = (f32[1024,1]{0,1:T(1,128)}, f32[1024,1]{0,1:T(1,128)S(1)}, u32[]{:S(2)}) copy-start(f32[1024,1]{0,1:T(1,128)S(1)} %copy.231) | copy-start | bytes 12292
  52.6 10.0 %copy-start.29 = (f32[1024,1]{0,1:T(1,128)}, f32[1024,1]{0,1:T(1,128)S(1)}, u32[]{:S(2)}) copy-start(f32[1024,1]{0,1:T(1,128)S(1)} %copy.230) | copy-start | bytes 12292
  53.0 7.2 %copy-start.35 = (f32[1024,1]{0,1:T(1,128)}, f32[1024,1]{0,1:T(1,128)S(1)}, u32[]{:S(2)}) copy-start(f32[1024,1]{0,1:T(1,128)S(1)} %copy.229) | copy-start | bytes 12292
  53.2 9.3 %copy-start.15 = (bf16[256,1024]{1,0:T(8,128)(2,1)}, bf16[256,1024]{1,0:T(8,128)(2,1)S(1)}, u32[]{:S(2)}) copy-start(bf16[256,1024]{1,0:T(8,128)(2,1)S(1)} %fusion.44) | copy-start | bytes 1572868
  66.0 70.6 %copy-start.13 = (bf16[2,128,8,2,64]{1,0,4,3,2:T(2,128)(2,1)}, bf16[2,128,8,2,64]{1,0,4,3,2:T(2,128)(2,1)S(1)}, u32[]{:S(2)}) copy-start(bf16[2,128,8,2,64]{1,0,4,3,2:T(2,128)(2,1)S(1)} %fusion.40) | copy-start | bytes 1572868
  127.3 9.3 %copy-start.24 = (pred[2,128,1024]{1,2,0:T(8,128)(4,1)S(1)}, pred[2,128,1024]{1,2,0:T(8,128)(4,1)}, u32[]{:S(2)}) copy-start(pred[2,128,1024]{1,2,0:T(8,128)(4,1)} %and_or_fusion) | copy-start | bytes 786436
  144.3 8.4 %copy-start.4 = (bf16[2,1024,512]{1,2,0:T(8,128)(2,1)S(1)}, bf16[2,1024,512]{1,2,0:T(8,128)(2,1)}, u32[]{:S(2)}) copy-start(bf16[2,1024,512]{1,2,0:T(8,128)(2,1)} %copy.176) | copy-start | bytes 6291460
  152.7 8.0 %copy-start.11 = (bf16[2,128,1024]{2,1,0:T(8,128)(2,1)S(1)}, bf16[2,128,1024]{2,1,0:T(8,128)(2,1)}, u32[]{:S(2)}) copy-start(bf16[2,128,1024]{2,1,0:T(8,128)(2,1)} %param.15) | copy-start | bytes 1572868
  170.2 119.9 %copy-start.38 = (f32[256]{0:T(256)S(1)}, f32[256]{0:T(256)}, u32[]{:S(2)}) copy-start(f32[256]{0:T(256)} %copy-done.37) | copy-start | bytes 3076
  170.2 119.9 %copy-start.42 = (f32[256]{0:T(256)S(1)}, f32[256]{0:T(256)}, u32[]{:S(2)}) copy-start(f32[256]{0:T(256)} %copy-done.41) | copy-start | bytes 3076
  170.2 122.3 %copy-start.8 = (bf16[256,1024]{1,0:T(8,128)(2,1)S(1)}, bf16[256,1024]{1,0:T(8,128)(2,1)}, u32[]{:S(2)}) copy-start(bf16[256,1024]{1,0:T(8,128)(2,1)} %copy-done.7) | copy-start | bytes 1572868
  170.2 123.2 %copy-start.32 = (f32[1024,1]{0,1:T(1,128)S(1)}, f32[1024,1]{0,1:T(1,128)}, u32[]{:S(2)}) copy-start(f32[1024,1]{0,1:T(1,128)} %copy-done.31) | copy-start | bytes 12292
  170.2 123.2 %copy-start.47 = (f32[256]{0:T(256)S(1)}, f32[256]{0:T(256)}, u32[]{:S(2)}) copy-start(f32[256]{0:T(256)} %copy-done.46) | copy-start | bytes 3076
  262.7 30.6 %copy-start.19 = (f32[256,1152]{1,0:T(8,128)S(1)}, f32[256,1152]{1,0:T(8,128)}, u32[]{:S(2)}) copy-start(f32[256,1152]{1,0:T(8,128)} %get-tuple-element.25) | copy-start | bytes 3538948
  262.7 32.1 %copy-start.56 = (f32[256]{0:T(256)S(1)}, f32[256]{0:T(256)}, u32[]{:S(2)}) copy-start(f32[256]{0:T(256)} %copy-done.55) | copy-start | bytes 3076
  262.8 32.1 %copy-start.20 = (bf16[2,128,1024]{2,1,0:T(8,128)(2,1)S(1)}, bf16[2,128,1024]{2,1,0:T(8,128)(2,1)}, u32[]{:S(2)}) copy-start(bf16[2,128,1024]{2,1,0:T(8,128)(2,1)} %param.16) | copy-start | bytes 1572868
  357.9 40.6 %copy-start.9 = (f32[2,128,8,2,64]{1,4,3,2,0:T(8,128)S(1)}, f32[2,128,8,2,64]{1,4,3,2,0:T(8,128)}, u32[]{:S(2)}) copy-start(f32[2,128,8,2,64]{1,4,3,2,0:T(8,128)} %fusion.31) | copy-start | bytes 3145732
  398.5 6.4 %copy-start.6 = (f32[256,512]{1,0:T(8,128)S(1)}, f32[256,512]{1,0:T(8,128)}, u32[]{:S(2)}) copy-start(f32[256,512]{1,0:T(8,128)} %copy-done.5) | copy-start | bytes 1572868
  398.5 6.4 %copy-start.34 = (f32[512]{0:T(512)S(1)}, f32[512]{0:T(512)}, u32[]{:S(2)}) copy-start(f32[512]{0:T(512)} %copy-done.33) | copy-start | bytes 6148
  398.5 6.4 %copy-start.40 = (f32[256]{0:T(256)S(1)}, f32[256]{0:T(256)}, u32[]{:S(2)}) copy-start(f32[256]{0:T(256)} %copy-done.39) | copy-start | bytes 3076
  398.5 7.1 %copy-start.54 = (f32[256]{0:T(256)S(1)}, f32[256]{0:T(256)}, u32[]{:S(2)}) copy-start(f32[256]{0:T(256)} %copy-done.53) | copy-start | bytes 3076
  409.5 6.2 %copy-start.12 = (bf16[2,128,1024]{2,1,0:T(8,128)(2,1)S(1)}, bf16[2,128,1024]{2,1,0:T(8,128)(2,1)}, u32[]{:S(2)}) copy-start(bf16[2,128,1024]{2,1,0:T(8,128)(2,1)} %param.15) | copy-start | bytes 1572868
  409.5 6.2 %copy-start.22 = (bf16[256,1024]{1,0:T(8,128)(2,1)S(1)}, bf16[256,1024]{1,0:T(8,128)(2,1)}, u32[]{:S(2)}) copy-start(bf16[256,1024]{1,0:T(8,128)(2,1)} %copy-done.21) | copy-start | bytes 1572868
  410.5 7.3 %copy-start.51 = (f32[2,128]{1,0:T(2,128)S(1)}, f32[2,128]{1,0:T(2,128)}, u32[]{:S(2)}) copy-start(f32[2,128]{1,0:T(2,128)} %copy-done.50) | copy-start | bytes 3076
  410.5 7.3 %copy-start.1 = (f32[256,1024]{1,0:T(8,128)S(1)}, f32[256,1024]{1,0:T(8,128)}, u32[]{:S(2)}) copy-start(f32[256,1024]{1,0:T(8,128)} %copy-done) | copy-start | bytes 3145732
  411.6 7.4 %copy-start.28 = (bf16[1024,16]{0,1:T(8,128)(2,1)S(1)}, bf16[1024,16]{0,1:T(8,128)(2,1)}, u32[]{:S(2)}) copy-start(bf16[1024,16]{0,1:T(8,128)(2,1)} %convolution_convert_fusion.3) | copy-start | bytes 98308
  411.6 7.4 %copy-start.45 = (bf16[1024,1]{0,1:T(2,128)(2,1)S(1)}, bf16[1024,1]{0,1:T(2,128)(2,1)}, u32[]{:S(2)}) copy-start(bf16[1024,1]{0,1:T(2,128)(2,1)} %convert_element_type.271) | copy-start | bytes 6148
  411.6 7.4 %copy-start.16 = (bf16[256,1024]{1,0:T(8,128)(2,1)S(1)}, bf16[256,1024]{1,0:T(8,128)(2,1)}, u32[]{:S(2)}) copy-start(bf16[256,1024]{1,0:T(8,128)(2,1)} %copy-done.15) | copy-start | bytes 1572868
  415.8 6.9 %copy-start.23 = (bf16[256,1024]{1,0:T(8,128)(2,1)S(1)}, bf16[256,1024]{1,0:T(8,128)(2,1)}, u32[]{:S(2)}) copy-start(bf16[256,1024]{1,0:T(8,128)(2,1)} %copy-done.21) | copy-start | bytes 1572868
  417.7 6.4 %copy-start.18 = (bf16[2,128,8,2,64]{1,0,4,3,2:T(2,128)(2,1)S(1)}, bf16[2,128,8,2,64]{1,0,4,3,2:T(2,128)(2,1)}, u32[]{:S(2)}) copy-start(bf16[2,128,8,2,64]{1,0,4,3,2:T(2,128)(2,1)} %copy-done.17) | copy-start | bytes 1572868
  (25 other events, 77.5 us)

commit v3 on v2

--- a/solution.py
+++ b/solution.py
@@ -841,6 +841,284 @@
     )(sent, grad_all, inner, outer)
 
 
+WIDTH = 1024
+QUERY = HEADS * HEAD_DIM
+KEY = KV_HEADS * HEAD_DIM
+EXPERTS = 16
+SMALL = 128
+LANES = 128
+AT_K = QUERY
+AT_V = AT_K + KEY
+AT_S = AT_V + KEY
+AT_O = AT_S + SMALL
+PACKED = AT_O + WIDTH
+ROWS_OWN = WIDTH // GROUP
+KGAIN_OWN = KEY // GROUP
+HEAD_PAIRS = KV_HEADS // 2
+
+
+def root_mean(values):
+    return lax.rsqrt(jnp.mean(values * values, axis=1, keepdims=True) + norm_eps)
+
+
+def lane_of(shape):
+    return lax.broadcasted_iota(jnp.int32, shape, 1)
+
+
+def turned(values, cosine, sine):
+    first = lax.rem(lane_of(values.shape), HEAD_DIM) < HEAD_DIM // 2
+    swapped = jnp.where(
+        first, pltpu.roll(values, LANES - HEAD_DIM // 2, 1), pltpu.roll(values, HEAD_DIM // 2, 1)
+    )
+    return values * cosine + swapped * sine
+
+
+def short_rows():
+    row = lax.broadcasted_iota(jnp.int32, (WIDTH, KEY), 0)
+    column = lax.broadcasted_iota(jnp.int32, (WIDTH, KEY), 1)
+    same = (lax.div(row, ROWS_OWN) == lax.div(column, KGAIN_OWN)) & (
+        lax.rem(row, ROWS_OWN) == lax.rem(column, KGAIN_OWN)
+    )
+    return jnp.where(same, 1.0, 0.0).astype(bf16)
+
+
+def gain_rows(small):
+    rows = jnp.transpose(small.astype(f32))
+    gain_k = dot(rows[EXPERTS : EXPERTS + 8].astype(bf16), short_rows())[3:4]
+    return rows[EXPERTS : EXPERTS + 1], rows[EXPERTS + 1 : EXPERTS + 2], rows[EXPERTS + 2 : EXPERTS + 3], gain_k
+
+
+def four_heads(chunk_a, chunk_b):
+    low = lane_of(chunk_a.shape) < HEAD_DIM
+    zero = jnp.zeros_like(chunk_a)
+    return jnp.concatenate(
+        [
+            jnp.where(low, chunk_a, zero),
+            jnp.where(low, pltpu.roll(chunk_a, HEAD_DIM, 1), zero),
+            jnp.where(low, zero, pltpu.roll(chunk_b, HEAD_DIM, 1)),
+            jnp.where(low, zero, chunk_b),
+        ],
+        axis=0,
+    )
+
+
+def two_chunks(blocks):
+    rows = blocks.shape[0] // 4
+    one, two, three, four = (blocks[n * rows : (n + 1) * rows] for n in range(4))
+    low = lane_of(one.shape) < HEAD_DIM
+    return (
+        jnp.where(low, one, pltpu.roll(two, HEAD_DIM, 1)),
+        jnp.where(low, pltpu.roll(three, HEAD_DIM, 1), four),
+    )
+
+
+def chunk_at(index, base=0):
+    return pl.ds(pl.multiple_of(base + index * LANES, LANES), LANES)
+
+
+def front_call(collective_id, tokens, cotangent, packed, cosine, sine, bias, picked):
+    count, width = tokens.shape
+    seqs, positions, length = bias.shape
+    score_scale = HEAD_DIM ** (-0.5)
+
+    def kernel(
+        tokens_ref, grad_ref, packed_ref, cos_ref, sin_ref, bias_ref, picked_ref,
+        dense_out, grad_all, pairs_out, soft_out,
+        attn_in, query_raw, key_raw, query_low, mixed, middle, sent, gates_out,
+        dense, pairs, pair_own, soft_box,
+        ws0, wr0, ws1, wr1, gs, gr, ks0, kr0, ks1, kr1, own_sem, out_sem, soft_sem,
+    ):
+        place = Place()
+        core = place.core
+        lines = [Line(*v) for v in ((ws0, wr0), (ws1, wr1), (gs, gr), (ks0, kr0), (ks1, kr1))]
+
+        def weight_gather(index, low, size):
+            def block(which, row, n, other=False):
+                at = (which[0] * RING + which[1]) * 2 + ((1 - core) if other else core)
+                return dense.at[at, pl.ds(row, n), pl.ds(low, size)]
+
+            return gather_parts(
+                place.tokens, lines[index], packed_ref.at[:, pl.ds(low, size)], block, ROWS_OWN,
+                own_sem.at[index], place.twin,
+            )
+
+        def grad_block(which, row, n, other=False):
+            at = (which[0] * RING + which[1]) * 2 + ((1 - core) if other else core)
+            return grad_all.at[at, pl.ds(row, n)]
+
+        def pair_gather(seq):
+            def block(which, row, n, other=False):
+                return pairs.at[seq, which[0] * RING + which[1], pl.ds(row, n)]
+
+            return gather_parts(
+                place.copies, lines[3 + seq], pair_own.at[pl.ds(seq * positions, positions)], block,
+                positions, own_sem.at[3 + seq],
+            )
+
+        def soft_copy(seq, index, slot):
+            return pltpu.make_async_copy(
+                soft_box.at[slot], soft_out.at[seq, index], soft_sem.at[slot]
+            )
+
+        greet(place.tokens.neighbours() + place.copies.neighbours() + [place.twin])
+        first = weight_gather(0, 0, AT_O)
+        second = weight_gather(1, AT_O, WIDTH)
+        grads = gather_parts(
+            place.tokens, lines[2], grad_ref, grad_block, count, own_sem.at[2], place.twin
+        )
+        pair_gathers = [pair_gather(0), pair_gather(1)]
+        next(first)
+        inputs = tokens_ref[...].astype(f32)
+        middle[...] = inputs * root_mean(inputs)
+        next(first)
+        next(second)
+        next(first)
+        next(second)
+        for _ in first:
+            pass
+        next(second)
+        next(grads)
+
+        def weights(low, size):
+            return dense[:, :, pl.ds(low, size)].reshape(width, size)
+
+        small = weights(AT_S, SMALL)
+        gain_a, gain_q, gain_f, gain_k = gain_rows(small)
+        rows = (middle[...] * gain_a).astype(bf16)
+        attn_in[...] = rows
+        cos2 = jnp.concatenate([cos_ref[...]] * seqs, axis=0)
+        sin2 = jnp.concatenate([sin_ref[...]] * seqs, axis=0)
+        raw = dot(rows, weights(AT_K, KEY))
+        key_raw[...] = raw
+        scaled = raw * root_mean(raw) * gain_k
+        for chunk in range(KEY // LANES):
+            at = slice(chunk * LANES, (chunk + 1) * LANES)
+            pair_own[:, at] = turned(scaled[:, at], cos2, sin2).astype(bf16)
+        pair_own[:, KEY:] = dot(rows, weights(AT_V, KEY)).astype(bf16)
+        next(pair_gathers[0])
+        raw = dot(rows, weights(0, QUERY))
+        query_raw[...] = raw
+        scaled = raw * root_mean(raw) * gain_q
+        for chunk in range(QUERY // LANES):
+            at = slice(chunk * LANES, (chunk + 1) * LANES)
+            query_low[:, at] = turned(scaled[:, at], cos2, sin2).astype(bf16)
+        for _ in second:
+            pass
+        dense_copy = pltpu.make_async_copy(dense, dense_out, out_sem.at[0])
+        dense_copy.start()
+        next(pair_gathers[0])
+        next(pair_gathers[1])
+        next(pair_gathers[0])
+        for _ in pair_gathers[0]:
+            pass
+        next(grads)
+        next(pair_gathers[1])
+
+        def attend(seq, index, slot, wait_first):
+            rows_at = pl.ds(seq * positions, positions)
+            queries = four_heads(
+                query_low[rows_at, chunk_at(2 * index)].astype(f32),
+                query_low[rows_at, chunk_at(2 * index + 1)].astype(f32),
+            )
+            queries = (queries * score_scale).astype(bf16)
+            keys = pairs[seq, :, :, chunk_at(index)].reshape(length, LANES)
+            scores = dot_nt(queries, keys).reshape(4, positions, length) + bias_ref[seq][None]
+            scores = scores.reshape(4 * positions, length)
+            raised = jnp.exp(scores - jnp.max(scores, axis=1, keepdims=True))
+            soft = (raised * (1.0 / jnp.sum(raised, axis=1, keepdims=True))).astype(bf16)
+
+            @pl.when(wait_first)
+            def _():
+                soft_copy(seq, index, slot).wait()
+
+            soft_box[slot] = soft
+            soft_copy(seq, index, slot).start()
+            values = pairs[seq, :, :, chunk_at(index, KEY)].reshape(length, LANES)
+            chunk_a, chunk_b = two_chunks(dot(soft, values))
+            mixed[rows_at, chunk_at(2 * index)] = chunk_a.astype(bf16)
+            mixed[rows_at, chunk_at(2 * index + 1)] = chunk_b.astype(bf16)
+
+        def first_heads(index, carry):
+            @pl.when(index == 3)
+            def _():
+                next(pair_gathers[1])
+
+            attend(0, index, lax.rem(index, 2), index >= 2)
+            return carry
+
+        lax.fori_loop(0, HEAD_PAIRS, first_heads, 0)
+        for _ in pair_gathers[1]:
+            pass
+        pairs_copy = pltpu.make_async_copy(pairs, pairs_out, out_sem.at[1])
+        pairs_copy.start()
+
+        def second_heads(index, carry):
+            @pl.when(index == 0)
+            def _():
+                next(grads)
+
+            @pl.when(index == 3)
+            def _():
+                next(grads)
+
+            attend(1, index, lax.rem(index, 2), index >= 0)
+            return carry
+
+        lax.fori_loop(0, HEAD_PAIRS, second_heads, 0)
+        total = tokens_ref[...].astype(f32) + dot(mixed[...], weights(AT_O, WIDTH))
+        middle[...] = total
+        ffn_in = (total * root_mean(total) * gain_f).astype(bf16)
+        sent[:, pl.ds(0, width)] = ffn_in
+        chosen = picked_ref[...] > 0.5
+        logits = jnp.where(chosen, dot(ffn_in, small), masked_score)
+        raised = jnp.exp(logits - jnp.max(logits, axis=1, keepdims=True))
+        gates = raised * (1.0 / jnp.sum(raised, axis=1, keepdims=True))
+        gates = jnp.where(chosen, gates, 0.0)
+        gates_out[...] = gates
+        high = gates.astype(bf16).astype(f32)
+        tail = high + pltpu.roll(gates - high, EXPERTS, 1)
+        sent[:, pl.ds(width, SMALL)] = tail.astype(bf16)
+        for _ in grads:
+            pass
+        dense_copy.wait()
+        pairs_copy.wait()
+        for slot in range(2):
+            soft_copy(1, 0, slot).wait()
+
+    return pl.pallas_call(
+        kernel,
+        out_shape=[
+            jax.ShapeDtypeStruct((GROUP, ROWS_OWN, PACKED), bf16),
+            jax.ShapeDtypeStruct((GROUP, count, width), bf16),
+            jax.ShapeDtypeStruct((seqs, REPS, positions, 2 * KEY), bf16),
+            jax.ShapeDtypeStruct((seqs, HEAD_PAIRS, 4 * positions, length), bf16),
+            jax.ShapeDtypeStruct((count, width), bf16),
+            jax.ShapeDtypeStruct((count, QUERY), f32),
+            jax.ShapeDtypeStruct((count, KEY), f32),
+            jax.ShapeDtypeStruct((count, QUERY), bf16),
+            jax.ShapeDtypeStruct((count, QUERY), bf16),
+            jax.ShapeDtypeStruct((count, width), f32),
+            jax.ShapeDtypeStruct((count, width + SMALL), bf16),
+            jax.ShapeDtypeStruct((count, SMALL), f32),
+        ],
+        in_specs=[IN_VMEM, ANY, ANY, IN_VMEM, IN_VMEM, IN_VMEM, IN_VMEM],
+        out_specs=[ANY] * 4 + [IN_VMEM] * 8,
+        scratch_shapes=[
+            pltpu.VMEM((GROUP, ROWS_OWN, PACKED), bf16),
+            pltpu.VMEM((seqs, REPS, positions, 2 * KEY), bf16),
+            pltpu.VMEM((count, 2 * KEY), bf16),
+            pltpu.VMEM((2, 4 * positions, length), bf16),
+        ]
+        + sems(GATHER_SEMS) * 5
+        + [
+            pltpu.SemaphoreType.DMA((5,)),
+            pltpu.SemaphoreType.DMA((2,)),
+            pltpu.SemaphoreType.DMA((2,)),
+        ],
+        compiler_params=params(collective_id),
+    )(tokens, cotangent, packed, cosine, sine, bias, picked)
+
+
 def rms_scale(values, gain):
     return values * lax.rsqrt(jnp.mean(values * values, axis=-1, keepdims=True) + norm_eps) * gain
 
@@ -890,9 +1168,6 @@
     return (query_rot, key_rot)
 
 
-SMALL = 128
-
-
 def pack_rows(wide, router, gain_a, gain_q, gain_f, gain_k):
     rows = router.shape[0]
     short = jnp.concatenate([gain_k, jnp.zeros((rows - gain_k.shape[0],), gain_k.dtype)])
@@ -900,7 +1175,7 @@
         [router] + [v[:, None] for v in (gain_a, gain_q, gain_f, short)], axis=1
     )
     small = jnp.pad(small, ((0, 0), (0, SMALL - small.shape[1])))
-    return jnp.concatenate(list(wide) + [small], axis=1)
+    return jnp.concatenate(list(wide[:3]) + [small, wide[3]], axis=1)
 
 
 def shards(
@@ -946,79 +1221,48 @@
         ffn_gain,
         key_gain,
     )
-    (dense,) = gather_call(1, packed)
+    allowed = jax.vmap(lambda starts: allowed_mask(query_pos, key_pos, starts))(picture_starts)
+    bias = jnp.where(allowed, 0.0, masked_score).astype(f32)
+    route_ids = routes.reshape(count, top)
+    picked = jnp.sum(
+        (route_ids[:, :, None] == jnp.arange(SMALL)[None, None, :]).astype(f32), axis=1
+    )
+    sign = jnp.where(jnp.arange(HEAD_DIM) < HEAD_DIM // 2, -1.0, 1.0).astype(f32)
+    (
+        dense, grad_all, pairs_all, soft_low,
+        attn_in, query_raw, key_raw, query_low, mixed_low, middle, sent, gates,
+    ) = front_call(
+        1,
+        tokens.reshape(count, width),
+        cotangent.reshape(count, width),
+        packed,
+        jnp.tile(cosine_one, (1, 2)),
+        jnp.tile(sine_one * sign[None, :], (1, 2)),
+        bias,
+        picked,
+    )
     columns = packed.shape[1]
     dense = dense.reshape(GROUP * rows_own, columns)
-    at_o = query_width + 2 * kv_width
-    at_s = at_o + width
-    weight_q = dense[:, :query_width]
-    weight_k = dense[:, query_width : query_width + kv_width]
-    weight_v = dense[:, query_width + kv_width : at_o]
-    weight_o = dense[:, at_o:at_s]
-    weight_r = dense[:, at_s : at_s + experts]
-    gain_a = dense[:, at_s + experts].astype(f32)
-    gain_q = dense[:, at_s + experts + 1].astype(f32)
-    gain_f = dense[:, at_s + experts + 2].astype(f32)
+    weight_q = dense[:, :AT_K]
+    weight_k = dense[:, AT_K:AT_V]
+    weight_v = dense[:, AT_V:AT_S]
+    weight_o = dense[:, AT_O:]
+    weight_r = dense[:, AT_S : AT_S + experts]
+    gain_a = dense[:, AT_S + experts].astype(f32)
+    gain_q = dense[:, AT_S + experts + 1].astype(f32)
+    gain_f = dense[:, AT_S + experts + 2].astype(f32)
     gain_k = (
-        dense[:, at_s + experts + 3].reshape(GROUP, rows_own)[:, :kgain_own].reshape(-1).astype(f32)
-    )
-
+        dense[:, AT_S + experts + 3].reshape(GROUP, rows_own)[:, :kgain_own].reshape(-1).astype(f32)
+    )
     inputs = tokens.reshape(count, width).astype(f32)
-    grad_low = cotangent.reshape(count, width)
-    grad_out = grad_low.astype(f32)
-    attn_in = rms_scale(inputs, gain_a).astype(bf16)
-    query_raw = dot(attn_in, weight_q)
-    key_raw = dot(attn_in, weight_k)
-    value_low = dot(attn_in, weight_v).astype(bf16)
-    query_rot, key_rot = query_key(query_raw, key_raw, gain_q, gain_k, cosine_table, sine_table)
-    query_low = query_rot.astype(bf16).reshape(seqs, positions, KV_HEADS, group, HEAD_DIM)
-    key_low = key_rot.astype(bf16).reshape(count, kv_width)
-    grad_all, pairs_all = gather_call(
-        2, grad_low, jnp.concatenate([key_low, value_low], axis=1)
-    )
-    pairs_all = (
-        pairs_all.reshape(REPS, seqs, positions, 2 * kv_width)
-        .transpose(1, 0, 2, 3)
-        .reshape(seqs, length, 2 * kv_width)
-    )
+    grad_out = cotangent.reshape(count, width).astype(f32)
+    query_low = query_low.reshape(seqs, positions, KV_HEADS, group, HEAD_DIM)
+    pairs_all = pairs_all.reshape(seqs, length, 2 * kv_width)
     keys_all = pairs_all[..., :kv_width].reshape(seqs, length, KV_HEADS, HEAD_DIM)
     values_all = pairs_all[..., kv_width:].reshape(seqs, length, KV_HEADS, HEAD_DIM)
-    allowed = jax.vmap(lambda starts: allowed_mask(query_pos, key_pos, starts))(picture_starts)
-
-    def scores_of():
-        scores = (
-            jnp.einsum("bqkgd,bskd->bkgqs", query_low, keys_all, preferred_element_type=f32)
-            * score_scale
-        )
-        return jnp.where(allowed[:, None, None], scores, masked_score)
-
-    scores = scores_of()
-    row_top = jnp.max(scores, axis=-1, keepdims=True)
-    exponent = jnp.exp(scores - row_top)
-    row_total = jnp.sum(exponent, axis=-1, keepdims=True)
-    soft_low = (exponent / row_total).astype(bf16)
-    log_total = row_top + jnp.log(row_total)
-    mixed_low = (
-        jnp.einsum("bkgqs,bskd->bqkgd", soft_low, values_all, preferred_element_type=f32)
-        .reshape(count, query_width)
-        .astype(bf16)
-    )
-    middle = inputs + dot(mixed_low, weight_o)
-    ffn_in = rms_scale(middle, gain_f).astype(bf16)
-    logits = dot(ffn_in, weight_r)
-    route_ids = routes.reshape(count, top)
-    picked = (
-        jnp.sum((route_ids[:, :, None] == jnp.arange(experts)[None, None, :]).astype(f32), axis=1)
-        > 0.5
-    )
-    shown = jnp.where(picked, logits, masked_score)
-    raised = jnp.exp(shown - jnp.max(shown, axis=-1, keepdims=True))
-    gates = raised / jnp.sum(raised, axis=-1, keepdims=True)
-    gates_high = gates.astype(bf16)
-    gates_rest = (gates - gates_high.astype(f32)).astype(bf16)
-    sent = jnp.concatenate(
-        [ffn_in, gates_high, gates_rest, jnp.zeros((count, SMALL - 2 * experts), bf16)], axis=1
-    )
+    gates = gates[:, :experts]
+    picked = picked[:, :experts] > 0.5
+    ffn_in = sent[:, :width]
     out_terms, returned, expert_terms = moe_call(
         3, sent, grad_all, expert_in[0], expert_down[0]
     )
@@ -1037,7 +1281,7 @@
     grad_mixed = (
         dot_nt(grad_attn, weight_o).astype(bf16).reshape(seqs, positions, KV_HEADS, group, HEAD_DIM)
     )
-    soft_full = jnp.exp(scores_of() - log_total)
+    soft_full = soft_low.reshape(seqs, KV_HEADS, group, positions, length).astype(f32)
     grad_soft = jnp.einsum("bqkgd,bskd->bkgqs", grad_mixed, values_all, preferred_element_type=f32)
     grad_values = jnp.einsum(
         "bkgqs,bqkgd->bskd", soft_full.astype(bf16), grad_mixed, preferred_element_type=f32
@@ -1116,15 +1360,15 @@
     return (
         block_out.reshape(tokens.shape),
         tokens_grad.reshape(tokens.shape),
-        dense_sum[:, at_s + experts],
-        dense_sum[:, :query_width],
-        dense_sum[:, query_width : query_width + kv_width],
-        dense_sum[:, query_width + kv_width : at_o],
-        dense_sum[:, at_s + experts + 1],
-        dense_sum[:kgain_own, at_s + experts + 3],
-        dense_sum[:, at_o:at_s],
-        dense_sum[:, at_s + experts + 2],
-        dense_sum[:, at_s : at_s + experts],
+        dense_sum[:, AT_S + experts],
+        dense_sum[:, :AT_K],
+        dense_sum[:, AT_K:AT_V],
+        dense_sum[:, AT_V:AT_S],
+        dense_sum[:, AT_S + experts + 1],
+        dense_sum[:kgain_own, AT_S + experts + 3],
+        dense_sum[:, AT_O:],
+        dense_sum[:, AT_S + experts + 2],
+        dense_sum[:, AT_S : AT_S + experts],
         expert_in_grad,
         expert_down_grad,
     )

time: 529 us -> 505 us (0.955)
  matrix products: 70 us -> 46.2 us
  other arithmetic: 58.8 us -> 49.7 us
  local copies, waits for them, and re-layouts: 68.3 us -> 76.4 us
  Pallas kernels: 320 us -> 326 us
    dot_general x7 -> x0, matrix products: 25.7 us -> none  [the longest x5 10.6 us: dot(): return jnp.dot(a, b, preferred_element_type=f32)]
    reshape x1 -> x2, local copies, waits for them, and re-layouts: 2.63 us -> 15.1 us  [the longest x1 11.7 us: shards(): soft_low.reshape(seqs, KV_HEADS, group, positions, length).astype(f32)]
    reduce_sum x3 -> x1, other arithmetic: 9.31 us -> 1.04 us  [shards(): jnp.sum((route_ids[:, :, None] == jnp.arange(SMALL)[None, None, :]).astyp...]
    pallas_call x2 -> x1, Pallas kernels: 95.2 us -> 99.6 us  [front_call(): pl.pallas_call(kernel, out_shape=[jax.ShapeDtypeStruct((GROUP, ROWS_OWN,...]
    concatenate x6 -> x2, local copies, waits for them, and re-layouts: 12.8 us -> 10.3 us  [pack_rows(): return jnp.concatenate(list(wide[:3]) + [small, wide[3]], axis=1)]
    unnamed x126 -> x63, local copies, waits for them, and re-layouts: 13.2 us -> 11.2 us
where the time goes in v3:
time: 505 us; the launch traced here: 499 us
  Pallas kernels  326 us (65%)
  local copies, waits for them, and re-layouts  76.4 us (15%)
  other arithmetic  49.7 us (10%)
  matrix products  46.2 us (9%)
    pallas_call x1, Pallas kernels, front_call(): pl.pallas_call(kernel, out_shape=[jax.ShapeDtypeStruct((GROUP, ROWS_OWN,...  99.6 us
    pallas_call x1, Pallas kernels, moe_call(): pl.pallas_call(kernel, out_shape=[jax.ShapeDtypeStruct((GROUP, count, wid...  91.5 us
    pallas_call x2, Pallas kernels, sum_call(): pl.pallas_call(kernel, out_shape=[jax.ShapeDtypeStruct(v.shape[1:], resul...  65.3 us
    pallas_call x1, Pallas kernels, sum_gather_call(): pl.pallas_call(kernel, out_shape=[jax.ShapeDtypeStruct((rows, columns), f...  43.3 us
    pallas_call x1, Pallas kernels, copies_total_call(): pl.pallas_call(kernel, out_shape=jax.ShapeDtypeStruct(terms.shape, bf16),...  25.8 us
    dot_general x1, matrix products, shards(): jnp.einsum('bqkgd,bskd->bkgqs', grad_mixed, values_all, preferred_element...  12.4 us
    reshape x1, local copies, waits for them, and re-layouts, shards(): soft_low.reshape(seqs, KV_HEADS, group, positions, length).astype(f32)  11.7 us
    dot_general x5, matrix products, dot_tn(): lax.dot_general(a, b, (((0,), (0,)), ((), ())), preferred_element_type=f32)  11.3 us

profile of v3, /device:TPU:0, one launch (start us, length us, event | category | flops | bytes accessed | tf_op | source)
XLA Modules:
  0.0 499.4 jit_solution(5947405551287783436)
XLA Ops:
  16.2 99.6 %shard_map.246 = (bf16[16,64,3200]{2,1,0:T(8,128)(2,1)}, bf16[16,256,1024]{2,1,0:T(8,128)(2,1)}, bf16[2,8,128,1024]{3,2,1,0:T(8,128)(2,1)}, bf16[2,4,512,1024]{3...) custom-call(bf16[256,1024]{1,0:T(8,128)(2,1)} %bitcast.144, ...), custom_call_target="tpu_custom_call" | custom-call | tf_op jit(solution)/shard_map/pallas_call | solution.py:1088
  120.3 3.5 reshape.416
  126.3 4.5 fusion.40
  130.8 3.0 copy.161
  133.8 4.0 copy.152
  137.8 91.5 %shard_map.247 = (bf16[16,256,1024]{2,1,0:T(8,128)(2,1)}, f32[256,1152]{1,0:T(8,128)}, bf16[1536,1024]{1,0:T(8,128)(2,1)}) custom-call(bf16[256,1152]{1,0:T(8,128)(2,1)} %get-tuple-element.33.sent_ref, bf16[16,256,1024]{2,1,0:T(8,128)(2,1)} %get-tuple-element.34.grad_ref, bf16[1024,1024]{1,0:T(8,128)(2,1)} %bitcast.154, bf16[512,1024]{1,0:T(8,128)(2,1)} %bitcast.157), custom_call_target="tpu_custom_call" | custom-call | tf_op jit(solution)/shard_map/pallas_call | solution.py:817
  229.4 26.0 %shard_map.249 = f32[192,1024]{1,0:T(8,128)} custom-call(bf16[8,192,1024]{2,1,0:T(8,128)(2,1)} %bitcast.149), custom_call_target="tpu_custom_call" | custom-call | tf_op jit(solution)/shard_map/pallas_call | solution.py:476
  263.3 3.2 fusion.10
  266.4 3.8 reshape.417
  270.3 3.6 copy.155
  273.8 6.5 %bitcast_convert_fusion = bf16[2,8,64,1024]{3,2,1,0:T(8,128)(2,1)} fusion(bf16[2,128,8,2,64]{1,4,3,2,0:T(8,128)(2,1)} %copy.155, bf16[2,8,2,128,1024]{4,3,2,1,0:T(8,128)(2,1)} %bitcast.132), kind=kOutput, calls=%fused_computation.6 | convolution fusion | flops 537919488 | bytes 11010048 | tf_op jit(solution)/shard_map/bkgqs,bqkgd->bskd/dot_general | solution.py:1286
  280.3 11.7 %copy.151 = bf16[2,8,2,128,1024]{3,4,2,1,0:T(8,128)(2,1)} copy(bf16[2,8,2,128,1024]{4,3,2,1,0:T(8,128)(2,1)} %bitcast.133) | data formatting | bytes 16777216 | tf_op jit(solution)/shard_map/reshape | solution.py:1284
  292.0 3.5 copy.194
  295.5 4.3 copy.160
  299.8 12.4 %fusion = (f32[2,8,2,128]{3,2,1,0:T(2,128)S(1)}, f32[2,8,1024,128,2]{3,2,4,1,0:T(8,128)}) fusion(bf16[2,8,2,128,1024]{3,4,2,1,0:T(8,128)(2,1)} %copy.151, bf16[2,1024,8,64,1]{1,3,4,2,0:T(8,128)(2,1)} %bitcast.138, bf16[2,128,8,2,64]{1,4,3,2,0:T(8,128)(2,1)} %copy.155), kind=kOutput, calls=%fused_computation.2 | convolution fusion | flops 549449728 | bytes 27803648 | tf_op jit(solution)/shard_map/bqkgd,bskd->bkgqs/dot_general | solution.py:1285
  312.2 9.0 %fusion.1 = bf16[2,8,2,128,1024]{3,4,2,1,0:T(8,128)(2,1)S(1)} fusion(bf16[2,8,2,128,1024]{3,4,2,1,0:T(8,128)(2,1)} %copy.151, f32[2,8,1024,128,2]{3,2,4,1,0:T(8,128)} %get-tuple-element.147, f32[2,8,2,128]{3,2,1,0:T(2,128)S(1)} %get-tuple-element.146), kind=kLoop, calls=%fused_computation.3 | loop fusion | flops 16777216 | bytes 33570816 | tf_op jit(solution)/shard_map/convert_element_type | solution.py:1291
  321.2 2.6 fusion.15
  323.8 2.6 fusion.2
  327.1 2.7 copy.159
  329.7 4.8 pad_maximum_fusion
  334.6 39.4 %shard_map.248 = (f32[256,1024]{1,0:T(8,128)}, f32[256,1024]{1,0:T(8,128)}) custom-call(bf16[16,256,1024]{2,1,0:T(8,128)(2,1)} %get-tuple-element.35.refs_0_, bf16[8,256,1024]{2,1,0:T(8,128)(2,1)} %bitcast.135), custom_call_target="tpu_custom_call" | custom-call | tf_op jit(solution)/shard_map/pallas_call | solution.py:476
  373.9 2.1 add_convert_fusion
  388.3 2.5 fusion.4
  395.8 3.3 convert_dynamic-update-slice_fusion.1
  399.1 2.6 fusion.9
  401.7 2.5 fusion.8
  404.9 2.1 convert_dynamic-update-slice_fusion
  407.0 9.3 %copy.172 = bf16[1024,3200]{1,0:T(8,128)(2,1)} copy(bf16[1024,3200]{0,1:T(8,128)(2,1)} %convert_dynamic-update-slice_fusion) | data formatting | bytes 13107200 | tf_op jit(solution)/shard_map/concatenate | solution.py:1178
  416.4 43.3 %shard_map.250 = (f32[64,3200]{1,0:T(8,128)}, bf16[8,192,1024]{2,1,0:T(8,128)(2,1)}) custom-call(bf16[16,64,3200]{2,1,0:T(8,128)(2,1)} %bitcast.134, bf16[192,1024]{1,0:T(8,128)(2,1)} %convert_element_type.220.own), custom_call_target="tpu_custom_call" | custom-call | tf_op jit(solution)/shard_map/pallas_call | solution.py:520
  461.7 25.8 %shard_map.251 = bf16[8,64,512]{2,1,0:T(8,128)(2,1)} custom-call(bf16[8,64,512]{2,1,0:T(8,128)(2,1)} %bitcast.152), custom_call_target="tpu_custom_call" | custom-call | tf_op jit(solution)/shard_map/pallas_call | solution.py:557
  492.3 2.8 fusion.23
  495.1 4.1 fusion.3
  (148 shorter events, 55.4 us)
Async XLA Ops:
  4.1 0.6 copy-start.21
  14.9 1.3 copy-start.15
  117.2 0.6 copy-start.23
  118.9 263.5 %copy-start.20 = (f32[256]{0:T(256)}, f32[256]{0:T(256)S(1)}, u32[]{:S(2)}) copy-start(f32[256]{0:T(256)S(1)} %fusion.38) | copy-start | bytes 3076
  137.8 119.5 %copy-start.17 = (f32[256,128]{1,0:T(8,128)S(1)}, f32[256,128]{1,0:T(8,128)}, u32[]{:S(2)}) copy-start(f32[256,128]{1,0:T(8,128)} %get-tuple-element.39) | copy-start | bytes 393220
  137.8 120.7 %copy-start.14 = (f32[256,128]{1,0:T(8,128)S(1)}, f32[256,128]{1,0:T(8,128)}, u32[]{:S(2)}) copy-start(f32[256,128]{1,0:T(8,128)} %convert_reduce_fusion.picked_ref) | copy-start | bytes 393220
  137.8 121.9 %copy-start.16 = (bf16[256,1152]{1,0:T(8,128)(2,1)S(1)}, bf16[256,1152]{1,0:T(8,128)(2,1)}, u32[]{:S(2)}) copy-start(bf16[256,1152]{1,0:T(8,128)(2,1)} %get-tuple-element.33.sent_ref) | copy-start | bytes 1769476
  137.8 122.7 %copy-start = (f32[256,1024]{1,0:T(8,128)S(1)}, f32[256,1024]{1,0:T(8,128)}, u32[]{:S(2)}) copy-start(f32[256,1024]{1,0:T(8,128)} %get-tuple-element.32) | copy-start | bytes 3145732
  229.4 31.2 %copy-start.8 = (f32[256,1152]{1,0:T(8,128)S(1)}, f32[256,1152]{1,0:T(8,128)}, u32[]{:S(2)}) copy-start(f32[256,1152]{1,0:T(8,128)} %get-tuple-element.40) | copy-start | bytes 3538948
  229.4 32.6 %copy-start.9 = (bf16[2,128,1024]{2,1,0:T(8,128)(2,1)S(1)}, bf16[2,128,1024]{2,1,0:T(8,128)(2,1)}, u32[]{:S(2)}) copy-start(bf16[2,128,1024]{2,1,0:T(8,128)(2,1)} %param.16) | copy-start | bytes 1572868
  262.3 1.0 copy-start.2
  321.2 2.6 copy-start.7
  334.6 41.5 %copy-start.4 = (f32[2,128,8,2,64]{1,4,3,2,0:T(8,128)S(1)}, f32[2,128,8,2,64]{1,4,3,2,0:T(8,128)}, u32[]{:S(2)}) copy-start(f32[2,128,8,2,64]{1,4,3,2,0:T(8,128)} %fusion.15) | copy-start | bytes 3145732
  376.1 6.3 %copy-start.5 = (f32[256,512]{1,0:T(8,128)S(1)}, f32[256,512]{1,0:T(8,128)}, u32[]{:S(2)}) copy-start(f32[256,512]{1,0:T(8,128)} %get-tuple-element.45) | copy-start | bytes 1572868
  379.0 0.8 copy-start.11
  381.1 4.5 copy-start.1
  385.5 7.0 %copy-start.6 = (bf16[2,128,1024]{2,1,0:T(8,128)(2,1)S(1)}, bf16[2,128,1024]{2,1,0:T(8,128)(2,1)}, u32[]{:S(2)}) copy-start(bf16[2,128,1024]{2,1,0:T(8,128)(2,1)} %param.15) | copy-start | bytes 1572868
  385.5 7.0 %copy-start.12 = (bf16[256,1024]{1,0:T(8,128)(2,1)S(1)}, bf16[256,1024]{1,0:T(8,128)(2,1)}, u32[]{:S(2)}) copy-start(bf16[256,1024]{1,0:T(8,128)(2,1)} %copy-done.11) | copy-start | bytes 1572868
  385.5 7.0 %copy-start.24 = (f32[256]{0:T(256)S(1)}, f32[256]{0:T(256)}, u32[]{:S(2)}) copy-start(f32[256]{0:T(256)} %bitcast_rsqrt_fusion) | copy-start | bytes 3076
  387.3 7.3 %copy-start.22 = (f32[2,128]{1,0:T(2,128)S(1)}, f32[2,128]{1,0:T(2,128)}, u32[]{:S(2)}) copy-start(f32[2,128]{1,0:T(2,128)} %copy-done.21) | copy-start | bytes 3076
  387.3 7.3 %copy-start.3 = (f32[256,1024]{1,0:T(8,128)S(1)}, f32[256,1024]{1,0:T(8,128)}, u32[]{:S(2)}) copy-start(f32[256,1024]{1,0:T(8,128)} %copy-done.2) | copy-start | bytes 3145732
  388.3 7.5 %copy-start.18 = (bf16[256,1024]{1,0:T(8,128)(2,1)}, bf16[256,1024]{1,0:T(8,128)(2,1)S(1)}, u32[]{:S(2)}) copy-start(bf16[256,1024]{1,0:T(8,128)(2,1)S(1)} %fusion.17) | copy-start | bytes 1572868
  388.3 7.4 %copy-start.19 = (bf16[1024,16]{0,1:T(8,128)(2,1)S(1)}, bf16[1024,16]{0,1:T(8,128)(2,1)}, u32[]{:S(2)}) copy-start(bf16[1024,16]{0,1:T(8,128)(2,1)} %convolution_convert_fusion.2) | copy-start | bytes 98308
  392.6 9.1 %copy-start.13 = (bf16[256,1024]{1,0:T(8,128)(2,1)S(1)}, bf16[256,1024]{1,0:T(8,128)(2,1)}, u32[]{:S(2)}) copy-start(bf16[256,1024]{1,0:T(8,128)(2,1)} %copy-done.11) | copy-start | bytes 1572868
  394.6 10.3 %copy-start.10 = (bf16[256,1024]{1,0:T(8,128)(2,1)S(1)}, bf16[256,1024]{1,0:T(8,128)(2,1)}, u32[]{:S(2)}) copy-start(bf16[256,1024]{1,0:T(8,128)(2,1)} %get-tuple-element.47) | copy-start | bytes 1572868

commit v4 on v3

--- a/solution.py
+++ b/solution.py
@@ -14,7 +14,7 @@
 RING = 4
 GROUP = 16
 REPS = 8
-VMEM_LIMIT = 56 << 20
+VMEM_LIMIT = 62 << 20
 
 norm_eps = 1e-06
 rope_base = 10000.0
@@ -221,7 +221,7 @@
     return [axes.at(*v) for v in ((1, 2), (0, 2), (1, -1), (1, 1), (0, -1), (0, 1), (1, 0), (0, 0))]
 
 
-def sum_parts(axes, line, part, stage, rows, result, twin=None):
+def sum_parts(axes, line, part, stage, rows, result, twin=None, store=None):
     half, quarter = rows // 2, rows // 4
     mine, back, front, far = axes.at(0, 0), axes.at(0, -1), axes.at(0, 1), axes.at(0, 2)
     pair, pair_back, pair_front, pair_far = (axes.at(1, n) for n in (0, -1, 1, 2))
@@ -303,7 +303,10 @@
         total = part(mine, low, step)[...].astype(f32)
         for name in ("M3", "P3", "Y3"):
             total = total + stage[pl.ds(offsets[name][0] + low, step)].astype(f32)
-        result[pl.ds(low, step)] = total.astype(result.dtype)
+        if store is None:
+            result[pl.ds(low, step)] = total.astype(result.dtype)
+        else:
+            store(low, step, total)
         return carry
 
     lax.fori_loop(0, rows // step, body, 0)
@@ -1119,6 +1122,419 @@
     )(tokens, cotangent, packed, cosine, sine, bias, picked)
 
 
+def norm_back(values, gain, grad):
+    scale = root_mean(values)
+    weighted = grad * gain
+    mean = jnp.mean(values * weighted, axis=1, keepdims=True)
+    inner = weighted * scale - values * (scale * scale * scale * mean)
+    return inner, jnp.sum(grad * values * scale, axis=0, keepdims=True)
+
+
+REST = 2 * KEY + SMALL
+
+
+def back_call(
+    collective_id, returned, gates, middle, sent, dense, cotangent, tokens, attn_in, query_raw, key_raw,
+    query_low, mixed, pairs, soft, out_terms, expert_terms, cosine, sine,
+):
+    count, width = tokens.shape
+    seqs, _, positions, _ = pairs.shape
+    length = REPS * positions
+    expert_rows = expert_terms.shape[0] // REPS
+    score_scale = HEAD_DIM ** (-0.5)
+    chips = GROUP // 2
+
+    def kernel(
+        returned_ref, gates_ref, middle_ref, sent_ref, dense_ref, grad_ref, tokens_ref, attn_ref,
+        query_raw_ref, key_raw_ref, query_ref, mixed_ref, pairs_ref, soft_ref, out_ref, expert_ref,
+        cos_ref, sin_ref,
+        block_out, tokens_grad, dense_all, expert_all,
+        weight_box, weight_rest, o_terms, rest_terms, dense_own,
+        o_staged, q_staged, rest_staged, o_stage, q_stage, rest_stage,
+        out_held, out_staged, out_stage, expert_held, expert_stage, expert_own,
+        soft_box, key_box, value_box, pair_terms, pair_stage, pair_grads,
+        grad_mixed, grad_query, grad_middle, grad_attn_in, gain_box,
+        out_s, out_r, exp_s, exp_r, kv0_s, kv0_r, kv1_s, kv1_r, o_s, o_r, q_s, q_r, rest_s, rest_r,
+        ge_s, ge_r, go_s, go_r, gq_s, gq_r, grest_s, grest_r,
+        load_sem, out_load_sem, box_sem, own_sem,
+    ):
+        place = Place()
+        core = place.core
+        token_axes, copy_axes = place.tokens, place.copies
+        q_terms = expert_held
+
+        def chip_of(which):
+            return which[0] * RING + which[1]
+
+        def blocks(which, other=False):
+            return chip_of(which) * 2 + ((1 - core) if other else core)
+
+        def out_store(low, step, value):
+            at = pl.ds(low, step)
+            block_out[at] = (middle_ref[at] + value).astype(bf16)
+
+        out_sum = sum_parts(
+            token_axes, Line(out_s, out_r),
+            lambda which, low, n: out_held.at[chip_of(which), pl.ds(low, n)],
+            out_stage, count, None,
+            (place.twin, lambda which: out_ref.at[blocks(which, True)],
+             lambda which: out_staged.at[chip_of(which)]),
+            store=out_store,
+        )
+        expert_sum = sum_parts(
+            copy_axes, Line(exp_s, exp_r),
+            lambda which, low, n: expert_held.at[pl.ds(chip_of(which) * expert_rows + low, n)],
+            expert_stage, expert_rows, expert_own,
+        )
+
+        def pair_sum(seq, send_sem, recv_sem):
+            return sum_parts(
+                copy_axes, Line(send_sem, recv_sem),
+                lambda which, low, n: pair_terms.at[seq, chip_of(which), pl.ds(low, n)],
+                pair_stage.at[seq], positions, pair_grads.at[pl.ds(seq * positions, positions)],
+            )
+
+        pair_sums = [pair_sum(0, kv0_s, kv0_r), pair_sum(1, kv1_s, kv1_r)]
+
+        def rows_of_block(terms, index, low, n):
+            return terms.at[pl.ds(index * ROWS_OWN + low, n)]
+
+        def dense_sum(terms, staged, stage, low, size, send_sem, recv_sem):
+            return sum_parts(
+                token_axes, Line(send_sem, recv_sem),
+                lambda which, row, n: rows_of_block(terms, blocks(which), row, n),
+                stage, ROWS_OWN, dense_own.at[:, pl.ds(low, size)],
+                (place.twin, lambda which: rows_of_block(terms, blocks(which, True), 0, ROWS_OWN),
+                 lambda which: staged.at[chip_of(which)]),
+            )
+
+        o_sum = dense_sum(o_terms, o_staged, o_stage, AT_O, width, o_s, o_r)
+        q_sum = dense_sum(q_terms, q_staged, q_stage, 0, QUERY, q_s, q_r)
+        rest_sum = dense_sum(rest_terms, rest_staged, rest_stage, AT_K, REST, rest_s, rest_r)
+
+        def dense_gather(low, size, send_sem, recv_sem, index):
+            return gather_parts(
+                copy_axes, Line(send_sem, recv_sem), dense_own.at[:, pl.ds(low, size)],
+                lambda which, row, n, other=False: dense_all.at[
+                    chip_of(which), pl.ds(row, n), pl.ds(low, size)
+                ],
+                ROWS_OWN, own_sem.at[index],
+            )
+
+        o_gather = dense_gather(AT_O, width, go_s, go_r, 0)
+        q_gather = dense_gather(0, QUERY, gq_s, gq_r, 1)
+        rest_gather = dense_gather(AT_K, REST, grest_s, grest_r, 2)
+        expert_gather = gather_parts(
+            copy_axes, Line(ge_s, ge_r), expert_own,
+            lambda which, row, n, other=False: expert_all.at[chip_of(which), pl.ds(row, n)],
+            expert_rows, own_sem.at[3],
+        )
+
+        def weight_load(low, index):
+            return pltpu.make_async_copy(
+                dense_ref.at[:, :, pl.ds(low, width)], weight_box, load_sem.at[index]
+            )
+
+        rest_load = pltpu.make_async_copy(
+            dense_ref.at[:, :, pl.ds(AT_K, REST)], weight_rest, load_sem.at[1]
+        )
+        expert_load = pltpu.make_async_copy(expert_ref, expert_held, load_sem.at[2])
+        out_loads = [
+            pltpu.make_async_copy(
+                out_ref.at[2 * chip + core], out_held.at[chip], out_load_sem.at[chip]
+            )
+            for chip in range(chips)
+        ]
+
+        def box_loads(number, slot):
+            seq, index = lax.div(number, HEAD_PAIRS), lax.rem(number, HEAD_PAIRS)
+            return [
+                pltpu.make_async_copy(
+                    soft_ref.at[seq, index], soft_box.at[slot], box_sem.at[slot, 0]
+                ),
+                pltpu.make_async_copy(
+                    pairs_ref.at[seq, :, :, chunk_at(index)], key_box.at[slot], box_sem.at[slot, 1]
+                ),
+                pltpu.make_async_copy(
+                    pairs_ref.at[seq, :, :, chunk_at(index, KEY)],
+                    value_box.at[slot],
+                    box_sem.at[slot, 2],
+                ),
+            ]
+
+        expert_load.start()
+        rest_load.start()
+        weight_load(AT_O, 0).start()
+        for load in out_loads:
+            load.start()
+        for load in box_loads(0, 0):
+            load.start()
+        greet(token_axes.neighbours() + copy_axes.neighbours() + [place.twin])
+        next(out_sum)
+        expert_load.wait()
+        next(expert_sum)
+        next(expert_sum)
+        rest_load.wait()
+
+        small = weight_rest[:, :, pl.ds(2 * KEY, SMALL)].reshape(width, SMALL)
+        gain_a, gain_q, gain_f, gain_k = gain_rows(small)
+        gates = gates_ref[...]
+        tail = returned_ref[:, pl.ds(width, SMALL)]
+        grad_gates = tail + pltpu.roll(tail, SMALL - EXPERTS, 1)
+        grad_logits = gates * (
+            grad_gates - jnp.sum(gates * grad_gates, axis=1, keepdims=True)
+        )
+        grad_logits = grad_logits.astype(bf16)
+        router_terms = dot_tn(sent_ref[:, pl.ds(0, width)], grad_logits)
+        grad_ffn = returned_ref[:, pl.ds(0, width)] + dot_nt(grad_logits, small)
+        inner, gain_f_terms = norm_back(middle_ref[...], gain_f, grad_ffn)
+        inner = grad_ref[...].astype(f32) + inner
+        grad_middle[...] = inner
+        grad_attn = inner.astype(bf16)
+        gain_box[...] = jnp.zeros_like(gain_box)
+        gain_box[pl.ds(EXPERTS + 2, 1)] = gain_f_terms
+        for load in out_loads:
+            load.wait()
+        next(out_sum)
+        weight_load(AT_O, 0).wait()
+        weight_o = weight_box[...].reshape(QUERY, width)
+        grad_mixed[...] = dot_nt(grad_attn, weight_o).astype(bf16)
+        weight_load(0, 3).start()
+
+        def o_rows(index, carry):
+            at = chunk_256(index)
+            o_terms[at] = dot_tn(mixed_ref[:, at], grad_attn).astype(bf16)
+            return carry
+
+        lax.fori_loop(0, QUERY // 256, o_rows, 0)
+        next(o_sum)
+        next(o_sum)
+
+        def attend_back(seq, index):
+            number = seq * HEAD_PAIRS + index
+            slot = lax.rem(number, 2)
+            for load in box_loads(number, slot):
+                load.wait()
+
+            @pl.when(number + 1 < seqs * HEAD_PAIRS)
+            def _():
+                for load in box_loads(number + 1, 1 - slot):
+                    load.start()
+
+            rows_at = pl.ds(seq * positions, positions)
+            first, second = chunk_at(2 * index), chunk_at(2 * index + 1)
+            queries = four_heads(
+                query_ref[rows_at, first].astype(f32), query_ref[rows_at, second].astype(f32)
+            )
+            queries = (queries * score_scale).astype(bf16)
+            grads = four_heads(
+                grad_mixed[rows_at, first].astype(f32), grad_mixed[rows_at, second].astype(f32)
+            ).astype(bf16)
+            keys = key_box[slot].reshape(length, LANES)
+            values = value_box[slot].reshape(length, LANES)
+            soft_low = soft_box[slot]
+            value_terms = dot_tn(soft_low, grads)
+            pair_terms[seq, :, :, chunk_at(index, KEY)] = value_terms.astype(bf16).reshape(
+                REPS, positions, LANES
+            )
+            soft_full = soft_low.astype(f32)
+            grad_soft = dot_nt(grads, values)
+            weighted = soft_full * grad_soft
+            grad_scores = (
+                weighted - soft_full * jnp.sum(weighted, axis=1, keepdims=True)
+            ).astype(bf16)
+            key_terms = dot_tn(grad_scores, queries)
+            pair_terms[seq, :, :, chunk_at(index)] = key_terms.astype(bf16).reshape(
+                REPS, positions, LANES
+            )
+            chunk_a, chunk_b = two_chunks(dot(grad_scores, keys) * score_scale)
+            grad_query[rows_at, first] = chunk_a.astype(bf16)
+            grad_query[rows_at, second] = chunk_b.astype(bf16)
+
+        def hooks(index, steps):
+            for at, step in steps:
+                pl.when(index == at)(step)
+
+        def first_heads(index, carry):
+            hooks(
+                index,
+                (
+                    (1, lambda: next(expert_sum)),
+                    (2, lambda: next(out_sum)),
+                    (3, lambda: next(expert_sum)),
+                ),
+            )
+            attend_back(0, index)
+            return carry
+
+        lax.fori_loop(0, HEAD_PAIRS, first_heads, 0)
+        next(pair_sums[0])
+        next(pair_sums[0])
+
+        def drained(part):
+            for _ in part:
+                pass
+
+        def second_heads(index, carry):
+            hooks(
+                index,
+                (
+                    (0, lambda: next(out_sum)),
+                    (1, lambda: (drained(expert_sum), next(o_sum))[0]),
+                    (2, lambda: next(pair_sums[0])),
+                    (3, lambda: (drained(out_sum), next(o_sum))[0]),
+                ),
+            )
+            attend_back(1, index)
+            return carry
+
+        lax.fori_loop(0, HEAD_PAIRS, second_heads, 0)
+        next(pair_sums[0])
+        next(pair_sums[1])
+        next(pair_sums[1])
+
+        cos2 = jnp.concatenate([cos_ref[...]] * seqs, axis=0)
+        sin2 = -jnp.concatenate([sin_ref[...]] * seqs, axis=0)
+
+        def turned_back(values):
+            return jnp.concatenate(
+                [
+                    turned(values[:, low : low + LANES], cos2, sin2)
+                    for low in range(0, values.shape[1], LANES)
+                ],
+                axis=1,
+            )
+
+        grad, gain_q_terms = norm_back(
+            query_raw_ref[...], gain_q, turned_back(grad_query[...].astype(f32))
+        )
+        gain_box[pl.ds(EXPERTS + 1, 1)] = gain_q_terms
+        grad_query_low = grad.astype(bf16)
+        weight_load(0, 3).wait()
+        grad_attn_in[...] = dot_nt(grad_query_low, weight_box[...].reshape(width, QUERY))
+
+        def q_rows(index, carry):
+            at = chunk_256(index)
+            q_terms[at] = dot_tn(attn_ref[:, at], grad_query_low).astype(bf16)
+            return carry
+
+        lax.fori_loop(0, width // 256, q_rows, 0)
+        next(q_sum)
+        next(q_sum)
+        drained(pair_sums[0])
+        next(pair_sums[1])
+        next(pair_sums[1])
+        drained(o_sum)
+        next(expert_gather)
+        next(q_sum)
+        drained(pair_sums[1])
+
+        grads = pair_grads[...]
+        grad, gain_k_terms = norm_back(
+            key_raw_ref[...],
+            gain_k,
+            turned_back(grads[:, :KEY].astype(bf16).astype(f32)),
+        )
+        grad_pairs = jnp.concatenate([grad.astype(bf16), grads[:, KEY:].astype(bf16)], axis=1)
+        gain_k_row = dot_nt(
+            jnp.broadcast_to(gain_k_terms, (8, KEY)).astype(bf16), short_rows()
+        )
+        gain_box[pl.ds(EXPERTS + 3, 1)] = gain_k_row[:1]
+        grad = grad_attn_in[...] + dot_nt(
+            grad_pairs, weight_rest[:, :, pl.ds(0, 2 * KEY)].reshape(width, 2 * KEY)
+        )
+        values = tokens_ref[...].astype(f32)
+        inner, gain_a_terms = norm_back(values, gain_a, grad)
+        tokens_grad[...] = (grad_middle[...] + inner).astype(bf16)
+        gain_box[pl.ds(EXPERTS, 1)] = gain_a_terms
+        rest_terms[:, pl.ds(2 * KEY, SMALL)] = (
+            router_terms + jnp.transpose(gain_box[...])
+        ).astype(bf16)
+
+        def rest_rows(index, carry):
+            at = chunk_256(index)
+            rest_terms[at, pl.ds(0, 2 * KEY)] = dot_tn(attn_ref[:, at], grad_pairs).astype(bf16)
+            return carry
+
+        lax.fori_loop(0, width // 256, rest_rows, 0)
+        next(rest_sum)
+        next(rest_sum)
+        next(o_gather)
+        next(expert_gather)
+        next(q_sum)
+        next(rest_sum)
+        drained(q_sum)
+        next(q_gather)
+        next(o_gather)
+        next(expert_gather)
+        next(rest_sum)
+        next(q_gather)
+        next(o_gather)
+        drained(rest_sum)
+        next(rest_gather)
+        abreast(expert_gather, o_gather, q_gather, rest_gather)
+
+    block = pltpu.VMEM((GROUP, ROWS_OWN, width), bf16)
+    scratch = [
+        block,
+        pltpu.VMEM((GROUP, ROWS_OWN, REST), bf16),
+        pltpu.VMEM((width, width), bf16),
+        pltpu.VMEM((width, REST), bf16),
+        pltpu.VMEM((ROWS_OWN, PACKED), bf16),
+        pltpu.VMEM((chips, ROWS_OWN, width), bf16),
+        pltpu.VMEM((chips, ROWS_OWN, QUERY), bf16),
+        pltpu.VMEM((chips, ROWS_OWN, REST), bf16),
+        pltpu.VMEM((stage_rows(ROWS_OWN), width), bf16),
+        pltpu.VMEM((stage_rows(ROWS_OWN), QUERY), bf16),
+        pltpu.VMEM((stage_rows(ROWS_OWN), REST), bf16),
+        pltpu.VMEM((chips, count, width), bf16),
+        pltpu.VMEM((chips, count, width), bf16),
+        pltpu.VMEM((stage_rows(count), width), bf16),
+        pltpu.VMEM(expert_terms.shape, bf16),
+        pltpu.VMEM((stage_rows(expert_rows), width), bf16),
+        pltpu.VMEM((expert_rows, width), bf16),
+        pltpu.VMEM((2, 4 * positions, length), bf16),
+        pltpu.VMEM((2, REPS, positions, LANES), bf16),
+        pltpu.VMEM((2, REPS, positions, LANES), bf16),
+        pltpu.VMEM((seqs, REPS, positions, 2 * KEY), bf16),
+        pltpu.VMEM((seqs, stage_rows(positions), 2 * KEY), bf16),
+        pltpu.VMEM((count, 2 * KEY), f32),
+        pltpu.VMEM((count, QUERY), bf16),
+        pltpu.VMEM((count, QUERY), bf16),
+        pltpu.VMEM((count, width), f32),
+        pltpu.VMEM((count, width), f32),
+        pltpu.VMEM((SMALL, width), f32),
+    ]
+    return pl.pallas_call(
+        kernel,
+        out_shape=[
+            jax.ShapeDtypeStruct((count, width), bf16),
+            jax.ShapeDtypeStruct((count, width), bf16),
+            jax.ShapeDtypeStruct((REPS, ROWS_OWN, PACKED), bf16),
+            jax.ShapeDtypeStruct((REPS, expert_rows, width), bf16),
+        ],
+        in_specs=[IN_VMEM] * 4 + [ANY] + [IN_VMEM] * 7 + [ANY] * 4 + [IN_VMEM] * 2,
+        out_specs=[IN_VMEM, IN_VMEM, ANY, ANY],
+        scratch_shapes=scratch
+        + sems(SUM_SEMS) * 7
+        + sems(GATHER_SEMS) * 4
+        + [
+            pltpu.SemaphoreType.DMA((4,)),
+            pltpu.SemaphoreType.DMA((chips,)),
+            pltpu.SemaphoreType.DMA((2, 3)),
+            pltpu.SemaphoreType.DMA((4,)),
+        ],
+        compiler_params=params(collective_id),
+    )(
+        returned, gates, middle, sent, dense, cotangent, tokens, attn_in, query_raw, key_raw,
+        query_low, mixed, pairs, soft, out_terms, expert_terms, cosine, sine,
+    )
+
+
+def chunk_256(index):
+    return pl.ds(pl.multiple_of(index * 256, 256), 256)
+
+
 def rms_scale(values, gain):
     return values * lax.rsqrt(jnp.mean(values * values, axis=-1, keepdims=True) + norm_eps) * gain
 
@@ -1209,9 +1625,6 @@
     shard = lax.axis_index("shard")
     query_pos = lax.axis_index("rep") * positions + jnp.arange(positions, dtype=jnp.int32)
     key_pos = jnp.arange(length, dtype=jnp.int32)
-    cosine_one, sine_one = rotary_tables(query_pos, HEAD_DIM)
-    cosine_table = jnp.tile(cosine_one, (seqs, 1))
-    sine_table = jnp.tile(sine_one, (seqs, 1))
 
     packed = pack_rows(
         (query_weight, key_weight, value_weight, output_weight),
@@ -1227,7 +1640,10 @@
     picked = jnp.sum(
         (route_ids[:, :, None] == jnp.arange(SMALL)[None, None, :]).astype(f32), axis=1
     )
+    cosine_one, sine_one = rotary_tables(query_pos, HEAD_DIM)
     sign = jnp.where(jnp.arange(HEAD_DIM) < HEAD_DIM // 2, -1.0, 1.0).astype(f32)
+    cosine_two = jnp.tile(cosine_one, (1, 2))
+    sine_two = jnp.tile(sine_one * sign[None, :], (1, 2))
     (
         dense, grad_all, pairs_all, soft_low,
         attn_in, query_raw, key_raw, query_low, mixed_low, middle, sent, gates,
@@ -1236,127 +1652,24 @@
         tokens.reshape(count, width),
         cotangent.reshape(count, width),
         packed,
-        jnp.tile(cosine_one, (1, 2)),
-        jnp.tile(sine_one * sign[None, :], (1, 2)),
+        cosine_two,
+        sine_two,
         bias,
         picked,
     )
-    columns = packed.shape[1]
-    dense = dense.reshape(GROUP * rows_own, columns)
-    weight_q = dense[:, :AT_K]
-    weight_k = dense[:, AT_K:AT_V]
-    weight_v = dense[:, AT_V:AT_S]
-    weight_o = dense[:, AT_O:]
-    weight_r = dense[:, AT_S : AT_S + experts]
-    gain_a = dense[:, AT_S + experts].astype(f32)
-    gain_q = dense[:, AT_S + experts + 1].astype(f32)
-    gain_f = dense[:, AT_S + experts + 2].astype(f32)
-    gain_k = (
-        dense[:, AT_S + experts + 3].reshape(GROUP, rows_own)[:, :kgain_own].reshape(-1).astype(f32)
-    )
-    inputs = tokens.reshape(count, width).astype(f32)
-    grad_out = cotangent.reshape(count, width).astype(f32)
-    query_low = query_low.reshape(seqs, positions, KV_HEADS, group, HEAD_DIM)
-    pairs_all = pairs_all.reshape(seqs, length, 2 * kv_width)
-    keys_all = pairs_all[..., :kv_width].reshape(seqs, length, KV_HEADS, HEAD_DIM)
-    values_all = pairs_all[..., kv_width:].reshape(seqs, length, KV_HEADS, HEAD_DIM)
-    gates = gates[:, :experts]
-    picked = picked[:, :experts] > 0.5
-    ffn_in = sent[:, :width]
     out_terms, returned, expert_terms = moe_call(
         3, sent, grad_all, expert_in[0], expert_down[0]
     )
-    (expert_own,) = sum_call(4, None, expert_terms.reshape(REPS, -1, width))
-
-    grad_gates = returned[:, width : width + experts] + returned[:, width + experts : width + 2 * experts]
-    grad_chosen = gates * (grad_gates - jnp.sum(gates * grad_gates, axis=-1, keepdims=True))
-    grad_logits = jnp.where(picked, grad_chosen, 0.0).astype(bf16)
-    grad_router = dot_tn(ffn_in, grad_logits)
-    grad_ffn_in = dot_nt(grad_logits, weight_r) + returned[:, :width]
-    _, norm_pull = jax.vjp(rms_scale, middle, gain_f)
-    grad_middle_part, grad_gain_f = norm_pull(grad_ffn_in)
-    grad_middle = grad_out + grad_middle_part
-    grad_attn = grad_middle.astype(bf16)
-    grad_weight_o = dot_tn(mixed_low, grad_attn)
-    grad_mixed = (
-        dot_nt(grad_attn, weight_o).astype(bf16).reshape(seqs, positions, KV_HEADS, group, HEAD_DIM)
+    block_out, tokens_grad, dense_all, expert_all = back_call(
+        2, returned, gates, middle, sent, dense, cotangent.reshape(count, width),
+        tokens.reshape(count, width), attn_in, query_raw, key_raw, query_low, mixed_low, pairs_all,
+        soft_low, out_terms, expert_terms, cosine_two, sine_two,
     )
-    soft_full = soft_low.reshape(seqs, KV_HEADS, group, positions, length).astype(f32)
-    grad_soft = jnp.einsum("bqkgd,bskd->bkgqs", grad_mixed, values_all, preferred_element_type=f32)
-    grad_values = jnp.einsum(
-        "bkgqs,bqkgd->bskd", soft_full.astype(bf16), grad_mixed, preferred_element_type=f32
-    )
-    grad_scores = (
-        soft_full * (grad_soft - jnp.sum(soft_full * grad_soft, axis=-1, keepdims=True))
-    ).astype(bf16)
-    grad_query_rot = (
-        jnp.einsum("bkgqs,bskd->bqkgd", grad_scores, keys_all, preferred_element_type=f32)
-        * score_scale
-    )
-    grad_keys = (
-        jnp.einsum("bkgqs,bqkgd->bskd", grad_scores, query_low, preferred_element_type=f32)
-        * score_scale
-    )
-    grad_pairs = (
-        jnp.concatenate(
-            [
-                grad_keys.reshape(seqs, length, kv_width),
-                grad_values.reshape(seqs, length, kv_width),
-            ],
-            axis=-1,
-        )
-        .astype(bf16)
-        .reshape(seqs, REPS, positions, 2 * kv_width)
-        .transpose(1, 0, 2, 3)
-        .reshape(REPS, count, 2 * kv_width)
-    )
-    out_sum, pairs_own = sum_call(5, out_terms, grad_pairs)
-    block_out = (middle + out_sum).astype(bf16)
-
-    grad_query_rot = grad_query_rot.astype(bf16).astype(f32).reshape(count, HEADS, HEAD_DIM)
-    grad_key_rot = (
-        pairs_own[:, :kv_width].astype(bf16).astype(f32).reshape(count, KV_HEADS, HEAD_DIM)
-    )
-    grad_value_low = pairs_own[:, kv_width:].astype(bf16)
-
-    def turned_pair(query_in, key_in, query_scale, key_scale):
-        return query_key(query_in, key_in, query_scale, key_scale, cosine_table, sine_table)
-
-    _, pair_pull = jax.vjp(turned_pair, query_raw, key_raw, gain_q, gain_k)
-    grad_query_raw, grad_key_raw, grad_gain_q, grad_gain_k = pair_pull(
-        (grad_query_rot, grad_key_rot)
-    )
-    grad_query_low = grad_query_raw.astype(bf16)
-    grad_key_low = grad_key_raw.astype(bf16)
-    grad_weight_q = dot_tn(attn_in, grad_query_low)
-    grad_weight_k = dot_tn(attn_in, grad_key_low)
-    grad_weight_v = dot_tn(attn_in, grad_value_low)
-    grad_attn_in = (
-        dot_nt(grad_query_low, weight_q)
-        + dot_nt(grad_key_low, weight_k)
-        + dot_nt(grad_value_low, weight_v)
-    )
-    _, norm_pull = jax.vjp(rms_scale, inputs, gain_a)
-    grad_inputs_part, grad_gain_a = norm_pull(grad_attn_in)
-    tokens_grad = (grad_middle + grad_inputs_part).astype(bf16)
-
-    gain_k_rows = jnp.pad(
-        grad_gain_k.reshape(GROUP, kgain_own), ((0, 0), (0, rows_own - kgain_own))
-    ).reshape(-1)
-    dense_terms = pack_rows(
-        tuple(v.astype(bf16) for v in (grad_weight_q, grad_weight_k, grad_weight_v, grad_weight_o)),
-        grad_router.astype(bf16),
-        grad_gain_a.astype(bf16),
-        grad_gain_q.astype(bf16),
-        grad_gain_f.astype(bf16),
-        gain_k_rows.astype(bf16),
-    ).reshape(GROUP, rows_own, columns)
-    dense_own, expert_all = sum_gather_call(6, dense_terms, expert_own.astype(bf16))
+    dense_sum = jnp.sum(dense_all.astype(f32), axis=0)
     expert_all = expert_all.reshape(-1, width)
     inner_rows = expert_in.shape[1]
     expert_in_grad = expert_all[:inner_rows].astype(f32)[None]
     expert_down_grad = expert_all[inner_rows:].astype(f32)[None]
-    dense_sum = copies_total(dense_own)
     return (
         block_out.reshape(tokens.shape),
         tokens_grad.reshape(tokens.shape),

time: 505 us -> 341 us (0.68)
  local copies, waits for them, and re-layouts: 76.4 us -> 13.3 us
  matrix products: 46.2 us -> 0 us
  other arithmetic: 49.7 us -> 12.7 us
  Pallas kernels: 326 us -> 313 us
    dot_general x14 -> x0, matrix products: 46.2 us -> none  [the longest x1 12.4 us: shards(): jnp.einsum('bqkgd,bskd->bkgqs', grad_mixed, values_all, preferred_element...]
    reshape x12 -> x0, local copies, waits for them, and re-layouts: 28.7 us -> none  [the longest x1 11.7 us: shards(): soft_low.reshape(seqs, KV_HEADS, group, positions, length).astype(f32)]
    convert_element_type x11 -> x0, other arithmetic: 20.3 us -> none  [the longest x1 9.05 us: shards(): grad_scores = (soft_full * (grad_soft - jnp.sum(soft_full * grad_soft, ax...]
    pallas_call x4 -> x1, Pallas kernels: 134 us -> 122 us  [back_call(): pl.pallas_call(kernel, out_shape=[jax.ShapeDtypeStruct((count, width), bf...]
    slice x3 -> x0, local copies, waits for them, and re-layouts: 11.5 us -> none  [the longest x2 7.5 us: shards(): pairs_all[..., :kv_width].reshape(seqs, length, KV_HEADS, HEAD_DIM)]
    concatenate x2 -> x1, local copies, waits for them, and re-layouts: 10.3 us -> 0.92 us  [pack_rows(): return jnp.concatenate(list(wide[:3]) + [small, wide[3]], axis=1)]
    concatenate x2 -> x0, local copies, waits for them, and re-layouts: 6.92 us -> none  [shards(): jnp.concatenate([grad_keys.reshape(seqs, length, kv_width), grad_values.r...]
    unnamed x63 -> x15, local copies, waits for them, and re-layouts: 11.2 us -> 4.89 us
where the time goes in v4:
time: 341 us; the launch traced here: 339 us
  Pallas kernels  313 us (92%)
  local copies, waits for them, and re-layouts  13.3 us (4%)
  other arithmetic  12.7 us (4%)
    pallas_call x1, Pallas kernels, back_call(): pl.pallas_call(kernel, out_shape=[jax.ShapeDtypeStruct((count, width), bf...  122 us
    pallas_call x1, Pallas kernels, front_call(): pl.pallas_call(kernel, out_shape=[jax.ShapeDtypeStruct((GROUP, ROWS_OWN,...  99.6 us
    pallas_call x1, Pallas kernels, moe_call(): pl.pallas_call(kernel, out_shape=[jax.ShapeDtypeStruct((GROUP, count, wid...  91.3 us

profile of v4, /device:TPU:0, one launch (start us, length us, event | category | flops | bytes accessed | tf_op | source)
XLA Modules:
  0.0 339.2 jit_solution(12227214120707840053)
XLA Ops:
  0.7 0.7 pad_bitcast_fusion
  1.4 0.7 broadcast_add_fusion.2
  2.0 0.8 fusion.3
  2.8 1.4 concatenate.20
  4.2 0.8 fusion.2
  5.0 0.1 copy.65
  5.1 0.1 multiply_sine_fusion
  5.3 0.1 maximum_multiply_fusion
  5.4 0.7 copy.68.sin_ref
  6.1 0.7 copy.67.cos_ref
  6.8 0.1 iota_compare_fusion.1
  7.0 0.8 copy.66
  7.8 1.0 convert_reduce_fusion.1.picked_ref
  8.9 0.9 constant_dynamic-update-slice_fusion.3
  9.8 0.8 constant_dynamic-update-slice_fusion.2
  10.6 0.8 constant_dynamic-update-slice_fusion.1
  11.5 0.9 constant_dynamic-update-slice_fusion.packed_ref
  12.4 0.0 copy-start.1
  12.4 1.3 or_select_fusion.bias_ref
  13.7 99.6 %shard_map.246 = (bf16[16,64,3200]{2,1,0:T(8,128)(2,1)}, bf16[16,256,1024]{2,1,0:T(8,128)(2,1)}, bf16[2,8,128,1024]{3,2,1,0:T(8,128)(2,1)}, bf16[2,4,512,1024]{3...) custom-call(bf16[256,1024]{1,0:T(8,128)(2,1)} %bitcast.27, ...), custom_call_target="tpu_custom_call" | custom-call | tf_op jit(solution)/shard_map/pallas_call | solution.py:1091
  113.3 91.3 %shard_map.247 = (bf16[16,256,1024]{2,1,0:T(8,128)(2,1)}, f32[256,1152]{1,0:T(8,128)}, bf16[1536,1024]{1,0:T(8,128)(2,1)}) custom-call(bf16[256,1152]{1,0:T(8,128)(2,1)} %get-tuple-element.32.sent_ref, bf16[16,256,1024]{2,1,0:T(8,128)(2,1)} %get-tuple-element.33.grad_ref, bf16[1024,1024]{1,0:T(8,128)(2,1)} %bitcast.31, bf16[512,1024]{1,0:T(8,128)(2,1)} %bitcast.32), custom_call_target="tpu_custom_call" | custom-call | tf_op jit(solution)/shard_map/pallas_call | solution.py:820
  204.6 121.6 %shard_map.248 = (bf16[256,1024]{1,0:T(8,128)(2,1)}, bf16[256,1024]{1,0:T(8,128)(2,1)}, bf16[8,64,3200]{2,1,0:T(8,128)(2,1)}, bf16[8,192,1024]{2,1,0:T(8,128)(2,1)}) custom-call(f32[256,1152]{1,0:T(8,128)} %get-tuple-element.34.returned_ref, f32[256,128]{1,0:T(8,128)} %get-tuple-element.35.gates_ref, f32[256,1024]{1,0:T(8,128)} %get-tuple-element.36.middle_ref, ...), custom_call_target="tpu_custom_call" | custom-call | tf_op jit(solution)/shard_map/pallas_call | solution.py:1508
  326.2 2.5 convert_reduce_fusion
  328.7 0.7 slice_reduce_fusion.3
  329.4 0.7 slice_reduce_fusion
  330.1 0.7 copy.71
  330.8 0.7 fusion.6
  331.5 0.8 fusion.5
  332.4 2.8 fusion.1
  335.2 2.5 fusion
  337.6 0.8 copy.78
  338.4 0.8 copy.79
  (19 shorter events, 0.1 us)
Async XLA Ops:
  12.4 1.3 copy-start.1
  330.8 4.4 %copy-start = (bf16[8,192,1024]{2,1,0:T(8,128)(2,1)S(1)}, bf16[8,192,1024]{2,1,0:T(8,128)(2,1)}, u32[]{:S(2)}) copy-start(bf16[8,192,1024]{2,1,0:T(8,128)(2,1)} %get-tuple-element.50) | copy-start | bytes 9437188
  335.2 2.5 copy-start.3
  335.2 3.3 copy-start.2

commit v5 on v4

v5 whole, which is shorter than its diff:
```python
import jax
import jax.numpy as jnp
from jax import lax
from jax.experimental import pallas as pl
from jax.experimental.pallas import tpu as pltpu
from jax.sharding import PartitionSpec as P

HEADS = 16
KV_HEADS = 8
HEAD_DIM = 64
PIC = 256
RING = 4
GROUP = 16
REPS = 8
VMEM_LIMIT = 62 << 20

norm_eps = 1e-06
rope_base = 10000.0
masked_score = -1e30

bf16 = jnp.bfloat16
f32 = jnp.float32


class Place:
    def __init__(self):
        shard = lax.axis_index("shard")
        rep = lax.axis_index("rep")
        self.shard, self.rep = shard, rep
        core = lax.rem(shard, 2)
        ring_z = lax.rem(lax.div(shard, 2), RING)
        y_hi = lax.div(shard, 8)
        ring_x = lax.rem(rep, RING)
        y_lo = lax.div(rep, RING)
        self.core = core

        def shard_of(hi, z, c):
            return (hi * RING + z) * 2 + c

        def rep_of(lo, x):
            return lo * RING + x

        def up(v):
            return lax.rem(v + 1, RING)

        def down(v):
            return lax.rem(v + RING - 1, RING)

        self.twin = (shard_of(y_hi, ring_z, 1 - core), rep)
        self.tokens = Axes(
            y_hi,
            ring_z,
            (shard_of(y_hi, up(ring_z), core), rep),
            (shard_of(y_hi, down(ring_z), core), rep),
            (shard_of(1 - y_hi, ring_z, core), rep_of(1 - y_lo, ring_x)),
        )
        self.copies = Axes(
            y_lo,
            ring_x,
            (shard, rep_of(y_lo, up(ring_x))),
            (shard, rep_of(y_lo, down(ring_x))),
            (shard, rep_of(1 - y_lo, ring_x)),
        )


class Axes:
    def __init__(self, side, spot, ahead, behind, across):
        self.side, self.spot = side, spot
        self.ahead, self.behind, self.across = ahead, behind, across
        sides = (side, 1 - side)
        spots = [lax.rem(spot + step, RING) for step in range(RING)]
        self.places = [[(sides[flip], spots[step]) for step in range(RING)] for flip in range(2)]

    def at(self, flip, step):
        return self.places[flip][step % RING]

    def neighbours(self):
        return [self.ahead, self.behind, self.across]


def greet(devices):
    barrier = pltpu.get_barrier_semaphore()
    for device in devices:
        pl.semaphore_signal(barrier, inc=1, device_id=device, device_id_type=pl.DeviceIdType.MESH)
    pl.semaphore_wait(barrier, len(devices))


class Line:
    def __init__(self, send_sem, recv_sem):
        self.send_sem, self.recv_sem = send_sem, recv_sem
        self.sent = []

    def copy(self, index, source, target, device):
        return pltpu.make_async_remote_copy(
            src_ref=source(),
            dst_ref=target(),
            send_sem=self.send_sem.at[index],
            recv_sem=self.recv_sem.at[index],
            device_id=device,
            device_id_type=pl.DeviceIdType.MESH,
        )

    def send(self, index, source, target, device):
        self.copy(index, source, target, device).start()
        self.sent.append((index, source, target, device))

    def take(self, index, target, device):
        self.copy(index, target, target, device).wait_recv()

    def finish(self):
        for sent in self.sent:
            self.copy(*sent).wait_send()


def abreast(*parts):
    running = list(parts)
    while running:
        for part in list(running):
            try:
                next(part)
            except StopIteration:
                running.remove(part)


GATHER_SEMS = 20


def gather_parts(axes, line, own, block, rows, local_sem, twin=None, twin_later=False):
    half, quarter = rows // 2, rows // 4
    mine, back, front, far = axes.at(0, 0), axes.at(0, -1), axes.at(0, 1), axes.at(0, 2)
    pair, pair_back, pair_front, pair_far = (axes.at(1, n) for n in (0, -1, 1, 2))
    ahead, behind, across = axes.ahead, axes.behind, axes.across

    def rows_of(which, low=0, count=rows, other=False):
        return lambda: block(which, low, count, other)

    def first(index, device):
        line.send(index, lambda: own, rows_of(mine), device)

    def relay(index, device, which, low=0, count=rows):
        line.send(index, rows_of(which, low, count), rows_of(which, low, count), device)

    def share(index, which):
        if twin is not None:
            relay(12 + index, twin, which)

    def keep():
        return pltpu.make_async_copy(own, block(mine, 0, rows), local_sem)

    keep().start()
    if twin is not None:
        first(12, twin)
    first(0, ahead)
    first(1, behind)
    first(2, across)
    keep().wait()
    yield
    line.take(0, rows_of(back), ahead)
    relay(3, ahead, back, 0, half)
    relay(4, across, back, half, half)
    share(1, back)
    line.take(1, rows_of(front), behind)
    relay(5, behind, front, half, half)
    relay(6, across, front, half, half)
    share(2, front)
    line.take(2, rows_of(pair), across)
    relay(7, ahead, pair, 0, half)
    relay(8, behind, pair, 0, half)
    share(3, pair)
    yield
    line.take(3, rows_of(far, 0, half), ahead)
    line.take(5, rows_of(far, half, half), behind)
    relay(9, across, far, half, half)
    share(4, far)
    line.take(7, rows_of(pair_back, 0, half), ahead)
    relay(10, ahead, pair_back, 0, quarter)
    line.take(8, rows_of(pair_front, 0, half), behind)
    relay(11, behind, pair_front, quarter, quarter)
    line.take(4, rows_of(pair_back, half, half), across)
    share(5, pair_back)
    line.take(6, rows_of(pair_front, half, half), across)
    share(6, pair_front)
    yield
    line.take(10, rows_of(pair_far, 0, quarter), ahead)
    line.take(11, rows_of(pair_far, quarter, quarter), behind)
    line.take(9, rows_of(pair_far, half, half), across)
    share(7, pair_far)
    yield
    if twin is not None and not twin_later:
        for index, which in enumerate(gather_order(axes)):
            line.take(12 + index, rows_of(which, other=True), twin)
    line.finish()


SUM_SEMS = 20


def add_rows(target, source, rows):
    step = 16
    count = rows // step

    def body(index, carry):
        at = pl.ds(pl.multiple_of(index * step, step), step)
        target[at] = target[at] + source[at]
        return carry

    lax.fori_loop(0, count, body, 0)


def stage_rows(rows):
    return 7 * rows


def gather_order(axes):
    return [axes.at(*v) for v in ((0, 0), (0, -1), (0, 1), (1, 0), (0, 2), (1, -1), (1, 1), (1, 2))]


def sum_order(axes):
    return [axes.at(*v) for v in ((1, 2), (0, 2), (1, -1), (1, 1), (0, -1), (0, 1), (1, 0), (0, 0))]


def sum_parts(axes, line, part, stage, rows, result, twin=None, store=None):
    half, quarter = rows // 2, rows // 4
    mine, back, front, far = axes.at(0, 0), axes.at(0, -1), axes.at(0, 1), axes.at(0, 2)
    pair, pair_back, pair_front, pair_far = (axes.at(1, n) for n in (0, -1, 1, 2))
    ahead, behind, across = axes.ahead, axes.behind, axes.across
    order = sum_order(axes)
    offsets, used = {}, 0
    for name, size in (
        ("Y0", half), ("M0", quarter), ("P0", quarter), ("M1", half), ("Y1", half), ("Y2", half),
        ("P1", half), ("M2", half), ("P2", half), ("M3", rows), ("P3", rows), ("Y3", rows),
    ):
        offsets[name] = (used, size, len(offsets))
        used += size

    def landing(name):
        low, size, _ = offsets[name]
        return lambda: stage.at[pl.ds(low, size)]

    def send(name, which, low, device):
        _, size, index = offsets[name]
        line.send(index, lambda: part(which, low, size), landing(name), device)

    def add(name, which, low, device):
        _, size, index = offsets[name]
        line.take(index, landing(name), device)
        add_rows(part(which, low, size), landing(name)(), size)

    def join(*places):
        if twin is not None:
            for place in places:
                line.take(12 + place, lambda: twin[2](order[place]), twin[0])
                add_rows(part(order[place], 0, rows), twin[2](order[place]), rows)

    def hand(*places):
        if twin is not None:
            for place in places:
                which = order[place]
                line.send(
                    12 + place, lambda w=which: twin[1](w), lambda w=which: twin[2](w), twin[0]
                )

    hand(0, 1, 2, 3)
    yield
    join(0)
    send("Y0", pair_far, half, across)
    send("M0", pair_far, 0, behind)
    send("P0", pair_far, quarter, ahead)
    join(1)
    send("M1", far, 0, behind)
    join(2)
    send("Y1", pair_back, half, across)
    join(3)
    send("Y2", pair_front, half, across)
    yield
    hand(4, 5, 6, 7)
    add("M0", pair_back, 0, behind)
    send("M2", pair_back, 0, behind)
    add("P0", pair_front, quarter, ahead)
    send("P2", pair_front, 0, ahead)
    add("Y0", far, half, across)
    send("P1", far, half, ahead)
    yield
    join(4, 5, 6, 7)
    add("M1", back, 0, behind)
    add("Y1", back, half, across)
    send("M3", back, 0, behind)
    add("M2", pair, 0, behind)
    add("P2", pair, 0, ahead)
    send("Y3", pair, 0, across)
    add("P1", front, half, ahead)
    add("Y2", front, half, across)
    send("P3", front, 0, ahead)
    yield
    for name, device in (("M3", behind), ("P3", ahead), ("Y3", across)):
        line.take(offsets[name][2], landing(name), device)
    step = 16

    def body(index, carry):
        low = pl.multiple_of(index * step, step)
        total = part(mine, low, step)[...].astype(f32)
        for name in ("M3", "P3", "Y3"):
            total = total + stage[pl.ds(offsets[name][0] + low, step)].astype(f32)
        if store is None:
            result[pl.ds(low, step)] = total.astype(result.dtype)
        else:
            store(low, step, total)
        return carry

    lax.fori_loop(0, rows // step, body, 0)
    line.finish()


def sems(count):
    return [pltpu.SemaphoreType.DMA((count,)), pltpu.SemaphoreType.DMA((count,))]


ANY = pl.BlockSpec(memory_space=pl.ANY)
IN_VMEM = pl.BlockSpec(memory_space=pltpu.VMEM)


def params(collective_id):
    return pltpu.CompilerParams(
        collective_id=collective_id, has_side_effects=True, vmem_limit_bytes=VMEM_LIMIT
    )


def dot(a, b):
    return jnp.dot(a, b, preferred_element_type=f32)


def dot_nt(a, b):
    return lax.dot_general(a, b, (((1,), (1,)), ((), ())), preferred_element_type=f32)


def dot_tn(a, b):
    return lax.dot_general(a, b, (((0,), (0,)), ((), ())), preferred_element_type=f32)


def pick(index, values):
    chosen = values[-1]
    for at in range(len(values) - 2, -1, -1):
        chosen = jnp.where(index == at, values[at], chosen)
    return chosen


def moe_call(collective_id, sent, rows_first, grad_all, inner, outer):
    count, columns = sent.shape
    width = inner.shape[0]
    hidden_width = outer.shape[0]
    small = columns - width
    half = count // 2
    chips = GROUP // 2
    wide = 4

    def kernel(
        sent_ref, first_ref, grad_ref, inner_ref, outer_ref,
        returned, out_sum, back_terms, out_terms, terms,
        rows_in, grads, hidden, back_gu, back, back_staged, back_stage, out, out_staged, out_stage,
        back_box, out_box, term_box,
        gs, gr, bs, br, os, orr, own_sem, load_sem, box_sem, term_sem,
    ):
        place = Place()
        axes, core, shard = place.tokens, place.core, place.shard
        gather_line = Line(gs, gr)

        def chip_of(which):
            return which[0] * RING + which[1]

        def blocks(which, other=False):
            return chip_of(which) * 2 + ((1 - core) if other else core)

        gather = gather_parts(
            axes, gather_line, sent_ref.at[pl.ds(half, half)],
            lambda which, low, n, other=False: rows_in.at[1, blocks(which, other), pl.ds(low, n)],
            half, own_sem, place.twin, twin_later=True,
        )

        def sum_of(terms_ref, staged, stage, result, send_sem, recv_sem):
            return sum_parts(
                axes, Line(send_sem, recv_sem),
                lambda which, low, n: terms_ref.at[blocks(which), pl.ds(low, n)],
                stage, half, result,
                (place.twin, lambda which: terms_ref.at[blocks(which, True)],
                 lambda which: staged.at[chip_of(which)]),
            )

        back_sum = sum_of(back, back_staged, back_stage, returned, bs, br)
        outs_sum = sum_of(out, out_staged, out_stage, out_sum, os, orr)

        def loads(t):
            at = pl.ds(t * wide, wide)
            return [
                pltpu.make_async_copy(first_ref.at[at], rows_in.at[0, at], load_sem.at[t, 0]),
                pltpu.make_async_copy(
                    grad_ref.at[at, pl.ds(0, half)], grads.at[0, at], load_sem.at[t, 1]
                ),
            ]

        second_grads = pltpu.make_async_copy(
            grad_ref.at[:, pl.ds(half, half)], grads.at[1], load_sem.at[GROUP // wide, 0]
        )

        def box_copies(chip, slot):
            at = pl.ds(chip * 2, 2)
            return [
                pltpu.make_async_copy(back_box.at[slot], back_terms.at[at], box_sem.at[slot, 0]),
                pltpu.make_async_copy(out_box.at[slot], out_terms.at[at], box_sem.at[slot, 1]),
            ]

        def tile(chunk, first, number):
            rows_count = number * half
            at = pl.ds(first, number)
            lanes = lane_of((rows_count, small))
            is_high, is_rest = lanes == shard, lanes == shard + GROUP
            row_block = rows_in[chunk, at].reshape(rows_count, columns)
            gate = jnp.sum(
                jnp.where(is_high | is_rest, row_block[:, width:].astype(f32), 0.0),
                axis=1, keepdims=True,
            )
            gate_up = dot(row_block[:, :width], inner_ref[...])
            gate_part, up_part = gate_up[:, :hidden_width], gate_up[:, hidden_width:]
            sigmoid = 1.0 / (1.0 + jnp.exp(-gate_part))
            active = gate_part * sigmoid
            product = active * up_part
            hidden_low = product.astype(bf16)
            hidden[chunk, at] = hidden_low.reshape(number, half, hidden_width)
            out_rows = (gate * dot(hidden_low, outer_ref[...])).astype(bf16)
            grad = grads[chunk, at].reshape(rows_count, width)
            grad_hidden = dot_nt(grad, outer_ref[...])
            grad_gate = jnp.sum(grad_hidden * product, axis=1, keepdims=True)
            grad_hidden = grad_hidden * gate
            grad_gate_up = jnp.concatenate(
                [
                    grad_hidden * up_part * sigmoid * (1.0 + gate_part * (1.0 - sigmoid)),
                    grad_hidden * active,
                ],
                axis=1,
            ).astype(bf16)
            back_gu[chunk, at] = grad_gate_up.reshape(number, half, 2 * hidden_width)
            grads[chunk, at] = (gate * grad.astype(f32)).astype(bf16).reshape(number, half, width)
            grad_rows = dot_nt(grad_gate_up, inner_ref[...]).astype(bf16)
            high = grad_gate.astype(bf16).astype(f32)
            tail = jnp.where(is_high, high, jnp.where(is_rest, grad_gate - high, 0.0)).astype(bf16)
            return (
                out_rows.reshape(number, half, width),
                grad_rows.reshape(number, half, width),
                tail.reshape(number, half, small),
            )

        for t in range(GROUP // wide):
            for load in loads(t):
                load.start()
        second_grads.start()
        greet(axes.neighbours() + [place.twin])
        next(gather)

        def first_tiles(t, carry):
            hooks(t, ((2, lambda: next(gather)),))
            for load in loads(t):
                load.wait()
            at = pl.ds(t * wide, wide)
            out_rows, grad_rows, tail = tile(0, t * wide, wide)
            out[at] = out_rows
            back[at, :, pl.ds(0, width)] = grad_rows
            back[at, :, pl.ds(width, small)] = tail
            return carry

        lax.fori_loop(0, GROUP // wide, first_tiles, 0)
        next(back_sum)
        second_grads.wait()
        chips1 = [chip_of(which) for which in gather_order(axes)]

        def second_tiles(t, carry):
            hooks(
                t,
                (
                    (1, lambda: next(back_sum)),
                    (2, lambda: next(gather)),
                    (3, lambda: next(outs_sum)),
                    (4, lambda: next(back_sum)),
                    (5, lambda: next(outs_sum)),
                    (7, lambda: next(gather)),
                ),
            )
            chip, slot = pick(t, chips1), lax.rem(t, 2)
            gather_line.take(12 + t, lambda: rows_in.at[1, chip * 2 + 1 - core], place.twin)
            out_rows, grad_rows, tail = tile(1, chip * 2, 2)

            @pl.when(t >= 2)
            def _():
                for copy in box_copies(chip, slot):
                    copy.wait()

            out_box[slot] = out_rows
            back_box[slot, :, :, pl.ds(0, width)] = grad_rows
            back_box[slot, :, :, pl.ds(width, small)] = tail
            for copy in box_copies(chip, slot):
                copy.start()
            return carry

        lax.fori_loop(0, chips, second_tiles, 0)

        def term_copy(low, slot):
            return pltpu.make_async_copy(
                term_box.at[slot], terms.at[pl.ds(low, 256)], term_sem.at[slot]
            )

        every = 2 * GROUP * half

        def keep(index, low, value):
            slot = lax.rem(index, 2)

            @pl.when(index >= 2)
            def _():
                term_copy(low, slot).wait()

            term_box[slot] = value.astype(bf16)
            term_copy(low, slot).start()

        downs = hidden_width // 256

        def down_terms(index, carry):
            hooks(index, ((0, lambda: next(back_sum)), (1, lambda: next(outs_sum))))
            at = chunk_256(index)
            value = dot_tn(hidden[:, :, :, at].reshape(every, 256), grads[...].reshape(every, width))
            keep(index, pl.multiple_of(width + index * 256, 256), value)
            return carry

        lax.fori_loop(0, downs, down_terms, 0)

        def inner_terms(index, carry):
            hooks(
                index,
                (
                    (1, lambda: drained(back_sum)),
                    (2, lambda: next(outs_sum)),
                ),
            )
            at = chunk_256(index)
            value = dot_tn(
                rows_in[:, :, :, at].reshape(every, 256),
                back_gu[...].reshape(every, 2 * hidden_width),
            )
            keep(index + downs, pl.multiple_of(index * 256, 256), value)
            return carry

        lax.fori_loop(0, width // 256, inner_terms, 0)
        drained(outs_sum)
        drained(gather)
        for slot in range(2):
            for copy in box_copies(0, slot):
                copy.wait()
            term_copy(0, slot).wait()

    term_rows = width + hidden_width
    return pl.pallas_call(
        kernel,
        out_shape=[
            jax.ShapeDtypeStruct((half, columns), f32),
            jax.ShapeDtypeStruct((half, width), f32),
            jax.ShapeDtypeStruct((GROUP, half, columns), bf16),
            jax.ShapeDtypeStruct((GROUP, half, width), bf16),
            jax.ShapeDtypeStruct((term_rows, width), bf16),
        ],
        in_specs=[ANY, ANY, ANY, IN_VMEM, IN_VMEM],
        out_specs=[IN_VMEM, IN_VMEM, ANY, ANY, ANY],
        scratch_shapes=[
            pltpu.VMEM((2, GROUP, half, columns), bf16),
            pltpu.VMEM((2, GROUP, half, width), bf16),
            pltpu.VMEM((2, GROUP, half, hidden_width), bf16),
            pltpu.VMEM((2, GROUP, half, 2 * hidden_width), bf16),
            pltpu.VMEM((GROUP, half, columns), bf16),
            pltpu.VMEM((chips, half, columns), bf16),
            pltpu.VMEM((stage_rows(half), columns), bf16),
            pltpu.VMEM((GROUP, half, width), bf16),
            pltpu.VMEM((chips, half, width), bf16),
            pltpu.VMEM((stage_rows(half), width), bf16),
            pltpu.VMEM((2, 2, half, columns), bf16),
            pltpu.VMEM((2, 2, half, width), bf16),
            pltpu.VMEM((2, 256, width), bf16),
        ]
        + sems(GATHER_SEMS)
        + sems(SUM_SEMS) * 2
        + [
            pltpu.SemaphoreType.DMA,
            pltpu.SemaphoreType.DMA((GROUP // wide + 1, 2)),
            pltpu.SemaphoreType.DMA((2, 2)),
            pltpu.SemaphoreType.DMA((2,)),
        ],
        compiler_params=params(collective_id),
    )(sent, rows_first, grad_all, inner, outer)


WIDTH = 1024
QUERY = HEADS * HEAD_DIM
KEY = KV_HEADS * HEAD_DIM
EXPERTS = 16
SMALL = 128
LANES = 128
AT_K = QUERY
AT_V = AT_K + KEY
AT_S = AT_V + KEY
AT_O = AT_S + SMALL
PACKED = AT_O + WIDTH
ROWS_OWN = WIDTH // GROUP
KGAIN_OWN = KEY // GROUP
HEAD_PAIRS = KV_HEADS // 2
REST = 2 * KEY + SMALL


def drained(part):
    for _ in part:
        pass


def hooks(index, steps):
    for at, step in steps:
        pl.when(index == at)(step)


def chunk_256(index):
    return pl.ds(pl.multiple_of(index * 256, 256), 256)


def root_mean(values):
    return lax.rsqrt(jnp.mean(values * values, axis=1, keepdims=True) + norm_eps)


def lane_of(shape):
    return lax.broadcasted_iota(jnp.int32, shape, 1)


def turned(values, cosine, sine):
    first = lax.rem(lane_of(values.shape), HEAD_DIM) < HEAD_DIM // 2
    swapped = jnp.where(
        first, pltpu.roll(values, LANES - HEAD_DIM // 2, 1), pltpu.roll(values, HEAD_DIM // 2, 1)
    )
    return values * cosine + swapped * sine


def short_rows():
    row = lax.broadcasted_iota(jnp.int32, (WIDTH, KEY), 0)
    column = lax.broadcasted_iota(jnp.int32, (WIDTH, KEY), 1)
    same = (lax.div(row, ROWS_OWN) == lax.div(column, KGAIN_OWN)) & (
        lax.rem(row, ROWS_OWN) == lax.rem(column, KGAIN_OWN)
    )
    return jnp.where(same, 1.0, 0.0).astype(bf16)


def gain_rows(small):
    rows = jnp.transpose(small.astype(f32))
    gain_k = dot(rows[EXPERTS : EXPERTS + 8].astype(bf16), short_rows())[3:4]
    return rows[EXPERTS : EXPERTS + 1], rows[EXPERTS + 1 : EXPERTS + 2], rows[EXPERTS + 2 : EXPERTS + 3], gain_k


def four_heads(chunk_a, chunk_b):
    low = lane_of(chunk_a.shape) < HEAD_DIM
    zero = jnp.zeros_like(chunk_a)
    return jnp.concatenate(
        [
            jnp.where(low, chunk_a, zero),
            jnp.where(low, pltpu.roll(chunk_a, HEAD_DIM, 1), zero),
            jnp.where(low, zero, pltpu.roll(chunk_b, HEAD_DIM, 1)),
            jnp.where(low, zero, chunk_b),
        ],
        axis=0,
    )


def two_chunks(blocks):
    rows = blocks.shape[0] // 4
    one, two, three, four = (blocks[n * rows : (n + 1) * rows] for n in range(4))
    low = lane_of(one.shape) < HEAD_DIM
    return (
        jnp.where(low, one, pltpu.roll(two, HEAD_DIM, 1)),
        jnp.where(low, pltpu.roll(three, HEAD_DIM, 1), four),
    )


def chunk_at(index, base=0):
    return pl.ds(pl.multiple_of(base + index * LANES, LANES), LANES)


def front_call(collective_id, tokens, cotangent, weights_own, small_own, cosine, sine, routes, starts):
    count, width = tokens.shape
    seqs = starts.shape[0]
    positions = count // seqs
    length = REPS * positions
    score_scale = HEAD_DIM ** (-0.5)
    sent_width = width + SMALL

    def kernel(
        starts_ref, tokens_ref, grad_ref, query_w, key_w, value_w, output_w, small_ref,
        cos_ref, sin_ref, routes_ref,
        dense_out, grad_all, pairs_out, soft_out, rows_first,
        attn_in, query_raw, key_raw, query_low, mixed, middle, sent, gates_out,
        packed, dense, pairs, pair_own, soft_box, bias_box,
        ws0, wr0, ws1, wr1, ws2, wr2, gs, gr, ks0, kr0, ks1, kr1, rs, rr, own_sem, out_sem, soft_sem, pack_sem,
    ):
        place = Place()
        core = place.core
        packing = [
            pltpu.make_async_copy(
                source, packed.at[:, pl.ds(low, source.shape[1])], pack_sem.at[index]
            )
            for index, (source, low) in enumerate(
                ((key_w, AT_K), (value_w, AT_V), (small_ref, AT_S), (query_w, 0), (output_w, AT_O))
            )
        ]
        for copy in packing:
            copy.start()

        def token_block(index, low, size):
            def block(which, row, n, other=False):
                at = (which[0] * RING + which[1]) * 2 + ((1 - core) if other else core)
                return dense.at[at, pl.ds(row, n), pl.ds(low, size)]

            return block

        def weight_gather(index, low, size, send_sem, recv_sem):
            return gather_parts(
                place.tokens, Line(send_sem, recv_sem), packed.at[:, pl.ds(low, size)],
                token_block(index, low, size), ROWS_OWN, own_sem.at[index], place.twin,
            )

        def rows_of(target):
            def block(which, row, n, other=False):
                at = (which[0] * RING + which[1]) * 2 + ((1 - core) if other else core)
                return target.at[at, pl.ds(row, n)]

            return block

        def pair_gather(seq, send_sem, recv_sem):
            def block(which, row, n, other=False):
                return pairs.at[seq, which[0] * RING + which[1], pl.ds(row, n)]

            return gather_parts(
                place.copies, Line(send_sem, recv_sem),
                pair_own.at[pl.ds(seq * positions, positions)], block, positions, own_sem.at[3 + seq],
            )

        def soft_copy(seq, index, slot):
            return pltpu.make_async_copy(
                soft_box.at[slot], soft_out.at[seq, index], soft_sem.at[slot]
            )

        rest_gather = weight_gather(0, AT_K, REST, ws0, wr0)
        query_gather = weight_gather(1, 0, QUERY, ws1, wr1)
        output_gather = weight_gather(2, AT_O, WIDTH, ws2, wr2)
        grads = gather_parts(
            place.tokens, Line(gs, gr), grad_ref, rows_of(grad_all), count, own_sem.at[5], place.twin
        )
        first_rows = gather_parts(
            place.tokens, Line(rs, rr), sent.at[pl.ds(0, positions)], rows_of(rows_first), positions,
            own_sem.at[6], place.twin,
        )
        pair_gathers = [pair_gather(0, ks0, kr0), pair_gather(1, ks1, kr1)]

        greet(place.tokens.neighbours() + place.copies.neighbours() + [place.twin])
        for copy in packing:
            copy.wait()
        next(rest_gather)
        next(query_gather)
        inputs = tokens_ref[...].astype(f32)
        middle[...] = inputs * root_mean(inputs)
        next(rest_gather)
        next(query_gather)
        next(output_gather)
        query_at = place.rep * positions + lax.broadcasted_iota(jnp.int32, (positions, 1), 0)
        key_at = lax.broadcasted_iota(jnp.int32, (1, length), 1)
        for seq in range(seqs):
            allowed = key_at <= query_at
            for piece in range(starts_ref.shape[1]):
                start = starts_ref[seq, piece]
                query_inside = (query_at >= start) & (query_at < start + PIC)
                key_inside = (key_at >= start) & (key_at < start + PIC)
                allowed = allowed | (query_inside & key_inside)
            bias_box[seq] = jnp.where(allowed, 0.0, masked_score)
        next(rest_gather)
        next(query_gather)
        next(output_gather)
        drained(rest_gather)

        def weights(low, size):
            return dense[:, :, pl.ds(low, size)].reshape(width, size)

        small = weights(AT_S, SMALL)
        gain_a, gain_q, gain_f, gain_k = gain_rows(small)
        rows = (middle[...] * gain_a).astype(bf16)
        attn_in[...] = rows
        cos2 = jnp.concatenate([cos_ref[...]] * seqs, axis=0)
        sin2 = jnp.concatenate([sin_ref[...]] * seqs, axis=0)
        raw = dot(rows, weights(AT_K, KEY))
        key_raw[...] = raw
        scaled = raw * root_mean(raw) * gain_k
        for chunk in range(KEY // LANES):
            at = slice(chunk * LANES, (chunk + 1) * LANES)
            pair_own[:, at] = turned(scaled[:, at], cos2, sin2).astype(bf16)
        pair_own[:, KEY:] = dot(rows, weights(AT_V, KEY)).astype(bf16)
        next(pair_gathers[0])
        drained(query_gather)
        next(output_gather)
        next(grads)
        raw = dot(rows, weights(0, QUERY))
        query_raw[...] = raw
        scaled = raw * root_mean(raw) * gain_q
        for chunk in range(QUERY // LANES):
            at = slice(chunk * LANES, (chunk + 1) * LANES)
            query_low[:, at] = turned(scaled[:, at], cos2, sin2).astype(bf16)
        next(pair_gathers[0])
        next(pair_gathers[1])
        drained(output_gather)
        dense_copy = pltpu.make_async_copy(dense, dense_out, out_sem.at[0])
        dense_copy.start()
        next(pair_gathers[0])
        next(pair_gathers[1])
        drained(pair_gathers[0])
        next(grads)

        def attend(seq, index, slot, wait_first):
            rows_at = pl.ds(seq * positions, positions)
            queries = four_heads(
                query_low[rows_at, chunk_at(2 * index)].astype(f32),
                query_low[rows_at, chunk_at(2 * index + 1)].astype(f32),
            )
            queries = (queries * score_scale).astype(bf16)
            keys = pairs[seq, :, :, chunk_at(index)].reshape(length, LANES)
            scores = dot_nt(queries, keys).reshape(4, positions, length) + bias_box[seq][None]
            scores = scores.reshape(4 * positions, length)
            raised = jnp.exp(scores - jnp.max(scores, axis=1, keepdims=True))
            soft = (raised * (1.0 / jnp.sum(raised, axis=1, keepdims=True))).astype(bf16)

            @pl.when(wait_first)
            def _():
                soft_copy(seq, index, slot).wait()

            soft_box[slot] = soft
            soft_copy(seq, index, slot).start()
            values = pairs[seq, :, :, chunk_at(index, KEY)].reshape(length, LANES)
            chunk_a, chunk_b = two_chunks(dot(soft, values))
            mixed[rows_at, chunk_at(2 * index)] = chunk_a.astype(bf16)
            mixed[rows_at, chunk_at(2 * index + 1)] = chunk_b.astype(bf16)

        def features(seq):
            at = pl.ds(seq * positions, positions)
            total = tokens_ref[at].astype(f32) + dot(mixed[at], weights(AT_O, WIDTH))
            middle[at] = total
            ffn_in = (total * root_mean(total) * gain_f).astype(bf16)
            sent[at, pl.ds(0, width)] = ffn_in
            lanes = lane_of((positions, SMALL))
            named = routes_ref[at]
            chosen = lanes == named[:, :1]
            for choice in range(1, named.shape[1]):
                chosen = chosen | (lanes == named[:, choice : choice + 1])
            logits = jnp.where(chosen, dot(ffn_in, small), masked_score)
            raised = jnp.exp(logits - jnp.max(logits, axis=1, keepdims=True))
            gates = raised * (1.0 / jnp.sum(raised, axis=1, keepdims=True))
            gates = jnp.where(chosen, gates, 0.0)
            gates_out[at] = gates
            high = gates.astype(bf16).astype(f32)
            tail = high + pltpu.roll(gates - high, EXPERTS, 1)
            sent[at, pl.ds(width, SMALL)] = tail.astype(bf16)

        def first_heads(index, carry):
            hooks(index, ((2, lambda: next(pair_gathers[1])),))
            attend(0, index, lax.rem(index, 2), index >= 2)
            return carry

        lax.fori_loop(0, HEAD_PAIRS, first_heads, 0)
        features(0)
        next(first_rows)
        drained(pair_gathers[1])
        pairs_copy = pltpu.make_async_copy(pairs, pairs_out, out_sem.at[1])
        pairs_copy.start()
        next(grads)

        def second_heads(index, carry):
            hooks(
                index,
                (
                    (2, lambda: next(grads)),
                    (3, lambda: next(first_rows)),
                ),
            )
            attend(1, index, lax.rem(index, 2), index >= 0)
            return carry

        lax.fori_loop(0, HEAD_PAIRS, second_heads, 0)
        features(1)
        next(first_rows)
        drained(grads)
        drained(first_rows)
        dense_copy.wait()
        pairs_copy.wait()
        for slot in range(2):
            soft_copy(1, 0, slot).wait()

    return pl.pallas_call(
        kernel,
        out_shape=[
            jax.ShapeDtypeStruct((GROUP, ROWS_OWN, PACKED), bf16),
            jax.ShapeDtypeStruct((GROUP, count, width), bf16),
            jax.ShapeDtypeStruct((seqs, REPS, positions, 2 * KEY), bf16),
            jax.ShapeDtypeStruct((seqs, HEAD_PAIRS, 4 * positions, length), bf16),
            jax.ShapeDtypeStruct((GROUP, positions, sent_width), bf16),
            jax.ShapeDtypeStruct((count, width), bf16),
            jax.ShapeDtypeStruct((count, QUERY), f32),
            jax.ShapeDtypeStruct((count, KEY), f32),
            jax.ShapeDtypeStruct((count, QUERY), bf16),
            jax.ShapeDtypeStruct((count, QUERY), bf16),
            jax.ShapeDtypeStruct((count, width), f32),
            jax.ShapeDtypeStruct((count, width + SMALL), bf16),
            jax.ShapeDtypeStruct((count, SMALL), f32),
        ],
        in_specs=[pl.BlockSpec(memory_space=pltpu.SMEM), IN_VMEM] + [ANY] * 6 + [IN_VMEM] * 3,
        out_specs=[ANY] * 5 + [IN_VMEM] * 8,
        scratch_shapes=[
            pltpu.VMEM((ROWS_OWN, PACKED), bf16),
            pltpu.VMEM((GROUP, ROWS_OWN, PACKED), bf16),
            pltpu.VMEM((seqs, REPS, positions, 2 * KEY), bf16),
            pltpu.VMEM((count, 2 * KEY), bf16),
            pltpu.VMEM((2, 4 * positions, length), bf16),
            pltpu.VMEM((seqs, positions, length), f32),
        ]
        + sems(GATHER_SEMS) * 7
        + [
            pltpu.SemaphoreType.DMA((7,)),
            pltpu.SemaphoreType.DMA((2,)),
            pltpu.SemaphoreType.DMA((2,)),
            pltpu.SemaphoreType.DMA((5,)),
        ],
        compiler_params=params(collective_id),
    )(starts, tokens, cotangent, *weights_own, small_own, cosine, sine, routes)


def norm_back(values, gain, grad):
    scale = root_mean(values)
    weighted = grad * gain
    mean = jnp.mean(values * weighted, axis=1, keepdims=True)
    inner = weighted * scale - values * (scale * scale * scale * mean)
    return inner, jnp.sum(grad * values * scale, axis=0, keepdims=True)


def back_call(
    collective_id, returned, out_first, back_terms, gates, middle, sent, dense, cotangent, tokens, attn_in, query_raw, key_raw,
    query_low, mixed, pairs, soft, out_terms, expert_terms, cosine, sine,
):
    count, width = tokens.shape
    seqs, _, positions, _ = pairs.shape
    columns = back_terms.shape[2]
    length = REPS * positions
    expert_rows = expert_terms.shape[0] // REPS
    score_scale = HEAD_DIM ** (-0.5)
    chips = GROUP // 2

    def kernel(
        returned_ref, out_first_ref, back_ref, gates_ref, middle_ref, sent_ref, dense_ref, grad_ref, tokens_ref, attn_ref,
        query_raw_ref, key_raw_ref, query_ref, mixed_ref, pairs_ref, soft_ref, out_ref, expert_ref,
        cos_ref, sin_ref,
        block_out, tokens_grad, dense_all, expert_all,
        weight_box, weight_rest, rest_terms, dense_own,
        o_staged, q_staged, rest_staged, o_stage, q_stage, rest_stage,
        out_held, out_staged, out_stage, back_held, back_staged, back_stage, returned_second,
        expert_held, expert_stage, expert_own,
        soft_box, key_box, value_box, pair_terms, pair_stage, pair_grads,
        grad_mixed, grad_query, grad_middle, grad_attn, grad_attn_in, logit_box, gain_box,
        out_s, out_r, back_s, back_r, exp_s, exp_r, kv0_s, kv0_r, kv1_s, kv1_r, o_s, o_r, q_s, q_r, rest_s, rest_r,
        ge_s, ge_r, go_s, go_r, gq_s, gq_r, grest_s, grest_r,
        load_sem, held_sem, box_sem, own_sem,
    ):
        place = Place()
        core = place.core
        token_axes, copy_axes = place.tokens, place.copies
        q_terms = expert_held

        def chip_of(which):
            return which[0] * RING + which[1]

        def blocks(which, other=False):
            return chip_of(which) * 2 + ((1 - core) if other else core)

        def out_store(low, step, value):
            at = pl.ds(positions + low, step)
            block_out[at] = (middle_ref[at] + value).astype(bf16)

        def second_sum(source, held, staged, stage, send_sem, recv_sem, result, store=None):
            return sum_parts(
                token_axes, Line(send_sem, recv_sem),
                lambda which, low, n: held.at[chip_of(which), pl.ds(low, n)],
                stage, positions, result,
                (place.twin, lambda which: source.at[blocks(which, True)],
                 lambda which: staged.at[chip_of(which)]),
                store=store,
            )

        out_sum = second_sum(
            out_ref, out_held, out_staged, out_stage, out_s, out_r, None, store=out_store
        )
        back_sum = second_sum(
            back_ref, back_held, back_staged, back_stage, back_s, back_r, returned_second
        )
        expert_sum = sum_parts(
            copy_axes, Line(exp_s, exp_r),
            lambda which, low, n: expert_held.at[pl.ds(chip_of(which) * expert_rows + low, n)],
            expert_stage, expert_rows, expert_own,
        )

        def pair_sum(seq, send_sem, recv_sem):
            return sum_parts(
                copy_axes, Line(send_sem, recv_sem),
                lambda which, low, n: pair_terms.at[seq, chip_of(which), pl.ds(low, n)],
                pair_stage.at[seq], positions, pair_grads.at[pl.ds(seq * positions, positions)],
            )

        pair_sums = [pair_sum(0, kv0_s, kv0_r), pair_sum(1, kv1_s, kv1_r)]

        def rows_of_block(terms, index, low, n):
            return terms.at[pl.ds(index * ROWS_OWN + low, n)]

        def rows_of_pairs(terms, index, low, n):
            at = lax.rem(index, 2) * ROWS_OWN + low
            return terms.at[0, lax.div(index, 2), pl.ds(at, n)]

        def dense_sum(rows_of, terms, staged, stage, low, size, send_sem, recv_sem):
            return sum_parts(
                token_axes, Line(send_sem, recv_sem),
                lambda which, row, n: rows_of(terms, blocks(which), row, n),
                stage, ROWS_OWN, dense_own.at[:, pl.ds(low, size)],
                (place.twin, lambda which: rows_of(terms, blocks(which, True), 0, ROWS_OWN),
                 lambda which: staged.at[chip_of(which)]),
            )

        o_sum = dense_sum(rows_of_pairs, pair_terms, o_staged, o_stage, AT_O, width, o_s, o_r)
        q_sum = dense_sum(rows_of_block, q_terms, q_staged, q_stage, 0, QUERY, q_s, q_r)
        rest_sum = dense_sum(rows_of_block, rest_terms, rest_staged, rest_stage, AT_K, REST, rest_s, rest_r)

        def dense_gather(low, size, send_sem, recv_sem, index):
            return gather_parts(
                copy_axes, Line(send_sem, recv_sem), dense_own.at[:, pl.ds(low, size)],
                lambda which, row, n, other=False: dense_all.at[
                    chip_of(which), pl.ds(row, n), pl.ds(low, size)
                ],
                ROWS_OWN, own_sem.at[index],
            )

        o_gather = dense_gather(AT_O, width, go_s, go_r, 0)
        q_gather = dense_gather(0, QUERY, gq_s, gq_r, 1)
        rest_gather = dense_gather(AT_K, REST, grest_s, grest_r, 2)
        expert_gather = gather_parts(
            copy_axes, Line(ge_s, ge_r), expert_own,
            lambda which, row, n, other=False: expert_all.at[chip_of(which), pl.ds(row, n)],
            expert_rows, own_sem.at[3],
        )

        def weight_load(low, index):
            return pltpu.make_async_copy(
                dense_ref.at[:, :, pl.ds(low, width)], weight_box, load_sem.at[index]
            )

        rest_load = pltpu.make_async_copy(
            dense_ref.at[:, :, pl.ds(AT_K, REST)], weight_rest, load_sem.at[1]
        )
        expert_load = pltpu.make_async_copy(expert_ref, expert_held, load_sem.at[2])
        held_loads = [
            [
                pltpu.make_async_copy(
                    source.at[2 * chip + core], held.at[chip], held_sem.at[kind, chip]
                )
                for chip in range(chips)
            ]
            for kind, (source, held) in enumerate(((back_ref, back_held), (out_ref, out_held)))
        ]

        def box_loads(number, slot):
            seq, index = lax.div(number, HEAD_PAIRS), lax.rem(number, HEAD_PAIRS)
            return [
                pltpu.make_async_copy(
                    soft_ref.at[seq, index], soft_box.at[slot], box_sem.at[slot, 0]
                ),
                pltpu.make_async_copy(
                    pairs_ref.at[seq, :, :, chunk_at(index)], key_box.at[slot], box_sem.at[slot, 1]
                ),
                pltpu.make_async_copy(
                    pairs_ref.at[seq, :, :, chunk_at(index, KEY)],
                    value_box.at[slot],
                    box_sem.at[slot, 2],
                ),
            ]

        for load in held_loads[0]:
            load.start()
        expert_load.start()
        rest_load.start()
        weight_load(AT_O, 0).start()
        for load in held_loads[1]:
            load.start()
        for load in box_loads(0, 0):
            load.start()
        greet(token_axes.neighbours() + copy_axes.neighbours() + [place.twin])
        next(back_sum)
        expert_load.wait()
        next(expert_sum)
        next(expert_sum)
        for load in held_loads[0]:
            load.wait()
        next(back_sum)
        rest_load.wait()

        small = weight_rest[:, :, pl.ds(2 * KEY, SMALL)].reshape(width, SMALL)
        gain_a, gain_q, gain_f, gain_k = gain_rows(small)
        gain_box[...] = jnp.zeros_like(gain_box)

        def features_back(seq, source):
            at = pl.ds(seq * positions, positions)
            gates = gates_ref[at]
            tail = source[:, pl.ds(width, SMALL)]
            grad_gates = tail + pltpu.roll(tail, SMALL - EXPERTS, 1)
            grad_logits = gates * (
                grad_gates - jnp.sum(gates * grad_gates, axis=1, keepdims=True)
            )
            grad_logits = grad_logits.astype(bf16)
            logit_box[at] = grad_logits
            grad_ffn = source[:, pl.ds(0, width)] + dot_nt(grad_logits, small)
            inner, gain_terms = norm_back(middle_ref[at], gain_f, grad_ffn)
            inner = grad_ref[at].astype(f32) + inner
            grad_middle[at] = inner
            low = inner.astype(bf16)
            grad_attn[at] = low
            gain_at = pl.ds(EXPERTS + 2, 1)
            gain_box[gain_at] = gain_box[gain_at] + gain_terms
            weight_o = weight_box[...].reshape(QUERY, width)
            grad_mixed[at] = dot_nt(low, weight_o).astype(bf16)

        weight_load(AT_O, 0).wait()
        features_back(0, returned_ref)
        first_at = pl.ds(0, positions)
        block_out[first_at] = (middle_ref[first_at] + out_first_ref[...]).astype(bf16)

        def attend_back(seq, index):
            number = seq * HEAD_PAIRS + index
            slot = lax.rem(number, 2)
            for load in box_loads(number, slot):
                load.wait()

            @pl.when(number + 1 < seqs * HEAD_PAIRS)
            def _():
                for load in box_loads(number + 1, 1 - slot):
                    load.start()

            rows_at = pl.ds(seq * positions, positions)
            first, second = chunk_at(2 * index), chunk_at(2 * index + 1)
            queries = four_heads(
                query_ref[rows_at, first].astype(f32), query_ref[rows_at, second].astype(f32)
            )
            queries = (queries * score_scale).astype(bf16)
            grads = four_heads(
                grad_mixed[rows_at, first].astype(f32), grad_mixed[rows_at, second].astype(f32)
            ).astype(bf16)
            keys = key_box[slot].reshape(length, LANES)
            values = value_box[slot].reshape(length, LANES)
            soft_low = soft_box[slot]
            value_terms = dot_tn(soft_low, grads)
            pair_terms[seq, :, :, chunk_at(index, KEY)] = value_terms.astype(bf16).reshape(
                REPS, positions, LANES
            )
            soft_full = soft_low.astype(f32)
            grad_soft = dot_nt(grads, values)
            weighted = soft_full * grad_soft
            grad_scores = (
                weighted - soft_full * jnp.sum(weighted, axis=1, keepdims=True)
            ).astype(bf16)
            key_terms = dot_tn(grad_scores, queries)
            pair_terms[seq, :, :, chunk_at(index)] = key_terms.astype(bf16).reshape(
                REPS, positions, LANES
            )
            chunk_a, chunk_b = two_chunks(dot(grad_scores, keys) * score_scale)
            grad_query[rows_at, first] = chunk_a.astype(bf16)
            grad_query[rows_at, second] = chunk_b.astype(bf16)

        def first_heads(index, carry):
            hooks(index, ((2, lambda: next(back_sum)), (3, lambda: next(expert_sum))))
            attend_back(0, index)
            return carry

        lax.fori_loop(0, HEAD_PAIRS, first_heads, 0)
        next(pair_sums[0])
        next(pair_sums[0])
        next(back_sum)
        for load in held_loads[1]:
            load.wait()
        next(out_sum)
        next(expert_sum)
        next(out_sum)
        drained(expert_sum)
        next(pair_sums[0])
        drained(back_sum)
        features_back(1, returned_second)
        weight_load(0, 3).start()

        def second_heads(index, carry):
            hooks(
                index,
                (
                    (0, lambda: next(pair_sums[0])),
                    (1, lambda: next(out_sum)),
                    (2, lambda: (drained(pair_sums[0]), next(expert_gather))[0]),
                    (3, lambda: next(out_sum)),
                ),
            )
            attend_back(1, index)
            return carry

        lax.fori_loop(0, HEAD_PAIRS, second_heads, 0)
        next(pair_sums[1])
        next(pair_sums[1])
        drained(out_sum)
        next(expert_gather)

        def o_rows(index, carry):
            at = chunk_256(index)
            value = dot_tn(mixed_ref[:, at], grad_attn[...]).astype(bf16)
            pair_terms[0, pl.ds(2 * index, 2)] = value.reshape(2, positions, width)
            return carry

        lax.fori_loop(0, QUERY // 256, o_rows, 0)
        next(o_sum)
        next(o_sum)

        cos2 = jnp.concatenate([cos_ref[...]] * seqs, axis=0)
        sin2 = -jnp.concatenate([sin_ref[...]] * seqs, axis=0)

        def turned_back(values):
            return jnp.concatenate(
                [
                    turned(values[:, low : low + LANES], cos2, sin2)
                    for low in range(0, values.shape[1], LANES)
                ],
                axis=1,
            )

        grad, gain_q_terms = norm_back(
            query_raw_ref[...], gain_q, turned_back(grad_query[...].astype(f32))
        )
        gain_box[pl.ds(EXPERTS + 1, 1)] = gain_q_terms
        grad_query_low = grad.astype(bf16)
        weight_load(0, 3).wait()
        grad_attn_in[...] = dot_nt(grad_query_low, weight_box[...].reshape(width, QUERY))

        def q_rows(index, carry):
            at = chunk_256(index)
            q_terms[at] = dot_tn(attn_ref[:, at], grad_query_low).astype(bf16)
            return carry

        lax.fori_loop(0, width // 256, q_rows, 0)
        next(q_sum)
        next(pair_sums[1])
        next(q_sum)
        next(expert_gather)
        next(o_sum)
        next(pair_sums[1])
        next(o_sum)
        next(q_sum)
        router_terms = dot_tn(sent_ref[:, pl.ds(0, width)], logit_box[...])
        drained(o_sum)
        drained(pair_sums[1])
        next(o_gather)

        grads = pair_grads[...]
        grad, gain_k_terms = norm_back(
            key_raw_ref[...],
            gain_k,
            turned_back(grads[:, :KEY].astype(bf16).astype(f32)),
        )
        grad_pairs = jnp.concatenate([grad.astype(bf16), grads[:, KEY:].astype(bf16)], axis=1)
        gain_k_row = dot_nt(
            jnp.broadcast_to(gain_k_terms, (8, KEY)).astype(bf16), short_rows()
        )
        gain_box[pl.ds(EXPERTS + 3, 1)] = gain_k_row[:1]
        grad = grad_attn_in[...] + dot_nt(
            grad_pairs, weight_rest[:, :, pl.ds(0, 2 * KEY)].reshape(width, 2 * KEY)
        )
        values = tokens_ref[...].astype(f32)
        inner, gain_a_terms = norm_back(values, gain_a, grad)
        tokens_grad[...] = (grad_middle[...] + inner).astype(bf16)
        gain_box[pl.ds(EXPERTS, 1)] = gain_a_terms
        rest_terms[:, pl.ds(2 * KEY, SMALL)] = (
            router_terms + jnp.transpose(gain_box[...])
        ).astype(bf16)

        def rest_rows(index, carry):
            at = chunk_256(index)
            rest_terms[at, pl.ds(0, 2 * KEY)] = dot_tn(attn_ref[:, at], grad_pairs).astype(bf16)
            return carry

        lax.fori_loop(0, width // 256, rest_rows, 0)
        next(rest_sum)
        next(rest_sum)
        next(q_sum)
        next(o_gather)
        drained(q_sum)
        next(q_gather)
        next(rest_sum)
        drained(expert_gather)
        next(o_gather)
        next(q_gather)
        next(rest_sum)
        next(o_gather)
        next(q_gather)
        drained(rest_sum)
        next(rest_gather)
        abreast(o_gather, q_gather, rest_gather)

    block = pltpu.VMEM((GROUP, ROWS_OWN, width), bf16)
    scratch = [
        block,
        pltpu.VMEM((GROUP, ROWS_OWN, REST), bf16),
        pltpu.VMEM((width, REST), bf16),
        pltpu.VMEM((ROWS_OWN, PACKED), bf16),
        pltpu.VMEM((chips, ROWS_OWN, width), bf16),
        pltpu.VMEM((chips, ROWS_OWN, QUERY), bf16),
        pltpu.VMEM((chips, ROWS_OWN, REST), bf16),
        pltpu.VMEM((stage_rows(ROWS_OWN), width), bf16),
        pltpu.VMEM((stage_rows(ROWS_OWN), QUERY), bf16),
        pltpu.VMEM((stage_rows(ROWS_OWN), REST), bf16),
        pltpu.VMEM((chips, positions, width), bf16),
        pltpu.VMEM((chips, positions, width), bf16),
        pltpu.VMEM((stage_rows(positions), width), bf16),
        pltpu.VMEM((chips, positions, columns), bf16),
        pltpu.VMEM((chips, positions, columns), bf16),
        pltpu.VMEM((stage_rows(positions), columns), bf16),
        pltpu.VMEM((positions, columns), f32),
        pltpu.VMEM(expert_terms.shape, bf16),
        pltpu.VMEM((stage_rows(expert_rows), width), bf16),
        pltpu.VMEM((expert_rows, width), bf16),
        pltpu.VMEM((2, 4 * positions, length), bf16),
        pltpu.VMEM((2, REPS, positions, LANES), bf16),
        pltpu.VMEM((2, REPS, positions, LANES), bf16),
        pltpu.VMEM((seqs, REPS, positions, 2 * KEY), bf16),
        pltpu.VMEM((seqs, stage_rows(positions), 2 * KEY), bf16),
        pltpu.VMEM((count, 2 * KEY), f32),
        pltpu.VMEM((count, QUERY), bf16),
        pltpu.VMEM((count, QUERY), bf16),
        pltpu.VMEM((count, width), f32),
        pltpu.VMEM((count, width), bf16),
        pltpu.VMEM((count, width), f32),
        pltpu.VMEM((count, SMALL), bf16),
        pltpu.VMEM((SMALL, width), f32),
    ]
    return pl.pallas_call(
        kernel,
        out_shape=[
            jax.ShapeDtypeStruct((count, width), bf16),
            jax.ShapeDtypeStruct((count, width), bf16),
            jax.ShapeDtypeStruct((REPS, ROWS_OWN, PACKED), bf16),
            jax.ShapeDtypeStruct((REPS, expert_rows, width), bf16),
        ],
        in_specs=[IN_VMEM] * 2 + [ANY] + [IN_VMEM] * 3 + [ANY] + [IN_VMEM] * 7 + [ANY] * 4 + [IN_VMEM] * 2,
        out_specs=[IN_VMEM, IN_VMEM, ANY, ANY],
        scratch_shapes=scratch
        + sems(SUM_SEMS) * 8
        + sems(GATHER_SEMS) * 4
        + [
            pltpu.SemaphoreType.DMA((4,)),
            pltpu.SemaphoreType.DMA((2, chips)),
            pltpu.SemaphoreType.DMA((2, 3)),
            pltpu.SemaphoreType.DMA((4,)),
        ],
        compiler_params=params(collective_id),
    )(
        returned, out_first, back_terms, gates, middle, sent, dense, cotangent, tokens, attn_in, query_raw, key_raw,
        query_low, mixed, pairs, soft, out_terms, expert_terms, cosine, sine,
    )


def finish_call(dense_all, expert_all, inner_rows):
    total_rows, width = expert_all.shape
    step = 256
    inner_steps, steps = inner_rows // step, total_rows // step

    def kernel(dense_ref, expert_ref, inner, outer, query, key, value, output, small):
        at = pl.program_id(0)
        rows = expert_ref[...].astype(f32)

        @pl.when(at < inner_steps)
        def _():
            inner[...] = rows

        @pl.when(at >= inner_steps)
        def _():
            outer[...] = rows

        @pl.when(at == 1)
        def _():
            for low, target in ((0, query), (AT_K, key), (AT_V, value), (AT_O, output), (AT_S, small)):
                columns = pl.ds(low, target.shape[1])
                total = dense_ref[0, :, columns].astype(f32)
                for rep in range(1, REPS):
                    total = total + dense_ref[rep, :, columns].astype(f32)
                target[...] = total

    def whole(columns):
        return pl.BlockSpec((ROWS_OWN, columns), lambda i: (0, 0))

    sizes = (QUERY, KEY, KEY, WIDTH, SMALL)
    return pl.pallas_call(
        kernel,
        grid=(steps,),
        out_shape=[
            jax.ShapeDtypeStruct((inner_rows, width), f32),
            jax.ShapeDtypeStruct((total_rows - inner_rows, width), f32),
        ]
        + [jax.ShapeDtypeStruct((ROWS_OWN, size), f32) for size in sizes],
        in_specs=[
            pl.BlockSpec(dense_all.shape, lambda i: (0, 0, 0)),
            pl.BlockSpec((step, width), lambda i: (i, 0)),
        ],
        out_specs=[
            pl.BlockSpec((step, width), lambda i: (jnp.minimum(i, inner_steps - 1), 0)),
            pl.BlockSpec((step, width), lambda i: (jnp.maximum(i - inner_steps, 0), 0)),
        ]
        + [whole(size) for size in sizes],
        compiler_params=pltpu.CompilerParams(vmem_limit_bytes=VMEM_LIMIT),
    )(dense_all, expert_all)


def rotary_tables(positions):
    lane = jnp.arange(LANES, dtype=jnp.int32)
    half = HEAD_DIM // 2
    exponent = (lane % half).astype(f32) * (2.0 / HEAD_DIM)
    frequency = rope_base ** (-exponent)
    angles = positions.astype(f32)[:, None] * frequency[None, :]
    sign = jnp.where(lane % HEAD_DIM < half, -1.0, 1.0).astype(f32)
    return jnp.cos(angles), jnp.sin(angles) * sign[None, :]


def small_columns(router, gain_a, gain_q, gain_f, gain_k):
    rows = router.shape[0]
    lane = jnp.arange(SMALL)[None, :]
    small = jnp.pad(router, ((0, 0), (0, SMALL - EXPERTS)))
    short = jnp.pad(gain_k, (0, rows - gain_k.shape[0]))
    for at, gain in enumerate((gain_a, gain_q, gain_f, short)):
        small = jnp.where(lane == EXPERTS + at, gain[:, None], small)
    return small


def shards(
    tokens,
    cotangent,
    routes,
    picture_starts,
    attn_gain,
    query_weight,
    key_weight,
    value_weight,
    query_gain,
    key_gain,
    output_weight,
    ffn_gain,
    router_weight,
    expert_in,
    expert_down,
):
    seqs, positions, width = tokens.shape
    count = seqs * positions
    query_pos = lax.axis_index("rep") * positions + jnp.arange(positions, dtype=jnp.int32)
    cosine, sine = rotary_tables(query_pos)
    rows = tokens.reshape(count, width)
    grad_rows = cotangent.reshape(count, width)
    (
        dense, grad_all, pairs, soft, rows_first,
        attn_in, query_raw, key_raw, query_low, mixed, middle, sent, gates,
    ) = front_call(
        1, rows, grad_rows, (query_weight, key_weight, value_weight, output_weight),
        small_columns(router_weight, attn_gain, query_gain, ffn_gain, key_gain),
        cosine, sine, routes.reshape(count, routes.shape[2]), picture_starts,
    )
    returned, out_first, back_terms, out_terms, expert_terms = moe_call(
        2, sent, rows_first, grad_all, expert_in[0], expert_down[0]
    )
    block_out, tokens_grad, dense_all, expert_all = back_call(
        3, returned, out_first, back_terms, gates, middle, sent, dense, grad_rows, rows, attn_in,
        query_raw, key_raw, query_low, mixed, pairs, soft, out_terms, expert_terms, cosine, sine,
    )
    inner, outer, query, key, value, output, small = finish_call(
        dense_all, expert_all.reshape(-1, width), expert_in.shape[1]
    )
    return (
        block_out.reshape(tokens.shape),
        tokens_grad.reshape(tokens.shape),
        small[:, EXPERTS],
        query,
        key,
        value,
        small[:, EXPERTS + 1],
        small[: key_gain.shape[0], EXPERTS + 3],
        output,
        small[:, EXPERTS + 2],
        small[:, :EXPERTS],
        inner[None],
        outer[None],
    )


def solution(mesh):
    by_tokens = P("shard", "rep", None)
    rows, line, block = P("shard", None), P("shard"), P("shard", None, None)
    in_specs = (
        by_tokens, by_tokens, by_tokens, rows, line, rows, rows, rows, line, line, rows, line, rows, block, block,
    )
    out_specs = (
        by_tokens, by_tokens, line, rows, rows, rows, line, line, rows, line, rows, block, block,
    )
    return jax.shard_map(shards, mesh=mesh, in_specs=in_specs, out_specs=out_specs, check_vma=False)
```

time: 341 us -> 333 us (0.977)
  other arithmetic: 12.7 us -> 2.39 us
  Pallas kernels: 313 us -> 320 us
  local copies, waits for them, and re-layouts: 13.3 us -> 8.98 us
    pallas_call x1 -> x2, Pallas kernels: 91.3 us -> 77.1 us  [the longest x1 69.6 us: moe_call(): pl.pallas_call(kernel, out_shape=[jax.ShapeDtypeStruct((half, columns), f...]
    pallas_call x1, Pallas kernels: 122 us -> 133 us  [back_call(): pl.pallas_call(kernel, out_shape=[jax.ShapeDtypeStruct((count, width), bf...]
    pallas_call x1, Pallas kernels: 99.6 us -> 110 us  [front_call(): pl.pallas_call(kernel, out_shape=[jax.ShapeDtypeStruct((GROUP, ROWS_OWN,...]
    broadcast_in_dim x2 -> x0, other arithmetic: 5.27 us -> none  [the longest x1 2.79 us: shards(): expert_down_grad = expert_all[inner_rows:].astype(f32)[None]]
    reduce_sum x4 -> x0, other arithmetic: 5.04 us -> none  [the longest x1 2.45 us: shards(): dense_sum = jnp.sum(dense_all.astype(f32), axis=0)]
where the time goes in v5:
time: 333 us; the launch traced here: 332 us
  Pallas kernels  320 us (96%)
  local copies, waits for them, and re-layouts  8.98 us (3%)
    pallas_call x1, Pallas kernels, back_call(): pl.pallas_call(kernel, out_shape=[jax.ShapeDtypeStruct((count, width), bf...  133 us
    pallas_call x1, Pallas kernels, front_call(): pl.pallas_call(kernel, out_shape=[jax.ShapeDtypeStruct((GROUP, ROWS_OWN,...  110 us
    pallas_call x1, Pallas kernels, moe_call(): pl.pallas_call(kernel, out_shape=[jax.ShapeDtypeStruct((half, columns), f...  69.6 us
    pallas_call x1, Pallas kernels, finish_call(): pl.pallas_call(kernel, grid=(steps,), out_shape=[jax.ShapeDtypeStruct((in...  7.57 us

profile of v5, /device:TPU:0, one launch (start us, length us, event | category | flops | bytes accessed | tf_op | source)
XLA Modules:
  0.0 332.3 jit_solution(12693254247374339915)
XLA Ops:
  0.7 0.7 pad.8
  1.3 0.8 copy.31
  2.1 1.4 select_select_fusion.small_ref
  3.5 1.0 fusion
  4.5 1.5 copy.32
  6.0 110.0 %shard_map.246 = (bf16[16,64,3200]{2,1,0:T(8,128)(2,1)}, bf16[16,256,1024]{2,1,0:T(8,128)(2,1)}, bf16[2,8,128,1024]{3,2,1,0:T(8,128)(2,1)}, bf16[2,4,512,1024]{3...) custom-call(s32[2,2]{1,0:T(2,128)} %starts_ref.1, ...), custom_call_target="tpu_custom_call" | custom-call | tf_op jit(solution)/shard_map/pallas_call | solution.py:899
  116.0 69.6 %shard_map.247 = (f32[128,1152]{1,0:T(8,128)}, f32[128,1024]{1,0:T(8,128)}, bf16[16,128,1152]{2,1,0:T(8,128)(2,1)}, bf16[16,128,1024]{2,1,0:T(8,128)(2,1)}, bf16[1536,1024]{1,0:T(8,128)(2,1)}) custom-call(bf16[256,1152]{1,0:T(8,128)(2,1)} %get-tuple-element.42.sent_ref, bf16[16,128,1152]{2,1,0:T(8,128)(2,1)} %get-tuple-element.43.first_ref, ...), custom_call_target="tpu_custom_call" | custom-call | tf_op jit(solution)/shard_map/pallas_call | solution.py:557
  185.5 133.1 %shard_map.248 = (bf16[256,1024]{1,0:T(8,128)(2,1)}, bf16[256,1024]{1,0:T(8,128)(2,1)}, bf16[8,64,3200]{2,1,0:T(8,128)(2,1)}, bf16[8,192,1024]{2,1,0:T(8,128)(2,1)}) custom-call(f32[128,1152]{1,0:T(8,128)} %get-tuple-element.45.returned_ref, f32[128,1024]{1,0:T(8,128)} %get-tuple-element.46.out_first_ref, bf16[16,128,1152]{2,1,0:T(8,128)(2,1)} %get-tuple-element.47.back_ref, ...), custom_call_target="tpu_custom_call" | custom-call | tf_op jit(solution)/shard_map/pallas_call | solution.py:1350
  318.6 0.0 copy-start.1
  318.6 0.0 copy-start
  318.6 7.6 %shard_map.249 = (f32[1024,1024]{1,0:T(8,128)}, f32[512,1024]{1,0:T(8,128)}, f32[64,1024]{1,0:T(8,128)}, f32[64,512]{1,0:T(8,128)}, f32[64,512]{1,0:T(8,128)}, /*index=5*/f32[64,1024]{1,0:T(8,128)}, f32[64,128]{1,0:T(8,128)}) custom-call(bf16[8,64,3200]{2,1,0:T(8,128)(2,1)} %get-tuple-element.62.dense_ref, bf16[1536,1024]{1,0:T(8,128)(2,1)} %bitcast.11), custom_call_target="tpu_custom_call" | custom-call | tf_op jit(solution)/shard_map/pallas_call | solution.py:1406
  326.2 1.4 slice_reduce_fusion.3
  327.6 1.6 slice_reduce_fusion
  329.2 1.4 copy.33
  330.7 0.0 copy-done.1
  330.7 0.8 copy.36
  331.5 0.0 copy-done
  331.5 0.8 copy.37
  (4 shorter events, 0.0 us)
Async XLA Ops:
  318.6 12.1 %copy-start.1 = (bf16[256,1024]{1,0:T(8,128)(2,1)S(1)}, bf16[256,1024]{1,0:T(8,128)(2,1)}, u32[]{:S(2)}) copy-start(bf16[256,1024]{1,0:T(8,128)(2,1)} %get-tuple-element.60) | copy-start | bytes 1572868
  318.6 12.8 %copy-start = (bf16[256,1024]{1,0:T(8,128)(2,1)S(1)}, bf16[256,1024]{1,0:T(8,128)(2,1)}, u32[]{:S(2)}) copy-start(bf16[256,1024]{1,0:T(8,128)(2,1)} %get-tuple-element.61) | copy-start | bytes 1572868

commit v6 on v5

--- a/solution.py
+++ b/solution.py
@@ -47,6 +47,7 @@
             return lax.rem(v + RING - 1, RING)
 
         self.twin = (shard_of(y_hi, ring_z, 1 - core), rep)
+        self.others = [lax.rem(rep + step, REPS) for step in range(REPS)]
         self.tokens = Axes(
             y_hi,
             ring_z,
@@ -193,6 +194,49 @@
 
 
 SUM_SEMS = 20
+TOTAL_SEMS = 24
+
+
+def total_parts(place, line, own, got, total, target, local_sem, tail=None):
+    rep = place.rep
+    steps = range(1, REPS)
+    peers = {step: (place.shard, place.others[step]) for step in steps}
+    before = {step: place.others[REPS - step] for step in steps}
+
+    def added(mine, received):
+        value = mine[...].astype(f32)
+        for step in steps:
+            value = value + received[before[step]].astype(f32)
+        return value.astype(bf16)
+
+    def kept(index, source, place_of):
+        return pltpu.make_async_copy(source, place_of, local_sem.at[index])
+
+    for step in steps:
+        line.send(
+            step, lambda p=place.others[step]: own(p), lambda: got.at[rep], peers[step]
+        )
+        if tail is not None:
+            line.send(16 + step, lambda: tail[0], lambda: tail[1].at[rep], peers[step])
+    yield
+    for step in steps:
+        line.take(step, lambda b=before[step]: got.at[b], peers[step])
+    total[...] = added(own(rep), got)
+    kept(0, total, target(rep)).start()
+    for step in steps:
+        line.send(8 + step, lambda: total, lambda: target(rep), peers[step])
+    if tail is not None:
+        for step in steps:
+            line.take(16 + step, lambda b=before[step]: tail[1].at[b], peers[step])
+        tail[2][...] = added(tail[0], tail[1])
+        kept(1, tail[2], tail[3]).start()
+    yield
+    for step in steps:
+        line.take(8 + step, lambda b=before[step]: target(b), peers[step])
+    kept(0, total, target(rep)).wait()
+    if tail is not None:
+        kept(1, tail[2], tail[3]).wait()
+    line.finish()
 
 
 def add_rows(target, source, rows):
@@ -274,6 +318,7 @@
     send("Y2", pair_front, half, across)
     yield
     hand(4, 5, 6, 7)
+    yield
     add("M0", pair_back, 0, behind)
     send("M2", pair_back, 0, behind)
     add("P0", pair_front, quarter, ahead)
@@ -352,13 +397,13 @@
     half = count // 2
     chips = GROUP // 2
     wide = 4
+    rounds = GROUP // wide
 
     def kernel(
         sent_ref, first_ref, grad_ref, inner_ref, outer_ref,
-        returned, out_sum, back_terms, out_terms, terms,
-        rows_in, grads, hidden, back_gu, back, back_staged, back_stage, out, out_staged, out_stage,
-        back_box, out_box, term_box,
-        gs, gr, bs, br, os, orr, own_sem, load_sem, box_sem, term_sem,
+        returned, out_terms, terms,
+        rows_in, grads, hidden, back_gu, back, back_staged, back_stage, out_box, term_box,
+        gs, gr, bs0, br0, bs1, br1, own_sem, load_sem, box_sem, term_sem,
     ):
         place = Place()
         axes, core, shard = place.tokens, place.core, place.shard
@@ -376,17 +421,16 @@
             half, own_sem, place.twin, twin_later=True,
         )
 
-        def sum_of(terms_ref, staged, stage, result, send_sem, recv_sem):
+        def sum_of(chunk, send_sem, recv_sem):
             return sum_parts(
                 axes, Line(send_sem, recv_sem),
-                lambda which, low, n: terms_ref.at[blocks(which), pl.ds(low, n)],
-                stage, half, result,
-                (place.twin, lambda which: terms_ref.at[blocks(which, True)],
-                 lambda which: staged.at[chip_of(which)]),
-            )
-
-        back_sum = sum_of(back, back_staged, back_stage, returned, bs, br)
-        outs_sum = sum_of(out, out_staged, out_stage, out_sum, os, orr)
+                lambda which, low, n: back.at[chunk, blocks(which), pl.ds(low, n)],
+                back_stage.at[chunk], half, returned.at[pl.ds(chunk * half, half)],
+                (place.twin, lambda which: back.at[chunk, blocks(which, True)],
+                 lambda which: back_staged.at[chunk, chip_of(which)]),
+            )
+
+        sums = [sum_of(0, bs0, br0), sum_of(1, bs1, br1)]
 
         def loads(t):
             at = pl.ds(t * wide, wide)
@@ -398,21 +442,22 @@
             ]
 
         second_grads = pltpu.make_async_copy(
-            grad_ref.at[:, pl.ds(half, half)], grads.at[1], load_sem.at[GROUP // wide, 0]
-        )
-
-        def box_copies(chip, slot):
-            at = pl.ds(chip * 2, 2)
-            return [
-                pltpu.make_async_copy(back_box.at[slot], back_terms.at[at], box_sem.at[slot, 0]),
-                pltpu.make_async_copy(out_box.at[slot], out_terms.at[at], box_sem.at[slot, 1]),
-            ]
-
-        def tile(chunk, first, number):
-            rows_count = number * half
-            at = pl.ds(first, number)
-            lanes = lane_of((rows_count, small))
-            is_high, is_rest = lanes == shard, lanes == shard + GROUP
+            grad_ref.at[:, pl.ds(half, half)], grads.at[1], load_sem.at[rounds, 0]
+        )
+
+        def box_copy(chunk, first, slot):
+            return pltpu.make_async_copy(
+                out_box.at[slot],
+                out_terms.at[pl.ds(first, wide), pl.ds(chunk * half, half)],
+                box_sem.at[slot],
+            )
+
+        rows_count = wide * half
+        lanes = lane_of((rows_count, small))
+        is_high, is_rest = lanes == shard, lanes == shard + GROUP
+
+        def tile(chunk, first, slot, wait_first):
+            at = pl.ds(first, wide)
             row_block = rows_in[chunk, at].reshape(rows_count, columns)
             gate = jnp.sum(
                 jnp.where(is_high | is_rest, row_block[:, width:].astype(f32), 0.0),
@@ -424,8 +469,15 @@
             active = gate_part * sigmoid
             product = active * up_part
             hidden_low = product.astype(bf16)
-            hidden[chunk, at] = hidden_low.reshape(number, half, hidden_width)
+            hidden[chunk, at] = hidden_low.reshape(wide, half, hidden_width)
             out_rows = (gate * dot(hidden_low, outer_ref[...])).astype(bf16)
+
+            @pl.when(wait_first)
+            def _():
+                box_copy(chunk, first, slot).wait()
+
+            out_box[slot] = out_rows.reshape(wide, half, width)
+            box_copy(chunk, first, slot).start()
             grad = grads[chunk, at].reshape(rows_count, width)
             grad_hidden = dot_nt(grad, outer_ref[...])
             grad_gate = jnp.sum(grad_hidden * product, axis=1, keepdims=True)
@@ -437,18 +489,15 @@
                 ],
                 axis=1,
             ).astype(bf16)
-            back_gu[chunk, at] = grad_gate_up.reshape(number, half, 2 * hidden_width)
-            grads[chunk, at] = (gate * grad.astype(f32)).astype(bf16).reshape(number, half, width)
+            back_gu[chunk, at] = grad_gate_up.reshape(wide, half, 2 * hidden_width)
+            grads[chunk, at] = (gate * grad.astype(f32)).astype(bf16).reshape(wide, half, width)
             grad_rows = dot_nt(grad_gate_up, inner_ref[...]).astype(bf16)
+            back[chunk, at, :, pl.ds(0, width)] = grad_rows.reshape(wide, half, width)
             high = grad_gate.astype(bf16).astype(f32)
-            tail = jnp.where(is_high, high, jnp.where(is_rest, grad_gate - high, 0.0)).astype(bf16)
-            return (
-                out_rows.reshape(number, half, width),
-                grad_rows.reshape(number, half, width),
-                tail.reshape(number, half, small),
-            )
-
-        for t in range(GROUP // wide):
+            tail = jnp.where(is_high, high, jnp.where(is_rest, grad_gate - high, 0.0))
+            back[chunk, at, :, pl.ds(width, small)] = tail.astype(bf16).reshape(wide, half, small)
+
+        for t in range(rounds):
             for load in loads(t):
                 load.start()
         second_grads.start()
@@ -459,47 +508,45 @@
             hooks(t, ((2, lambda: next(gather)),))
             for load in loads(t):
                 load.wait()
-            at = pl.ds(t * wide, wide)
-            out_rows, grad_rows, tail = tile(0, t * wide, wide)
-            out[at] = out_rows
-            back[at, :, pl.ds(0, width)] = grad_rows
-            back[at, :, pl.ds(width, small)] = tail
+            tile(0, t * wide, lax.rem(t, 2), t >= 2)
             return carry
 
-        lax.fori_loop(0, GROUP // wide, first_tiles, 0)
-        next(back_sum)
+        lax.fori_loop(0, rounds, first_tiles, 0)
+        next(sums[0])
+        next(gather)
         second_grads.wait()
-        chips1 = [chip_of(which) for which in gather_order(axes)]
+        near, beyond = lax.div(axes.spot, 2), 1 - lax.div(axes.spot, 2)
+        chips_per_round = wide // 2
+        firsts = [
+            (side * RING + part * chips_per_round) * 2
+            for side, part in (
+                (axes.side, beyond), (1 - axes.side, near), (1 - axes.side, beyond), (axes.side, near),
+            )
+        ]
+        arrivals = gather_order(axes)
+
+        def arrived(*numbers):
+            for number in numbers:
+                gather_line.take(
+                    12 + number, lambda: rows_in.at[1, blocks(arrivals[number], True)], place.twin
+                )
 
         def second_tiles(t, carry):
             hooks(
                 t,
                 (
-                    (1, lambda: next(back_sum)),
-                    (2, lambda: next(gather)),
-                    (3, lambda: next(outs_sum)),
-                    (4, lambda: next(back_sum)),
-                    (5, lambda: next(outs_sum)),
-                    (7, lambda: next(gather)),
+                    (0, lambda: arrived(0, 1, 2, 4)),
+                    (1, lambda: (next(sums[0]), next(sums[0]), arrived(3, 5, 6))[2]),
+                    (2, lambda: (next(gather), arrived(7))[1]),
+                    (3, lambda: (next(sums[1]), next(sums[0]))[0]),
                 ),
             )
-            chip, slot = pick(t, chips1), lax.rem(t, 2)
-            gather_line.take(12 + t, lambda: rows_in.at[1, chip * 2 + 1 - core], place.twin)
-            out_rows, grad_rows, tail = tile(1, chip * 2, 2)
-
-            @pl.when(t >= 2)
-            def _():
-                for copy in box_copies(chip, slot):
-                    copy.wait()
-
-            out_box[slot] = out_rows
-            back_box[slot, :, :, pl.ds(0, width)] = grad_rows
-            back_box[slot, :, :, pl.ds(width, small)] = tail
-            for copy in box_copies(chip, slot):
-                copy.start()
+            tile(1, pick(t, firsts), lax.rem(t, 2), t >= 0)
             return carry
 
-        lax.fori_loop(0, chips, second_tiles, 0)
+        lax.fori_loop(0, rounds, second_tiles, 0)
+        next(sums[1])
+        next(sums[1])
 
         def term_copy(low, slot):
             return pltpu.make_async_copy(
@@ -521,7 +568,6 @@
         downs = hidden_width // 256
 
         def down_terms(index, carry):
-            hooks(index, ((0, lambda: next(back_sum)), (1, lambda: next(outs_sum))))
             at = chunk_256(index)
             value = dot_tn(hidden[:, :, :, at].reshape(every, 256), grads[...].reshape(every, width))
             keep(index, pl.multiple_of(width + index * 256, 256), value)
@@ -533,8 +579,8 @@
             hooks(
                 index,
                 (
-                    (1, lambda: drained(back_sum)),
-                    (2, lambda: next(outs_sum)),
+                    (0, lambda: next(sums[0])),
+                    (1, lambda: next(sums[1])),
                 ),
             )
             at = chunk_256(index)
@@ -546,46 +592,40 @@
             return carry
 
         lax.fori_loop(0, width // 256, inner_terms, 0)
-        drained(outs_sum)
+        drained(sums[0])
+        drained(sums[1])
         drained(gather)
         for slot in range(2):
-            for copy in box_copies(0, slot):
-                copy.wait()
+            box_copy(1, 0, slot).wait()
             term_copy(0, slot).wait()
 
     term_rows = width + hidden_width
     return pl.pallas_call(
         kernel,
         out_shape=[
-            jax.ShapeDtypeStruct((half, columns), f32),
-            jax.ShapeDtypeStruct((half, width), f32),
-            jax.ShapeDtypeStruct((GROUP, half, columns), bf16),
-            jax.ShapeDtypeStruct((GROUP, half, width), bf16),
+            jax.ShapeDtypeStruct((count, columns), f32),
+            jax.ShapeDtypeStruct((GROUP, count, width), bf16),
             jax.ShapeDtypeStruct((term_rows, width), bf16),
         ],
         in_specs=[ANY, ANY, ANY, IN_VMEM, IN_VMEM],
-        out_specs=[IN_VMEM, IN_VMEM, ANY, ANY, ANY],
+        out_specs=[IN_VMEM, ANY, ANY],
         scratch_shapes=[
             pltpu.VMEM((2, GROUP, half, columns), bf16),
             pltpu.VMEM((2, GROUP, half, width), bf16),
             pltpu.VMEM((2, GROUP, half, hidden_width), bf16),
             pltpu.VMEM((2, GROUP, half, 2 * hidden_width), bf16),
-            pltpu.VMEM((GROUP, half, columns), bf16),
-            pltpu.VMEM((chips, half, columns), bf16),
-            pltpu.VMEM((stage_rows(half), columns), bf16),
-            pltpu.VMEM((GROUP, half, width), bf16),
-            pltpu.VMEM((chips, half, width), bf16),
-            pltpu.VMEM((stage_rows(half), width), bf16),
-            pltpu.VMEM((2, 2, half, columns), bf16),
-            pltpu.VMEM((2, 2, half, width), bf16),
+            pltpu.VMEM((2, GROUP, half, columns), bf16),
+            pltpu.VMEM((2, chips, half, columns), bf16),
+            pltpu.VMEM((2, stage_rows(half), columns), bf16),
+            pltpu.VMEM((2, wide, half, width), bf16),
             pltpu.VMEM((2, 256, width), bf16),
         ]
         + sems(GATHER_SEMS)
         + sems(SUM_SEMS) * 2
         + [
             pltpu.SemaphoreType.DMA,
-            pltpu.SemaphoreType.DMA((GROUP // wide + 1, 2)),
-            pltpu.SemaphoreType.DMA((2, 2)),
+            pltpu.SemaphoreType.DMA((rounds + 1, 2)),
+            pltpu.SemaphoreType.DMA((2,)),
             pltpu.SemaphoreType.DMA((2,)),
         ],
         compiler_params=params(collective_id),
@@ -696,7 +736,7 @@
         dense_out, grad_all, pairs_out, soft_out, rows_first,
         attn_in, query_raw, key_raw, query_low, mixed, middle, sent, gates_out,
         packed, dense, pairs, pair_own, soft_box, bias_box,
-        ws0, wr0, ws1, wr1, ws2, wr2, gs, gr, ks0, kr0, ks1, kr1, rs, rr, own_sem, out_sem, soft_sem, pack_sem,
+        ws0, wr0, ws1, wr1, ws2, wr2, gs0, gr0, gs1, gr1, ks0, kr0, ks1, kr1, rs, rr, own_sem, out_sem, soft_sem, pack_sem,
     ):
         place = Place()
         core = place.core
@@ -748,12 +788,22 @@
         rest_gather = weight_gather(0, AT_K, REST, ws0, wr0)
         query_gather = weight_gather(1, 0, QUERY, ws1, wr1)
         output_gather = weight_gather(2, AT_O, WIDTH, ws2, wr2)
-        grads = gather_parts(
-            place.tokens, Line(gs, gr), grad_ref, rows_of(grad_all), count, own_sem.at[5], place.twin
-        )
+        def grad_gather(seq, send_sem, recv_sem):
+            base = seq * positions
+
+            def block(which, row, n, other=False):
+                at = (which[0] * RING + which[1]) * 2 + ((1 - core) if other else core)
+                return grad_all.at[at, pl.ds(base + row, n)]
+
+            return gather_parts(
+                place.tokens, Line(send_sem, recv_sem), grad_ref.at[pl.ds(base, positions)], block,
+                positions, own_sem.at[5 + seq], place.twin,
+            )
+
+        grads = [grad_gather(0, gs0, gr0), grad_gather(1, gs1, gr1)]
         first_rows = gather_parts(
             place.tokens, Line(rs, rr), sent.at[pl.ds(0, positions)], rows_of(rows_first), positions,
-            own_sem.at[6], place.twin,
+            own_sem.at[7], place.twin,
         )
         pair_gathers = [pair_gather(0, ks0, kr0), pair_gather(1, ks1, kr1)]
 
@@ -801,7 +851,7 @@
         next(pair_gathers[0])
         drained(query_gather)
         next(output_gather)
-        next(grads)
+        next(grads[0])
         raw = dot(rows, weights(0, QUERY))
         query_raw[...] = raw
         scaled = raw * root_mean(raw) * gain_q
@@ -813,10 +863,13 @@
         drained(output_gather)
         dense_copy = pltpu.make_async_copy(dense, dense_out, out_sem.at[0])
         dense_copy.start()
+        next(grads[0])
+        next(grads[1])
         next(pair_gathers[0])
         next(pair_gathers[1])
+        next(grads[0])
         drained(pair_gathers[0])
-        next(grads)
+        next(grads[1])
 
         def attend(seq, index, slot, wait_first):
             rows_at = pl.ds(seq * positions, positions)
@@ -863,7 +916,14 @@
             sent[at, pl.ds(width, SMALL)] = tail.astype(bf16)
 
         def first_heads(index, carry):
-            hooks(index, ((2, lambda: next(pair_gathers[1])),))
+            hooks(
+                index,
+                (
+                    (1, lambda: next(grads[0])),
+                    (2, lambda: next(pair_gathers[1])),
+                    (3, lambda: next(grads[1])),
+                ),
+            )
             attend(0, index, lax.rem(index, 2), index >= 2)
             return carry
 
@@ -873,13 +933,12 @@
         drained(pair_gathers[1])
         pairs_copy = pltpu.make_async_copy(pairs, pairs_out, out_sem.at[1])
         pairs_copy.start()
-        next(grads)
 
         def second_heads(index, carry):
             hooks(
                 index,
                 (
-                    (2, lambda: next(grads)),
+                    (1, lambda: next(grads[1])),
                     (3, lambda: next(first_rows)),
                 ),
             )
@@ -889,7 +948,8 @@
         lax.fori_loop(0, HEAD_PAIRS, second_heads, 0)
         features(1)
         next(first_rows)
-        drained(grads)
+        drained(grads[0])
+        drained(grads[1])
         drained(first_rows)
         dense_copy.wait()
         pairs_copy.wait()
@@ -923,9 +983,9 @@
             pltpu.VMEM((2, 4 * positions, length), bf16),
             pltpu.VMEM((seqs, positions, length), f32),
         ]
-        + sems(GATHER_SEMS) * 7
+        + sems(GATHER_SEMS) * 8
         + [
-            pltpu.SemaphoreType.DMA((7,)),
+            pltpu.SemaphoreType.DMA((8,)),
             pltpu.SemaphoreType.DMA((2,)),
             pltpu.SemaphoreType.DMA((2,)),
             pltpu.SemaphoreType.DMA((5,)),
@@ -943,31 +1003,30 @@
 
 
 def back_call(
-    collective_id, returned, out_first, back_terms, gates, middle, sent, dense, cotangent, tokens, attn_in, query_raw, key_raw,
+    collective_id, returned, gates, middle, sent, dense, cotangent, tokens, attn_in, query_raw, key_raw,
     query_low, mixed, pairs, soft, out_terms, expert_terms, cosine, sine,
 ):
     count, width = tokens.shape
     seqs, _, positions, _ = pairs.shape
-    columns = back_terms.shape[2]
     length = REPS * positions
     expert_rows = expert_terms.shape[0] // REPS
     score_scale = HEAD_DIM ** (-0.5)
     chips = GROUP // 2
 
     def kernel(
-        returned_ref, out_first_ref, back_ref, gates_ref, middle_ref, sent_ref, dense_ref, grad_ref, tokens_ref, attn_ref,
+        returned_ref, gates_ref, middle_ref, sent_ref, dense_ref, grad_ref, tokens_ref, attn_ref,
         query_raw_ref, key_raw_ref, query_ref, mixed_ref, pairs_ref, soft_ref, out_ref, expert_ref,
         cos_ref, sin_ref,
-        block_out, tokens_grad, dense_all, expert_all,
+        block_out, tokens_grad, dense_out, expert_all,
         weight_box, weight_rest, rest_terms, dense_own,
         o_staged, q_staged, rest_staged, o_stage, q_stage, rest_stage,
-        out_held, out_staged, out_stage, back_held, back_staged, back_stage, returned_second,
-        expert_held, expert_stage, expert_own,
+        out_held, out_staged, out_stage, expert_held, expert_stage, expert_own,
         soft_box, key_box, value_box, pair_terms, pair_stage, pair_grads,
-        grad_mixed, grad_query, grad_middle, grad_attn, grad_attn_in, logit_box, gain_box,
-        out_s, out_r, back_s, back_r, exp_s, exp_r, kv0_s, kv0_r, kv1_s, kv1_r, o_s, o_r, q_s, q_r, rest_s, rest_r,
+        grad_mixed, grad_query, grad_middle, grad_attn, grad_attn_in, gain_box,
+        o_got, q_got, rest_got, small_got, totals,
+        out_s, out_r, exp_s, exp_r, kv0_s, kv0_r, kv1_s, kv1_r, o_s, o_r, q_s, q_r, rest_s, rest_r,
         ge_s, ge_r, go_s, go_r, gq_s, gq_r, grest_s, grest_r,
-        load_sem, held_sem, box_sem, own_sem,
+        load_sem, held_sem, box_sem, own_sem, total_sem,
     ):
         place = Place()
         core = place.core
@@ -981,24 +1040,16 @@
             return chip_of(which) * 2 + ((1 - core) if other else core)
 
         def out_store(low, step, value):
-            at = pl.ds(positions + low, step)
+            at = pl.ds(low, step)
             block_out[at] = (middle_ref[at] + value).astype(bf16)
 
-        def second_sum(source, held, staged, stage, send_sem, recv_sem, result, store=None):
-            return sum_parts(
-                token_axes, Line(send_sem, recv_sem),
-                lambda which, low, n: held.at[chip_of(which), pl.ds(low, n)],
-                stage, positions, result,
-                (place.twin, lambda which: source.at[blocks(which, True)],
-                 lambda which: staged.at[chip_of(which)]),
-                store=store,
-            )
-
-        out_sum = second_sum(
-            out_ref, out_held, out_staged, out_stage, out_s, out_r, None, store=out_store
-        )
-        back_sum = second_sum(
-            back_ref, back_held, back_staged, back_stage, back_s, back_r, returned_second
+        out_sum = sum_parts(
+            token_axes, Line(out_s, out_r),
+            lambda which, low, n: out_held.at[chip_of(which), pl.ds(low, n)],
+            out_stage, count, None,
+            (place.twin, lambda which: out_ref.at[blocks(which, True)],
+             lambda which: out_staged.at[chip_of(which)]),
+            store=out_store,
         )
         expert_sum = sum_parts(
             copy_axes, Line(exp_s, exp_r),
@@ -1035,22 +1086,29 @@
         q_sum = dense_sum(rows_of_block, q_terms, q_staged, q_stage, 0, QUERY, q_s, q_r)
         rest_sum = dense_sum(rows_of_block, rest_terms, rest_staged, rest_stage, AT_K, REST, rest_s, rest_r)
 
-        def dense_gather(low, size, send_sem, recv_sem, index):
-            return gather_parts(
-                copy_axes, Line(send_sem, recv_sem), dense_own.at[:, pl.ds(low, size)],
-                lambda which, row, n, other=False: dense_all.at[
-                    chip_of(which), pl.ds(row, n), pl.ds(low, size)
-                ],
-                ROWS_OWN, own_sem.at[index],
-            )
-
-        o_gather = dense_gather(AT_O, width, go_s, go_r, 0)
-        q_gather = dense_gather(0, QUERY, gq_s, gq_r, 1)
-        rest_gather = dense_gather(AT_K, REST, grest_s, grest_r, 2)
+        def dense_total(index, low, got, send_sem, recv_sem, tail=None):
+            def own(rep):
+                return dense_own.at[:, chunk_at(rep, low)]
+
+            def target(rep):
+                return dense_out.at[:, chunk_at(rep, low)]
+
+            return total_parts(
+                place, Line(send_sem, recv_sem), own, got, totals.at[index], target,
+                total_sem.at[index], tail,
+            )
+
+        o_total = dense_total(0, AT_O, o_got, go_s, go_r)
+        q_total = dense_total(1, 0, q_got, gq_s, gq_r)
+        small_at = pl.ds(AT_S, SMALL)
+        rest_total = dense_total(
+            2, AT_K, rest_got, grest_s, grest_r,
+            (dense_own.at[:, small_at], small_got, totals.at[3], dense_out.at[:, small_at]),
+        )
         expert_gather = gather_parts(
             copy_axes, Line(ge_s, ge_r), expert_own,
             lambda which, row, n, other=False: expert_all.at[chip_of(which), pl.ds(row, n)],
-            expert_rows, own_sem.at[3],
+            expert_rows, own_sem,
         )
 
         def weight_load(low, index):
@@ -1063,13 +1121,10 @@
         )
         expert_load = pltpu.make_async_copy(expert_ref, expert_held, load_sem.at[2])
         held_loads = [
-            [
-                pltpu.make_async_copy(
-                    source.at[2 * chip + core], held.at[chip], held_sem.at[kind, chip]
-                )
-                for chip in range(chips)
-            ]
-            for kind, (source, held) in enumerate(((back_ref, back_held), (out_ref, out_held)))
+            pltpu.make_async_copy(
+                out_ref.at[2 * chip + core], out_held.at[chip], held_sem.at[chip]
+            )
+            for chip in range(chips)
         ]
 
         def box_loads(number, slot):
@@ -1088,54 +1143,42 @@
                 ),
             ]
 
-        for load in held_loads[0]:
-            load.start()
         expert_load.start()
         rest_load.start()
         weight_load(AT_O, 0).start()
-        for load in held_loads[1]:
+        for load in held_loads + box_loads(0, 0):
             load.start()
-        for load in box_loads(0, 0):
-            load.start()
-        greet(token_axes.neighbours() + copy_axes.neighbours() + [place.twin])
-        next(back_sum)
+        greet(
+            token_axes.neighbours()
+            + [place.twin]
+            + [(place.shard, other) for other in place.others[1:]]
+        )
+        next(out_sum)
         expert_load.wait()
         next(expert_sum)
         next(expert_sum)
-        for load in held_loads[0]:
-            load.wait()
-        next(back_sum)
+        next(expert_sum)
         rest_load.wait()
 
         small = weight_rest[:, :, pl.ds(2 * KEY, SMALL)].reshape(width, SMALL)
         gain_a, gain_q, gain_f, gain_k = gain_rows(small)
+        gates = gates_ref[...]
+        tail = returned_ref[:, pl.ds(width, SMALL)]
+        grad_gates = tail + pltpu.roll(tail, SMALL - EXPERTS, 1)
+        grad_logits = gates * (grad_gates - jnp.sum(gates * grad_gates, axis=1, keepdims=True))
+        grad_logits = grad_logits.astype(bf16)
+        grad_ffn = returned_ref[:, pl.ds(0, width)] + dot_nt(grad_logits, small)
+        inner, gain_f_terms = norm_back(middle_ref[...], gain_f, grad_ffn)
+        inner = grad_ref[...].astype(f32) + inner
+        grad_middle[...] = inner
+        grad_attn[...] = inner.astype(bf16)
         gain_box[...] = jnp.zeros_like(gain_box)
-
-        def features_back(seq, source):
-            at = pl.ds(seq * positions, positions)
-            gates = gates_ref[at]
-            tail = source[:, pl.ds(width, SMALL)]
-            grad_gates = tail + pltpu.roll(tail, SMALL - EXPERTS, 1)
-            grad_logits = gates * (
-                grad_gates - jnp.sum(gates * grad_gates, axis=1, keepdims=True)
-            )
-            grad_logits = grad_logits.astype(bf16)
-            logit_box[at] = grad_logits
-            grad_ffn = source[:, pl.ds(0, width)] + dot_nt(grad_logits, small)
-            inner, gain_terms = norm_back(middle_ref[at], gain_f, grad_ffn)
-            inner = grad_ref[at].astype(f32) + inner
-            grad_middle[at] = inner
-            low = inner.astype(bf16)
-            grad_attn[at] = low
-            gain_at = pl.ds(EXPERTS + 2, 1)
-            gain_box[gain_at] = gain_box[gain_at] + gain_terms
-            weight_o = weight_box[...].reshape(QUERY, width)
-            grad_mixed[at] = dot_nt(low, weight_o).astype(bf16)
-
+        gain_box[pl.ds(EXPERTS + 2, 1)] = gain_f_terms
         weight_load(AT_O, 0).wait()
-        features_back(0, returned_ref)
-        first_at = pl.ds(0, positions)
-        block_out[first_at] = (middle_ref[first_at] + out_first_ref[...]).astype(bf16)
+        grad_mixed[...] = dot_nt(
+            grad_attn[...], weight_box[...].reshape(QUERY, width)
+        ).astype(bf16)
+        weight_load(0, 3).start()
 
         def attend_back(seq, index):
             number = seq * HEAD_PAIRS + index
@@ -1178,54 +1221,33 @@
             grad_query[rows_at, first] = chunk_a.astype(bf16)
             grad_query[rows_at, second] = chunk_b.astype(bf16)
 
+        def out_ready():
+            for load in held_loads:
+                load.wait()
+            next(out_sum)
+            next(out_sum)
+
         def first_heads(index, carry):
-            hooks(index, ((2, lambda: next(back_sum)), (3, lambda: next(expert_sum))))
+            hooks(index, ((2, lambda: next(expert_sum)), (3, out_ready)))
             attend_back(0, index)
             return carry
 
         lax.fori_loop(0, HEAD_PAIRS, first_heads, 0)
         next(pair_sums[0])
         next(pair_sums[0])
-        next(back_sum)
-        for load in held_loads[1]:
-            load.wait()
-        next(out_sum)
-        next(expert_sum)
-        next(out_sum)
-        drained(expert_sum)
         next(pair_sums[0])
-        drained(back_sum)
-        features_back(1, returned_second)
-        weight_load(0, 3).start()
 
         def second_heads(index, carry):
-            hooks(
-                index,
-                (
-                    (0, lambda: next(pair_sums[0])),
-                    (1, lambda: next(out_sum)),
-                    (2, lambda: (drained(pair_sums[0]), next(expert_gather))[0]),
-                    (3, lambda: next(out_sum)),
-                ),
-            )
+            hooks(index, ((3, lambda: next(out_sum)),))
             attend_back(1, index)
             return carry
 
         lax.fori_loop(0, HEAD_PAIRS, second_heads, 0)
         next(pair_sums[1])
         next(pair_sums[1])
-        drained(out_sum)
-        next(expert_gather)
-
-        def o_rows(index, carry):
-            at = chunk_256(index)
-            value = dot_tn(mixed_ref[:, at], grad_attn[...]).astype(bf16)
-            pair_terms[0, pl.ds(2 * index, 2)] = value.reshape(2, positions, width)
-            return carry
-
-        lax.fori_loop(0, QUERY // 256, o_rows, 0)
-        next(o_sum)
-        next(o_sum)
+        next(pair_sums[1])
+        next(pair_sums[0])
+        router_terms = dot_tn(sent_ref[:, pl.ds(0, width)], grad_logits)
 
         cos2 = jnp.concatenate([cos_ref[...]] * seqs, axis=0)
         sin2 = -jnp.concatenate([sin_ref[...]] * seqs, axis=0)
@@ -1247,6 +1269,24 @@
         weight_load(0, 3).wait()
         grad_attn_in[...] = dot_nt(grad_query_low, weight_box[...].reshape(width, QUERY))
 
+        next(pair_sums[1])
+        next(expert_sum)
+        next(out_sum)
+        next(pair_sums[0])
+        drained(pair_sums[0])
+        next(pair_sums[1])
+
+        def o_rows(index, carry):
+            at = chunk_256(index)
+            value = dot_tn(mixed_ref[:, at], grad_attn[...]).astype(bf16)
+            pair_terms[0, pl.ds(2 * index, 2)] = value.reshape(2, positions, width)
+            return carry
+
+        lax.fori_loop(0, QUERY // 256, o_rows, 0)
+        next(o_sum)
+        drained(expert_sum)
+        next(expert_gather)
+
         def q_rows(index, carry):
             at = chunk_256(index)
             q_terms[at] = dot_tn(attn_ref[:, at], grad_query_low).astype(bf16)
@@ -1254,17 +1294,13 @@
 
         lax.fori_loop(0, width // 256, q_rows, 0)
         next(q_sum)
-        next(pair_sums[1])
+        next(o_sum)
+        next(o_sum)
+        drained(out_sum)
         next(q_sum)
-        next(expert_gather)
+        next(q_sum)
         next(o_sum)
-        next(pair_sums[1])
-        next(o_sum)
-        next(q_sum)
-        router_terms = dot_tn(sent_ref[:, pl.ds(0, width)], logit_box[...])
-        drained(o_sum)
         drained(pair_sums[1])
-        next(o_gather)
 
         grads = pair_grads[...]
         grad, gain_k_terms = norm_back(
@@ -1296,20 +1332,27 @@
         lax.fori_loop(0, width // 256, rest_rows, 0)
         next(rest_sum)
         next(rest_sum)
+        next(rest_sum)
         next(q_sum)
-        next(o_gather)
+        next(o_sum)
+        next(expert_gather)
+        next(rest_sum)
+        drained(o_sum)
+        next(o_total)
+        next(q_sum)
+        next(expert_gather)
+        next(rest_sum)
+        next(o_total)
         drained(q_sum)
-        next(q_gather)
-        next(rest_sum)
+        next(q_total)
+        drained(rest_sum)
+        next(rest_total)
+        next(q_total)
+        next(rest_total)
+        drained(o_total)
+        drained(q_total)
         drained(expert_gather)
-        next(o_gather)
-        next(q_gather)
-        next(rest_sum)
-        next(o_gather)
-        next(q_gather)
-        drained(rest_sum)
-        next(rest_gather)
-        abreast(o_gather, q_gather, rest_gather)
+        drained(rest_total)
 
     block = pltpu.VMEM((GROUP, ROWS_OWN, width), bf16)
     scratch = [
@@ -1323,13 +1366,9 @@
         pltpu.VMEM((stage_rows(ROWS_OWN), width), bf16),
         pltpu.VMEM((stage_rows(ROWS_OWN), QUERY), bf16),
         pltpu.VMEM((stage_rows(ROWS_OWN), REST), bf16),
-        pltpu.VMEM((chips, positions, width), bf16),
-        pltpu.VMEM((chips, positions, width), bf16),
-        pltpu.VMEM((stage_rows(positions), width), bf16),
-        pltpu.VMEM((chips, positions, columns), bf16),
-        pltpu.VMEM((chips, positions, columns), bf16),
-        pltpu.VMEM((stage_rows(positions), columns), bf16),
-        pltpu.VMEM((positions, columns), f32),
+        pltpu.VMEM((chips, count, width), bf16),
+        pltpu.VMEM((chips, count, width), bf16),
+        pltpu.VMEM((stage_rows(count), width), bf16),
         pltpu.VMEM(expert_terms.shape, bf16),
         pltpu.VMEM((stage_rows(expert_rows), width), bf16),
         pltpu.VMEM((expert_rows, width), bf16),
@@ -1344,36 +1383,39 @@
         pltpu.VMEM((count, width), f32),
         pltpu.VMEM((count, width), bf16),
         pltpu.VMEM((count, width), f32),
-        pltpu.VMEM((count, SMALL), bf16),
         pltpu.VMEM((SMALL, width), f32),
     ]
+    scratch += [pltpu.VMEM((REPS, ROWS_OWN, LANES), bf16)] * 4
+    scratch += [pltpu.VMEM((4, ROWS_OWN, LANES), bf16)]
     return pl.pallas_call(
         kernel,
         out_shape=[
             jax.ShapeDtypeStruct((count, width), bf16),
             jax.ShapeDtypeStruct((count, width), bf16),
-            jax.ShapeDtypeStruct((REPS, ROWS_OWN, PACKED), bf16),
+            jax.ShapeDtypeStruct((ROWS_OWN, PACKED), bf16),
             jax.ShapeDtypeStruct((REPS, expert_rows, width), bf16),
         ],
-        in_specs=[IN_VMEM] * 2 + [ANY] + [IN_VMEM] * 3 + [ANY] + [IN_VMEM] * 7 + [ANY] * 4 + [IN_VMEM] * 2,
+        in_specs=[IN_VMEM] * 4 + [ANY] + [IN_VMEM] * 7 + [ANY] * 4 + [IN_VMEM] * 2,
         out_specs=[IN_VMEM, IN_VMEM, ANY, ANY],
         scratch_shapes=scratch
-        + sems(SUM_SEMS) * 8
-        + sems(GATHER_SEMS) * 4
+        + sems(SUM_SEMS) * 7
+        + sems(GATHER_SEMS)
+        + sems(TOTAL_SEMS) * 3
         + [
             pltpu.SemaphoreType.DMA((4,)),
-            pltpu.SemaphoreType.DMA((2, chips)),
+            pltpu.SemaphoreType.DMA((chips,)),
             pltpu.SemaphoreType.DMA((2, 3)),
-            pltpu.SemaphoreType.DMA((4,)),
+            pltpu.SemaphoreType.DMA,
+            pltpu.SemaphoreType.DMA((3, 2)),
         ],
         compiler_params=params(collective_id),
     )(
-        returned, out_first, back_terms, gates, middle, sent, dense, cotangent, tokens, attn_in, query_raw, key_raw,
+        returned, gates, middle, sent, dense, cotangent, tokens, attn_in, query_raw, key_raw,
         query_low, mixed, pairs, soft, out_terms, expert_terms, cosine, sine,
     )
 
 
-def finish_call(dense_all, expert_all, inner_rows):
+def finish_call(dense_own, expert_all, inner_rows):
     total_rows, width = expert_all.shape
     step = 256
     inner_steps, steps = inner_rows // step, total_rows // step
@@ -1393,11 +1435,7 @@
         @pl.when(at == 1)
         def _():
             for low, target in ((0, query), (AT_K, key), (AT_V, value), (AT_O, output), (AT_S, small)):
-                columns = pl.ds(low, target.shape[1])
-                total = dense_ref[0, :, columns].astype(f32)
-                for rep in range(1, REPS):
-                    total = total + dense_ref[rep, :, columns].astype(f32)
-                target[...] = total
+                target[...] = dense_ref[:, pl.ds(low, target.shape[1])].astype(f32)
 
     def whole(columns):
         return pl.BlockSpec((ROWS_OWN, columns), lambda i: (0, 0))
@@ -1412,7 +1450,7 @@
         ]
         + [jax.ShapeDtypeStruct((ROWS_OWN, size), f32) for size in sizes],
         in_specs=[
-            pl.BlockSpec(dense_all.shape, lambda i: (0, 0, 0)),
+            pl.BlockSpec(dense_own.shape, lambda i: (0, 0)),
             pl.BlockSpec((step, width), lambda i: (i, 0)),
         ],
         out_specs=[
@@ -1421,7 +1459,7 @@
         ]
         + [whole(size) for size in sizes],
         compiler_params=pltpu.CompilerParams(vmem_limit_bytes=VMEM_LIMIT),
-    )(dense_all, expert_all)
+    )(dense_own, expert_all)
 
 
 def rotary_tables(positions):
@@ -1475,15 +1513,15 @@
         small_columns(router_weight, attn_gain, query_gain, ffn_gain, key_gain),
         cosine, sine, routes.reshape(count, routes.shape[2]), picture_starts,
     )
-    returned, out_first, back_terms, out_terms, expert_terms = moe_call(
+    returned, out_terms, expert_terms = moe_call(
         2, sent, rows_first, grad_all, expert_in[0], expert_down[0]
     )
-    block_out, tokens_grad, dense_all, expert_all = back_call(
-        3, returned, out_first, back_terms, gates, middle, sent, dense, grad_rows, rows, attn_in,
+    block_out, tokens_grad, dense_out, expert_all = back_call(
+        3, returned, gates, middle, sent, dense, grad_rows, rows, attn_in,
         query_raw, key_raw, query_low, mixed, pairs, soft, out_terms, expert_terms, cosine, sine,
     )
     inner, outer, query, key, value, output, small = finish_call(
-        dense_all, expert_all.reshape(-1, width), expert_in.shape[1]
+        dense_out, expert_all.reshape(-1, width), expert_in.shape[1]
     )
     return (
         block_out.reshape(tokens.shape),

time: 333 us -> 291 us (0.87)
  Pallas kernels: 320 us -> 277 us
    pallas_call x1, Pallas kernels: 133 us -> 99.9 us  [back_call(): pl.pallas_call(kernel, out_shape=[jax.ShapeDtypeStruct((count, width), bf...]
    pallas_call x1, Pallas kernels: 110 us -> 94.4 us  [front_call(): pl.pallas_call(kernel, out_shape=[jax.ShapeDtypeStruct((GROUP, ROWS_OWN,...]
    pallas_call x1, Pallas kernels: 69.6 us -> 75.9 us  [moe_call(): pl.pallas_call(kernel, out_shape=[jax.ShapeDtypeStruct((count, columns),...]
where the time goes in v6:
time: 291 us; the launch traced here: 290 us
  Pallas kernels  277 us (95%)
  local copies, waits for them, and re-layouts  10.1 us (3%)
    pallas_call x1, Pallas kernels, back_call(): pl.pallas_call(kernel, out_shape=[jax.ShapeDtypeStruct((count, width), bf...  99.9 us
    pallas_call x1, Pallas kernels, front_call(): pl.pallas_call(kernel, out_shape=[jax.ShapeDtypeStruct((GROUP, ROWS_OWN,...  94.4 us
    pallas_call x1, Pallas kernels, moe_call(): pl.pallas_call(kernel, out_shape=[jax.ShapeDtypeStruct((count, columns),...  75.9 us
    pallas_call x1, Pallas kernels, finish_call(): pl.pallas_call(kernel, grid=(steps,), out_shape=[jax.ShapeDtypeStruct((in...  6.66 us
    unnamed x7, local copies, waits for them, and re-layouts  6.36 us

profile of v6, /device:TPU:0, one launch (start us, length us, event | category | flops | bytes accessed | tf_op | source)
XLA Modules:
  0.0 289.9 jit_solution(8612111159540966420)
XLA Ops:
  0.7 0.7 pad.8
  1.3 0.8 copy.31
  2.1 1.4 select_select_fusion.small_ref
  3.5 1.0 fusion
  4.5 1.5 copy.32
  6.0 94.4 %shard_map.246 = (bf16[16,64,3200]{2,1,0:T(8,128)(2,1)}, bf16[16,256,1024]{2,1,0:T(8,128)(2,1)}, bf16[2,8,128,1024]{3,2,1,0:T(8,128)(2,1)}, bf16[2,4,512,1024]{3...) custom-call(s32[2,2]{1,0:T(2,128)} %starts_ref.1, ...), custom_call_target="tpu_custom_call" | custom-call | tf_op jit(solution)/shard_map/pallas_call | solution.py:959
  100.3 75.9 %shard_map.247 = (f32[256,1152]{1,0:T(8,128)}, bf16[16,256,1024]{2,1,0:T(8,128)(2,1)}, bf16[1536,1024]{1,0:T(8,128)(2,1)}) custom-call(bf16[256,1152]{1,0:T(8,128)(2,1)} %get-tuple-element.40.sent_ref, bf16[16,128,1152]{2,1,0:T(8,128)(2,1)} %get-tuple-element.41.first_ref, bf16[16,256,1024]{2,1,0:T(8,128)(2,1)} %get-tuple-element.42.grad_ref, ...), custom_call_target="tpu_custom_call" | custom-call | tf_op jit(solution)/shard_map/pallas_call | solution.py:603
  176.3 99.9 %shard_map.248 = (bf16[256,1024]{1,0:T(8,128)(2,1)}, bf16[256,1024]{1,0:T(8,128)(2,1)}, bf16[64,3200]{1,0:T(8,128)(2,1)}, bf16[8,192,1024]{2,1,0:T(8,128)(2,1)}) custom-call(f32[256,1152]{1,0:T(8,128)} %get-tuple-element.43.returned_ref, f32[256,128]{1,0:T(8,128)} %get-tuple-element.44.gates_ref, f32[256,1024]{1,0:T(8,128)} %get-tuple-element.45.middle_ref, ...), custom_call_target="tpu_custom_call" | custom-call | tf_op jit(solution)/shard_map/pallas_call | solution.py:1390
  276.2 0.0 copy-start
  276.2 6.7 %shard_map.249 = (f32[1024,1024]{1,0:T(8,128)}, f32[512,1024]{1,0:T(8,128)}, f32[64,1024]{1,0:T(8,128)}, f32[64,512]{1,0:T(8,128)}, f32[64,512]{1,0:T(8,128)}, /*index=5*/f32[64,1024]{1,0:T(8,128)}, f32[64,128]{1,0:T(8,128)}) custom-call(bf16[64,3200]{1,0:T(8,128)(2,1)} %get-tuple-element.58.dense_ref, bf16[1536,1024]{1,0:T(8,128)(2,1)} %bitcast.11), custom_call_target="tpu_custom_call" | custom-call | tf_op jit(solution)/shard_map/pallas_call | solution.py:1444
  282.8 1.4 slice_reduce_fusion.3
  284.2 1.6 slice_reduce_fusion
  285.9 1.4 copy.33
  287.3 1.9 copy.36
  289.2 0.0 copy-done
  289.2 0.8 copy.37
  (4 shorter events, 0.0 us)
Async XLA Ops:
  276.2 13.0 %copy-start = (bf16[256,1024]{1,0:T(8,128)(2,1)S(1)}, bf16[256,1024]{1,0:T(8,128)(2,1)}, u32[]{:S(2)}) copy-start(bf16[256,1024]{1,0:T(8,128)(2,1)} %get-tuple-element.57) | copy-start | bytes 1572868

commit v7 on v6

--- a/solution.py
+++ b/solution.py
@@ -12,7 +12,7 @@
 RING = 4
 GROUP = 16
 REPS = 8
-VMEM_LIMIT = 62 << 20
+VMEM_LIMIT = 63 << 20
 
 norm_eps = 1e-06
 rope_base = 10000.0
@@ -194,48 +194,49 @@
 
 
 SUM_SEMS = 20
-TOTAL_SEMS = 24
-
-
-def total_parts(place, line, own, got, total, target, local_sem, tail=None):
+TOTAL_SEMS = 16
+
+
+def total_parts(place, line, own, got, total, target, local_sem):
     rep = place.rep
     steps = range(1, REPS)
     peers = {step: (place.shard, place.others[step]) for step in steps}
     before = {step: place.others[REPS - step] for step in steps}
 
-    def added(mine, received):
-        value = mine[...].astype(f32)
-        for step in steps:
-            value = value + received[before[step]].astype(f32)
-        return value.astype(bf16)
-
-    def kept(index, source, place_of):
-        return pltpu.make_async_copy(source, place_of, local_sem.at[index])
+    def kept():
+        return pltpu.make_async_copy(total, target(rep), local_sem)
 
     for step in steps:
-        line.send(
-            step, lambda p=place.others[step]: own(p), lambda: got.at[rep], peers[step]
-        )
-        if tail is not None:
-            line.send(16 + step, lambda: tail[0], lambda: tail[1].at[rep], peers[step])
+        line.send(step, lambda p=place.others[step]: own(p), lambda: got.at[rep], peers[step])
     yield
+    value = own(rep)[...].astype(f32)
     for step in steps:
         line.take(step, lambda b=before[step]: got.at[b], peers[step])
-    total[...] = added(own(rep), got)
-    kept(0, total, target(rep)).start()
+        value = value + got[before[step]].astype(f32)
+    total[...] = value.astype(bf16)
+    kept().start()
     for step in steps:
         line.send(8 + step, lambda: total, lambda: target(rep), peers[step])
-    if tail is not None:
-        for step in steps:
-            line.take(16 + step, lambda b=before[step]: tail[1].at[b], peers[step])
-        tail[2][...] = added(tail[0], tail[1])
-        kept(1, tail[2], tail[3]).start()
     yield
     for step in steps:
         line.take(8 + step, lambda b=before[step]: target(b), peers[step])
-    kept(0, total, target(rep)).wait()
-    if tail is not None:
-        kept(1, tail[2], tail[3]).wait()
+    kept().wait()
+    line.finish()
+
+
+def spread_parts(place, line, own, got, total):
+    rep = place.rep
+    steps = range(1, REPS)
+    for step in steps:
+        peer = (place.shard, place.others[step])
+        line.send(step, lambda: own, lambda: got.at[rep], peer)
+    yield
+    value = own[...].astype(f32)
+    for step in steps:
+        before = place.others[REPS - step]
+        line.take(step, lambda: got.at[before], (place.shard, place.others[step]))
+        value = value + got[before].astype(f32)
+    total[...] = value
     line.finish()
 
 
@@ -401,9 +402,10 @@
 
     def kernel(
         sent_ref, first_ref, grad_ref, inner_ref, outer_ref,
-        returned, out_terms, terms,
-        rows_in, grads, hidden, back_gu, back, back_staged, back_stage, out_box, term_box,
-        gs, gr, bs0, br0, bs1, br1, own_sem, load_sem, box_sem, term_sem,
+        returned, expert_own, out_terms,
+        rows_in, grads, hidden, back_gu, back, back_staged, back_stage, out_box,
+        inner_stage, down_stage,
+        gs, gr, bs0, br0, bs1, br1, is_, ir, ds_, dr, own_sem, load_sem, box_sem,
     ):
         place = Place()
         axes, core, shard = place.tokens, place.core, place.shard
@@ -431,6 +433,25 @@
             )
 
         sums = [sum_of(0, bs0, br0), sum_of(1, bs1, br1)]
+        inner_rows, down_rows = width // REPS, hidden_width // REPS
+
+        def inner_part(which, low, n):
+            at = chip_of(which)
+            return out_box.at[lax.div(at, wide), lax.rem(at, wide), pl.ds(low, n)]
+
+        def down_part(which, low, n):
+            at = chip_of(which)
+            row = lax.rem(at, 2) * down_rows + low
+            return back_gu.at[0, lax.div(at, 2), pl.ds(row, n)]
+
+        inner_sum = sum_parts(
+            place.copies, Line(is_, ir), inner_part, inner_stage, inner_rows,
+            expert_own.at[pl.ds(0, inner_rows)],
+        )
+        down_sum = sum_parts(
+            place.copies, Line(ds_, dr), down_part, down_stage, down_rows,
+            expert_own.at[pl.ds(inner_rows, down_rows)],
+        )
 
         def loads(t):
             at = pl.ds(t * wide, wide)
@@ -501,7 +522,7 @@
             for load in loads(t):
                 load.start()
         second_grads.start()
-        greet(axes.neighbours() + [place.twin])
+        greet(axes.neighbours() + place.copies.neighbours() + [place.twin])
         next(gather)
 
         def first_tiles(t, carry):
@@ -548,67 +569,56 @@
         next(sums[1])
         next(sums[1])
 
-        def term_copy(low, slot):
-            return pltpu.make_async_copy(
-                term_box.at[slot], terms.at[pl.ds(low, 256)], term_sem.at[slot]
-            )
-
         every = 2 * GROUP * half
-
-        def keep(index, low, value):
-            slot = lax.rem(index, 2)
-
-            @pl.when(index >= 2)
-            def _():
-                term_copy(low, slot).wait()
-
-            term_box[slot] = value.astype(bf16)
-            term_copy(low, slot).start()
-
-        downs = hidden_width // 256
-
-        def down_terms(index, carry):
-            at = chunk_256(index)
-            value = dot_tn(hidden[:, :, :, at].reshape(every, 256), grads[...].reshape(every, width))
-            keep(index, pl.multiple_of(width + index * 256, 256), value)
-            return carry
-
-        lax.fori_loop(0, downs, down_terms, 0)
+        for slot in range(2):
+            box_copy(1, 0, slot).wait()
 
         def inner_terms(index, carry):
-            hooks(
-                index,
-                (
-                    (0, lambda: next(sums[0])),
-                    (1, lambda: next(sums[1])),
-                ),
-            )
+            hooks(index, ((2, lambda: next(sums[0])), (3, lambda: next(sums[1]))))
             at = chunk_256(index)
             value = dot_tn(
                 rows_in[:, :, :, at].reshape(every, 256),
                 back_gu[...].reshape(every, 2 * hidden_width),
             )
-            keep(index + downs, pl.multiple_of(index * 256, 256), value)
+            out_box[lax.div(index, 2), pl.ds(2 * lax.rem(index, 2), 2)] = value.astype(bf16).reshape(
+                2, half, width
+            )
             return carry
 
         lax.fori_loop(0, width // 256, inner_terms, 0)
+        for _ in range(3):
+            next(inner_sum)
+
+        def down_terms(index, carry):
+            at = chunk_256(index)
+            value = dot_tn(hidden[:, :, :, at].reshape(every, 256), grads[...].reshape(every, width))
+            back_gu[0, pl.ds(2 * index, 2)] = value.astype(bf16).reshape(2, half, width)
+            return carry
+
+        lax.fori_loop(0, hidden_width // 256, down_terms, 0)
+        for _ in range(3):
+            next(down_sum)
         drained(sums[0])
+        next(inner_sum)
+        next(sums[1])
+        next(down_sum)
+        next(inner_sum)
+        next(down_sum)
         drained(sums[1])
+        drained(inner_sum)
+        drained(down_sum)
         drained(gather)
-        for slot in range(2):
-            box_copy(1, 0, slot).wait()
-            term_copy(0, slot).wait()
-
-    term_rows = width + hidden_width
+
+    own_rows = (width + hidden_width) // REPS
     return pl.pallas_call(
         kernel,
         out_shape=[
-            jax.ShapeDtypeStruct((count, columns), f32),
+            jax.ShapeDtypeStruct((count, columns), bf16),
+            jax.ShapeDtypeStruct((own_rows, width), bf16),
             jax.ShapeDtypeStruct((GROUP, count, width), bf16),
-            jax.ShapeDtypeStruct((term_rows, width), bf16),
         ],
         in_specs=[ANY, ANY, ANY, IN_VMEM, IN_VMEM],
-        out_specs=[IN_VMEM, ANY, ANY],
+        out_specs=[IN_VMEM, IN_VMEM, ANY],
         scratch_shapes=[
             pltpu.VMEM((2, GROUP, half, columns), bf16),
             pltpu.VMEM((2, GROUP, half, width), bf16),
@@ -618,14 +628,14 @@
             pltpu.VMEM((2, chips, half, columns), bf16),
             pltpu.VMEM((2, stage_rows(half), columns), bf16),
             pltpu.VMEM((2, wide, half, width), bf16),
-            pltpu.VMEM((2, 256, width), bf16),
+            pltpu.VMEM((stage_rows(width // REPS), width), bf16),
+            pltpu.VMEM((stage_rows(hidden_width // REPS), width), bf16),
         ]
         + sems(GATHER_SEMS)
-        + sems(SUM_SEMS) * 2
+        + sems(SUM_SEMS) * 4
         + [
             pltpu.SemaphoreType.DMA,
             pltpu.SemaphoreType.DMA((rounds + 1, 2)),
-            pltpu.SemaphoreType.DMA((2,)),
             pltpu.SemaphoreType.DMA((2,)),
         ],
         compiler_params=params(collective_id),
@@ -672,26 +682,23 @@
 
 
 def turned(values, cosine, sine):
-    first = lax.rem(lane_of(values.shape), HEAD_DIM) < HEAD_DIM // 2
+    first = (lane_of(values.shape) & (HEAD_DIM - 1)) < HEAD_DIM // 2
     swapped = jnp.where(
         first, pltpu.roll(values, LANES - HEAD_DIM // 2, 1), pltpu.roll(values, HEAD_DIM // 2, 1)
     )
     return values * cosine + swapped * sine
 
 
-def short_rows():
-    row = lax.broadcasted_iota(jnp.int32, (WIDTH, KEY), 0)
-    column = lax.broadcasted_iota(jnp.int32, (WIDTH, KEY), 1)
-    same = (lax.div(row, ROWS_OWN) == lax.div(column, KGAIN_OWN)) & (
-        lax.rem(row, ROWS_OWN) == lax.rem(column, KGAIN_OWN)
-    )
-    return jnp.where(same, 1.0, 0.0).astype(bf16)
-
-
 def gain_rows(small):
     rows = jnp.transpose(small.astype(f32))
-    gain_k = dot(rows[EXPERTS : EXPERTS + 8].astype(bf16), short_rows())[3:4]
+    short = small.reshape(GROUP, ROWS_OWN, SMALL)[:, :KGAIN_OWN].reshape(KEY, SMALL)
+    gain_k = jnp.transpose(short.astype(f32))[EXPERTS + 3 : EXPERTS + 4]
     return rows[EXPERTS : EXPERTS + 1], rows[EXPERTS + 1 : EXPERTS + 2], rows[EXPERTS + 2 : EXPERTS + 3], gain_k
+
+
+def long_column(columns):
+    cut = columns.reshape(GROUP, KGAIN_OWN, SMALL)
+    return jnp.concatenate([cut, jnp.zeros_like(cut)], axis=1).reshape(WIDTH, SMALL)
 
 
 def four_heads(chunk_a, chunk_b):
@@ -722,7 +729,7 @@
     return pl.ds(pl.multiple_of(base + index * LANES, LANES), LANES)
 
 
-def front_call(collective_id, tokens, cotangent, weights_own, small_own, cosine, sine, routes, starts):
+def front_call(collective_id, tokens, cotangent, weights_own, gains, router, cosine, sine, routes, starts):
     count, width = tokens.shape
     seqs = starts.shape[0]
     positions = count // seqs
@@ -731,11 +738,11 @@
     sent_width = width + SMALL
 
     def kernel(
-        starts_ref, tokens_ref, grad_ref, query_w, key_w, value_w, output_w, small_ref,
-        cos_ref, sin_ref, routes_ref,
+        starts_ref, tokens_ref, grad_ref, query_w, key_w, value_w, output_w,
+        gain_a_ref, gain_q_ref, gain_f_ref, gain_k_ref, router_ref, cos_ref, sin_ref, routes_ref,
         dense_out, grad_all, pairs_out, soft_out, rows_first,
         attn_in, query_raw, key_raw, query_low, mixed, middle, sent, gates_out,
-        packed, dense, pairs, pair_own, soft_box, bias_box,
+        packed, small_box, dense, pairs, pair_own, soft_box, bias_box,
         ws0, wr0, ws1, wr1, ws2, wr2, gs0, gr0, gs1, gr1, ks0, kr0, ks1, kr1, rs, rr, own_sem, out_sem, soft_sem, pack_sem,
     ):
         place = Place()
@@ -745,11 +752,19 @@
                 source, packed.at[:, pl.ds(low, source.shape[1])], pack_sem.at[index]
             )
             for index, (source, low) in enumerate(
-                ((key_w, AT_K), (value_w, AT_V), (small_ref, AT_S), (query_w, 0), (output_w, AT_O))
+                ((key_w, AT_K), (value_w, AT_V), (query_w, 0), (output_w, AT_O))
             )
         ]
         for copy in packing:
             copy.start()
+        small_box[...] = jnp.zeros_like(small_box)
+        small_box[pl.ds(0, EXPERTS), pl.ds(0, ROWS_OWN)] = router_ref[...].astype(f32)
+        for at, ref in enumerate((gain_a_ref, gain_q_ref, gain_f_ref, gain_k_ref)):
+            size = ref.shape[0]
+            small_box[pl.ds(EXPERTS + at, 1), pl.ds(0, size)] = (
+                ref[...].astype(f32).reshape(1, size)
+            )
+        packed[:, pl.ds(AT_S, SMALL)] = jnp.transpose(small_box[...])[:ROWS_OWN].astype(bf16)
 
         def token_block(index, low, size):
             def block(which, row, n, other=False):
@@ -811,12 +826,10 @@
         for copy in packing:
             copy.wait()
         next(rest_gather)
-        next(query_gather)
         inputs = tokens_ref[...].astype(f32)
         middle[...] = inputs * root_mean(inputs)
         next(rest_gather)
         next(query_gather)
-        next(output_gather)
         query_at = place.rep * positions + lax.broadcasted_iota(jnp.int32, (positions, 1), 0)
         key_at = lax.broadcasted_iota(jnp.int32, (1, length), 1)
         for seq in range(seqs):
@@ -831,6 +844,8 @@
         next(query_gather)
         next(output_gather)
         drained(rest_gather)
+        next(query_gather)
+        next(output_gather)
 
         def weights(low, size):
             return dense[:, :, pl.ds(low, size)].reshape(width, size)
@@ -902,7 +917,7 @@
             ffn_in = (total * root_mean(total) * gain_f).astype(bf16)
             sent[at, pl.ds(0, width)] = ffn_in
             lanes = lane_of((positions, SMALL))
-            named = routes_ref[at]
+            named = jnp.transpose(routes_ref[seq].astype(f32)).astype(jnp.int32)
             chosen = lanes == named[:, :1]
             for choice in range(1, named.shape[1]):
                 chosen = chosen | (lanes == named[:, choice : choice + 1])
@@ -973,10 +988,11 @@
             jax.ShapeDtypeStruct((count, width + SMALL), bf16),
             jax.ShapeDtypeStruct((count, SMALL), f32),
         ],
-        in_specs=[pl.BlockSpec(memory_space=pltpu.SMEM), IN_VMEM] + [ANY] * 6 + [IN_VMEM] * 3,
+        in_specs=[pl.BlockSpec(memory_space=pltpu.SMEM), IN_VMEM] + [ANY] * 5 + [IN_VMEM] * 8,
         out_specs=[ANY] * 5 + [IN_VMEM] * 8,
         scratch_shapes=[
             pltpu.VMEM((ROWS_OWN, PACKED), bf16),
+            pltpu.VMEM((SMALL, LANES), f32),
             pltpu.VMEM((GROUP, ROWS_OWN, PACKED), bf16),
             pltpu.VMEM((seqs, REPS, positions, 2 * KEY), bf16),
             pltpu.VMEM((count, 2 * KEY), bf16),
@@ -988,10 +1004,10 @@
             pltpu.SemaphoreType.DMA((8,)),
             pltpu.SemaphoreType.DMA((2,)),
             pltpu.SemaphoreType.DMA((2,)),
-            pltpu.SemaphoreType.DMA((5,)),
+            pltpu.SemaphoreType.DMA((4,)),
         ],
         compiler_params=params(collective_id),
-    )(starts, tokens, cotangent, *weights_own, small_own, cosine, sine, routes)
+    )(starts, tokens, cotangent, *weights_own, *gains, router, cosine, sine, routes)
 
 
 def norm_back(values, gain, grad):
@@ -1004,12 +1020,12 @@
 
 def back_call(
     collective_id, returned, gates, middle, sent, dense, cotangent, tokens, attn_in, query_raw, key_raw,
-    query_low, mixed, pairs, soft, out_terms, expert_terms, cosine, sine,
+    query_low, mixed, pairs, soft, out_terms, expert_own, cosine, sine,
 ):
     count, width = tokens.shape
     seqs, _, positions, _ = pairs.shape
     length = REPS * positions
-    expert_rows = expert_terms.shape[0] // REPS
+    expert_rows = expert_own.shape[0]
     score_scale = HEAD_DIM ** (-0.5)
     chips = GROUP // 2
 
@@ -1017,21 +1033,20 @@
         returned_ref, gates_ref, middle_ref, sent_ref, dense_ref, grad_ref, tokens_ref, attn_ref,
         query_raw_ref, key_raw_ref, query_ref, mixed_ref, pairs_ref, soft_ref, out_ref, expert_ref,
         cos_ref, sin_ref,
-        block_out, tokens_grad, dense_out, expert_all,
+        block_out, tokens_grad, small_out, dense_out, expert_all,
         weight_box, weight_rest, rest_terms, dense_own,
         o_staged, q_staged, rest_staged, o_stage, q_stage, rest_stage,
-        out_held, out_staged, out_stage, expert_held, expert_stage, expert_own,
+        out_held, out_staged, out_stage, small_terms, small_staged, small_stage, small_own, q_terms,
         soft_box, key_box, value_box, pair_terms, pair_stage, pair_grads,
         grad_mixed, grad_query, grad_middle, grad_attn, grad_attn_in, gain_box,
         o_got, q_got, rest_got, small_got, totals,
-        out_s, out_r, exp_s, exp_r, kv0_s, kv0_r, kv1_s, kv1_r, o_s, o_r, q_s, q_r, rest_s, rest_r,
-        ge_s, ge_r, go_s, go_r, gq_s, gq_r, grest_s, grest_r,
+        out_s, out_r, small_s, small_r, kv0_s, kv0_r, kv1_s, kv1_r, o_s, o_r, q_s, q_r, rest_s, rest_r,
+        ge_s, ge_r, go_s, go_r, gq_s, gq_r, grest_s, grest_r, gsmall_s, gsmall_r,
         load_sem, held_sem, box_sem, own_sem, total_sem,
     ):
         place = Place()
         core = place.core
         token_axes, copy_axes = place.tokens, place.copies
-        q_terms = expert_held
 
         def chip_of(which):
             return which[0] * RING + which[1]
@@ -1051,12 +1066,6 @@
              lambda which: out_staged.at[chip_of(which)]),
             store=out_store,
         )
-        expert_sum = sum_parts(
-            copy_axes, Line(exp_s, exp_r),
-            lambda which, low, n: expert_held.at[pl.ds(chip_of(which) * expert_rows + low, n)],
-            expert_stage, expert_rows, expert_own,
-        )
-
         def pair_sum(seq, send_sem, recv_sem):
             return sum_parts(
                 copy_axes, Line(send_sem, recv_sem),
@@ -1073,20 +1082,28 @@
             at = lax.rem(index, 2) * ROWS_OWN + low
             return terms.at[0, lax.div(index, 2), pl.ds(at, n)]
 
-        def dense_sum(rows_of, terms, staged, stage, low, size, send_sem, recv_sem):
+        def dense_sum(rows_of, terms, staged, stage, own, send_sem, recv_sem):
             return sum_parts(
                 token_axes, Line(send_sem, recv_sem),
                 lambda which, row, n: rows_of(terms, blocks(which), row, n),
-                stage, ROWS_OWN, dense_own.at[:, pl.ds(low, size)],
+                stage, ROWS_OWN, own,
                 (place.twin, lambda which: rows_of(terms, blocks(which, True), 0, ROWS_OWN),
                  lambda which: staged.at[chip_of(which)]),
             )
 
-        o_sum = dense_sum(rows_of_pairs, pair_terms, o_staged, o_stage, AT_O, width, o_s, o_r)
-        q_sum = dense_sum(rows_of_block, q_terms, q_staged, q_stage, 0, QUERY, q_s, q_r)
-        rest_sum = dense_sum(rows_of_block, rest_terms, rest_staged, rest_stage, AT_K, REST, rest_s, rest_r)
-
-        def dense_total(index, low, got, send_sem, recv_sem, tail=None):
+        def own_columns(low):
+            return dense_own.at[:, pl.ds(low, width)]
+
+        o_sum = dense_sum(rows_of_pairs, pair_terms, o_staged, o_stage, own_columns(AT_O), o_s, o_r)
+        q_sum = dense_sum(rows_of_block, q_terms, q_staged, q_stage, own_columns(0), q_s, q_r)
+        rest_sum = dense_sum(
+            rows_of_block, rest_terms, rest_staged, rest_stage, own_columns(AT_K), rest_s, rest_r
+        )
+        small_sum = dense_sum(
+            rows_of_block, small_terms, small_staged, small_stage, small_own, small_s, small_r
+        )
+
+        def dense_total(index, low, got, send_sem, recv_sem):
             def own(rep):
                 return dense_own.at[:, chunk_at(rep, low)]
 
@@ -1095,18 +1112,15 @@
 
             return total_parts(
                 place, Line(send_sem, recv_sem), own, got, totals.at[index], target,
-                total_sem.at[index], tail,
+                total_sem.at[index],
             )
 
         o_total = dense_total(0, AT_O, o_got, go_s, go_r)
         q_total = dense_total(1, 0, q_got, gq_s, gq_r)
-        small_at = pl.ds(AT_S, SMALL)
-        rest_total = dense_total(
-            2, AT_K, rest_got, grest_s, grest_r,
-            (dense_own.at[:, small_at], small_got, totals.at[3], dense_out.at[:, small_at]),
-        )
+        rest_total = dense_total(2, AT_K, rest_got, grest_s, grest_r)
+        small_total = spread_parts(place, Line(gsmall_s, gsmall_r), small_own, small_got, small_out)
         expert_gather = gather_parts(
-            copy_axes, Line(ge_s, ge_r), expert_own,
+            copy_axes, Line(ge_s, ge_r), expert_ref,
             lambda which, row, n, other=False: expert_all.at[chip_of(which), pl.ds(row, n)],
             expert_rows, own_sem,
         )
@@ -1119,7 +1133,6 @@
         rest_load = pltpu.make_async_copy(
             dense_ref.at[:, :, pl.ds(AT_K, REST)], weight_rest, load_sem.at[1]
         )
-        expert_load = pltpu.make_async_copy(expert_ref, expert_held, load_sem.at[2])
         held_loads = [
             pltpu.make_async_copy(
                 out_ref.at[2 * chip + core], out_held.at[chip], held_sem.at[chip]
@@ -1143,7 +1156,6 @@
                 ),
             ]
 
-        expert_load.start()
         rest_load.start()
         weight_load(AT_O, 0).start()
         for load in held_loads + box_loads(0, 0):
@@ -1154,20 +1166,17 @@
             + [(place.shard, other) for other in place.others[1:]]
         )
         next(out_sum)
-        expert_load.wait()
-        next(expert_sum)
-        next(expert_sum)
-        next(expert_sum)
+        next(expert_gather)
         rest_load.wait()
 
         small = weight_rest[:, :, pl.ds(2 * KEY, SMALL)].reshape(width, SMALL)
         gain_a, gain_q, gain_f, gain_k = gain_rows(small)
         gates = gates_ref[...]
-        tail = returned_ref[:, pl.ds(width, SMALL)]
+        tail = returned_ref[:, pl.ds(width, SMALL)].astype(f32)
         grad_gates = tail + pltpu.roll(tail, SMALL - EXPERTS, 1)
         grad_logits = gates * (grad_gates - jnp.sum(gates * grad_gates, axis=1, keepdims=True))
         grad_logits = grad_logits.astype(bf16)
-        grad_ffn = returned_ref[:, pl.ds(0, width)] + dot_nt(grad_logits, small)
+        grad_ffn = returned_ref[:, pl.ds(0, width)].astype(f32) + dot_nt(grad_logits, small)
         inner, gain_f_terms = norm_back(middle_ref[...], gain_f, grad_ffn)
         inner = grad_ref[...].astype(f32) + inner
         grad_middle[...] = inner
@@ -1228,7 +1237,7 @@
             next(out_sum)
 
         def first_heads(index, carry):
-            hooks(index, ((2, lambda: next(expert_sum)), (3, out_ready)))
+            hooks(index, ((2, out_ready), (3, lambda: next(expert_gather))))
             attend_back(0, index)
             return carry
 
@@ -1238,7 +1247,7 @@
         next(pair_sums[0])
 
         def second_heads(index, carry):
-            hooks(index, ((3, lambda: next(out_sum)),))
+            hooks(index, ((2, lambda: next(out_sum)), (3, lambda: next(expert_gather))))
             attend_back(1, index)
             return carry
 
@@ -1269,12 +1278,10 @@
         weight_load(0, 3).wait()
         grad_attn_in[...] = dot_nt(grad_query_low, weight_box[...].reshape(width, QUERY))
 
+        next(pair_sums[0])
         next(pair_sums[1])
-        next(expert_sum)
         next(out_sum)
-        next(pair_sums[0])
         drained(pair_sums[0])
-        next(pair_sums[1])
 
         def o_rows(index, carry):
             at = chunk_256(index)
@@ -1284,8 +1291,7 @@
 
         lax.fori_loop(0, QUERY // 256, o_rows, 0)
         next(o_sum)
-        drained(expert_sum)
-        next(expert_gather)
+        next(pair_sums[1])
 
         def q_rows(index, carry):
             at = chunk_256(index)
@@ -1300,6 +1306,7 @@
         next(q_sum)
         next(q_sum)
         next(o_sum)
+        next(expert_gather)
         drained(pair_sums[1])
 
         grads = pair_grads[...]
@@ -1309,69 +1316,79 @@
             turned_back(grads[:, :KEY].astype(bf16).astype(f32)),
         )
         grad_pairs = jnp.concatenate([grad.astype(bf16), grads[:, KEY:].astype(bf16)], axis=1)
-        gain_k_row = dot_nt(
-            jnp.broadcast_to(gain_k_terms, (8, KEY)).astype(bf16), short_rows()
-        )
-        gain_box[pl.ds(EXPERTS + 3, 1)] = gain_k_row[:1]
+
+        def rest_rows(index, carry):
+            at = chunk_256(index)
+            rest_terms[at] = dot_tn(attn_ref[:, at], grad_pairs).astype(bf16)
+            return carry
+
+        lax.fori_loop(0, width // 256, rest_rows, 0)
+        next(rest_sum)
         grad = grad_attn_in[...] + dot_nt(
             grad_pairs, weight_rest[:, :, pl.ds(0, 2 * KEY)].reshape(width, 2 * KEY)
         )
+        next(rest_sum)
+        next(rest_sum)
         values = tokens_ref[...].astype(f32)
         inner, gain_a_terms = norm_back(values, gain_a, grad)
+        gain_box[pl.ds(EXPERTS, 1)] = gain_a_terms
+        lanes = lane_of((KEY, SMALL))
+        gain_k_column = jnp.where(
+            lanes == EXPERTS + 3,
+            jnp.transpose(jnp.broadcast_to(gain_k_terms, (SMALL, KEY))),
+            0.0,
+        )
+        small_terms[...] = (
+            router_terms + jnp.transpose(gain_box[...]) + long_column(gain_k_column)
+        ).astype(bf16)
+        next(small_sum)
         tokens_grad[...] = (grad_middle[...] + inner).astype(bf16)
-        gain_box[pl.ds(EXPERTS, 1)] = gain_a_terms
-        rest_terms[:, pl.ds(2 * KEY, SMALL)] = (
-            router_terms + jnp.transpose(gain_box[...])
-        ).astype(bf16)
-
-        def rest_rows(index, carry):
-            at = chunk_256(index)
-            rest_terms[at, pl.ds(0, 2 * KEY)] = dot_tn(attn_ref[:, at], grad_pairs).astype(bf16)
-            return carry
-
-        lax.fori_loop(0, width // 256, rest_rows, 0)
+        next(small_sum)
+        next(small_sum)
+        next(q_sum)
         next(rest_sum)
-        next(rest_sum)
-        next(rest_sum)
+        next(small_sum)
+        next(o_sum)
+        next(small_sum)
         next(q_sum)
-        next(o_sum)
-        next(expert_gather)
         next(rest_sum)
         drained(o_sum)
         next(o_total)
-        next(q_sum)
-        next(expert_gather)
-        next(rest_sum)
-        next(o_total)
+        drained(small_sum)
+        next(small_total)
         drained(q_sum)
         next(q_total)
+        next(o_total)
         drained(rest_sum)
         next(rest_total)
         next(q_total)
+        drained(small_total)
         next(rest_total)
+        drained(expert_gather)
         drained(o_total)
         drained(q_total)
-        drained(expert_gather)
         drained(rest_total)
 
     block = pltpu.VMEM((GROUP, ROWS_OWN, width), bf16)
     scratch = [
         block,
         pltpu.VMEM((GROUP, ROWS_OWN, REST), bf16),
-        pltpu.VMEM((width, REST), bf16),
+        pltpu.VMEM((width, 2 * KEY), bf16),
         pltpu.VMEM((ROWS_OWN, PACKED), bf16),
         pltpu.VMEM((chips, ROWS_OWN, width), bf16),
         pltpu.VMEM((chips, ROWS_OWN, QUERY), bf16),
-        pltpu.VMEM((chips, ROWS_OWN, REST), bf16),
+        pltpu.VMEM((chips, ROWS_OWN, 2 * KEY), bf16),
         pltpu.VMEM((stage_rows(ROWS_OWN), width), bf16),
         pltpu.VMEM((stage_rows(ROWS_OWN), QUERY), bf16),
-        pltpu.VMEM((stage_rows(ROWS_OWN), REST), bf16),
+        pltpu.VMEM((stage_rows(ROWS_OWN), 2 * KEY), bf16),
         pltpu.VMEM((chips, count, width), bf16),
         pltpu.VMEM((chips, count, width), bf16),
         pltpu.VMEM((stage_rows(count), width), bf16),
-        pltpu.VMEM(expert_terms.shape, bf16),
-        pltpu.VMEM((stage_rows(expert_rows), width), bf16),
-        pltpu.VMEM((expert_rows, width), bf16),
+        pltpu.VMEM((width, SMALL), bf16),
+        pltpu.VMEM((chips, ROWS_OWN, SMALL), bf16),
+        pltpu.VMEM((stage_rows(ROWS_OWN), SMALL), bf16),
+        pltpu.VMEM((ROWS_OWN, SMALL), bf16),
+        pltpu.VMEM((width, QUERY), bf16),
         pltpu.VMEM((2, 4 * positions, length), bf16),
         pltpu.VMEM((2, REPS, positions, LANES), bf16),
         pltpu.VMEM((2, REPS, positions, LANES), bf16),
@@ -1386,80 +1403,83 @@
         pltpu.VMEM((SMALL, width), f32),
     ]
     scratch += [pltpu.VMEM((REPS, ROWS_OWN, LANES), bf16)] * 4
-    scratch += [pltpu.VMEM((4, ROWS_OWN, LANES), bf16)]
+    scratch += [pltpu.VMEM((3, ROWS_OWN, LANES), bf16)]
     return pl.pallas_call(
         kernel,
         out_shape=[
             jax.ShapeDtypeStruct((count, width), bf16),
             jax.ShapeDtypeStruct((count, width), bf16),
+            jax.ShapeDtypeStruct((ROWS_OWN, SMALL), f32),
             jax.ShapeDtypeStruct((ROWS_OWN, PACKED), bf16),
             jax.ShapeDtypeStruct((REPS, expert_rows, width), bf16),
         ],
         in_specs=[IN_VMEM] * 4 + [ANY] + [IN_VMEM] * 7 + [ANY] * 4 + [IN_VMEM] * 2,
-        out_specs=[IN_VMEM, IN_VMEM, ANY, ANY],
+        out_specs=[IN_VMEM, IN_VMEM, IN_VMEM, ANY, ANY],
         scratch_shapes=scratch
         + sems(SUM_SEMS) * 7
         + sems(GATHER_SEMS)
-        + sems(TOTAL_SEMS) * 3
+        + sems(TOTAL_SEMS) * 4
         + [
             pltpu.SemaphoreType.DMA((4,)),
             pltpu.SemaphoreType.DMA((chips,)),
             pltpu.SemaphoreType.DMA((2, 3)),
             pltpu.SemaphoreType.DMA,
-            pltpu.SemaphoreType.DMA((3, 2)),
+            pltpu.SemaphoreType.DMA((3,)),
         ],
         compiler_params=params(collective_id),
     )(
         returned, gates, middle, sent, dense, cotangent, tokens, attn_in, query_raw, key_raw,
-        query_low, mixed, pairs, soft, out_terms, expert_terms, cosine, sine,
+        query_low, mixed, pairs, soft, out_terms, expert_own, cosine, sine,
     )
 
 
-def finish_call(dense_own, expert_all, inner_rows):
-    total_rows, width = expert_all.shape
-    step = 256
-    inner_steps, steps = inner_rows // step, total_rows // step
-
-    def kernel(dense_ref, expert_ref, inner, outer, query, key, value, output, small):
-        at = pl.program_id(0)
-        rows = expert_ref[...].astype(f32)
-
-        @pl.when(at < inner_steps)
+def finish_call(small_sum, dense_own, expert_all, inner_rows):
+    reps, expert_rows, width = expert_all.shape
+    inner_own = inner_rows // reps
+    outer_own = expert_rows - inner_own
+
+    def kernel(
+        small_ref, dense_ref, expert_ref,
+        inner, outer, query, key, value, output, router, gain_a, gain_q, gain_f, gain_k,
+    ):
+        inner[...] = expert_ref[0, :inner_own].astype(f32)
+        outer[...] = expert_ref[0, inner_own:].astype(f32)
+
+        @pl.when(pl.program_id(0) == 1)
         def _():
-            inner[...] = rows
-
-        @pl.when(at >= inner_steps)
-        def _():
-            outer[...] = rows
-
-        @pl.when(at == 1)
-        def _():
-            for low, target in ((0, query), (AT_K, key), (AT_V, value), (AT_O, output), (AT_S, small)):
+            for low, target in ((0, query), (AT_K, key), (AT_V, value), (AT_O, output)):
                 target[...] = dense_ref[:, pl.ds(low, target.shape[1])].astype(f32)
-
-    def whole(columns):
-        return pl.BlockSpec((ROWS_OWN, columns), lambda i: (0, 0))
-
-    sizes = (QUERY, KEY, KEY, WIDTH, SMALL)
+            rows = jnp.transpose(small_ref[...])
+            router[...] = rows[:EXPERTS, :ROWS_OWN]
+            for at, target in enumerate((gain_a, gain_q, gain_f, gain_k)):
+                size = target.shape[0]
+                target[...] = rows[EXPERTS + at, :size].reshape(size)
+
+    def whole(*shape):
+        return pl.BlockSpec(shape, lambda i: (0,) * len(shape))
+
+    shapes = [(ROWS_OWN, QUERY), (ROWS_OWN, KEY), (ROWS_OWN, KEY), (ROWS_OWN, WIDTH)]
+    shapes += [(EXPERTS, ROWS_OWN), (ROWS_OWN,), (ROWS_OWN,), (ROWS_OWN,), (KGAIN_OWN,)]
     return pl.pallas_call(
         kernel,
-        grid=(steps,),
+        grid=(reps,),
         out_shape=[
             jax.ShapeDtypeStruct((inner_rows, width), f32),
-            jax.ShapeDtypeStruct((total_rows - inner_rows, width), f32),
+            jax.ShapeDtypeStruct((reps * outer_own, width), f32),
         ]
-        + [jax.ShapeDtypeStruct((ROWS_OWN, size), f32) for size in sizes],
+        + [jax.ShapeDtypeStruct(shape, f32) for shape in shapes],
         in_specs=[
-            pl.BlockSpec(dense_own.shape, lambda i: (0, 0)),
-            pl.BlockSpec((step, width), lambda i: (i, 0)),
+            whole(*small_sum.shape),
+            whole(*dense_own.shape),
+            pl.BlockSpec((1, expert_rows, width), lambda i: (i, 0, 0)),
         ],
         out_specs=[
-            pl.BlockSpec((step, width), lambda i: (jnp.minimum(i, inner_steps - 1), 0)),
-            pl.BlockSpec((step, width), lambda i: (jnp.maximum(i - inner_steps, 0), 0)),
+            pl.BlockSpec((inner_own, width), lambda i: (i, 0)),
+            pl.BlockSpec((outer_own, width), lambda i: (i, 0)),
         ]
-        + [whole(size) for size in sizes],
+        + [whole(*shape) for shape in shapes],
         compiler_params=pltpu.CompilerParams(vmem_limit_bytes=VMEM_LIMIT),
-    )(dense_own, expert_all)
+    )(small_sum, dense_own, expert_all)
 
 
 def rotary_tables(positions):
@@ -1470,16 +1490,6 @@
     angles = positions.astype(f32)[:, None] * frequency[None, :]
     sign = jnp.where(lane % HEAD_DIM < half, -1.0, 1.0).astype(f32)
     return jnp.cos(angles), jnp.sin(angles) * sign[None, :]
-
-
-def small_columns(router, gain_a, gain_q, gain_f, gain_k):
-    rows = router.shape[0]
-    lane = jnp.arange(SMALL)[None, :]
-    small = jnp.pad(router, ((0, 0), (0, SMALL - EXPERTS)))
-    short = jnp.pad(gain_k, (0, rows - gain_k.shape[0]))
-    for at, gain in enumerate((gain_a, gain_q, gain_f, short)):
-        small = jnp.where(lane == EXPERTS + at, gain[:, None], small)
-    return small
 
 
 def shards(
@@ -1510,31 +1520,31 @@
         attn_in, query_raw, key_raw, query_low, mixed, middle, sent, gates,
     ) = front_call(
         1, rows, grad_rows, (query_weight, key_weight, value_weight, output_weight),
-        small_columns(router_weight, attn_gain, query_gain, ffn_gain, key_gain),
-        cosine, sine, routes.reshape(count, routes.shape[2]), picture_starts,
+        (attn_gain, query_gain, ffn_gain, key_gain), router_weight.T,
+        cosine, sine, jnp.transpose(routes, (0, 2, 1)), picture_starts,
     )
-    returned, out_terms, expert_terms = moe_call(
+    returned, expert_own, out_terms = moe_call(
         2, sent, rows_first, grad_all, expert_in[0], expert_down[0]
     )
-    block_out, tokens_grad, dense_out, expert_all = back_call(
+    block_out, tokens_grad, small_sum, dense_out, expert_all = back_call(
         3, returned, gates, middle, sent, dense, grad_rows, rows, attn_in,
-        query_raw, key_raw, query_low, mixed, pairs, soft, out_terms, expert_terms, cosine, sine,
+        query_raw, key_raw, query_low, mixed, pairs, soft, out_terms, expert_own, cosine, sine,
     )
-    inner, outer, query, key, value, output, small = finish_call(
-        dense_out, expert_all.reshape(-1, width), expert_in.shape[1]
+    inner, outer, query, key, value, output, router, gain_a, gain_q, gain_f, gain_k = finish_call(
+        small_sum, dense_out, expert_all, expert_in.shape[1]
     )
     return (
         block_out.reshape(tokens.shape),
         tokens_grad.reshape(tokens.shape),
-        small[:, EXPERTS],
+        gain_a,
         query,
         key,
         value,
-        small[:, EXPERTS + 1],
-        small[: key_gain.shape[0], EXPERTS + 3],
+        gain_q,
+        gain_k,
         output,
-        small[:, EXPERTS + 2],
-        small[:, :EXPERTS],
+        gain_f,
+        router.T,
         inner[None],
         outer[None],
     )

time: 291 us -> 301 us (1.034)
  Pallas kernels: 277 us -> 297 us
  local copies, waits for them, and re-layouts: 10.1 us -> 2.67 us
    pallas_call x1, Pallas kernels: 75.9 us -> 85.1 us  [moe_call(): pl.pallas_call(kernel, out_shape=[jax.ShapeDtypeStruct((count, columns),...]
    pallas_call x1, Pallas kernels: 99.9 us -> 107 us  [back_call(): pl.pallas_call(kernel, out_shape=[jax.ShapeDtypeStruct((count, width), bf...]
    unnamed x7 -> x4, local copies, waits for them, and re-layouts: 6.36 us -> 2.67 us
    pallas_call x1, Pallas kernels: 94.4 us -> 97.5 us  [front_call(): pl.pallas_call(kernel, out_shape=[jax.ShapeDtypeStruct((GROUP, ROWS_OWN,...]
    slice x2 -> x0, local copies, waits for them, and re-layouts: 3.03 us -> none  [the longest x1 1.62 us: shards(): small[:, EXPERTS + 2]]
where the time goes in v7:
time: 301 us
  Pallas kernels  297 us (99%)
    pallas_call x1, Pallas kernels, back_call(): pl.pallas_call(kernel, out_shape=[jax.ShapeDtypeStruct((count, width), bf...  107 us
    pallas_call x1, Pallas kernels, front_call(): pl.pallas_call(kernel, out_shape=[jax.ShapeDtypeStruct((GROUP, ROWS_OWN,...  97.5 us
    pallas_call x1, Pallas kernels, moe_call(): pl.pallas_call(kernel, out_shape=[jax.ShapeDtypeStruct((count, columns),...  85.1 us
    pallas_call x1, Pallas kernels, finish_call(): pl.pallas_call(kernel, grid=(reps,), out_shape=[jax.ShapeDtypeStruct((inn...  7.14 us

profile of v7, /device:TPU:0, one launch (start us, length us, event | category | flops | bytes accessed | tf_op | source)
XLA Modules:
  0.0 301.1 jit_solution(4581096073048351320)
XLA Ops:
  0.7 1.0 fusion
  1.6 97.5 %shard_map.246 = (bf16[16,64,3200]{2,1,0:T(8,128)(2,1)}, bf16[16,256,1024]{2,1,0:T(8,128)(2,1)}, bf16[2,8,128,1024]{3,2,1,0:T(8,128)(2,1)}, bf16[2,4,512,1024]{3...) custom-call(s32[2,2]{1,0:T(2,128)} %starts_ref.1, ...), custom_call_target="tpu_custom_call" | custom-call | tf_op jit(solution)/shard_map/pallas_call | solution.py:974
  99.1 85.1 %shard_map.247 = (bf16[256,1152]{1,0:T(8,128)(2,1)}, bf16[192,1024]{1,0:T(8,128)(2,1)}, bf16[16,256,1024]{2,1,0:T(8,128)(2,1)}) custom-call(bf16[256,1152]{1,0:T(8,128)(2,1)} %get-tuple-element.45.sent_ref, bf16[16,128,1152]{2,1,0:T(8,128)(2,1)} %get-tuple-element.46.first_ref, bf16[16,256,1024]{2,1,0:T(8,128)(2,1)} %get-tuple-element.47.grad_ref, ...), custom_call_target="tpu_custom_call" | custom-call | tf_op jit(solution)/shard_map/pallas_call | solution.py:613
  184.2 107.1 %shard_map.248 = (bf16[256,1024]{1,0:T(8,128)(2,1)}, bf16[256,1024]{1,0:T(8,128)(2,1)}, f32[64,128]{1,0:T(8,128)}, bf16[64,3200]{1,0:T(8,128)(2,1)}, bf16[8,192,1024]{2,1,0:T(8,128)(2,1)}) custom-call(bf16[256,1152]{1,0:T(8,128)(2,1)} %get-tuple-element.48.returned_ref, f32[256,128]{1,0:T(8,128)} %get-tuple-element.49.gates_ref, ...), custom_call_target="tpu_custom_call" | custom-call | tf_op jit(solution)/shard_map/pallas_call | solution.py:1407
  291.3 0.0 copy-start
  291.3 7.1 %shard_map.249 = (f32[1024,1024]{1,0:T(8,128)}, f32[512,1024]{1,0:T(8,128)}, f32[64,1024]{1,0:T(8,128)}, f32[64,512]{1,0:T(8,128)}, f32[64,512]{1,0:T(8,128)}, /...) custom-call(f32[64,128]{1,0:T(8,128)} %get-tuple-element.63.small_re, ...), custom_call_target="tpu_custom_call" | custom-call | tf_op jit(solution)/shard_map/pallas_call | solution.py:1463
  298.4 1.9 copy.30
  300.3 0.0 copy-done
  300.3 0.8 copy.31
  (2 shorter events, 0.0 us)
Async XLA Ops:
  291.3 9.0 %copy-start = (bf16[256,1024]{1,0:T(8,128)(2,1)S(1)}, bf16[256,1024]{1,0:T(8,128)(2,1)}, u32[]{:S(2)}) copy-start(bf16[256,1024]{1,0:T(8,128)(2,1)} %get-tuple-element.62) | copy-start | bytes 1572868

commit v8 on v7

--- a/solution.py
+++ b/solution.py
@@ -404,8 +404,8 @@
         sent_ref, first_ref, grad_ref, inner_ref, outer_ref,
         returned, expert_own, out_terms,
         rows_in, grads, hidden, back_gu, back, back_staged, back_stage, out_box,
-        inner_stage, down_stage,
-        gs, gr, bs0, br0, bs1, br1, is_, ir, ds_, dr, own_sem, load_sem, box_sem,
+        term_stage,
+        gs, gr, bs0, br0, bs1, br1, ia, ja, ib, jb, ds_, dr, own_sem, load_sem, box_sem,
     ):
         place = Place()
         axes, core, shard = place.tokens, place.core, place.shard
@@ -433,24 +433,29 @@
             )
 
         sums = [sum_of(0, bs0, br0), sum_of(1, bs1, br1)]
-        inner_rows, down_rows = width // REPS, hidden_width // REPS
-
-        def inner_part(which, low, n):
-            at = chip_of(which)
-            return out_box.at[lax.div(at, wide), lax.rem(at, wide), pl.ds(low, n)]
+        piece = hidden_width // REPS
+
+        def inner_part(part):
+            def rows(which, low, n):
+                at = chip_of(which)
+                return out_box.at[part, lax.div(at, 2), pl.ds(lax.rem(at, 2) * piece + low, n)]
+
+            return rows
 
         def down_part(which, low, n):
             at = chip_of(which)
-            row = lax.rem(at, 2) * down_rows + low
-            return back_gu.at[0, lax.div(at, 2), pl.ds(row, n)]
-
-        inner_sum = sum_parts(
-            place.copies, Line(is_, ir), inner_part, inner_stage, inner_rows,
-            expert_own.at[pl.ds(0, inner_rows)],
-        )
+            return back_gu.at[0, lax.div(at, 2), pl.ds(lax.rem(at, 2) * piece + low, n)]
+
+        inner_sums = [
+            sum_parts(
+                place.copies, Line(send_sem, recv_sem), inner_part(part), term_stage.at[part], piece,
+                expert_own.at[pl.ds(part * piece, piece)],
+            )
+            for part, (send_sem, recv_sem) in enumerate(((ia, ja), (ib, jb)))
+        ]
         down_sum = sum_parts(
-            place.copies, Line(ds_, dr), down_part, down_stage, down_rows,
-            expert_own.at[pl.ds(inner_rows, down_rows)],
+            place.copies, Line(ds_, dr), down_part, term_stage.at[2], piece,
+            expert_own.at[pl.ds(2 * piece, piece)],
         )
 
         def loads(t):
@@ -573,8 +578,18 @@
         for slot in range(2):
             box_copy(1, 0, slot).wait()
 
+        def begin(part):
+            for _ in range(3):
+                next(part)
+
         def inner_terms(index, carry):
-            hooks(index, ((2, lambda: next(sums[0])), (3, lambda: next(sums[1]))))
+            hooks(
+                index,
+                (
+                    (2, lambda: (begin(inner_sums[0]), next(sums[0]))[0]),
+                    (3, lambda: next(sums[1])),
+                ),
+            )
             at = chunk_256(index)
             value = dot_tn(
                 rows_in[:, :, :, at].reshape(every, 256),
@@ -586,26 +601,27 @@
             return carry
 
         lax.fori_loop(0, width // 256, inner_terms, 0)
-        for _ in range(3):
-            next(inner_sum)
+        begin(inner_sums[1])
 
         def down_terms(index, carry):
+            hooks(index, ((1, lambda: next(inner_sums[0])),))
             at = chunk_256(index)
             value = dot_tn(hidden[:, :, :, at].reshape(every, 256), grads[...].reshape(every, width))
             back_gu[0, pl.ds(2 * index, 2)] = value.astype(bf16).reshape(2, half, width)
             return carry
 
         lax.fori_loop(0, hidden_width // 256, down_terms, 0)
-        for _ in range(3):
-            next(down_sum)
+        begin(down_sum)
         drained(sums[0])
-        next(inner_sum)
+        next(inner_sums[1])
+        next(inner_sums[0])
         next(sums[1])
         next(down_sum)
-        next(inner_sum)
+        next(inner_sums[1])
+        drained(inner_sums[0])
         next(down_sum)
         drained(sums[1])
-        drained(inner_sum)
+        drained(inner_sums[1])
         drained(down_sum)
         drained(gather)
 
@@ -628,11 +644,10 @@
             pltpu.VMEM((2, chips, half, columns), bf16),
             pltpu.VMEM((2, stage_rows(half), columns), bf16),
             pltpu.VMEM((2, wide, half, width), bf16),
-            pltpu.VMEM((stage_rows(width // REPS), width), bf16),
-            pltpu.VMEM((stage_rows(hidden_width // REPS), width), bf16),
+            pltpu.VMEM((3, stage_rows(hidden_width // REPS), width), bf16),
         ]
         + sems(GATHER_SEMS)
-        + sems(SUM_SEMS) * 4
+        + sems(SUM_SEMS) * 5
         + [
             pltpu.SemaphoreType.DMA,
             pltpu.SemaphoreType.DMA((rounds + 1, 2)),
@@ -729,6 +744,15 @@
     return pl.ds(pl.multiple_of(base + index * LANES, LANES), LANES)
 
 
+def key_low(index):
+    return (index // 2) * KEY + (index % 2) * LANES
+
+
+def key_chunk(index, base=0):
+    low = lax.div(index, 2) * KEY + lax.rem(index, 2) * LANES + base
+    return pl.ds(pl.multiple_of(low, LANES), LANES)
+
+
 def front_call(collective_id, tokens, cotangent, weights_own, gains, router, cosine, sine, routes, starts):
     count, width = tokens.shape
     seqs = starts.shape[0]
@@ -743,7 +767,8 @@
         dense_out, grad_all, pairs_out, soft_out, rows_first,
         attn_in, query_raw, key_raw, query_low, mixed, middle, sent, gates_out,
         packed, small_box, dense, pairs, pair_own, soft_box, bias_box,
-        ws0, wr0, ws1, wr1, ws2, wr2, gs0, gr0, gs1, gr1, ks0, kr0, ks1, kr1, rs, rr, own_sem, out_sem, soft_sem, pack_sem,
+        ws0, wr0, ws1, wr1, ws2, wr2, gs0, gr0, gs1, gr1,
+        ka0, la0, kb0, lb0, ka1, la1, kb1, lb1, rs, rr, own_sem, out_sem, soft_sem, pack_sem,
     ):
         place = Place()
         core = place.core
@@ -786,13 +811,16 @@
 
             return block
 
-        def pair_gather(seq, send_sem, recv_sem):
+        def pair_gather(seq, part, send_sem, recv_sem):
+            columns = pl.ds(part * KEY, KEY)
+
             def block(which, row, n, other=False):
-                return pairs.at[seq, which[0] * RING + which[1], pl.ds(row, n)]
+                return pairs.at[seq, which[0] * RING + which[1], pl.ds(row, n), columns]
 
             return gather_parts(
                 place.copies, Line(send_sem, recv_sem),
-                pair_own.at[pl.ds(seq * positions, positions)], block, positions, own_sem.at[3 + seq],
+                pair_own.at[pl.ds(seq * positions, positions), columns], block, positions,
+                own_sem.at[8 + 2 * seq + part],
             )
 
         def soft_copy(seq, index, slot):
@@ -820,7 +848,8 @@
             place.tokens, Line(rs, rr), sent.at[pl.ds(0, positions)], rows_of(rows_first), positions,
             own_sem.at[7], place.twin,
         )
-        pair_gathers = [pair_gather(0, ks0, kr0), pair_gather(1, ks1, kr1)]
+        heads_a0, heads_b0 = pair_gather(0, 0, ka0, la0), pair_gather(0, 1, kb0, lb0)
+        heads_a1, heads_b1 = pair_gather(1, 0, ka1, la1), pair_gather(1, 1, kb1, lb1)
 
         greet(place.tokens.neighbours() + place.copies.neighbours() + [place.twin])
         for copy in packing:
@@ -861,9 +890,13 @@
         scaled = raw * root_mean(raw) * gain_k
         for chunk in range(KEY // LANES):
             at = slice(chunk * LANES, (chunk + 1) * LANES)
-            pair_own[:, at] = turned(scaled[:, at], cos2, sin2).astype(bf16)
-        pair_own[:, KEY:] = dot(rows, weights(AT_V, KEY)).astype(bf16)
-        next(pair_gathers[0])
+            pair_own[:, pl.ds(key_low(chunk), LANES)] = turned(scaled[:, at], cos2, sin2).astype(bf16)
+        raw = dot(rows, weights(AT_V, KEY)).astype(bf16)
+        for chunk in range(KEY // LANES):
+            at = slice(chunk * LANES, (chunk + 1) * LANES)
+            pair_own[:, pl.ds(key_low(chunk) + KEY // 2, LANES)] = raw[:, at]
+        next(heads_a0)
+        next(heads_b0)
         drained(query_gather)
         next(output_gather)
         next(grads[0])
@@ -873,18 +906,18 @@
         for chunk in range(QUERY // LANES):
             at = slice(chunk * LANES, (chunk + 1) * LANES)
             query_low[:, at] = turned(scaled[:, at], cos2, sin2).astype(bf16)
-        next(pair_gathers[0])
-        next(pair_gathers[1])
+        next(heads_a0)
+        next(heads_b0)
+        next(heads_a1)
         drained(output_gather)
         dense_copy = pltpu.make_async_copy(dense, dense_out, out_sem.at[0])
         dense_copy.start()
+        next(heads_a0)
         next(grads[0])
         next(grads[1])
-        next(pair_gathers[0])
-        next(pair_gathers[1])
-        next(grads[0])
-        drained(pair_gathers[0])
-        next(grads[1])
+        next(heads_b0)
+        next(heads_b1)
+        drained(heads_a0)
 
         def attend(seq, index, slot, wait_first):
             rows_at = pl.ds(seq * positions, positions)
@@ -893,7 +926,7 @@
                 query_low[rows_at, chunk_at(2 * index + 1)].astype(f32),
             )
             queries = (queries * score_scale).astype(bf16)
-            keys = pairs[seq, :, :, chunk_at(index)].reshape(length, LANES)
+            keys = pairs[seq, :, :, key_chunk(index)].reshape(length, LANES)
             scores = dot_nt(queries, keys).reshape(4, positions, length) + bias_box[seq][None]
             scores = scores.reshape(4 * positions, length)
             raised = jnp.exp(scores - jnp.max(scores, axis=1, keepdims=True))
@@ -905,7 +938,7 @@
 
             soft_box[slot] = soft
             soft_copy(seq, index, slot).start()
-            values = pairs[seq, :, :, chunk_at(index, KEY)].reshape(length, LANES)
+            values = pairs[seq, :, :, key_chunk(index, KEY // 2)].reshape(length, LANES)
             chunk_a, chunk_b = two_chunks(dot(soft, values))
             mixed[rows_at, chunk_at(2 * index)] = chunk_a.astype(bf16)
             mixed[rows_at, chunk_at(2 * index + 1)] = chunk_b.astype(bf16)
@@ -934,9 +967,10 @@
             hooks(
                 index,
                 (
+                    (0, lambda: next(heads_a1)),
                     (1, lambda: next(grads[0])),
-                    (2, lambda: next(pair_gathers[1])),
-                    (3, lambda: next(grads[1])),
+                    (2, lambda: (drained(heads_b0), next(heads_a1))[0]),
+                    (3, lambda: (next(heads_b1), next(grads[1]))[0]),
                 ),
             )
             attend(0, index, lax.rem(index, 2), index >= 2)
@@ -945,15 +979,16 @@
         lax.fori_loop(0, HEAD_PAIRS, first_heads, 0)
         features(0)
         next(first_rows)
-        drained(pair_gathers[1])
-        pairs_copy = pltpu.make_async_copy(pairs, pairs_out, out_sem.at[1])
-        pairs_copy.start()
+        next(heads_b1)
+        drained(heads_a1)
+        next(grads[0])
 
         def second_heads(index, carry):
             hooks(
                 index,
                 (
                     (1, lambda: next(grads[1])),
+                    (2, lambda: drained(heads_b1)),
                     (3, lambda: next(first_rows)),
                 ),
             )
@@ -961,6 +996,8 @@
             return carry
 
         lax.fori_loop(0, HEAD_PAIRS, second_heads, 0)
+        pairs_copy = pltpu.make_async_copy(pairs, pairs_out, out_sem.at[1])
+        pairs_copy.start()
         features(1)
         next(first_rows)
         drained(grads[0])
@@ -999,9 +1036,9 @@
             pltpu.VMEM((2, 4 * positions, length), bf16),
             pltpu.VMEM((seqs, positions, length), f32),
         ]
-        + sems(GATHER_SEMS) * 8
+        + sems(GATHER_SEMS) * 10
         + [
-            pltpu.SemaphoreType.DMA((8,)),
+            pltpu.SemaphoreType.DMA((12,)),
             pltpu.SemaphoreType.DMA((2,)),
             pltpu.SemaphoreType.DMA((2,)),
             pltpu.SemaphoreType.DMA((4,)),
@@ -1040,7 +1077,7 @@
         soft_box, key_box, value_box, pair_terms, pair_stage, pair_grads,
         grad_mixed, grad_query, grad_middle, grad_attn, grad_attn_in, gain_box,
         o_got, q_got, rest_got, small_got, totals,
-        out_s, out_r, small_s, small_r, kv0_s, kv0_r, kv1_s, kv1_r, o_s, o_r, q_s, q_r, rest_s, rest_r,
+        out_s, out_r, small_s, small_r, kv0_s, kv0_r, kva_s, kva_r, kvb_s, kvb_r, o_s, o_r, q_s, q_r, rest_s, rest_r,
         ge_s, ge_r, go_s, go_r, gq_s, gq_r, grest_s, grest_r, gsmall_s, gsmall_r,
         load_sem, held_sem, box_sem, own_sem, total_sem,
     ):
@@ -1066,14 +1103,19 @@
              lambda which: out_staged.at[chip_of(which)]),
             store=out_store,
         )
-        def pair_sum(seq, send_sem, recv_sem):
+        def pair_sum(seq, low, size, index, send_sem, recv_sem):
+            columns = pl.ds(low, size)
             return sum_parts(
                 copy_axes, Line(send_sem, recv_sem),
-                lambda which, low, n: pair_terms.at[seq, chip_of(which), pl.ds(low, n)],
-                pair_stage.at[seq], positions, pair_grads.at[pl.ds(seq * positions, positions)],
-            )
-
-        pair_sums = [pair_sum(0, kv0_s, kv0_r), pair_sum(1, kv1_s, kv1_r)]
+                lambda which, row, n: pair_terms.at[seq, chip_of(which), pl.ds(row, n), columns],
+                pair_stage.at[index, :, columns], positions,
+                pair_grads.at[pl.ds(seq * positions, positions), columns],
+            )
+
+        first_pairs = pair_sum(0, 0, 2 * KEY, 0, kv0_s, kv0_r)
+        second_pairs = [
+            pair_sum(1, 0, KEY, 1, kva_s, kva_r), pair_sum(1, KEY, KEY, 1, kvb_s, kvb_r)
+        ]
 
         def rows_of_block(terms, index, low, n):
             return terms.at[pl.ds(index * ROWS_OWN + low, n)]
@@ -1147,10 +1189,10 @@
                     soft_ref.at[seq, index], soft_box.at[slot], box_sem.at[slot, 0]
                 ),
                 pltpu.make_async_copy(
-                    pairs_ref.at[seq, :, :, chunk_at(index)], key_box.at[slot], box_sem.at[slot, 1]
+                    pairs_ref.at[seq, :, :, key_chunk(index)], key_box.at[slot], box_sem.at[slot, 1]
                 ),
                 pltpu.make_async_copy(
-                    pairs_ref.at[seq, :, :, chunk_at(index, KEY)],
+                    pairs_ref.at[seq, :, :, key_chunk(index, KEY // 2)],
                     value_box.at[slot],
                     box_sem.at[slot, 2],
                 ),
@@ -1213,7 +1255,7 @@
             values = value_box[slot].reshape(length, LANES)
             soft_low = soft_box[slot]
             value_terms = dot_tn(soft_low, grads)
-            pair_terms[seq, :, :, chunk_at(index, KEY)] = value_terms.astype(bf16).reshape(
+            pair_terms[seq, :, :, key_chunk(index, KEY // 2)] = value_terms.astype(bf16).reshape(
                 REPS, positions, LANES
             )
             soft_full = soft_low.astype(f32)
@@ -1223,7 +1265,7 @@
                 weighted - soft_full * jnp.sum(weighted, axis=1, keepdims=True)
             ).astype(bf16)
             key_terms = dot_tn(grad_scores, queries)
-            pair_terms[seq, :, :, chunk_at(index)] = key_terms.astype(bf16).reshape(
+            pair_terms[seq, :, :, key_chunk(index)] = key_terms.astype(bf16).reshape(
                 REPS, positions, LANES
             )
             chunk_a, chunk_b = two_chunks(dot(grad_scores, keys) * score_scale)
@@ -1236,26 +1278,33 @@
             next(out_sum)
             next(out_sum)
 
+        def begin(part):
+            for _ in range(3):
+                next(part)
+
         def first_heads(index, carry):
-            hooks(index, ((2, out_ready), (3, lambda: next(expert_gather))))
+            hooks(index, ((2, out_ready),))
             attend_back(0, index)
             return carry
 
         lax.fori_loop(0, HEAD_PAIRS, first_heads, 0)
-        next(pair_sums[0])
-        next(pair_sums[0])
-        next(pair_sums[0])
+        begin(first_pairs)
 
         def second_heads(index, carry):
-            hooks(index, ((2, lambda: next(out_sum)), (3, lambda: next(expert_gather))))
+            hooks(
+                index,
+                (
+                    (1, lambda: next(out_sum)),
+                    (2, lambda: begin(second_pairs[0])),
+                    (3, lambda: next(first_pairs)),
+                ),
+            )
             attend_back(1, index)
             return carry
 
         lax.fori_loop(0, HEAD_PAIRS, second_heads, 0)
-        next(pair_sums[1])
-        next(pair_sums[1])
-        next(pair_sums[1])
-        next(pair_sums[0])
+        begin(second_pairs[1])
+        next(second_pairs[0])
         router_terms = dot_tn(sent_ref[:, pl.ds(0, width)], grad_logits)
 
         cos2 = jnp.concatenate([cos_ref[...]] * seqs, axis=0)
@@ -1278,10 +1327,13 @@
         weight_load(0, 3).wait()
         grad_attn_in[...] = dot_nt(grad_query_low, weight_box[...].reshape(width, QUERY))
 
-        next(pair_sums[0])
-        next(pair_sums[1])
+        next(second_pairs[1])
+        next(first_pairs)
+        next(second_pairs[0])
+        next(second_pairs[1])
+        next(expert_gather)
         next(out_sum)
-        drained(pair_sums[0])
+        drained(first_pairs)
 
         def o_rows(index, carry):
             at = chunk_256(index)
@@ -1291,7 +1343,6 @@
 
         lax.fori_loop(0, QUERY // 256, o_rows, 0)
         next(o_sum)
-        next(pair_sums[1])
 
         def q_rows(index, carry):
             at = chunk_256(index)
@@ -1302,20 +1353,17 @@
         next(q_sum)
         next(o_sum)
         next(o_sum)
-        drained(out_sum)
-        next(q_sum)
-        next(q_sum)
-        next(o_sum)
-        next(expert_gather)
-        drained(pair_sums[1])
+        drained(second_pairs[0])
+        drained(second_pairs[1])
 
         grads = pair_grads[...]
+        half = KEY // 2
+        key_grads = jnp.concatenate([grads[:, :half], grads[:, KEY : KEY + half]], axis=1)
+        value_grads = jnp.concatenate([grads[:, half:KEY], grads[:, KEY + half :]], axis=1)
         grad, gain_k_terms = norm_back(
-            key_raw_ref[...],
-            gain_k,
-            turned_back(grads[:, :KEY].astype(bf16).astype(f32)),
+            key_raw_ref[...], gain_k, turned_back(key_grads.astype(bf16).astype(f32))
         )
-        grad_pairs = jnp.concatenate([grad.astype(bf16), grads[:, KEY:].astype(bf16)], axis=1)
+        grad_pairs = jnp.concatenate([grad.astype(bf16), value_grads.astype(bf16)], axis=1)
 
         def rest_rows(index, carry):
             at = chunk_256(index)
@@ -1346,12 +1394,17 @@
         next(small_sum)
         next(small_sum)
         next(q_sum)
+        next(q_sum)
         next(rest_sum)
-        next(small_sum)
         next(o_sum)
         next(small_sum)
+        next(expert_gather)
         next(q_sum)
+        next(o_sum)
+        next(small_sum)
         next(rest_sum)
+        next(q_sum)
+        drained(out_sum)
         drained(o_sum)
         next(o_total)
         drained(small_sum)
@@ -1363,6 +1416,7 @@
         next(rest_total)
         next(q_total)
         drained(small_total)
+        next(expert_gather)
         next(rest_total)
         drained(expert_gather)
         drained(o_total)
@@ -1416,7 +1470,7 @@
         in_specs=[IN_VMEM] * 4 + [ANY] + [IN_VMEM] * 7 + [ANY] * 4 + [IN_VMEM] * 2,
         out_specs=[IN_VMEM, IN_VMEM, IN_VMEM, ANY, ANY],
         scratch_shapes=scratch
-        + sems(SUM_SEMS) * 7
+        + sems(SUM_SEMS) * 8
         + sems(GATHER_SEMS)
         + sems(TOTAL_SEMS) * 4
         + [
@@ -1433,53 +1487,63 @@
     )
 
 
-def finish_call(small_sum, dense_own, expert_all, inner_rows):
+def finish_call(block_out, tokens_grad, small_sum, dense_own, expert_all):
     reps, expert_rows, width = expert_all.shape
-    inner_own = inner_rows // reps
-    outer_own = expert_rows - inner_own
+    piece = expert_rows // 3
+    rows = block_out.shape[0] // reps
 
     def kernel(
-        small_ref, dense_ref, expert_ref,
-        inner, outer, query, key, value, output, router, gain_a, gain_q, gain_f, gain_k,
+        block_ref, tokens_ref, small_ref, dense_ref, expert_ref,
+        block, tokens, inner, outer, query, key, value, output, router, gain_a, gain_q, gain_f, gain_k,
     ):
-        inner[...] = expert_ref[0, :inner_own].astype(f32)
-        outer[...] = expert_ref[0, inner_own:].astype(f32)
+        block[...] = block_ref[...]
+        tokens[...] = tokens_ref[...]
+        inner[0] = expert_ref[0, :piece].astype(f32)
+        inner[1] = expert_ref[0, piece : 2 * piece].astype(f32)
+        outer[...] = expert_ref[0, 2 * piece :].astype(f32)
 
         @pl.when(pl.program_id(0) == 1)
         def _():
             for low, target in ((0, query), (AT_K, key), (AT_V, value), (AT_O, output)):
                 target[...] = dense_ref[:, pl.ds(low, target.shape[1])].astype(f32)
-            rows = jnp.transpose(small_ref[...])
-            router[...] = rows[:EXPERTS, :ROWS_OWN]
+            turned_small = jnp.transpose(small_ref[...])
+            router[...] = turned_small[:EXPERTS, :ROWS_OWN]
             for at, target in enumerate((gain_a, gain_q, gain_f, gain_k)):
                 size = target.shape[0]
-                target[...] = rows[EXPERTS + at, :size].reshape(size)
+                target[...] = turned_small[EXPERTS + at, :size].reshape(size)
 
     def whole(*shape):
         return pl.BlockSpec(shape, lambda i: (0,) * len(shape))
 
+    by_rows = pl.BlockSpec((rows, width), lambda i: (i, 0))
     shapes = [(ROWS_OWN, QUERY), (ROWS_OWN, KEY), (ROWS_OWN, KEY), (ROWS_OWN, WIDTH)]
     shapes += [(EXPERTS, ROWS_OWN), (ROWS_OWN,), (ROWS_OWN,), (ROWS_OWN,), (KGAIN_OWN,)]
     return pl.pallas_call(
         kernel,
         grid=(reps,),
         out_shape=[
-            jax.ShapeDtypeStruct((inner_rows, width), f32),
-            jax.ShapeDtypeStruct((reps * outer_own, width), f32),
+            jax.ShapeDtypeStruct(block_out.shape, bf16),
+            jax.ShapeDtypeStruct(tokens_grad.shape, bf16),
+            jax.ShapeDtypeStruct((2, reps * piece, width), f32),
+            jax.ShapeDtypeStruct((reps * piece, width), f32),
         ]
         + [jax.ShapeDtypeStruct(shape, f32) for shape in shapes],
         in_specs=[
+            by_rows,
+            by_rows,
             whole(*small_sum.shape),
             whole(*dense_own.shape),
             pl.BlockSpec((1, expert_rows, width), lambda i: (i, 0, 0)),
         ],
         out_specs=[
-            pl.BlockSpec((inner_own, width), lambda i: (i, 0)),
-            pl.BlockSpec((outer_own, width), lambda i: (i, 0)),
+            by_rows,
+            by_rows,
+            pl.BlockSpec((2, piece, width), lambda i: (0, i, 0)),
+            pl.BlockSpec((piece, width), lambda i: (i, 0)),
         ]
         + [whole(*shape) for shape in shapes],
         compiler_params=pltpu.CompilerParams(vmem_limit_bytes=VMEM_LIMIT),
-    )(small_sum, dense_own, expert_all)
+    )(block_out, tokens_grad, small_sum, dense_own, expert_all)
 
 
 def rotary_tables(positions):
@@ -1530,9 +1594,9 @@
         3, returned, gates, middle, sent, dense, grad_rows, rows, attn_in,
         query_raw, key_raw, query_low, mixed, pairs, soft, out_terms, expert_own, cosine, sine,
     )
-    inner, outer, query, key, value, output, router, gain_a, gain_q, gain_f, gain_k = finish_call(
-        small_sum, dense_out, expert_all, expert_in.shape[1]
-    )
+    (
+        block_out, tokens_grad, inner, outer, query, key, value, output, router, gain_a, gain_q, gain_f, gain_k,
+    ) = finish_call(block_out, tokens_grad, small_sum, dense_out, expert_all)
     return (
         block_out.reshape(tokens.shape),
         tokens_grad.reshape(tokens.shape),
@@ -1545,7 +1609,7 @@
         output,
         gain_f,
         router.T,
-        inner[None],
+        inner.reshape(expert_in.shape),
         outer[None],
     )
 

time: 301 us -> 298 us (0.990)
  no operation moved by 1% of the time
where the time goes in v8:
time: 298 us
  Pallas kernels  296 us (99%)
    pallas_call x1, Pallas kernels, back_call(): pl.pallas_call(kernel, out_shape=[jax.ShapeDtypeStruct((count, width), bf...  106 us
    pallas_call x1, Pallas kernels, front_call(): pl.pallas_call(kernel, out_shape=[jax.ShapeDtypeStruct((GROUP, ROWS_OWN,...  99.1 us
    pallas_call x1, Pallas kernels, moe_call(): pl.pallas_call(kernel, out_shape=[jax.ShapeDtypeStruct((count, columns),...  82.9 us
    pallas_call x1, Pallas kernels, finish_call(): pl.pallas_call(kernel, grid=(reps,), out_shape=[jax.ShapeDtypeStruct(bloc...  7.8 us

profile of v8, /device:TPU:0, one launch (start us, length us, event | category | flops | bytes accessed | tf_op | source)
XLA Modules:
  0.0 298.2 jit_solution(8243961081450682188)
XLA Ops:
  0.7 1.0 fusion
  1.6 99.1 %shard_map.246 = (bf16[16,64,3200]{2,1,0:T(8,128)(2,1)}, bf16[16,256,1024]{2,1,0:T(8,128)(2,1)}, bf16[2,8,128,1024]{3,2,1,0:T(8,128)(2,1)}, bf16[2,4,512,1024]{3...) custom-call(s32[2,2]{1,0:T(2,128)} %starts_ref.1, ...), custom_call_target="tpu_custom_call" | custom-call | tf_op jit(solution)/shard_map/pallas_call | solution.py:1011
  100.8 82.9 %shard_map.247 = (bf16[256,1152]{1,0:T(8,128)(2,1)}, bf16[192,1024]{1,0:T(8,128)(2,1)}, bf16[16,256,1024]{2,1,0:T(8,128)(2,1)}) custom-call(bf16[256,1152]{1,0:T(8,128)(2,1)} %get-tuple-element.47.sent_ref, bf16[16,128,1152]{2,1,0:T(8,128)(2,1)} %get-tuple-element.48.first_ref, bf16[16,256,1024]{2,1,0:T(8,128)(2,1)} %get-tuple-element.49.grad_ref, ...), custom_call_target="tpu_custom_call" | custom-call | tf_op jit(solution)/shard_map/pallas_call | solution.py:629
  183.7 106.5 %shard_map.248 = (bf16[256,1024]{1,0:T(8,128)(2,1)}, bf16[256,1024]{1,0:T(8,128)(2,1)}, f32[64,128]{1,0:T(8,128)}, bf16[64,3200]{1,0:T(8,128)(2,1)}, bf16[8,192,1024]{2,1,0:T(8,128)(2,1)}) custom-call(bf16[256,1152]{1,0:T(8,128)(2,1)} %get-tuple-element.50.returned_ref, f32[256,128]{1,0:T(8,128)} %get-tuple-element.51.gates_ref, ...), custom_call_target="tpu_custom_call" | custom-call | tf_op jit(solution)/shard_map/pallas_call | solution.py:1461
  290.2 7.8 %shard_map.249 = (bf16[256,1024]{1,0:T(8,128)(2,1)}, bf16[256,1024]{1,0:T(8,128)(2,1)}, f32[2,512,1024]{2,1,0:T(8,128)}, f32[512,1024]{1,0:T(8,128)}, f32[64,102...) custom-call(bf16[256,1024]{1,0:T(8,128)(2,1)} %get-tuple-element.63., ...), custom_call_target="tpu_custom_call" | custom-call | tf_op jit(solution)/shard_map/pallas_call | solution.py:1521
  (2 shorter events, 0.0 us)

commit v9 on v8

--- a/solution.py
+++ b/solution.py
@@ -672,6 +672,7 @@
 KGAIN_OWN = KEY // GROUP
 HEAD_PAIRS = KV_HEADS // 2
 REST = 2 * KEY + SMALL
+DENSE = QUERY + WIDTH + 2 * KEY
 
 
 def drained(part):
@@ -744,15 +745,6 @@
     return pl.ds(pl.multiple_of(base + index * LANES, LANES), LANES)
 
 
-def key_low(index):
-    return (index // 2) * KEY + (index % 2) * LANES
-
-
-def key_chunk(index, base=0):
-    low = lax.div(index, 2) * KEY + lax.rem(index, 2) * LANES + base
-    return pl.ds(pl.multiple_of(low, LANES), LANES)
-
-
 def front_call(collective_id, tokens, cotangent, weights_own, gains, router, cosine, sine, routes, starts):
     count, width = tokens.shape
     seqs = starts.shape[0]
@@ -767,8 +759,7 @@
         dense_out, grad_all, pairs_out, soft_out, rows_first,
         attn_in, query_raw, key_raw, query_low, mixed, middle, sent, gates_out,
         packed, small_box, dense, pairs, pair_own, soft_box, bias_box,
-        ws0, wr0, ws1, wr1, ws2, wr2, gs0, gr0, gs1, gr1,
-        ka0, la0, kb0, lb0, ka1, la1, kb1, lb1, rs, rr, own_sem, out_sem, soft_sem, pack_sem,
+        ws0, wr0, ws1, wr1, ws2, wr2, gs0, gr0, gs1, gr1, ks0, kr0, ks1, kr1, rs, rr, own_sem, out_sem, soft_sem, pack_sem,
     ):
         place = Place()
         core = place.core
@@ -811,16 +802,13 @@
 
             return block
 
-        def pair_gather(seq, part, send_sem, recv_sem):
-            columns = pl.ds(part * KEY, KEY)
-
+        def pair_gather(seq, send_sem, recv_sem):
             def block(which, row, n, other=False):
-                return pairs.at[seq, which[0] * RING + which[1], pl.ds(row, n), columns]
+                return pairs.at[seq, which[0] * RING + which[1], pl.ds(row, n)]
 
             return gather_parts(
                 place.copies, Line(send_sem, recv_sem),
-                pair_own.at[pl.ds(seq * positions, positions), columns], block, positions,
-                own_sem.at[8 + 2 * seq + part],
+                pair_own.at[pl.ds(seq * positions, positions)], block, positions, own_sem.at[3 + seq],
             )
 
         def soft_copy(seq, index, slot):
@@ -848,8 +836,7 @@
             place.tokens, Line(rs, rr), sent.at[pl.ds(0, positions)], rows_of(rows_first), positions,
             own_sem.at[7], place.twin,
         )
-        heads_a0, heads_b0 = pair_gather(0, 0, ka0, la0), pair_gather(0, 1, kb0, lb0)
-        heads_a1, heads_b1 = pair_gather(1, 0, ka1, la1), pair_gather(1, 1, kb1, lb1)
+        pair_gathers = [pair_gather(0, ks0, kr0), pair_gather(1, ks1, kr1)]
 
         greet(place.tokens.neighbours() + place.copies.neighbours() + [place.twin])
         for copy in packing:
@@ -890,13 +877,9 @@
         scaled = raw * root_mean(raw) * gain_k
         for chunk in range(KEY // LANES):
             at = slice(chunk * LANES, (chunk + 1) * LANES)
-            pair_own[:, pl.ds(key_low(chunk), LANES)] = turned(scaled[:, at], cos2, sin2).astype(bf16)
-        raw = dot(rows, weights(AT_V, KEY)).astype(bf16)
-        for chunk in range(KEY // LANES):
-            at = slice(chunk * LANES, (chunk + 1) * LANES)
-            pair_own[:, pl.ds(key_low(chunk) + KEY // 2, LANES)] = raw[:, at]
-        next(heads_a0)
-        next(heads_b0)
+            pair_own[:, at] = turned(scaled[:, at], cos2, sin2).astype(bf16)
+        pair_own[:, KEY:] = dot(rows, weights(AT_V, KEY)).astype(bf16)
+        next(pair_gathers[0])
         drained(query_gather)
         next(output_gather)
         next(grads[0])
@@ -906,18 +889,18 @@
         for chunk in range(QUERY // LANES):
             at = slice(chunk * LANES, (chunk + 1) * LANES)
             query_low[:, at] = turned(scaled[:, at], cos2, sin2).astype(bf16)
-        next(heads_a0)
-        next(heads_b0)
-        next(heads_a1)
+        next(pair_gathers[0])
+        next(pair_gathers[1])
         drained(output_gather)
         dense_copy = pltpu.make_async_copy(dense, dense_out, out_sem.at[0])
         dense_copy.start()
-        next(heads_a0)
         next(grads[0])
         next(grads[1])
-        next(heads_b0)
-        next(heads_b1)
-        drained(heads_a0)
+        next(pair_gathers[0])
+        next(pair_gathers[1])
+        next(grads[0])
+        drained(pair_gathers[0])
+        next(grads[1])
 
         def attend(seq, index, slot, wait_first):
             rows_at = pl.ds(seq * positions, positions)
@@ -926,7 +909,7 @@
                 query_low[rows_at, chunk_at(2 * index + 1)].astype(f32),
             )
             queries = (queries * score_scale).astype(bf16)
-            keys = pairs[seq, :, :, key_chunk(index)].reshape(length, LANES)
+            keys = pairs[seq, :, :, chunk_at(index)].reshape(length, LANES)
             scores = dot_nt(queries, keys).reshape(4, positions, length) + bias_box[seq][None]
             scores = scores.reshape(4 * positions, length)
             raised = jnp.exp(scores - jnp.max(scores, axis=1, keepdims=True))
@@ -938,7 +921,7 @@
 
             soft_box[slot] = soft
             soft_copy(seq, index, slot).start()
-            values = pairs[seq, :, :, key_chunk(index, KEY // 2)].reshape(length, LANES)
+            values = pairs[seq, :, :, chunk_at(index, KEY)].reshape(length, LANES)
             chunk_a, chunk_b = two_chunks(dot(soft, values))
             mixed[rows_at, chunk_at(2 * index)] = chunk_a.astype(bf16)
             mixed[rows_at, chunk_at(2 * index + 1)] = chunk_b.astype(bf16)
@@ -967,10 +950,9 @@
             hooks(
                 index,
                 (
-                    (0, lambda: next(heads_a1)),
                     (1, lambda: next(grads[0])),
-                    (2, lambda: (drained(heads_b0), next(heads_a1))[0]),
-                    (3, lambda: (next(heads_b1), next(grads[1]))[0]),
+                    (2, lambda: next(pair_gathers[1])),
+                    (3, lambda: next(grads[1])),
                 ),
             )
             attend(0, index, lax.rem(index, 2), index >= 2)
@@ -979,16 +961,15 @@
         lax.fori_loop(0, HEAD_PAIRS, first_heads, 0)
         features(0)
         next(first_rows)
-        next(heads_b1)
-        drained(heads_a1)
-        next(grads[0])
+        drained(pair_gathers[1])
+        pairs_copy = pltpu.make_async_copy(pairs, pairs_out, out_sem.at[1])
+        pairs_copy.start()
 
         def second_heads(index, carry):
             hooks(
                 index,
                 (
                     (1, lambda: next(grads[1])),
-                    (2, lambda: drained(heads_b1)),
                     (3, lambda: next(first_rows)),
                 ),
             )
@@ -996,8 +977,6 @@
             return carry
 
         lax.fori_loop(0, HEAD_PAIRS, second_heads, 0)
-        pairs_copy = pltpu.make_async_copy(pairs, pairs_out, out_sem.at[1])
-        pairs_copy.start()
         features(1)
         next(first_rows)
         drained(grads[0])
@@ -1036,15 +1015,20 @@
             pltpu.VMEM((2, 4 * positions, length), bf16),
             pltpu.VMEM((seqs, positions, length), f32),
         ]
-        + sems(GATHER_SEMS) * 10
+        + sems(GATHER_SEMS) * 8
         + [
-            pltpu.SemaphoreType.DMA((12,)),
+            pltpu.SemaphoreType.DMA((8,)),
             pltpu.SemaphoreType.DMA((2,)),
             pltpu.SemaphoreType.DMA((2,)),
             pltpu.SemaphoreType.DMA((4,)),
         ],
         compiler_params=params(collective_id),
     )(starts, tokens, cotangent, *weights_own, *gains, router, cosine, sine, routes)
+
+
+def key_chunk(index, base=0):
+    low = lax.div(index, 2) * KEY + lax.rem(index, 2) * LANES + base
+    return pl.ds(pl.multiple_of(low, LANES), LANES)
 
 
 def norm_back(values, gain, grad):
@@ -1071,14 +1055,14 @@
         query_raw_ref, key_raw_ref, query_ref, mixed_ref, pairs_ref, soft_ref, out_ref, expert_ref,
         cos_ref, sin_ref,
         block_out, tokens_grad, small_out, dense_out, expert_all,
-        weight_box, weight_rest, rest_terms, dense_own,
-        o_staged, q_staged, rest_staged, o_stage, q_stage, rest_stage,
-        out_held, out_staged, out_stage, small_terms, small_staged, small_stage, small_own, q_terms,
+        weight_box, weight_rest, wide_terms, rest_terms, dense_own,
+        wide_staged, rest_staged, wide_stage, rest_stage,
+        out_held, out_staged, out_stage, small_terms, small_staged, small_stage, small_own,
         soft_box, key_box, value_box, pair_terms, pair_stage, pair_grads,
         grad_mixed, grad_query, grad_middle, grad_attn, grad_attn_in, gain_box,
-        o_got, q_got, rest_got, small_got, totals,
-        out_s, out_r, small_s, small_r, kv0_s, kv0_r, kva_s, kva_r, kvb_s, kvb_r, o_s, o_r, q_s, q_r, rest_s, rest_r,
-        ge_s, ge_r, go_s, go_r, gq_s, gq_r, grest_s, grest_r, gsmall_s, gsmall_r,
+        wide_got, rest_got, small_got, wide_total_box, rest_total_box,
+        out_s, out_r, small_s, small_r, kv0_s, kv0_r, kva_s, kva_r, kvb_s, kvb_r, wide_s, wide_r, rest_s, rest_r,
+        ge_s, ge_r, gwide_s, gwide_r, grest_s, grest_r, gsmall_s, gsmall_r,
         load_sem, held_sem, box_sem, own_sem, total_sem,
     ):
         place = Place()
@@ -1120,46 +1104,39 @@
         def rows_of_block(terms, index, low, n):
             return terms.at[pl.ds(index * ROWS_OWN + low, n)]
 
-        def rows_of_pairs(terms, index, low, n):
-            at = lax.rem(index, 2) * ROWS_OWN + low
-            return terms.at[0, lax.div(index, 2), pl.ds(at, n)]
-
-        def dense_sum(rows_of, terms, staged, stage, own, send_sem, recv_sem):
+        def dense_sum(terms, staged, stage, own, send_sem, recv_sem):
             return sum_parts(
                 token_axes, Line(send_sem, recv_sem),
-                lambda which, row, n: rows_of(terms, blocks(which), row, n),
+                lambda which, row, n: rows_of_block(terms, blocks(which), row, n),
                 stage, ROWS_OWN, own,
-                (place.twin, lambda which: rows_of(terms, blocks(which, True), 0, ROWS_OWN),
+                (place.twin, lambda which: rows_of_block(terms, blocks(which, True), 0, ROWS_OWN),
                  lambda which: staged.at[chip_of(which)]),
             )
 
-        def own_columns(low):
-            return dense_own.at[:, pl.ds(low, width)]
-
-        o_sum = dense_sum(rows_of_pairs, pair_terms, o_staged, o_stage, own_columns(AT_O), o_s, o_r)
-        q_sum = dense_sum(rows_of_block, q_terms, q_staged, q_stage, own_columns(0), q_s, q_r)
+        wide_sum = dense_sum(
+            wide_terms, wide_staged, wide_stage, dense_own.at[:, pl.ds(0, QUERY + width)], wide_s, wide_r
+        )
         rest_sum = dense_sum(
-            rows_of_block, rest_terms, rest_staged, rest_stage, own_columns(AT_K), rest_s, rest_r
-        )
-        small_sum = dense_sum(
-            rows_of_block, small_terms, small_staged, small_stage, small_own, small_s, small_r
-        )
-
-        def dense_total(index, low, got, send_sem, recv_sem):
-            def own(rep):
-                return dense_own.at[:, chunk_at(rep, low)]
-
-            def target(rep):
-                return dense_out.at[:, chunk_at(rep, low)]
+            rest_terms, rest_staged, rest_stage, dense_own.at[:, pl.ds(QUERY + width, 2 * KEY)],
+            rest_s, rest_r,
+        )
+        small_sum = dense_sum(small_terms, small_staged, small_stage, small_own, small_s, small_r)
+
+        def dense_total(index, low, size, got, total, send_sem, recv_sem):
+            share = size // REPS
+
+            def columns(rep):
+                return pl.ds(pl.multiple_of(low + rep * share, LANES), share)
 
             return total_parts(
-                place, Line(send_sem, recv_sem), own, got, totals.at[index], target,
-                total_sem.at[index],
-            )
-
-        o_total = dense_total(0, AT_O, o_got, go_s, go_r)
-        q_total = dense_total(1, 0, q_got, gq_s, gq_r)
-        rest_total = dense_total(2, AT_K, rest_got, grest_s, grest_r)
+                place, Line(send_sem, recv_sem), lambda rep: dense_own.at[:, columns(rep)], got, total,
+                lambda rep: dense_out.at[:, columns(rep)], total_sem.at[index],
+            )
+
+        wide_total = dense_total(0, 0, QUERY + width, wide_got, wide_total_box, gwide_s, gwide_r)
+        rest_total = dense_total(
+            1, QUERY + width, 2 * KEY, rest_got, rest_total_box, grest_s, grest_r
+        )
         small_total = spread_parts(place, Line(gsmall_s, gsmall_r), small_own, small_got, small_out)
         expert_gather = gather_parts(
             copy_axes, Line(ge_s, ge_r), expert_ref,
@@ -1189,10 +1166,10 @@
                     soft_ref.at[seq, index], soft_box.at[slot], box_sem.at[slot, 0]
                 ),
                 pltpu.make_async_copy(
-                    pairs_ref.at[seq, :, :, key_chunk(index)], key_box.at[slot], box_sem.at[slot, 1]
+                    pairs_ref.at[seq, :, :, chunk_at(index)], key_box.at[slot], box_sem.at[slot, 1]
                 ),
                 pltpu.make_async_copy(
-                    pairs_ref.at[seq, :, :, key_chunk(index, KEY // 2)],
+                    pairs_ref.at[seq, :, :, chunk_at(index, KEY)],
                     value_box.at[slot],
                     box_sem.at[slot, 2],
                 ),
@@ -1208,7 +1185,6 @@
             + [(place.shard, other) for other in place.others[1:]]
         )
         next(out_sum)
-        next(expert_gather)
         rest_load.wait()
 
         small = weight_rest[:, :, pl.ds(2 * KEY, SMALL)].reshape(width, SMALL)
@@ -1330,31 +1306,23 @@
         next(second_pairs[1])
         next(first_pairs)
         next(second_pairs[0])
-        next(second_pairs[1])
-        next(expert_gather)
-        next(out_sum)
-        drained(first_pairs)
-
-        def o_rows(index, carry):
-            at = chunk_256(index)
-            value = dot_tn(mixed_ref[:, at], grad_attn[...]).astype(bf16)
-            pair_terms[0, pl.ds(2 * index, 2)] = value.reshape(2, positions, width)
-            return carry
-
-        lax.fori_loop(0, QUERY // 256, o_rows, 0)
-        next(o_sum)
 
         def q_rows(index, carry):
             at = chunk_256(index)
-            q_terms[at] = dot_tn(attn_ref[:, at], grad_query_low).astype(bf16)
+            wide_terms[at, pl.ds(0, QUERY)] = dot_tn(attn_ref[:, at], grad_query_low).astype(bf16)
+            wide_terms[at, pl.ds(QUERY, width)] = dot_tn(mixed_ref[:, at], grad_attn[...]).astype(bf16)
             return carry
 
         lax.fori_loop(0, width // 256, q_rows, 0)
-        next(q_sum)
-        next(o_sum)
-        next(o_sum)
+        next(wide_sum)
+        next(second_pairs[1])
+        next(out_sum)
+        next(wide_sum)
+        next(wide_sum)
+        drained(first_pairs)
         drained(second_pairs[0])
         drained(second_pairs[1])
+        next(expert_gather)
 
         grads = pair_grads[...]
         half = KEY // 2
@@ -1393,47 +1361,39 @@
         tokens_grad[...] = (grad_middle[...] + inner).astype(bf16)
         next(small_sum)
         next(small_sum)
-        next(q_sum)
-        next(q_sum)
+        next(wide_sum)
         next(rest_sum)
-        next(o_sum)
+        next(expert_gather)
         next(small_sum)
-        next(expert_gather)
-        next(q_sum)
-        next(o_sum)
+        next(wide_sum)
         next(small_sum)
         next(rest_sum)
-        next(q_sum)
         drained(out_sum)
-        drained(o_sum)
-        next(o_total)
+        drained(wide_sum)
+        next(wide_total)
         drained(small_sum)
         next(small_total)
-        drained(q_sum)
-        next(q_total)
-        next(o_total)
+        next(expert_gather)
         drained(rest_sum)
         next(rest_total)
-        next(q_total)
+        next(wide_total)
+        next(expert_gather)
         drained(small_total)
-        next(expert_gather)
         next(rest_total)
         drained(expert_gather)
-        drained(o_total)
-        drained(q_total)
+        drained(wide_total)
         drained(rest_total)
 
     block = pltpu.VMEM((GROUP, ROWS_OWN, width), bf16)
     scratch = [
         block,
         pltpu.VMEM((GROUP, ROWS_OWN, REST), bf16),
+        pltpu.VMEM((width, QUERY + width), bf16),
         pltpu.VMEM((width, 2 * KEY), bf16),
-        pltpu.VMEM((ROWS_OWN, PACKED), bf16),
-        pltpu.VMEM((chips, ROWS_OWN, width), bf16),
-        pltpu.VMEM((chips, ROWS_OWN, QUERY), bf16),
+        pltpu.VMEM((ROWS_OWN, DENSE), bf16),
+        pltpu.VMEM((chips, ROWS_OWN, QUERY + width), bf16),
         pltpu.VMEM((chips, ROWS_OWN, 2 * KEY), bf16),
-        pltpu.VMEM((stage_rows(ROWS_OWN), width), bf16),
-        pltpu.VMEM((stage_rows(ROWS_OWN), QUERY), bf16),
+        pltpu.VMEM((stage_rows(ROWS_OWN), QUERY + width), bf16),
         pltpu.VMEM((stage_rows(ROWS_OWN), 2 * KEY), bf16),
         pltpu.VMEM((chips, count, width), bf16),
         pltpu.VMEM((chips, count, width), bf16),
@@ -1442,7 +1402,6 @@
         pltpu.VMEM((chips, ROWS_OWN, SMALL), bf16),
         pltpu.VMEM((stage_rows(ROWS_OWN), SMALL), bf16),
         pltpu.VMEM((ROWS_OWN, SMALL), bf16),
-        pltpu.VMEM((width, QUERY), bf16),
         pltpu.VMEM((2, 4 * positions, length), bf16),
         pltpu.VMEM((2, REPS, positions, LANES), bf16),
         pltpu.VMEM((2, REPS, positions, LANES), bf16),
@@ -1456,29 +1415,35 @@
         pltpu.VMEM((count, width), f32),
         pltpu.VMEM((SMALL, width), f32),
     ]
-    scratch += [pltpu.VMEM((REPS, ROWS_OWN, LANES), bf16)] * 4
-    scratch += [pltpu.VMEM((3, ROWS_OWN, LANES), bf16)]
+    wide_share, rest_share = (QUERY + width) // REPS, 2 * KEY // REPS
+    scratch += [
+        pltpu.VMEM((REPS, ROWS_OWN, wide_share), bf16),
+        pltpu.VMEM((REPS, ROWS_OWN, rest_share), bf16),
+        pltpu.VMEM((REPS, ROWS_OWN, SMALL), bf16),
+        pltpu.VMEM((ROWS_OWN, wide_share), bf16),
+        pltpu.VMEM((ROWS_OWN, rest_share), bf16),
+    ]
     return pl.pallas_call(
         kernel,
         out_shape=[
             jax.ShapeDtypeStruct((count, width), bf16),
             jax.ShapeDtypeStruct((count, width), bf16),
             jax.ShapeDtypeStruct((ROWS_OWN, SMALL), f32),
-            jax.ShapeDtypeStruct((ROWS_OWN, PACKED), bf16),
+            jax.ShapeDtypeStruct((ROWS_OWN, DENSE), bf16),
             jax.ShapeDtypeStruct((REPS, expert_rows, width), bf16),
         ],
         in_specs=[IN_VMEM] * 4 + [ANY] + [IN_VMEM] * 7 + [ANY] * 4 + [IN_VMEM] * 2,
         out_specs=[IN_VMEM, IN_VMEM, IN_VMEM, ANY, ANY],
         scratch_shapes=scratch
-        + sems(SUM_SEMS) * 8
+        + sems(SUM_SEMS) * 7
         + sems(GATHER_SEMS)
-        + sems(TOTAL_SEMS) * 4
+        + sems(TOTAL_SEMS) * 3
         + [
             pltpu.SemaphoreType.DMA((4,)),
             pltpu.SemaphoreType.DMA((chips,)),
             pltpu.SemaphoreType.DMA((2, 3)),
             pltpu.SemaphoreType.DMA,
-            pltpu.SemaphoreType.DMA((3,)),
+            pltpu.SemaphoreType.DMA((2,)),
         ],
         compiler_params=params(collective_id),
     )(
@@ -1504,7 +1469,8 @@
 
         @pl.when(pl.program_id(0) == 1)
         def _():
-            for low, target in ((0, query), (AT_K, key), (AT_V, value), (AT_O, output)):
+            at_k = QUERY + WIDTH
+            for low, target in ((0, query), (at_k, key), (at_k + KEY, value), (QUERY, output)):
                 target[...] = dense_ref[:, pl.ds(low, target.shape[1])].astype(f32)
             turned_small = jnp.transpose(small_ref[...])
             router[...] = turned_small[:EXPERTS, :ROWS_OWN]

time: 298 us -> 296 us (level)
  no operation moved by 1% of the time
where the time goes in v9:
time: 296 us
  Pallas kernels  294 us (99%)
    pallas_call x1, Pallas kernels, back_call(): pl.pallas_call(kernel, out_shape=[jax.ShapeDtypeStruct((count, width), bf...  106 us
    pallas_call x1, Pallas kernels, front_call(): pl.pallas_call(kernel, out_shape=[jax.ShapeDtypeStruct((GROUP, ROWS_OWN,...  97.5 us
    pallas_call x1, Pallas kernels, moe_call(): pl.pallas_call(kernel, out_shape=[jax.ShapeDtypeStruct((count, columns),...  82.6 us
    pallas_call x1, Pallas kernels, finish_call(): pl.pallas_call(kernel, grid=(reps,), out_shape=[jax.ShapeDtypeStruct(bloc...  7.8 us

profile of v9, /device:TPU:0, one launch (start us, length us, event | category | flops | bytes accessed | tf_op | source)
XLA Modules:
  0.0 295.8 jit_solution(333175922087100091)
XLA Ops:
  0.7 1.0 fusion
  1.6 97.5 %shard_map.246 = (bf16[16,64,3200]{2,1,0:T(8,128)(2,1)}, bf16[16,256,1024]{2,1,0:T(8,128)(2,1)}, bf16[2,8,128,1024]{3,2,1,0:T(8,128)(2,1)}, bf16[2,4,512,1024]{3...) custom-call(s32[2,2]{1,0:T(2,128)} %starts_ref.1, ...), custom_call_target="tpu_custom_call" | custom-call | tf_op jit(solution)/shard_map/pallas_call | solution.py:990
  99.1 82.6 %shard_map.247 = (bf16[256,1152]{1,0:T(8,128)(2,1)}, bf16[192,1024]{1,0:T(8,128)(2,1)}, bf16[16,256,1024]{2,1,0:T(8,128)(2,1)}) custom-call(bf16[256,1152]{1,0:T(8,128)(2,1)} %get-tuple-element.47.sent_ref, bf16[16,128,1152]{2,1,0:T(8,128)(2,1)} %get-tuple-element.48.first_ref, bf16[16,256,1024]{2,1,0:T(8,128)(2,1)} %get-tuple-element.49.grad_ref, ...), custom_call_target="tpu_custom_call" | custom-call | tf_op jit(solution)/shard_map/pallas_call | solution.py:629
  181.7 106.1 %shard_map.248 = (bf16[256,1024]{1,0:T(8,128)(2,1)}, bf16[256,1024]{1,0:T(8,128)(2,1)}, f32[64,128]{1,0:T(8,128)}, bf16[64,3072]{1,0:T(8,128)(2,1)}, bf16[8,192,1024]{2,1,0:T(8,128)(2,1)}) custom-call(bf16[256,1152]{1,0:T(8,128)(2,1)} %get-tuple-element.50.returned_ref, f32[256,128]{1,0:T(8,128)} %get-tuple-element.51.gates_ref, ...), custom_call_target="tpu_custom_call" | custom-call | tf_op jit(solution)/shard_map/pallas_call | solution.py:1426
  287.8 7.8 %shard_map.249 = (bf16[256,1024]{1,0:T(8,128)(2,1)}, bf16[256,1024]{1,0:T(8,128)(2,1)}, f32[2,512,1024]{2,1,0:T(8,128)}, f32[512,1024]{1,0:T(8,128)}, f32[64,102...) custom-call(bf16[256,1024]{1,0:T(8,128)(2,1)} %get-tuple-element.63., ...), custom_call_target="tpu_custom_call" | custom-call | tf_op jit(solution)/shard_map/pallas_call | solution.py:1487
  (2 shorter events, 0.0 us)

commit v10 on v6

--- a/solution.py
+++ b/solution.py
@@ -12,7 +12,7 @@
 RING = 4
 GROUP = 16
 REPS = 8
-VMEM_LIMIT = 62 << 20
+VMEM_LIMIT = 63 << 20
 
 norm_eps = 1e-06
 rope_base = 10000.0
@@ -672,26 +672,23 @@
 
 
 def turned(values, cosine, sine):
-    first = lax.rem(lane_of(values.shape), HEAD_DIM) < HEAD_DIM // 2
+    first = (lane_of(values.shape) & (HEAD_DIM - 1)) < HEAD_DIM // 2
     swapped = jnp.where(
         first, pltpu.roll(values, LANES - HEAD_DIM // 2, 1), pltpu.roll(values, HEAD_DIM // 2, 1)
     )
     return values * cosine + swapped * sine
 
 
-def short_rows():
-    row = lax.broadcasted_iota(jnp.int32, (WIDTH, KEY), 0)
-    column = lax.broadcasted_iota(jnp.int32, (WIDTH, KEY), 1)
-    same = (lax.div(row, ROWS_OWN) == lax.div(column, KGAIN_OWN)) & (
-        lax.rem(row, ROWS_OWN) == lax.rem(column, KGAIN_OWN)
-    )
-    return jnp.where(same, 1.0, 0.0).astype(bf16)
-
-
 def gain_rows(small):
     rows = jnp.transpose(small.astype(f32))
-    gain_k = dot(rows[EXPERTS : EXPERTS + 8].astype(bf16), short_rows())[3:4]
+    short = small.reshape(GROUP, ROWS_OWN, SMALL)[:, :KGAIN_OWN].reshape(KEY, SMALL)
+    gain_k = jnp.transpose(short.astype(f32))[EXPERTS + 3 : EXPERTS + 4]
     return rows[EXPERTS : EXPERTS + 1], rows[EXPERTS + 1 : EXPERTS + 2], rows[EXPERTS + 2 : EXPERTS + 3], gain_k
+
+
+def long_column(columns):
+    cut = columns.reshape(GROUP, KGAIN_OWN, SMALL)
+    return jnp.concatenate([cut, jnp.zeros_like(cut)], axis=1).reshape(WIDTH, SMALL)
 
 
 def four_heads(chunk_a, chunk_b):
@@ -722,7 +719,7 @@
     return pl.ds(pl.multiple_of(base + index * LANES, LANES), LANES)
 
 
-def front_call(collective_id, tokens, cotangent, weights_own, small_own, cosine, sine, routes, starts):
+def front_call(collective_id, tokens, cotangent, weights_own, gains, router, cosine, sine, routes, starts):
     count, width = tokens.shape
     seqs = starts.shape[0]
     positions = count // seqs
@@ -731,11 +728,11 @@
     sent_width = width + SMALL
 
     def kernel(
-        starts_ref, tokens_ref, grad_ref, query_w, key_w, value_w, output_w, small_ref,
-        cos_ref, sin_ref, routes_ref,
+        starts_ref, tokens_ref, grad_ref, query_w, key_w, value_w, output_w,
+        gain_a_ref, gain_q_ref, gain_f_ref, gain_k_ref, router_ref, cos_ref, sin_ref, routes_ref,
         dense_out, grad_all, pairs_out, soft_out, rows_first,
         attn_in, query_raw, key_raw, query_low, mixed, middle, sent, gates_out,
-        packed, dense, pairs, pair_own, soft_box, bias_box,
+        packed, small_box, dense, pairs, pair_own, soft_box, bias_box,
         ws0, wr0, ws1, wr1, ws2, wr2, gs0, gr0, gs1, gr1, ks0, kr0, ks1, kr1, rs, rr, own_sem, out_sem, soft_sem, pack_sem,
     ):
         place = Place()
@@ -745,11 +742,19 @@
                 source, packed.at[:, pl.ds(low, source.shape[1])], pack_sem.at[index]
             )
             for index, (source, low) in enumerate(
-                ((key_w, AT_K), (value_w, AT_V), (small_ref, AT_S), (query_w, 0), (output_w, AT_O))
+                ((key_w, AT_K), (value_w, AT_V), (query_w, 0), (output_w, AT_O))
             )
         ]
         for copy in packing:
             copy.start()
+        small_box[...] = jnp.zeros_like(small_box)
+        small_box[pl.ds(0, EXPERTS), pl.ds(0, ROWS_OWN)] = router_ref[...].astype(f32)
+        for at, ref in enumerate((gain_a_ref, gain_q_ref, gain_f_ref, gain_k_ref)):
+            size = ref.shape[0]
+            small_box[pl.ds(EXPERTS + at, 1), pl.ds(0, size)] = (
+                ref[...].astype(f32).reshape(1, size)
+            )
+        packed[:, pl.ds(AT_S, SMALL)] = jnp.transpose(small_box[...])[:ROWS_OWN].astype(bf16)
 
         def token_block(index, low, size):
             def block(which, row, n, other=False):
@@ -811,12 +816,10 @@
         for copy in packing:
             copy.wait()
         next(rest_gather)
-        next(query_gather)
         inputs = tokens_ref[...].astype(f32)
         middle[...] = inputs * root_mean(inputs)
         next(rest_gather)
         next(query_gather)
-        next(output_gather)
         query_at = place.rep * positions + lax.broadcasted_iota(jnp.int32, (positions, 1), 0)
         key_at = lax.broadcasted_iota(jnp.int32, (1, length), 1)
         for seq in range(seqs):
@@ -831,6 +834,8 @@
         next(query_gather)
         next(output_gather)
         drained(rest_gather)
+        next(query_gather)
+        next(output_gather)
 
         def weights(low, size):
             return dense[:, :, pl.ds(low, size)].reshape(width, size)
@@ -902,7 +907,7 @@
             ffn_in = (total * root_mean(total) * gain_f).astype(bf16)
             sent[at, pl.ds(0, width)] = ffn_in
             lanes = lane_of((positions, SMALL))
-            named = routes_ref[at]
+            named = jnp.transpose(routes_ref[seq].astype(f32)).astype(jnp.int32)
             chosen = lanes == named[:, :1]
             for choice in range(1, named.shape[1]):
                 chosen = chosen | (lanes == named[:, choice : choice + 1])
@@ -973,10 +978,11 @@
             jax.ShapeDtypeStruct((count, width + SMALL), bf16),
             jax.ShapeDtypeStruct((count, SMALL), f32),
         ],
-        in_specs=[pl.BlockSpec(memory_space=pltpu.SMEM), IN_VMEM] + [ANY] * 6 + [IN_VMEM] * 3,
+        in_specs=[pl.BlockSpec(memory_space=pltpu.SMEM), IN_VMEM] + [ANY] * 5 + [IN_VMEM] * 8,
         out_specs=[ANY] * 5 + [IN_VMEM] * 8,
         scratch_shapes=[
             pltpu.VMEM((ROWS_OWN, PACKED), bf16),
+            pltpu.VMEM((SMALL, LANES), f32),
             pltpu.VMEM((GROUP, ROWS_OWN, PACKED), bf16),
             pltpu.VMEM((seqs, REPS, positions, 2 * KEY), bf16),
             pltpu.VMEM((count, 2 * KEY), bf16),
@@ -988,10 +994,15 @@
             pltpu.SemaphoreType.DMA((8,)),
             pltpu.SemaphoreType.DMA((2,)),
             pltpu.SemaphoreType.DMA((2,)),
-            pltpu.SemaphoreType.DMA((5,)),
+            pltpu.SemaphoreType.DMA((4,)),
         ],
         compiler_params=params(collective_id),
-    )(starts, tokens, cotangent, *weights_own, small_own, cosine, sine, routes)
+    )(starts, tokens, cotangent, *weights_own, *gains, router, cosine, sine, routes)
+
+
+def key_chunk(index, base=0):
+    low = lax.div(index, 2) * KEY + lax.rem(index, 2) * LANES + base
+    return pl.ds(pl.multiple_of(low, LANES), LANES)
 
 
 def norm_back(values, gain, grad):
@@ -1024,7 +1035,7 @@
         soft_box, key_box, value_box, pair_terms, pair_stage, pair_grads,
         grad_mixed, grad_query, grad_middle, grad_attn, grad_attn_in, gain_box,
         o_got, q_got, rest_got, small_got, totals,
-        out_s, out_r, exp_s, exp_r, kv0_s, kv0_r, kv1_s, kv1_r, o_s, o_r, q_s, q_r, rest_s, rest_r,
+        out_s, out_r, exp_s, exp_r, kv0_s, kv0_r, kva_s, kva_r, kvb_s, kvb_r, o_s, o_r, q_s, q_r, rest_s, rest_r,
         ge_s, ge_r, go_s, go_r, gq_s, gq_r, grest_s, grest_r,
         load_sem, held_sem, box_sem, own_sem, total_sem,
     ):
@@ -1057,14 +1068,17 @@
             expert_stage, expert_rows, expert_own,
         )
 
-        def pair_sum(seq, send_sem, recv_sem):
+        def pair_sum(seq, low, size, send_sem, recv_sem):
+            columns = pl.ds(low, size)
             return sum_parts(
                 copy_axes, Line(send_sem, recv_sem),
-                lambda which, low, n: pair_terms.at[seq, chip_of(which), pl.ds(low, n)],
-                pair_stage.at[seq], positions, pair_grads.at[pl.ds(seq * positions, positions)],
-            )
-
-        pair_sums = [pair_sum(0, kv0_s, kv0_r), pair_sum(1, kv1_s, kv1_r)]
+                lambda which, row, n: pair_terms.at[seq, chip_of(which), pl.ds(row, n), columns],
+                pair_stage.at[seq, :, columns], positions,
+                pair_grads.at[pl.ds(seq * positions, positions), columns],
+            )
+
+        first_pairs = pair_sum(0, 0, 2 * KEY, kv0_s, kv0_r)
+        second_pairs = [pair_sum(1, 0, KEY, kva_s, kva_r), pair_sum(1, KEY, KEY, kvb_s, kvb_r)]
 
         def rows_of_block(terms, index, low, n):
             return terms.at[pl.ds(index * ROWS_OWN + low, n)]
@@ -1204,7 +1218,7 @@
             values = value_box[slot].reshape(length, LANES)
             soft_low = soft_box[slot]
             value_terms = dot_tn(soft_low, grads)
-            pair_terms[seq, :, :, chunk_at(index, KEY)] = value_terms.astype(bf16).reshape(
+            pair_terms[seq, :, :, key_chunk(index, KEY // 2)] = value_terms.astype(bf16).reshape(
                 REPS, positions, LANES
             )
             soft_full = soft_low.astype(f32)
@@ -1214,7 +1228,7 @@
                 weighted - soft_full * jnp.sum(weighted, axis=1, keepdims=True)
             ).astype(bf16)
             key_terms = dot_tn(grad_scores, queries)
-            pair_terms[seq, :, :, chunk_at(index)] = key_terms.astype(bf16).reshape(
+            pair_terms[seq, :, :, key_chunk(index)] = key_terms.astype(bf16).reshape(
                 REPS, positions, LANES
             )
             chunk_a, chunk_b = two_chunks(dot(grad_scores, keys) * score_scale)
@@ -1233,20 +1247,23 @@
             return carry
 
         lax.fori_loop(0, HEAD_PAIRS, first_heads, 0)
-        next(pair_sums[0])
-        next(pair_sums[0])
-        next(pair_sums[0])
+        for _ in range(3):
+            next(first_pairs)
+
+        def begin_second():
+            for _ in range(3):
+                next(second_pairs[0])
 
         def second_heads(index, carry):
-            hooks(index, ((3, lambda: next(out_sum)),))
+            hooks(index, ((2, begin_second), (3, lambda: next(out_sum))))
             attend_back(1, index)
             return carry
 
         lax.fori_loop(0, HEAD_PAIRS, second_heads, 0)
-        next(pair_sums[1])
-        next(pair_sums[1])
-        next(pair_sums[1])
-        next(pair_sums[0])
+        for _ in range(3):
+            next(second_pairs[1])
+        next(first_pairs)
+        next(second_pairs[0])
         router_terms = dot_tn(sent_ref[:, pl.ds(0, width)], grad_logits)
 
         cos2 = jnp.concatenate([cos_ref[...]] * seqs, axis=0)
@@ -1269,12 +1286,13 @@
         weight_load(0, 3).wait()
         grad_attn_in[...] = dot_nt(grad_query_low, weight_box[...].reshape(width, QUERY))
 
-        next(pair_sums[1])
+        next(second_pairs[1])
+        next(first_pairs)
+        next(second_pairs[0])
+        next(second_pairs[1])
         next(expert_sum)
         next(out_sum)
-        next(pair_sums[0])
-        drained(pair_sums[0])
-        next(pair_sums[1])
+        drained(first_pairs)
 
         def o_rows(index, carry):
             at = chunk_256(index)
@@ -1300,19 +1318,22 @@
         next(q_sum)
         next(q_sum)
         next(o_sum)
-        drained(pair_sums[1])
+        drained(second_pairs[0])
+        drained(second_pairs[1])
 
         grads = pair_grads[...]
+        half = KEY // 2
+        key_grads = jnp.concatenate([grads[:, :half], grads[:, KEY : KEY + half]], axis=1)
+        value_grads = jnp.concatenate([grads[:, half:KEY], grads[:, KEY + half :]], axis=1)
         grad, gain_k_terms = norm_back(
-            key_raw_ref[...],
-            gain_k,
-            turned_back(grads[:, :KEY].astype(bf16).astype(f32)),
-        )
-        grad_pairs = jnp.concatenate([grad.astype(bf16), grads[:, KEY:].astype(bf16)], axis=1)
-        gain_k_row = dot_nt(
-            jnp.broadcast_to(gain_k_terms, (8, KEY)).astype(bf16), short_rows()
-        )
-        gain_box[pl.ds(EXPERTS + 3, 1)] = gain_k_row[:1]
+            key_raw_ref[...], gain_k, turned_back(key_grads.astype(bf16).astype(f32))
+        )
+        grad_pairs = jnp.concatenate([grad.astype(bf16), value_grads.astype(bf16)], axis=1)
+        gain_k_column = jnp.where(
+            lane_of((KEY, SMALL)) == EXPERTS + 3,
+            jnp.transpose(jnp.broadcast_to(gain_k_terms, (SMALL, KEY))),
+            0.0,
+        )
         grad = grad_attn_in[...] + dot_nt(
             grad_pairs, weight_rest[:, :, pl.ds(0, 2 * KEY)].reshape(width, 2 * KEY)
         )
@@ -1321,7 +1342,7 @@
         tokens_grad[...] = (grad_middle[...] + inner).astype(bf16)
         gain_box[pl.ds(EXPERTS, 1)] = gain_a_terms
         rest_terms[:, pl.ds(2 * KEY, SMALL)] = (
-            router_terms + jnp.transpose(gain_box[...])
+            router_terms + jnp.transpose(gain_box[...]) + long_column(gain_k_column)
         ).astype(bf16)
 
         def rest_rows(index, carry):
@@ -1398,7 +1419,7 @@
         in_specs=[IN_VMEM] * 4 + [ANY] + [IN_VMEM] * 7 + [ANY] * 4 + [IN_VMEM] * 2,
         out_specs=[IN_VMEM, IN_VMEM, ANY, ANY],
         scratch_shapes=scratch
-        + sems(SUM_SEMS) * 7
+        + sems(SUM_SEMS) * 8
         + sems(GATHER_SEMS)
         + sems(TOTAL_SEMS) * 3
         + [
@@ -1415,51 +1436,71 @@
     )
 
 
-def finish_call(dense_own, expert_all, inner_rows):
+def finish_call(block_out, tokens_grad, dense_own, expert_all, inner_rows):
     total_rows, width = expert_all.shape
     step = 256
     inner_steps, steps = inner_rows // step, total_rows // step
-
-    def kernel(dense_ref, expert_ref, inner, outer, query, key, value, output, small):
+    rows = block_out.shape[0] // inner_steps
+
+    def kernel(
+        block_ref, tokens_ref, dense_ref, expert_ref,
+        block, tokens, inner, outer, query, key, value, output, router, gain_a, gain_q, gain_f, gain_k,
+    ):
         at = pl.program_id(0)
-        rows = expert_ref[...].astype(f32)
 
         @pl.when(at < inner_steps)
         def _():
-            inner[...] = rows
+            block[...] = block_ref[...]
+            tokens[...] = tokens_ref[...]
+            inner[...] = expert_ref[...].astype(f32)
 
         @pl.when(at >= inner_steps)
         def _():
-            outer[...] = rows
+            outer[...] = expert_ref[...].astype(f32)
 
         @pl.when(at == 1)
         def _():
-            for low, target in ((0, query), (AT_K, key), (AT_V, value), (AT_O, output), (AT_S, small)):
+            for low, target in ((0, query), (AT_K, key), (AT_V, value), (AT_O, output)):
                 target[...] = dense_ref[:, pl.ds(low, target.shape[1])].astype(f32)
-
-    def whole(columns):
-        return pl.BlockSpec((ROWS_OWN, columns), lambda i: (0, 0))
-
-    sizes = (QUERY, KEY, KEY, WIDTH, SMALL)
+            turned_small = jnp.transpose(dense_ref[:, pl.ds(AT_S, SMALL)].astype(f32))
+            router[...] = turned_small[:EXPERTS, :ROWS_OWN]
+            for index, target in enumerate((gain_a, gain_q, gain_f, gain_k)):
+                size = target.shape[0]
+                target[...] = turned_small[EXPERTS + index, :size].reshape(size)
+
+    def whole(*shape):
+        return pl.BlockSpec(shape, lambda i: (0,) * len(shape))
+
+    def by_rows(size):
+        return pl.BlockSpec((size, width), lambda i: (jnp.minimum(i, inner_steps - 1), 0))
+
+    shapes = [(ROWS_OWN, QUERY), (ROWS_OWN, KEY), (ROWS_OWN, KEY), (ROWS_OWN, WIDTH)]
+    shapes += [(EXPERTS, ROWS_OWN), (ROWS_OWN,), (ROWS_OWN,), (ROWS_OWN,), (KGAIN_OWN,)]
     return pl.pallas_call(
         kernel,
         grid=(steps,),
         out_shape=[
+            jax.ShapeDtypeStruct(block_out.shape, bf16),
+            jax.ShapeDtypeStruct(tokens_grad.shape, bf16),
             jax.ShapeDtypeStruct((inner_rows, width), f32),
             jax.ShapeDtypeStruct((total_rows - inner_rows, width), f32),
         ]
-        + [jax.ShapeDtypeStruct((ROWS_OWN, size), f32) for size in sizes],
+        + [jax.ShapeDtypeStruct(shape, f32) for shape in shapes],
         in_specs=[
-            pl.BlockSpec(dense_own.shape, lambda i: (0, 0)),
+            by_rows(rows),
+            by_rows(rows),
+            whole(*dense_own.shape),
             pl.BlockSpec((step, width), lambda i: (i, 0)),
         ],
         out_specs=[
-            pl.BlockSpec((step, width), lambda i: (jnp.minimum(i, inner_steps - 1), 0)),
+            by_rows(rows),
+            by_rows(rows),
+            by_rows(step),
             pl.BlockSpec((step, width), lambda i: (jnp.maximum(i - inner_steps, 0), 0)),
         ]
-        + [whole(size) for size in sizes],
+        + [whole(*shape) for shape in shapes],
         compiler_params=pltpu.CompilerParams(vmem_limit_bytes=VMEM_LIMIT),
-    )(dense_own, expert_all)
+    )(block_out, tokens_grad, dense_own, expert_all)
 
 
 def rotary_tables(positions):
@@ -1470,16 +1511,6 @@
     angles = positions.astype(f32)[:, None] * frequency[None, :]
     sign = jnp.where(lane % HEAD_DIM < half, -1.0, 1.0).astype(f32)
     return jnp.cos(angles), jnp.sin(angles) * sign[None, :]
-
-
-def small_columns(router, gain_a, gain_q, gain_f, gain_k):
-    rows = router.shape[0]
-    lane = jnp.arange(SMALL)[None, :]
-    small = jnp.pad(router, ((0, 0), (0, SMALL - EXPERTS)))
-    short = jnp.pad(gain_k, (0, rows - gain_k.shape[0]))
-    for at, gain in enumerate((gain_a, gain_q, gain_f, short)):
-        small = jnp.where(lane == EXPERTS + at, gain[:, None], small)
-    return small
 
 
 def shards(
@@ -1510,8 +1541,8 @@
         attn_in, query_raw, key_raw, query_low, mixed, middle, sent, gates,
     ) = front_call(
         1, rows, grad_rows, (query_weight, key_weight, value_weight, output_weight),
-        small_columns(router_weight, attn_gain, query_gain, ffn_gain, key_gain),
-        cosine, sine, routes.reshape(count, routes.shape[2]), picture_starts,
+        (attn_gain, query_gain, ffn_gain, key_gain), router_weight.T,
+        cosine, sine, jnp.transpose(routes, (0, 2, 1)), picture_starts,
     )
     returned, out_terms, expert_terms = moe_call(
         2, sent, rows_first, grad_all, expert_in[0], expert_down[0]
@@ -1520,21 +1551,23 @@
         3, returned, gates, middle, sent, dense, grad_rows, rows, attn_in,
         query_raw, key_raw, query_low, mixed, pairs, soft, out_terms, expert_terms, cosine, sine,
     )
-    inner, outer, query, key, value, output, small = finish_call(
-        dense_out, expert_all.reshape(-1, width), expert_in.shape[1]
+    (
+        block_out, tokens_grad, inner, outer, query, key, value, output, router, gain_a, gain_q, gain_f, gain_k,
+    ) = finish_call(
+        block_out, tokens_grad, dense_out, expert_all.reshape(-1, width), expert_in.shape[1]
     )
     return (
         block_out.reshape(tokens.shape),
         tokens_grad.reshape(tokens.shape),
-        small[:, EXPERTS],
+        gain_a,
         query,
         key,
         value,
-        small[:, EXPERTS + 1],
-        small[: key_gain.shape[0], EXPERTS + 3],
+        gain_q,
+        gain_k,
         output,
-        small[:, EXPERTS + 2],
-        small[:, :EXPERTS],
+        gain_f,
+        router.T,
         inner[None],
         outer[None],
     )

time: 291 us -> 285 us (0.979)
  local copies, waits for them, and re-layouts: 10.1 us -> 0 us
  Pallas kernels: 277 us -> 283 us
    unnamed x7 -> x0, local copies, waits for them, and re-layouts: 6.36 us -> none
    pallas_call x1, Pallas kernels: 99.9 us -> 103 us  [back_call(): pl.pallas_call(kernel, out_shape=[jax.ShapeDtypeStruct((count, width), bf...]
    pallas_call x1, Pallas kernels: 94.4 us -> 97.4 us  [front_call(): pl.pallas_call(kernel, out_shape=[jax.ShapeDtypeStruct((GROUP, ROWS_OWN,...]
    slice x2 -> x0, local copies, waits for them, and re-layouts: 3.03 us -> none  [the longest x1 1.62 us: shards(): small[:, EXPERTS + 2]]
where the time goes in v10:
time: 285 us
  Pallas kernels  283 us (99%)
    pallas_call x1, Pallas kernels, back_call(): pl.pallas_call(kernel, out_shape=[jax.ShapeDtypeStruct((count, width), bf...  103 us
    pallas_call x1, Pallas kernels, front_call(): pl.pallas_call(kernel, out_shape=[jax.ShapeDtypeStruct((GROUP, ROWS_OWN,...  97.4 us
    pallas_call x1, Pallas kernels, moe_call(): pl.pallas_call(kernel, out_shape=[jax.ShapeDtypeStruct((count, columns),...  75.1 us
    pallas_call x1, Pallas kernels, finish_call(): pl.pallas_call(kernel, grid=(steps,), out_shape=[jax.ShapeDtypeStruct(blo...  7.35 us

profile of v10, /device:TPU:0, one launch (start us, length us, event | category | flops | bytes accessed | tf_op | source)
XLA Modules:
  0.0 285.0 jit_solution(2508055543811135562)
XLA Ops:
  0.7 1.0 fusion
  1.6 97.4 %shard_map.246 = (bf16[16,64,3200]{2,1,0:T(8,128)(2,1)}, bf16[16,256,1024]{2,1,0:T(8,128)(2,1)}, bf16[2,8,128,1024]{3,2,1,0:T(8,128)(2,1)}, bf16[2,4,512,1024]{3...) custom-call(s32[2,2]{1,0:T(2,128)} %starts_ref.1, ...), custom_call_target="tpu_custom_call" | custom-call | tf_op jit(solution)/shard_map/pallas_call | solution.py:964
  99.1 75.1 %shard_map.247 = (f32[256,1152]{1,0:T(8,128)}, bf16[16,256,1024]{2,1,0:T(8,128)(2,1)}, bf16[1536,1024]{1,0:T(8,128)(2,1)}) custom-call(bf16[256,1152]{1,0:T(8,128)(2,1)} %get-tuple-element.46.sent_ref, bf16[16,128,1152]{2,1,0:T(8,128)(2,1)} %get-tuple-element.47.first_ref, bf16[16,256,1024]{2,1,0:T(8,128)(2,1)} %get-tuple-element.48.grad_ref, ...), custom_call_target="tpu_custom_call" | custom-call | tf_op jit(solution)/shard_map/pallas_call | solution.py:603
  174.2 103.2 %shard_map.248 = (bf16[256,1024]{1,0:T(8,128)(2,1)}, bf16[256,1024]{1,0:T(8,128)(2,1)}, bf16[64,3200]{1,0:T(8,128)(2,1)}, bf16[8,192,1024]{2,1,0:T(8,128)(2,1)}) custom-call(f32[256,1152]{1,0:T(8,128)} %get-tuple-element.49.returned_ref, f32[256,128]{1,0:T(8,128)} %get-tuple-element.50.gates_ref, f32[256,1024]{1,0:T(8,128)} %get-tuple-element.51.middle_ref, ...), custom_call_target="tpu_custom_call" | custom-call | tf_op jit(solution)/shard_map/pallas_call | solution.py:1411
  277.4 7.3 %shard_map.249 = (bf16[256,1024]{1,0:T(8,128)(2,1)}, bf16[256,1024]{1,0:T(8,128)(2,1)}, f32[1024,1024]{1,0:T(8,128)}, f32[512,1024]{1,0:T(8,128)}, f32[64,1024]{...) custom-call(bf16[256,1024]{1,0:T(8,128)(2,1)} %get-tuple-element.62., ...), custom_call_target="tpu_custom_call" | custom-call | tf_op jit(solution)/shard_map/pallas_call | solution.py:1479
  (2 shorter events, 0.0 us)

commit v11 on v9

--- a/solution.py
+++ b/solution.py
@@ -402,10 +402,9 @@
 
     def kernel(
         sent_ref, first_ref, grad_ref, inner_ref, outer_ref,
-        returned, expert_own, out_terms,
-        rows_in, grads, hidden, back_gu, back, back_staged, back_stage, out_box,
-        term_stage,
-        gs, gr, bs0, br0, bs1, br1, ia, ja, ib, jb, ds_, dr, own_sem, load_sem, box_sem,
+        returned, out_terms, terms,
+        rows_in, grads, hidden, back_gu, back, back_staged, back_stage, out_box, term_box,
+        gs, gr, bs0, br0, bs1, br1, own_sem, load_sem, box_sem, term_sem,
     ):
         place = Place()
         axes, core, shard = place.tokens, place.core, place.shard
@@ -433,30 +432,6 @@
             )
 
         sums = [sum_of(0, bs0, br0), sum_of(1, bs1, br1)]
-        piece = hidden_width // REPS
-
-        def inner_part(part):
-            def rows(which, low, n):
-                at = chip_of(which)
-                return out_box.at[part, lax.div(at, 2), pl.ds(lax.rem(at, 2) * piece + low, n)]
-
-            return rows
-
-        def down_part(which, low, n):
-            at = chip_of(which)
-            return back_gu.at[0, lax.div(at, 2), pl.ds(lax.rem(at, 2) * piece + low, n)]
-
-        inner_sums = [
-            sum_parts(
-                place.copies, Line(send_sem, recv_sem), inner_part(part), term_stage.at[part], piece,
-                expert_own.at[pl.ds(part * piece, piece)],
-            )
-            for part, (send_sem, recv_sem) in enumerate(((ia, ja), (ib, jb)))
-        ]
-        down_sum = sum_parts(
-            place.copies, Line(ds_, dr), down_part, term_stage.at[2], piece,
-            expert_own.at[pl.ds(2 * piece, piece)],
-        )
 
         def loads(t):
             at = pl.ds(t * wide, wide)
@@ -527,7 +502,7 @@
             for load in loads(t):
                 load.start()
         second_grads.start()
-        greet(axes.neighbours() + place.copies.neighbours() + [place.twin])
+        greet(axes.neighbours() + [place.twin])
         next(gather)
 
         def first_tiles(t, carry):
@@ -574,20 +549,39 @@
         next(sums[1])
         next(sums[1])
 
+        def term_copy(low, slot):
+            return pltpu.make_async_copy(
+                term_box.at[slot], terms.at[pl.ds(low, 256)], term_sem.at[slot]
+            )
+
         every = 2 * GROUP * half
-        for slot in range(2):
-            box_copy(1, 0, slot).wait()
-
-        def begin(part):
-            for _ in range(3):
-                next(part)
+
+        def keep(index, low, value):
+            slot = lax.rem(index, 2)
+
+            @pl.when(index >= 2)
+            def _():
+                term_copy(low, slot).wait()
+
+            term_box[slot] = value.astype(bf16)
+            term_copy(low, slot).start()
+
+        downs = hidden_width // 256
+
+        def down_terms(index, carry):
+            at = chunk_256(index)
+            value = dot_tn(hidden[:, :, :, at].reshape(every, 256), grads[...].reshape(every, width))
+            keep(index, pl.multiple_of(width + index * 256, 256), value)
+            return carry
+
+        lax.fori_loop(0, downs, down_terms, 0)
 
         def inner_terms(index, carry):
             hooks(
                 index,
                 (
-                    (2, lambda: (begin(inner_sums[0]), next(sums[0]))[0]),
-                    (3, lambda: next(sums[1])),
+                    (0, lambda: next(sums[0])),
+                    (1, lambda: next(sums[1])),
                 ),
             )
             at = chunk_256(index)
@@ -595,46 +589,27 @@
                 rows_in[:, :, :, at].reshape(every, 256),
                 back_gu[...].reshape(every, 2 * hidden_width),
             )
-            out_box[lax.div(index, 2), pl.ds(2 * lax.rem(index, 2), 2)] = value.astype(bf16).reshape(
-                2, half, width
-            )
+            keep(index + downs, pl.multiple_of(index * 256, 256), value)
             return carry
 
         lax.fori_loop(0, width // 256, inner_terms, 0)
-        begin(inner_sums[1])
-
-        def down_terms(index, carry):
-            hooks(index, ((1, lambda: next(inner_sums[0])),))
-            at = chunk_256(index)
-            value = dot_tn(hidden[:, :, :, at].reshape(every, 256), grads[...].reshape(every, width))
-            back_gu[0, pl.ds(2 * index, 2)] = value.astype(bf16).reshape(2, half, width)
-            return carry
-
-        lax.fori_loop(0, hidden_width // 256, down_terms, 0)
-        begin(down_sum)
         drained(sums[0])
-        next(inner_sums[1])
-        next(inner_sums[0])
-        next(sums[1])
-        next(down_sum)
-        next(inner_sums[1])
-        drained(inner_sums[0])
-        next(down_sum)
         drained(sums[1])
-        drained(inner_sums[1])
-        drained(down_sum)
         drained(gather)
-
-    own_rows = (width + hidden_width) // REPS
+        for slot in range(2):
+            box_copy(1, 0, slot).wait()
+            term_copy(0, slot).wait()
+
+    term_rows = width + hidden_width
     return pl.pallas_call(
         kernel,
         out_shape=[
-            jax.ShapeDtypeStruct((count, columns), bf16),
-            jax.ShapeDtypeStruct((own_rows, width), bf16),
+            jax.ShapeDtypeStruct((count, columns), f32),
             jax.ShapeDtypeStruct((GROUP, count, width), bf16),
+            jax.ShapeDtypeStruct((term_rows, width), bf16),
         ],
         in_specs=[ANY, ANY, ANY, IN_VMEM, IN_VMEM],
-        out_specs=[IN_VMEM, IN_VMEM, ANY],
+        out_specs=[IN_VMEM, ANY, ANY],
         scratch_shapes=[
             pltpu.VMEM((2, GROUP, half, columns), bf16),
             pltpu.VMEM((2, GROUP, half, width), bf16),
@@ -644,13 +619,14 @@
             pltpu.VMEM((2, chips, half, columns), bf16),
             pltpu.VMEM((2, stage_rows(half), columns), bf16),
             pltpu.VMEM((2, wide, half, width), bf16),
-            pltpu.VMEM((3, stage_rows(hidden_width // REPS), width), bf16),
+            pltpu.VMEM((2, 256, width), bf16),
         ]
         + sems(GATHER_SEMS)
-        + sems(SUM_SEMS) * 5
+        + sems(SUM_SEMS) * 2
         + [
             pltpu.SemaphoreType.DMA,
             pltpu.SemaphoreType.DMA((rounds + 1, 2)),
+            pltpu.SemaphoreType.DMA((2,)),
             pltpu.SemaphoreType.DMA((2,)),
         ],
         compiler_params=params(collective_id),
@@ -1041,12 +1017,13 @@
 
 def back_call(
     collective_id, returned, gates, middle, sent, dense, cotangent, tokens, attn_in, query_raw, key_raw,
-    query_low, mixed, pairs, soft, out_terms, expert_own, cosine, sine,
+    query_low, mixed, pairs, soft, out_terms, expert_terms, cosine, sine,
 ):
     count, width = tokens.shape
     seqs, _, positions, _ = pairs.shape
     length = REPS * positions
-    expert_rows = expert_own.shape[0]
+    expert_rows = expert_terms.shape[0] // REPS
+    side_rows = RING * expert_rows
     score_scale = HEAD_DIM ** (-0.5)
     chips = GROUP // 2
 
@@ -1058,10 +1035,11 @@
         weight_box, weight_rest, wide_terms, rest_terms, dense_own,
         wide_staged, rest_staged, wide_stage, rest_stage,
         out_held, out_staged, out_stage, small_terms, small_staged, small_stage, small_own,
+        expert_stage, expert_own,
         soft_box, key_box, value_box, pair_terms, pair_stage, pair_grads,
         grad_mixed, grad_query, grad_middle, grad_attn, grad_attn_in, gain_box,
         wide_got, rest_got, small_got, wide_total_box, rest_total_box,
-        out_s, out_r, small_s, small_r, kv0_s, kv0_r, kva_s, kva_r, kvb_s, kvb_r, wide_s, wide_r, rest_s, rest_r,
+        out_s, out_r, exp_s, exp_r, small_s, small_r, kv0_s, kv0_r, kva_s, kva_r, kvb_s, kvb_r, wide_s, wide_r, rest_s, rest_r,
         ge_s, ge_r, gwide_s, gwide_r, grest_s, grest_r, gsmall_s, gsmall_r,
         load_sem, held_sem, box_sem, own_sem, total_sem,
     ):
@@ -1087,6 +1065,14 @@
              lambda which: out_staged.at[chip_of(which)]),
             store=out_store,
         )
+        def expert_part(which, low, n):
+            columns = pl.ds(pl.multiple_of(which[0] * width, width), width)
+            return wide_terms.at[pl.ds(which[1] * expert_rows + low, n), columns]
+
+        expert_sum = sum_parts(
+            copy_axes, Line(exp_s, exp_r), expert_part, expert_stage, expert_rows, expert_own
+        )
+
         def pair_sum(seq, low, size, index, send_sem, recv_sem):
             columns = pl.ds(low, size)
             return sum_parts(
@@ -1139,10 +1125,14 @@
         )
         small_total = spread_parts(place, Line(gsmall_s, gsmall_r), small_own, small_got, small_out)
         expert_gather = gather_parts(
-            copy_axes, Line(ge_s, ge_r), expert_ref,
+            copy_axes, Line(ge_s, ge_r), expert_own,
             lambda which, row, n, other=False: expert_all.at[chip_of(which), pl.ds(row, n)],
             expert_rows, own_sem,
         )
+
+        def begin(part):
+            for _ in range(3):
+                next(part)
 
         def weight_load(low, index):
             return pltpu.make_async_copy(
@@ -1152,6 +1142,14 @@
         rest_load = pltpu.make_async_copy(
             dense_ref.at[:, :, pl.ds(AT_K, REST)], weight_rest, load_sem.at[1]
         )
+        expert_loads = [
+            pltpu.make_async_copy(
+                expert_ref.at[pl.ds(side * side_rows, side_rows)],
+                wide_terms.at[pl.ds(0, side_rows), pl.ds(side * width, width)],
+                load_sem.at[(2, 4)[side]],
+            )
+            for side in range(2)
+        ]
         held_loads = [
             pltpu.make_async_copy(
                 out_ref.at[2 * chip + core], out_held.at[chip], held_sem.at[chip]
@@ -1175,6 +1173,8 @@
                 ),
             ]
 
+        for load in expert_loads:
+            load.start()
         rest_load.start()
         weight_load(AT_O, 0).start()
         for load in held_loads + box_loads(0, 0):
@@ -1185,6 +1185,9 @@
             + [(place.shard, other) for other in place.others[1:]]
         )
         next(out_sum)
+        for load in expert_loads:
+            load.wait()
+        begin(expert_sum)
         rest_load.wait()
 
         small = weight_rest[:, :, pl.ds(2 * KEY, SMALL)].reshape(width, SMALL)
@@ -1254,12 +1257,8 @@
             next(out_sum)
             next(out_sum)
 
-        def begin(part):
-            for _ in range(3):
-                next(part)
-
         def first_heads(index, carry):
-            hooks(index, ((2, out_ready),))
+            hooks(index, ((2, lambda: next(expert_sum)), (3, out_ready)))
             attend_back(0, index)
             return carry
 
@@ -1270,9 +1269,8 @@
             hooks(
                 index,
                 (
-                    (1, lambda: next(out_sum)),
                     (2, lambda: begin(second_pairs[0])),
-                    (3, lambda: next(first_pairs)),
+                    (3, lambda: (next(out_sum), next(expert_sum))[0]),
                 ),
             )
             attend_back(1, index)
@@ -1303,9 +1301,12 @@
         weight_load(0, 3).wait()
         grad_attn_in[...] = dot_nt(grad_query_low, weight_box[...].reshape(width, QUERY))
 
+        next(first_pairs)
         next(second_pairs[1])
         next(first_pairs)
         next(second_pairs[0])
+
+        drained(expert_sum)
 
         def q_rows(index, carry):
             at = chunk_256(index)
@@ -1402,6 +1403,8 @@
         pltpu.VMEM((chips, ROWS_OWN, SMALL), bf16),
         pltpu.VMEM((stage_rows(ROWS_OWN), SMALL), bf16),
         pltpu.VMEM((ROWS_OWN, SMALL), bf16),
+        pltpu.VMEM((stage_rows(expert_rows), width), bf16),
+        pltpu.VMEM((expert_rows, width), bf16),
         pltpu.VMEM((2, 4 * positions, length), bf16),
         pltpu.VMEM((2, REPS, positions, LANES), bf16),
         pltpu.VMEM((2, REPS, positions, LANES), bf16),
@@ -1435,11 +1438,11 @@
         in_specs=[IN_VMEM] * 4 + [ANY] + [IN_VMEM] * 7 + [ANY] * 4 + [IN_VMEM] * 2,
         out_specs=[IN_VMEM, IN_VMEM, IN_VMEM, ANY, ANY],
         scratch_shapes=scratch
-        + sems(SUM_SEMS) * 7
+        + sems(SUM_SEMS) * 8
         + sems(GATHER_SEMS)
         + sems(TOTAL_SEMS) * 3
         + [
-            pltpu.SemaphoreType.DMA((4,)),
+            pltpu.SemaphoreType.DMA((5,)),
             pltpu.SemaphoreType.DMA((chips,)),
             pltpu.SemaphoreType.DMA((2, 3)),
             pltpu.SemaphoreType.DMA,
@@ -1448,64 +1451,73 @@
         compiler_params=params(collective_id),
     )(
         returned, gates, middle, sent, dense, cotangent, tokens, attn_in, query_raw, key_raw,
-        query_low, mixed, pairs, soft, out_terms, expert_own, cosine, sine,
+        query_low, mixed, pairs, soft, out_terms, expert_terms, cosine, sine,
     )
 
 
-def finish_call(block_out, tokens_grad, small_sum, dense_own, expert_all):
-    reps, expert_rows, width = expert_all.shape
-    piece = expert_rows // 3
-    rows = block_out.shape[0] // reps
+def finish_call(block_out, tokens_grad, small_sum, dense_own, expert_all, inner_rows):
+    total_rows, width = expert_all.shape
+    step = 256
+    inner_steps, steps = inner_rows // step, total_rows // step
+    rows = block_out.shape[0] // inner_steps
 
     def kernel(
         block_ref, tokens_ref, small_ref, dense_ref, expert_ref,
         block, tokens, inner, outer, query, key, value, output, router, gain_a, gain_q, gain_f, gain_k,
     ):
-        block[...] = block_ref[...]
-        tokens[...] = tokens_ref[...]
-        inner[0] = expert_ref[0, :piece].astype(f32)
-        inner[1] = expert_ref[0, piece : 2 * piece].astype(f32)
-        outer[...] = expert_ref[0, 2 * piece :].astype(f32)
-
-        @pl.when(pl.program_id(0) == 1)
+        at = pl.program_id(0)
+
+        @pl.when(at < inner_steps)
+        def _():
+            block[...] = block_ref[...]
+            tokens[...] = tokens_ref[...]
+            inner[...] = expert_ref[...].astype(f32)
+
+        @pl.when(at >= inner_steps)
+        def _():
+            outer[...] = expert_ref[...].astype(f32)
+
+        @pl.when(at == 1)
         def _():
             at_k = QUERY + WIDTH
             for low, target in ((0, query), (at_k, key), (at_k + KEY, value), (QUERY, output)):
                 target[...] = dense_ref[:, pl.ds(low, target.shape[1])].astype(f32)
             turned_small = jnp.transpose(small_ref[...])
             router[...] = turned_small[:EXPERTS, :ROWS_OWN]
-            for at, target in enumerate((gain_a, gain_q, gain_f, gain_k)):
+            for index, target in enumerate((gain_a, gain_q, gain_f, gain_k)):
                 size = target.shape[0]
-                target[...] = turned_small[EXPERTS + at, :size].reshape(size)
+                target[...] = turned_small[EXPERTS + index, :size].reshape(size)
 
     def whole(*shape):
         return pl.BlockSpec(shape, lambda i: (0,) * len(shape))
 
-    by_rows = pl.BlockSpec((rows, width), lambda i: (i, 0))
+    def by_rows(size):
+        return pl.BlockSpec((size, width), lambda i: (jnp.minimum(i, inner_steps - 1), 0))
+
     shapes = [(ROWS_OWN, QUERY), (ROWS_OWN, KEY), (ROWS_OWN, KEY), (ROWS_OWN, WIDTH)]
     shapes += [(EXPERTS, ROWS_OWN), (ROWS_OWN,), (ROWS_OWN,), (ROWS_OWN,), (KGAIN_OWN,)]
     return pl.pallas_call(
         kernel,
-        grid=(reps,),
+        grid=(steps,),
         out_shape=[
             jax.ShapeDtypeStruct(block_out.shape, bf16),
             jax.ShapeDtypeStruct(tokens_grad.shape, bf16),
-            jax.ShapeDtypeStruct((2, reps * piece, width), f32),
-            jax.ShapeDtypeStruct((reps * piece, width), f32),
+            jax.ShapeDtypeStruct((inner_rows, width), f32),
+            jax.ShapeDtypeStruct((total_rows - inner_rows, width), f32),
         ]
         + [jax.ShapeDtypeStruct(shape, f32) for shape in shapes],
         in_specs=[
-            by_rows,
-            by_rows,
+            by_rows(rows),
+            by_rows(rows),
             whole(*small_sum.shape),
             whole(*dense_own.shape),
-            pl.BlockSpec((1, expert_rows, width), lambda i: (i, 0, 0)),
+            pl.BlockSpec((step, width), lambda i: (i, 0)),
         ],
         out_specs=[
-            by_rows,
-            by_rows,
-            pl.BlockSpec((2, piece, width), lambda i: (0, i, 0)),
-            pl.BlockSpec((piece, width), lambda i: (i, 0)),
+            by_rows(rows),
+            by_rows(rows),
+            by_rows(step),
+            pl.BlockSpec((step, width), lambda i: (jnp.maximum(i - inner_steps, 0), 0)),
         ]
         + [whole(*shape) for shape in shapes],
         compiler_params=pltpu.CompilerParams(vmem_limit_bytes=VMEM_LIMIT),
@@ -1553,16 +1565,18 @@
         (attn_gain, query_gain, ffn_gain, key_gain), router_weight.T,
         cosine, sine, jnp.transpose(routes, (0, 2, 1)), picture_starts,
     )
-    returned, expert_own, out_terms = moe_call(
+    returned, out_terms, expert_terms = moe_call(
         2, sent, rows_first, grad_all, expert_in[0], expert_down[0]
     )
     block_out, tokens_grad, small_sum, dense_out, expert_all = back_call(
         3, returned, gates, middle, sent, dense, grad_rows, rows, attn_in,
-        query_raw, key_raw, query_low, mixed, pairs, soft, out_terms, expert_own, cosine, sine,
+        query_raw, key_raw, query_low, mixed, pairs, soft, out_terms, expert_terms, cosine, sine,
     )
     (
         block_out, tokens_grad, inner, outer, query, key, value, output, router, gain_a, gain_q, gain_f, gain_k,
-    ) = finish_call(block_out, tokens_grad, small_sum, dense_out, expert_all)
+    ) = finish_call(
+        block_out, tokens_grad, small_sum, dense_out, expert_all.reshape(-1, width), expert_in.shape[1]
+    )
     return (
         block_out.reshape(tokens.shape),
         tokens_grad.reshape(tokens.shape),
@@ -1575,7 +1589,7 @@
         output,
         gain_f,
         router.T,
-        inner.reshape(expert_in.shape),
+        inner[None],
         outer[None],
     )
 

time: 296 us -> 284 us (0.959)
  Pallas kernels: 294 us -> 282 us
    pallas_call x1, Pallas kernels: 82.6 us -> 75.1 us  [moe_call(): pl.pallas_call(kernel, out_shape=[jax.ShapeDtypeStruct((count, columns),...]
    pallas_call x1, Pallas kernels: 106 us -> 102 us  [back_call(): pl.pallas_call(kernel, out_shape=[jax.ShapeDtypeStruct((count, width), bf...]
where the time goes in v11:
time: 284 us
  Pallas kernels  282 us (99%)
    pallas_call x1, Pallas kernels, back_call(): pl.pallas_call(kernel, out_shape=[jax.ShapeDtypeStruct((count, width), bf...  102 us
    pallas_call x1, Pallas kernels, front_call(): pl.pallas_call(kernel, out_shape=[jax.ShapeDtypeStruct((GROUP, ROWS_OWN,...  97.4 us
    pallas_call x1, Pallas kernels, moe_call(): pl.pallas_call(kernel, out_shape=[jax.ShapeDtypeStruct((count, columns),...  75.1 us
    pallas_call x1, Pallas kernels, finish_call(): pl.pallas_call(kernel, grid=(steps,), out_shape=[jax.ShapeDtypeStruct(blo...  7.28 us

profile of v11, /device:TPU:0, one launch (start us, length us, event | category | flops | bytes accessed | tf_op | source)
XLA Modules:
  0.0 284.1 jit_solution(2673969335603081425)
XLA Ops:
  0.7 1.0 fusion
  1.6 97.4 %shard_map.246 = (bf16[16,64,3200]{2,1,0:T(8,128)(2,1)}, bf16[16,256,1024]{2,1,0:T(8,128)(2,1)}, bf16[2,8,128,1024]{3,2,1,0:T(8,128)(2,1)}, bf16[2,4,512,1024]{3...) custom-call(s32[2,2]{1,0:T(2,128)} %starts_ref.1, ...), custom_call_target="tpu_custom_call" | custom-call | tf_op jit(solution)/shard_map/pallas_call | solution.py:966
  99.1 75.1 %shard_map.247 = (f32[256,1152]{1,0:T(8,128)}, bf16[16,256,1024]{2,1,0:T(8,128)(2,1)}, bf16[1536,1024]{1,0:T(8,128)(2,1)}) custom-call(bf16[256,1152]{1,0:T(8,128)(2,1)} %get-tuple-element.47.sent_ref, bf16[16,128,1152]{2,1,0:T(8,128)(2,1)} %get-tuple-element.48.first_ref, bf16[16,256,1024]{2,1,0:T(8,128)(2,1)} %get-tuple-element.49.grad_ref, ...), custom_call_target="tpu_custom_call" | custom-call | tf_op jit(solution)/shard_map/pallas_call | solution.py:604
  174.2 102.5 %shard_map.248 = (bf16[256,1024]{1,0:T(8,128)(2,1)}, bf16[256,1024]{1,0:T(8,128)(2,1)}, f32[64,128]{1,0:T(8,128)}, bf16[64,3072]{1,0:T(8,128)(2,1)}, bf16[8,192,1024]{2,1,0:T(8,128)(2,1)}) custom-call(f32[256,1152]{1,0:T(8,128)} %get-tuple-element.50.returned_ref, f32[256,128]{1,0:T(8,128)} %get-tuple-element.51.gates_ref, ...), custom_call_target="tpu_custom_call" | custom-call | tf_op jit(solution)/shard_map/pallas_call | solution.py:1429
  276.7 7.3 %shard_map.249 = (bf16[256,1024]{1,0:T(8,128)(2,1)}, bf16[256,1024]{1,0:T(8,128)(2,1)}, f32[1024,1024]{1,0:T(8,128)}, f32[512,1024]{1,0:T(8,128)}, f32[64,1024]{...) custom-call(bf16[256,1024]{1,0:T(8,128)(2,1)} %get-tuple-element.63., ...), custom_call_target="tpu_custom_call" | custom-call | tf_op jit(solution)/shard_map/pallas_call | solution.py:1499
  (2 shorter events, 0.0 us)

commit v12 on v11

--- a/solution.py
+++ b/solution.py
@@ -1459,46 +1459,49 @@
     total_rows, width = expert_all.shape
     step = 256
     inner_steps, steps = inner_rows // step, total_rows // step
-    rows = block_out.shape[0] // inner_steps
 
     def kernel(
         block_ref, tokens_ref, small_ref, dense_ref, expert_ref,
         block, tokens, inner, outer, query, key, value, output, router, gain_a, gain_q, gain_f, gain_k,
+        low_box, full_box, load_sem, store_sem, row_sem,
     ):
-        at = pl.program_id(0)
-
-        @pl.when(at < inner_steps)
-        def _():
-            block[...] = block_ref[...]
-            tokens[...] = tokens_ref[...]
-            inner[...] = expert_ref[...].astype(f32)
-
-        @pl.when(at >= inner_steps)
-        def _():
-            outer[...] = expert_ref[...].astype(f32)
-
-        @pl.when(at == 1)
-        def _():
-            at_k = QUERY + WIDTH
-            for low, target in ((0, query), (at_k, key), (at_k + KEY, value), (QUERY, output)):
-                target[...] = dense_ref[:, pl.ds(low, target.shape[1])].astype(f32)
-            turned_small = jnp.transpose(small_ref[...])
-            router[...] = turned_small[:EXPERTS, :ROWS_OWN]
-            for index, target in enumerate((gain_a, gain_q, gain_f, gain_k)):
-                size = target.shape[0]
-                target[...] = turned_small[EXPERTS + index, :size].reshape(size)
-
-    def whole(*shape):
-        return pl.BlockSpec(shape, lambda i: (0,) * len(shape))
-
-    def by_rows(size):
-        return pl.BlockSpec((size, width), lambda i: (jnp.minimum(i, inner_steps - 1), 0))
+        moves = [
+            pltpu.make_async_copy(block_ref, block, row_sem.at[0]),
+            pltpu.make_async_copy(tokens_ref, tokens, row_sem.at[1]),
+        ]
+        loads, stores = [], []
+        for at in range(steps):
+            loads.append(
+                pltpu.make_async_copy(
+                    expert_ref.at[pl.ds(at * step, step)], low_box.at[at], load_sem.at[at]
+                )
+            )
+            if at < inner_steps:
+                target = inner.at[pl.ds(at * step, step)]
+            else:
+                target = outer.at[pl.ds((at - inner_steps) * step, step)]
+            stores.append(pltpu.make_async_copy(full_box.at[at], target, store_sem.at[at]))
+        for copy in loads + moves:
+            copy.start()
+        for at in range(steps):
+            loads[at].wait()
+            full_box[at] = low_box[at].astype(f32)
+            stores[at].start()
+        at_k = QUERY + WIDTH
+        for low, target in ((0, query), (at_k, key), (at_k + KEY, value), (QUERY, output)):
+            target[...] = dense_ref[:, pl.ds(low, target.shape[1])].astype(f32)
+        turned_small = jnp.transpose(small_ref[...])
+        router[...] = turned_small[:EXPERTS, :ROWS_OWN]
+        for index, target in enumerate((gain_a, gain_q, gain_f, gain_k)):
+            size = target.shape[0]
+            target[...] = turned_small[EXPERTS + index, :size].reshape(size)
+        for copy in stores + moves:
+            copy.wait()
 
     shapes = [(ROWS_OWN, QUERY), (ROWS_OWN, KEY), (ROWS_OWN, KEY), (ROWS_OWN, WIDTH)]
     shapes += [(EXPERTS, ROWS_OWN), (ROWS_OWN,), (ROWS_OWN,), (ROWS_OWN,), (KGAIN_OWN,)]
     return pl.pallas_call(
         kernel,
-        grid=(steps,),
         out_shape=[
             jax.ShapeDtypeStruct(block_out.shape, bf16),
             jax.ShapeDtypeStruct(tokens_grad.shape, bf16),
@@ -1506,20 +1509,15 @@
             jax.ShapeDtypeStruct((total_rows - inner_rows, width), f32),
         ]
         + [jax.ShapeDtypeStruct(shape, f32) for shape in shapes],
-        in_specs=[
-            by_rows(rows),
-            by_rows(rows),
-            whole(*small_sum.shape),
-            whole(*dense_own.shape),
-            pl.BlockSpec((step, width), lambda i: (i, 0)),
+        in_specs=[ANY, ANY, IN_VMEM, IN_VMEM, ANY],
+        out_specs=[ANY] * 4 + [IN_VMEM] * len(shapes),
+        scratch_shapes=[
+            pltpu.VMEM((steps, step, width), bf16),
+            pltpu.VMEM((steps, step, width), f32),
+            pltpu.SemaphoreType.DMA((steps,)),
+            pltpu.SemaphoreType.DMA((steps,)),
+            pltpu.SemaphoreType.DMA((2,)),
         ],
-        out_specs=[
-            by_rows(rows),
-            by_rows(rows),
-            by_rows(step),
-            pl.BlockSpec((step, width), lambda i: (jnp.maximum(i - inner_steps, 0), 0)),
-        ]
-        + [whole(*shape) for shape in shapes],
         compiler_params=pltpu.CompilerParams(vmem_limit_bytes=VMEM_LIMIT),
     )(block_out, tokens_grad, small_sum, dense_own, expert_all)
 

time: 284 us -> 312 us (1.099)
  Pallas kernels: 282 us -> 310 us
    pallas_call x1, Pallas kernels: 7.28 us -> 34.9 us  [finish_call(): pl.pallas_call(kernel, out_shape=[jax.ShapeDtypeStruct(block_out.shape, b...]
where the time goes in v12:
time: 312 us
  Pallas kernels  310 us (99%)
    pallas_call x1, Pallas kernels, back_call(): pl.pallas_call(kernel, out_shape=[jax.ShapeDtypeStruct((count, width), bf...  102 us
    pallas_call x1, Pallas kernels, front_call(): pl.pallas_call(kernel, out_shape=[jax.ShapeDtypeStruct((GROUP, ROWS_OWN,...  97.4 us
    pallas_call x1, Pallas kernels, moe_call(): pl.pallas_call(kernel, out_shape=[jax.ShapeDtypeStruct((count, columns),...  75.1 us
    pallas_call x1, Pallas kernels, finish_call(): pl.pallas_call(kernel, out_shape=[jax.ShapeDtypeStruct(block_out.shape, b...  34.9 us

profile of v12, /device:TPU:0, one launch (start us, length us, event | category | flops | bytes accessed | tf_op | source)
XLA Modules:
  0.0 311.8 jit_solution(12817641342043567140)
XLA Ops:
  0.7 1.0 fusion
  1.6 97.4 %shard_map.246 = (bf16[16,64,3200]{2,1,0:T(8,128)(2,1)}, bf16[16,256,1024]{2,1,0:T(8,128)(2,1)}, bf16[2,8,128,1024]{3,2,1,0:T(8,128)(2,1)}, bf16[2,4,512,1024]{3...) custom-call(s32[2,2]{1,0:T(2,128)} %starts_ref.1, ...), custom_call_target="tpu_custom_call" | custom-call | tf_op jit(solution)/shard_map/pallas_call | solution.py:966
  99.1 75.1 %shard_map.247 = (f32[256,1152]{1,0:T(8,128)}, bf16[16,256,1024]{2,1,0:T(8,128)(2,1)}, bf16[1536,1024]{1,0:T(8,128)(2,1)}) custom-call(bf16[256,1152]{1,0:T(8,128)(2,1)} %get-tuple-element.47.sent_ref, bf16[16,128,1152]{2,1,0:T(8,128)(2,1)} %get-tuple-element.48.first_ref, bf16[16,256,1024]{2,1,0:T(8,128)(2,1)} %get-tuple-element.49.grad_ref, ...), custom_call_target="tpu_custom_call" | custom-call | tf_op jit(solution)/shard_map/pallas_call | solution.py:604
  174.2 102.5 %shard_map.248 = (bf16[256,1024]{1,0:T(8,128)(2,1)}, bf16[256,1024]{1,0:T(8,128)(2,1)}, f32[64,128]{1,0:T(8,128)}, bf16[64,3072]{1,0:T(8,128)(2,1)}, bf16[8,192,1024]{2,1,0:T(8,128)(2,1)}) custom-call(f32[256,1152]{1,0:T(8,128)} %get-tuple-element.50.returned_ref, f32[256,128]{1,0:T(8,128)} %get-tuple-element.51.gates_ref, ...), custom_call_target="tpu_custom_call" | custom-call | tf_op jit(solution)/shard_map/pallas_call | solution.py:1429
  276.7 34.9 %shard_map.249 = (bf16[256,1024]{1,0:T(8,128)(2,1)}, bf16[256,1024]{1,0:T(8,128)(2,1)}, f32[1024,1024]{1,0:T(8,128)}, f32[512,1024]{1,0:T(8,128)}, f32[64,1024]{...) custom-call(bf16[256,1024]{1,0:T(8,128)(2,1)} %get-tuple-element.63., ...), custom_call_target="tpu_custom_call" | custom-call | tf_op jit(solution)/shard_map/pallas_call | solution.py:1503
  (2 shorter events, 0.0 us)
